TPU v7x, 32 devices: a whole 2x2x4 slice. The times are simulated.
32 devices in a mesh: seq: 8 (over y, x, core), section: 4 (over z).
Axes of the slice: x: 2, y: 2, z: 4, core: 2. Of those that a mesh axis runs over, the one named last changes fastest.
Arguments:
- queries: bfloat16 [4, 1024, 2048], P('section', 'seq'), may hold values from -60 to 60
- keys_in: bfloat16 [4, 1024, 2048], P('section', 'seq'), may hold values from -15 to 15
- values: bfloat16 [4, 1024, 2048], P('section', 'seq'), may hold values from -6 to 6
- out_grads: bfloat16 [4, 1024, 2048], P('section', 'seq'), may hold values from -6 to 6
- offsets: int32 [3, 16], replicated, may hold values from 0 to 7
Outputs:
- grad_queries: bfloat16 [4, 1024, 2048], P('section', 'seq')
- grad_keys: bfloat16 [4, 1024, 2048], P('section', 'seq')
- grad_values: bfloat16 [4, 1024, 2048], P('section', 'seq')
Inputs may be any that keep to these rules, and one draw needn't show every extreme that they name: Level l uses offsets[l - 1, h] modulo 2^l.
All inputs are finite; a program needn't handle non-finite values.
Results may differ from a plain program's by a relative error of at most 0.029.
Values may be sent and summed in bfloat16 or wider, within the bound.
No kernel may reach another device: no remote copies, remote signals or barrier semaphores. Data moves between devices by JAX's collectives and lax.ppermute only.
A program may use at most 64 MiB of HBM per device.

v0:
```python
import jax
import jax.numpy as jnp
from jax import lax
from jax.sharding import PartitionSpec as P


def shifted(value, axis, steps):
    count = lax.axis_size(axis)
    pairs = [(source, (source + steps) % count) for source in range(count)]
    return lax.ppermute(value, axis, pairs)


def partner(block, axis, stride):
    count = lax.axis_size(axis)
    route = []
    for low in range(count):
        high = low | 1 << stride
        if high != low and high < count:
            route += [(low, high), (high, low)]
    return lax.ppermute(block, axis, route)


def pick_rows(tile_rows, dilation, chosen):
    row_count, head_count, head_dim = tile_rows.shape
    shaped = tile_rows.reshape(row_count // dilation, dilation, head_count, head_dim)
    keep_mask = (
        jnp.arange(dilation, dtype=jnp.int32)[None, :, None, None]
        == (chosen % dilation)[None, None, :, None]
    )
    return jnp.sum(jnp.where(keep_mask, shaped, jnp.zeros((), tile_rows.dtype)), axis=1)


def spread_rows(row_values, dilation, chosen):
    row_count, head_count, head_dim = row_values.shape
    keep_mask = (
        jnp.arange(dilation, dtype=jnp.int32)[None, :, None, None]
        == (chosen % dilation)[None, None, :, None]
    )
    spread = jnp.where(keep_mask, row_values[:, None], jnp.zeros((), row_values.dtype))
    return spread.reshape(row_count * dilation, head_count, head_dim)


def pick_stat(row_stat, dilation, chosen):
    head_count, row_count = row_stat.shape
    shaped = row_stat.reshape(head_count, row_count // dilation, dilation)
    keep_mask = (
        jnp.arange(dilation, dtype=jnp.int32)[None, None, :] == (chosen % dilation)[:, None, None]
    )
    return jnp.sum(jnp.where(keep_mask, shaped, 0.0), axis=2)


def spread_stat(row_stat, dilation, chosen, fill_value):
    head_count, row_count = row_stat.shape
    keep_mask = (
        jnp.arange(dilation, dtype=jnp.int32)[None, None, :] == (chosen % dilation)[:, None, None]
    )
    return jnp.where(keep_mask, row_stat[:, :, None], fill_value).reshape(
        head_count, row_count * dilation
    )


def doubling(stacked, depth, concat_axis, passer):
    my_index = lax.axis_index("seq")
    for bit in range(depth):
        received = passer(stacked, bit)
        low_side = jnp.bitwise_and(jnp.right_shift(my_index, bit), 1) == 0
        stacked = jnp.where(
            low_side,
            jnp.concatenate([stacked, received], concat_axis),
            jnp.concatenate([received, stacked], concat_axis),
        )
    return stacked


def halving(stacked, depth, passer):
    my_index = lax.axis_index("seq")
    for bit in reversed(range(depth)):
        middle = stacked.shape[1] // 2
        lower = stacked[:, :middle]
        upper = stacked[:, middle:]
        low_side = jnp.bitwise_and(jnp.right_shift(my_index, bit), 1) == 0
        kept = jnp.where(low_side, lower, upper)
        outgoing = jnp.where(low_side, upper, lower)
        stacked = kept + passer(outgoing, bit)
    return stacked


def per_device(queries, keys_in, values, out_grads, offsets):
    levels = offsets.shape[0]
    head_count = offsets.shape[1]
    tok_rows = queries.shape[1]
    head_dim = queries.shape[2] // head_count
    score_scale = head_dim ** (-0.5)
    arrived = shifted(out_grads, "section", -1)
    query_rows = queries[0].reshape(tok_rows, head_count, head_dim)
    key_rows = keys_in[0].reshape(tok_rows, head_count, head_dim)
    value_rows = values[0].reshape(tok_rows, head_count, head_dim)
    grad_rows = arrived[0].reshape(tok_rows, head_count, head_dim)
    sel_q = [query_rows]
    sel_g = [grad_rows]
    sel_k = [key_rows]
    sel_v = [value_rows]
    key_sets = [key_rows]
    value_sets = [value_rows]
    for bit_level in range(levels):
        dilation = 2 ** (bit_level + 1)
        chosen = offsets[bit_level]
        kept_keys = pick_rows(key_rows, dilation, chosen)
        kept_values = pick_rows(value_rows, dilation, chosen)
        grouped = doubling(
            jnp.stack([kept_keys, kept_values]),
            bit_level + 1,
            1,
            lambda tile, bit: partner(tile, "seq", bit),
        )
        sel_q.append(pick_rows(query_rows, dilation, chosen))
        sel_g.append(pick_rows(grad_rows, dilation, chosen))
        sel_k.append(kept_keys)
        sel_v.append(kept_values)
        key_sets.append(grouped[0])
        value_sets.append(grouped[1])
    scores = [
        jnp.einsum("qhe,khe->hqk", sel_q[i], key_sets[i], preferred_element_type=jnp.float32)
        * score_scale
        for i in range(levels + 1)
    ]
    part_lse = [jax.nn.logsumexp(level_scores, axis=-1) for level_scores in scores]
    total_lse = part_lse[0]
    for bit_level in range(levels):
        total_lse = jnp.logaddexp(
            total_lse,
            spread_stat(
                part_lse[bit_level + 1], 2 ** (bit_level + 1), offsets[bit_level], -jnp.inf
            ),
        )
    row_lse = [total_lse] + [pick_stat(total_lse, 2 ** (b + 1), offsets[b]) for b in range(levels)]
    weights = [jnp.exp(scores[i] - row_lse[i][:, :, None]) for i in range(levels + 1)]
    rounded = [w.astype(jnp.bfloat16) for w in weights]
    output = jnp.einsum(
        "hqk,khe->qhe", rounded[0], value_sets[0], preferred_element_type=jnp.float32
    )
    for bit_level in range(levels):
        level_out = jnp.einsum(
            "hqk,khe->qhe",
            rounded[bit_level + 1],
            value_sets[bit_level + 1],
            preferred_element_type=jnp.float32,
        )
        output = output + spread_rows(level_out, 2 ** (bit_level + 1), offsets[bit_level])
    delta_rows = jnp.sum(grad_rows * output, axis=2).T
    row_delta = [delta_rows] + [
        pick_stat(delta_rows, 2 ** (b + 1), offsets[b]) for b in range(levels)
    ]
    grad_q = jnp.zeros(query_rows.shape, jnp.float32)
    grad_k = jnp.zeros(query_rows.shape, jnp.float32)
    grad_v = jnp.zeros(query_rows.shape, jnp.float32)
    for level_index in range(levels + 1):
        pgrad = jnp.einsum(
            "qhe,khe->hqk",
            sel_g[level_index],
            value_sets[level_index],
            preferred_element_type=jnp.float32,
        )
        dround = (weights[level_index] * (pgrad - row_delta[level_index][:, :, None])).astype(
            jnp.bfloat16
        )
        q_part = (
            jnp.einsum(
                "hqk,khe->qhe", dround, key_sets[level_index], preferred_element_type=jnp.float32
            )
            * score_scale
        )
        if level_index == 0:
            grad_q = q_part
            grad_k = (
                jnp.einsum("hqk,qhe->khe", dround, sel_q[0], preferred_element_type=jnp.float32)
                * score_scale
            )
            grad_v = jnp.einsum(
                "hqk,qhe->khe", rounded[0], sel_g[0], preferred_element_type=jnp.float32
            )
        else:
            dilation = 2**level_index
            chosen = offsets[level_index - 1]
            grad_q = grad_q + spread_rows(q_part, dilation, chosen)
            key_part = (
                jnp.einsum(
                    "hqk,qhe->khe", dround, sel_q[level_index], preferred_element_type=jnp.float32
                )
                * score_scale
            )
            value_part = jnp.einsum(
                "hqk,qhe->khe",
                rounded[level_index],
                sel_g[level_index],
                preferred_element_type=jnp.float32,
            )
            summed = halving(
                jnp.stack([key_part, value_part]),
                level_index,
                lambda tile, bit: partner(tile, "seq", bit),
            )
            key_total = summed[0]
            value_total = summed[1]
            grad_k = grad_k + spread_rows(key_total, dilation, chosen)
            grad_v = grad_v + spread_rows(value_total, dilation, chosen)
    width_all = head_count * head_dim
    return (
        grad_q.astype(jnp.bfloat16).reshape(1, tok_rows, width_all),
        grad_k.astype(jnp.bfloat16).reshape(1, tok_rows, width_all),
        grad_v.astype(jnp.bfloat16).reshape(1, tok_rows, width_all),
    )


def solution(mesh):
    in_specs = (
        P("section", "seq", None),
        P("section", "seq", None),
        P("section", "seq", None),
        P("section", "seq", None),
        P(),
    )
    out_specs = (P("section", "seq", None), P("section", "seq", None), P("section", "seq", None))
    return jax.shard_map(
        per_device, mesh=mesh, in_specs=in_specs, out_specs=out_specs, check_vma=False
    )
```

profile of v0, /device:TPU:0, one launch (start us, length us, event | category | flops | bytes accessed | tf_op | source)
XLA Modules:
  0.0 183.1 jit_solution(9447822914622950358)
XLA Ops:
  0.6 5.1 %collective-permute-start.6 = (bf16[1,128,2048]{2,1,0:T(8,128)(2,1)}, bf16[1,128,2048]{2,1,0:T(8,128)(2,1)}, u32[]{:S(2)}, u32[]{:S(2)}) collective-permute-start(bf16[1,128,2048]{2,1,0:T(8,128)(2,1)} %param.8), channel_id=1, source_target_pairs={{0,3},{1,0},{2,1},{3,2},{4,7},{5,4},{6,5},{7,6},{8,11},{9,8},{10,9... | collective-permute-start | bytes 1572872 | tf_op jit(solution)/shard_map/ppermute | solution.py:10
  18.5 3.3 %select_reduce_fusion = (bf16[16,16,128]{2,1,0:T(8,128)(2,1)}, bf16[16,16,128]{2,1,0:T(8,128)(2,1)S(1)}, bf16[16,16,128]{2,1,0:T(8,128)(2,1)S(1)}, bf16[16,16,128]{2,1,0:T(8,128)(2,1)}) fusion(pred[8,16]{0,1:T(8,128)(4,1)S(1)} %copy.199, bf16[1,128,2048]{2,1,0:T(8,128)(2,1)} %collective-permute-done.6, bf16[1,128,2048]{2,1,0:T(8,128)(2,1)S(1)} %copy-done.22, ...), kind=kLoop, calls=%fused_computation.90 | loop fusion | flops 1966080 | bytes 2359424 | tf_op jit(solution)/shard_map/reduce_sum | solution.py:30
  23.2 1.4 select_reduce_fusion.1
  25.9 1.4 select_reduce_fusion.2
  27.8 1.6 collective-permute-start.4
  33.3 3.8 %collective-permute-done.4 = bf16[2,32,16,128]{3,1,2,0:T(8,128)(2,1)} collective-permute-done((bf16[2,32,16,128]{3,1,2,0:T(8,128)(2,1)S(1)}, bf16[2,32,16,128]{3,1,2,0:T(8,128)(2,1)}, u32[]{:S(2)}, u32[]{:S(2)}) %collective-permute-start.4) | collective-permute-done | bytes 262176 | tf_op jit(solution)/shard_map/ppermute | solution.py:20
  37.1 2.0 %maximum_select_fusion.4 = bf16[2,64,16,128]{3,1,2,0:T(8,128)(2,1)} fusion(bf16[2,32,16,128]{3,1,2,0:T(8,128)(2,1)} %collective-permute-done.4, bf16[2,32,16,128]{3,1,2,0:T(8,128)(2,1)S(1)} %maximum_select_fusion.5, pred[]{:T(512)S(6)} %eq.119), kind=kLoop, calls=%fused_computation.87 | loop fusion | flops 2359296 | bytes 1048577 | tf_op jit(solution)/shard_map/jit(_where)/select_n | solution.py:67
  39.1 1.5 collective-permute-start.5
  40.6 1.6 maximum_select_fusion
  43.8 4.0 %collective-permute-done.2 = bf16[2,64,16,128]{3,1,2,0:T(8,128)(2,1)S(1)} collective-permute-done((bf16[2,64,16,128]{3,1,2,0:T(8,128)(2,1)S(1)}, bf16[2,64,16,128]{3,1,2,0:T(8,128)(2,1)S(1)}, u32[]{:S(2)}, u32[]{:S(2)}) %collective-permute-start.2) | collective-permute-done | bytes 524320 | tf_op jit(solution)/shard_map/ppermute | solution.py:20
  50.7 1.7 collective-permute-done.5
  52.4 1.9 %maximum_select_fusion.2 = bf16[2,128,16,128]{3,1,2,0:T(8,128)(2,1)S(1)} fusion(bf16[2,64,16,128]{3,1,2,0:T(8,128)(2,1)} %collective-permute-done.5, bf16[2,64,16,128]{3,1,2,0:T(8,128)(2,1)} %maximum_select_fusion.4, pred[]{:T(512)S(6)} %eq.126), kind=kLoop, calls=%fused_computation.69 | loop fusion | flops 4718592 | bytes 2097153 | tf_op jit(solution)/shard_map/jit(_where)/select_n | solution.py:67
  59.3 1.4 copy.222
  60.8 2.0 %fusion.79 = (f32[16,64]{1,0:T(8,128)}, f32[16,64,2]{1,0,2:T(8,128)}) fusion(pred[16,64,2]{1,0,2:T(8,128)(4,1)} %copy.223, pred[16,64,2]{1,0,2:T(8,128)(4,1)} %copy.220, f32[16,64,2]{1,0,2:T(8,128)} %copy.217, f32[16,64,2]{1,0,2:T(8,128)} %copy.215, f32[16,64]{1,0:T(8,128)} %copy.222, f32[16,64]{1,0:T(8,128)} %copy.219, f32[16,64]{1,0:T(8,128)} %log_add_fusion.2, ...), kind=kLoop, calls=%fused_computation.203 | loop fusion | flops 64512 | bytes 45088 | tf_op jit(solution)/shard_map/reduce_sum | solution.py:49
  62.8 1.4 copy.188
  65.0 1.8 fusion.52
  67.4 1.6 select_bitcast_fusion
  71.6 2.5 %copy.242 = f32[128,16,128]{0,2,1:T(8,128)} copy(f32[128,16,128]{2,1,0:T(8,128)} %bitcast.298) | data formatting | bytes 2097152 | tf_op jit(solution)/shard_map/jit(_where)/broadcast_in_dim | solution.py:39
  77.5 2.6 %copy.235 = f32[128,16,128]{0,2,1:T(8,128)} copy(f32[128,16,128]{2,1,0:T(8,128)} %bitcast.294) | data formatting | bytes 2097152 | tf_op jit(solution)/shard_map/jit(_where)/broadcast_in_dim | solution.py:39
  82.0 2.6 %copy.227 = f32[128,16,128]{0,2,1:T(8,128)} copy(f32[128,16,128]{2,1,0:T(8,128)} %bitcast.299) | data formatting | bytes 2097152 | tf_op jit(solution)/shard_map/jit(_where)/broadcast_in_dim | solution.py:39
  84.6 1.5 copy.204
  86.1 1.5 copy.196
  87.6 1.5 copy.189
  89.9 3.1 %multiply_reduce_fusion = f32[128,16]{0,1:T(8,128)} fusion(bf16[128,16,128]{0,2,1:T(8,128)(2,1)S(1)} %bitcast.274, f32[128,16,128]{0,2,1:T(8,128)} %copy.242, f32[128,16,128]{0,2,1:T(8,128)} %copy.235, f32[128,16,128]{0,2,1:T(8,128)} %copy.227, bf16[128,16,128]{0,2,1:T(8,128)(2,1)} %bitcast.284, pred[128,16]{0,1:T(8,128)(4,1)} %copy.236, ...), kind=kOutput, calls=%fused_computation.73 | convolution fusion | flops 69990400 | bytes 5265408 | tf_op jit(solution)/shard_map/hqk,khe->qhe/dot_general | solution.py:139
  93.1 1.4 copy.247
  94.5 1.5 fusion.60
  97.3 2.5 %convolution_bitcast_fusion.3 = f32[1,128,16,128]{3,1,2,0:T(8,128)} fusion(bf16[16,16,128]{2,1,0:T(8,128)(2,1)} %get-tuple-element.15, f32[16,16,128]{2,1,0:T(8,128)S(1)} %get-tuple-element.43, f32[16,16]{1,0:T(8,128)} %copy-done.52), kind=kOutput, calls=%fused_computation.22 | convolution fusion | flops 8454144 | bytes 1246208 | tf_op jit(solution)/shard_map/hqk,qhe->khe/dot_general | solution.py:192
  104.6 1.6 convolution_bitcast_fusion.4
  109.5 2.6 %copy.262 = f32[128,16,128]{0,2,1:T(8,128)} copy(f32[128,16,128]{2,1,0:T(8,128)} %bitcast.300) | data formatting | bytes 2097152 | tf_op jit(solution)/shard_map/jit(_where)/broadcast_in_dim | solution.py:39
  113.3 2.6 %copy.257 = f32[128,16,128]{0,2,1:T(8,128)} copy(f32[128,16,128]{2,1,0:T(8,128)} %bitcast.295) | data formatting | bytes 2097152 | tf_op jit(solution)/shard_map/jit(_where)/broadcast_in_dim | solution.py:39
  116.1 1.4 fusion.24
  119.2 2.6 %copy.252 = f32[128,16,128]{0,2,1:T(8,128)} copy(f32[128,16,128]{2,1,0:T(8,128)} %bitcast.301) | data formatting | bytes 2097152 | tf_op jit(solution)/shard_map/jit(_where)/broadcast_in_dim | solution.py:39
  121.9 2.5 %broadcast_select_fusion = f32[2,64,16,128]{3,1,2,0:T(8,128)} fusion(pred[]{:T(512)S(6)} %eq.126, f32[1,128,16,128]{3,1,2,0:T(8,128)S(1)} %copy-done.2, f32[1,128,16,128]{3,1,2,0:T(8,128)} %fusion.11), kind=kLoop, calls=%fused_computation.104 | loop fusion | flops 786432 | bytes 3145729 | tf_op jit(solution)/shard_map/jit(_where)/select_n | solution.py:83
  124.4 1.5 collective-permute-start.10
  127.1 1.6 collective-permute-start.8
  130.4 2.1 %copy.284 = bf16[1,128,2048]{2,1,0:T(8,128)(2,1)} copy(bf16[1,128,2048]{1,2,0:T(8,128)(2,1)} %bitcast.307) | data formatting | bytes 1048576
  134.4 13.7 %collective-permute-done.10 = f32[2,64,16,128]{3,1,2,0:T(8,128)} collective-permute-done((f32[2,64,16,128]{3,1,2,0:T(8,128)}, f32[2,64,16,128]{3,1,2,0:T(8,128)}, u32[]{:S(2)}, u32[]{:S(2)}) %collective-permute-start.10) | collective-permute-done | bytes 1048608 | tf_op jit(solution)/shard_map/ppermute | solution.py:20
  148.1 1.6 select_add_fusion
  150.6 1.5 collective-permute-start.11
  152.1 1.5 select_add_fusion.1
  156.1 1.4 copy.268
  159.9 2.9 %copy.279 = f32[128,16,128]{0,2,1:T(8,128)} copy(f32[128,16,128]{2,1,0:T(8,128)} %bitcast.303) | data formatting | bytes 2097152 | tf_op jit(solution)/shard_map/jit(_where)/broadcast_in_dim | solution.py:39
  166.1 1.4 copy.272
  170.4 2.7 %copy.276 = f32[128,16,128]{0,2,1:T(8,128)} copy(f32[128,16,128]{2,1,0:T(8,128)} %bitcast.304) | data formatting | bytes 2097152 | tf_op jit(solution)/shard_map/jit(_where)/broadcast_in_dim | solution.py:39
  173.1 2.9 %fusion.18 = bf16[128,16,128]{0,2,1:T(8,128)(2,1)} fusion(bf16[16,128,128]{1,2,0:T(8,128)(2,1)S(1)} %copy-done.15, bf16[128,16,128]{0,2,1:T(8,128)(2,1)S(1)} %bitcast.278, f32[128,16,128]{0,2,1:T(8,128)} %copy.276, f32[128,16,128]{0,2,1:T(8,128)} %copy.272, f32[128,16,128]{0,2,1:T(8,128)S(1)} %copy-done.28, pred[128,16]{0,1:T(8,128)(4,1)S(1)} %copy-done.55, ...), kind=kOutput, calls=%fused_computation.36 | convolution fusion | flops 69206016 | bytes 4724736 | tf_op jit(solution)/shard_map/hqk,qhe->khe/dot_general | solution.py:176
  176.1 2.0 %copy.285 = bf16[1,128,2048]{2,1,0:T(8,128)(2,1)} copy(bf16[1,128,2048]{1,2,0:T(8,128)(2,1)} %bitcast.306) | data formatting | bytes 1048576
  178.3 1.4 copy.283
  179.7 2.4 %fusion.21 = bf16[128,16,128]{0,2,1:T(8,128)(2,1)S(1)} fusion(bf16[128,16,128]{0,2,1:T(8,128)(2,1)S(1)} %bitcast.276, f32[128,16,128]{0,2,1:T(8,128)} %copy.283, f32[128,16,128]{0,2,1:T(8,128)} %copy.281, f32[128,16,128]{0,2,1:T(8,128)} %copy.279, pred[128,16]{0,1:T(8,128)(4,1)S(1)} %copy-done.55, pred[128,16]{0,1:T(8,128)(4,1)S(1)} %copy-done.56, ...), kind=kOutput, calls=%fused_computation.39 | convolution fusion | flops 69468160 | bytes 5257216 | tf_op jit(solution)/shard_map/hqk,qhe->khe/dot_general | solution.py:179
  (276 shorter events, 69.0 us)
Async XLA Ops:
  0.6 7.3 %copy-start.24 = (bf16[1,128,2048]{2,1,0:T(8,128)(2,1)S(1)}, bf16[1,128,2048]{2,1,0:T(8,128)(2,1)}, u32[]{:S(2)}) copy-start(bf16[1,128,2048]{2,1,0:T(8,128)(2,1)} %param.5) | copy-start | bytes 1572868
  0.6 17.9 %collective-permute-start.6 = (bf16[1,128,2048]{2,1,0:T(8,128)(2,1)}, bf16[1,128,2048]{2,1,0:T(8,128)(2,1)}, u32[]{:S(2)}, u32[]{:S(2)}) collective-permute-start(bf16[1,128,2048]{2,1,0:T(8,128)(2,1)} %param.8), channel_id=1, source_target_pairs={{0,3},{1,0},{2,1},{3,2},{4,7},{5,4},{6,5},{7,6},{8,11},{9,8},{10,9... | collective-permute-start | bytes 1572872 | tf_op jit(solution)/shard_map/ppermute | solution.py:10
  6.5 10.7 %copy-start.66 = (s32[16]{0:T(128)}, s32[16]{0:T(128)S(1)}, u32[]{:S(2)}) copy-start(s32[16]{0:T(128)S(1)} %get-tuple-element.39) | copy-start | bytes 196
  6.6 4.6 %copy-start.59 = (pred[16,8]{0,1:T(8,128)(4,1)}, pred[16,8]{0,1:T(8,128)(4,1)S(1)}, u32[]{:S(2)}) copy-start(pred[16,8]{0,1:T(8,128)(4,1)S(1)} %iota_compare_fusion.1) | copy-start | bytes 388
  9.2 4.8 %copy-start.22 = (bf16[1,128,2048]{2,1,0:T(8,128)(2,1)S(1)}, bf16[1,128,2048]{2,1,0:T(8,128)(2,1)}, u32[]{:S(2)}) copy-start(bf16[1,128,2048]{2,1,0:T(8,128)(2,1)} %param.6) | copy-start | bytes 1572868
  9.3 4.9 %copy-start.61 = (pred[16,4]{0,1:T(4,128)(4,1)}, pred[16,4]{0,1:T(4,128)(4,1)S(1)}, u32[]{:S(2)}) copy-start(pred[16,4]{0,1:T(4,128)(4,1)S(1)} %iota_compare_fusion.3) | copy-start | bytes 196
  10.1 3.9 %copy-start.40 = (f32[16,128]{0,1:T(8,128)}, f32[16,128]{0,1:T(8,128)S(1)}, u32[]{:S(2)}) copy-start(f32[16,128]{0,1:T(8,128)S(1)} %copy.214) | copy-start | bytes 24580
  11.2 2.8 %copy-start.41 = (f32[16,128]{0,1:T(8,128)}, f32[16,128]{0,1:T(8,128)S(1)}, u32[]{:S(2)}) copy-start(f32[16,128]{0,1:T(8,128)S(1)} %copy.213) | copy-start | bytes 24580
  21.9 5.8 %collective-permute-start.3 = (bf16[2,16,16,128]{3,1,2,0:T(8,128)(2,1)S(1)}, bf16[2,16,16,128]{3,1,2,0:T(8,128)(2,1)S(1)}, u32[]{:S(2)}, u32[]{:S(2)}) collective-permute-start(bf16[2,16,16,128]{3,1,2,0:T(8,128)(2,1)S(1)} %pad_maximum_fusion.5), channel_id=1, source_target_pairs={{0,4},{4,0},{8,12},{12,8},{16,20},{20,16},{24,28},{28,24},{1,5},{5... | collective-permute-start | bytes 393224 | tf_op jit(solution)/shard_map/ppermute | solution.py:20
  24.7 23.5 %copy-start.35 = (bf16[32,16,128]{2,1,0:T(8,128)(2,1)}, bf16[32,16,128]{2,1,0:T(8,128)(2,1)S(1)}, u32[]{:S(2)}) copy-start(bf16[32,16,128]{2,1,0:T(8,128)(2,1)S(1)} %get-tuple-element.26) | copy-start | bytes 393220
  25.5 5.8 %collective-permute-start.1 = (bf16[2,32,16,128]{3,1,2,0:T(8,128)(2,1)}, bf16[2,32,16,128]{3,1,2,0:T(8,128)(2,1)}, u32[]{:S(2)}, u32[]{:S(2)}) collective-permute-start(bf16[2,32,16,128]{3,1,2,0:T(8,128)(2,1)} %pad_maximum_fusion.4), channel_id=1, source_target_pairs={{0,4},{4,0},{8,12},{12,8},{16,20},{20,16},{24,28},{28,24},{1,5},{5... | collective-permute-start | bytes 786440 | tf_op jit(solution)/shard_map/ppermute | solution.py:20
  27.3 14.9 %copy-start.33 = (bf16[64,16,128]{2,1,0:T(8,128)(2,1)}, bf16[64,16,128]{2,1,0:T(8,128)(2,1)S(1)}, u32[]{:S(2)}) copy-start(bf16[64,16,128]{2,1,0:T(8,128)(2,1)S(1)} %get-tuple-element.22) | copy-start | bytes 786436
  27.5 13.1 %collective-permute-start = (bf16[2,64,16,128]{3,1,2,0:T(8,128)(2,1)S(1)}, bf16[2,64,16,128]{3,1,2,0:T(8,128)(2,1)}, u32[]{:S(2)}, u32[]{:S(2)}) collective-permute-start(bf16[2,64,16,128]{3,1,2,0:T(8,128)(2,1)S(1)} %pad_maximum_fusion.3), channel_id=1, source_target_pairs={{0,4},{4,0},{8,12},{12,8},{16,20},{20,16},{24,28},{28,24},{1,5},{5... | collective-permute-start | bytes 1572872 | tf_op jit(solution)/shard_map/ppermute | solution.py:20
  27.8 9.3 %collective-permute-start.4 = (bf16[2,32,16,128]{3,1,2,0:T(8,128)(2,1)S(1)}, bf16[2,32,16,128]{3,1,2,0:T(8,128)(2,1)}, u32[]{:S(2)}, u32[]{:S(2)}) collective-permute-start(bf16[2,32,16,128]{3,1,2,0:T(8,128)(2,1)S(1)} %maximum_select_fusion.5), channel_id=1, source_target_pairs={{0,8},{8,0},{4,12},{12,4},{16,24},{24,16},{20,28},{28,20},{1,9},{9... | collective-permute-start | bytes 786440 | tf_op jit(solution)/shard_map/ppermute | solution.py:20
  31.3 97.4 %copy-start.10 = (bf16[1,128,2048]{1,2,0:T(8,128)(2,1)}, bf16[1,128,2048]{1,2,0:T(8,128)(2,1)S(1)}, u32[]{:S(2)}) copy-start(bf16[1,128,2048]{1,2,0:T(8,128)(2,1)S(1)} %copy.207) | copy-start | bytes 1572868
  32.7 15.1 %collective-permute-start.2 = (bf16[2,64,16,128]{3,1,2,0:T(8,128)(2,1)S(1)}, bf16[2,64,16,128]{3,1,2,0:T(8,128)(2,1)S(1)}, u32[]{:S(2)}, u32[]{:S(2)}) collective-permute-start(bf16[2,64,16,128]{3,1,2,0:T(8,128)(2,1)S(1)} %maximum_select_fusion.3), channel_id=1, source_target_pairs={{0,8},{8,0},{4,12},{12,4},{16,24},{24,16},{20,28},{28,20},{1,9},{9... | collective-permute-start | bytes 1572872 | tf_op jit(solution)/shard_map/ppermute | solution.py:20
  39.1 13.3 %collective-permute-start.5 = (bf16[2,64,16,128]{3,1,2,0:T(8,128)(2,1)}, bf16[2,64,16,128]{3,1,2,0:T(8,128)(2,1)}, u32[]{:S(2)}, u32[]{:S(2)}) collective-permute-start(bf16[2,64,16,128]{3,1,2,0:T(8,128)(2,1)} %maximum_select_fusion.4), channel_id=1, source_target_pairs={{0,16},{16,0},{4,20},{20,4},{8,24},{24,8},{12,28},{28,12},{1,17},{... | collective-permute-start | bytes 1572872 | tf_op jit(solution)/shard_map/ppermute | solution.py:20
  50.0 4.4 %copy-start.47 = (f32[16,32]{0,1:T(8,128)}, f32[16,32]{0,1:T(8,128)S(1)}, u32[]{:S(2)}) copy-start(f32[16,32]{0,1:T(8,128)S(1)} %copy.195) | copy-start | bytes 6148
  50.7 4.7 %copy-start.42 = (bf16[16,16,128]{2,1,0:T(8,128)(2,1)S(1)}, bf16[16,16,128]{2,1,0:T(8,128)(2,1)}, u32[]{:S(2)}) copy-start(bf16[16,16,128]{2,1,0:T(8,128)(2,1)} %get-tuple-element.18) | copy-start | bytes 196612
  69.1 2.5 %copy-start.52 = (f32[16,16]{1,0:T(8,128)}, f32[16,16]{1,0:T(8,128)S(1)}, u32[]{:S(2)}) copy-start(f32[16,16]{1,0:T(8,128)S(1)} %copy.240) | copy-start | bytes 3076
  77.5 2.6 %copy-start.48 = (f32[16,64]{1,0:T(8,128)S(1)}, f32[16,64]{1,0:T(8,128)}, u32[]{:S(2)}) copy-start(f32[16,64]{1,0:T(8,128)} %get-tuple-element.37) | copy-start | bytes 12292
  97.3 2.5 %copy-start.13 = (bf16[2,128,16,128]{3,1,2,0:T(8,128)(2,1)S(1)}, bf16[2,128,16,128]{3,1,2,0:T(8,128)(2,1)}, u32[]{:S(2)}) copy-start(bf16[2,128,16,128]{3,1,2,0:T(8,128)(2,1)} %copy-done.12) | copy-start | bytes 3145732
  97.3 2.5 %copy-start.46 = (bf16[16,16,128]{2,1,0:T(8,128)(2,1)S(1)}, bf16[16,16,128]{2,1,0:T(8,128)(2,1)}, u32[]{:S(2)}) copy-start(bf16[16,16,128]{2,1,0:T(8,128)(2,1)} %get-tuple-element.15) | copy-start | bytes 196612
  97.3 2.5 %copy-start.53 = (f32[16,16]{1,0:T(8,128)S(1)}, f32[16,16]{1,0:T(8,128)}, u32[]{:S(2)}) copy-start(f32[16,16]{1,0:T(8,128)} %copy-done.52) | copy-start | bytes 3076
  97.3 2.5 %copy-start.60 = (f32[16,16]{1,0:T(8,128)S(1)}, f32[16,16]{1,0:T(8,128)}, u32[]{:S(2)}) copy-start(f32[16,16]{1,0:T(8,128)} %copy.260) | copy-start | bytes 3076
  100.3 4.3 %copy-start.37 = (bf16[32,16,128]{2,1,0:T(8,128)(2,1)S(1)}, bf16[32,16,128]{2,1,0:T(8,128)(2,1)}, u32[]{:S(2)}) copy-start(bf16[32,16,128]{2,1,0:T(8,128)(2,1)} %get-tuple-element.23) | copy-start | bytes 393220
  113.3 2.6 %copy-start.39 = (f32[16,128]{0,1:T(8,128)S(1)}, f32[16,128]{0,1:T(8,128)}, u32[]{:S(2)}) copy-start(f32[16,128]{0,1:T(8,128)} %copy.247) | copy-start | bytes 24580
  113.3 2.7 %copy-start.63 = (pred[16,2]{0,1:T(4,128)(4,1)S(1)}, pred[16,2]{0,1:T(4,128)(4,1)}, u32[]{:S(2)}) copy-start(pred[16,2]{0,1:T(4,128)(4,1)} %iota_compare_fusion.5) | copy-start | bytes 100
  113.3 2.8 %copy-start.49 = (f32[16,64]{1,0:T(8,128)S(1)}, f32[16,64]{1,0:T(8,128)}, u32[]{:S(2)}) copy-start(f32[16,64]{1,0:T(8,128)} %get-tuple-element.37) | copy-start | bytes 12292
  119.2 2.6 %copy-start.2 = (f32[1,128,16,128]{3,1,2,0:T(8,128)S(1)}, f32[1,128,16,128]{3,1,2,0:T(8,128)}, u32[]{:S(2)}) copy-start(f32[1,128,16,128]{3,1,2,0:T(8,128)} %convolution_bitcast_fusion.3) | copy-start | bytes 3145732
  121.9 4.1 %copy-start.3 = (f32[1,128,16,128]{3,1,2,0:T(8,128)S(1)}, f32[1,128,16,128]{3,1,2,0:T(8,128)}, u32[]{:S(2)}) copy-start(f32[1,128,16,128]{3,1,2,0:T(8,128)} %convolution_bitcast_fusion.4) | copy-start | bytes 3145732
  121.9 4.1 %copy-start.6 = (f32[1,128,16,128]{3,1,2,0:T(8,128)S(1)}, f32[1,128,16,128]{3,1,2,0:T(8,128)}, u32[]{:S(2)}) copy-start(f32[1,128,16,128]{3,1,2,0:T(8,128)} %fusion.12) | copy-start | bytes 3145732
  124.4 4.3 %copy-start.25 = (bf16[1,128,2048]{1,2,0:T(8,128)(2,1)S(1)}, bf16[1,128,2048]{1,2,0:T(8,128)(2,1)}, u32[]{:S(2)}) copy-start(bf16[1,128,2048]{1,2,0:T(8,128)(2,1)} %copy.297) | copy-start | bytes 1572868
  124.4 4.3 %copy-start.51 = (f32[128,16]{0,1:T(8,128)S(1)}, f32[128,16]{0,1:T(8,128)}, u32[]{:S(2)}) copy-start(f32[128,16]{0,1:T(8,128)} %multiply_reduce_fusion) | copy-start | bytes 24580
  124.4 23.6 %collective-permute-start.10 = (f32[2,64,16,128]{3,1,2,0:T(8,128)}, f32[2,64,16,128]{3,1,2,0:T(8,128)}, u32[]{:S(2)}, u32[]{:S(2)}) collective-permute-start(f32[2,64,16,128]{3,1,2,0:T(8,128)} %broadcast_select_fusion), channel_id=1, source_target_pairs={{0,16},{16,0},{4,20},{20,4},{8,24},{24,8},{12,28},{28,12},{1,17},{... | collective-permute-start | bytes 3145736 | tf_op jit(solution)/shard_map/ppermute | solution.py:20
  125.9 3.1 %copy-start.31 = (f32[128,16,128]{0,2,1:T(8,128)S(1)}, f32[128,16,128]{0,2,1:T(8,128)}, u32[]{:S(2)}) copy-start(f32[128,16,128]{0,2,1:T(8,128)} %copy.252) | copy-start | bytes 3145732
  127.1 24.9 %collective-permute-start.8 = (f32[2,64,16,128]{3,1,2,0:T(8,128)}, f32[2,64,16,128]{3,1,2,0:T(8,128)}, u32[]{:S(2)}, u32[]{:S(2)}) collective-permute-start(f32[2,64,16,128]{3,1,2,0:T(8,128)} %broadcast_select_fusion.1), channel_id=1, source_target_pairs={{0,8},{8,0},{4,12},{12,4},{16,24},{24,16},{20,28},{28,20},{1,9},{9... | collective-permute-start | bytes 3145736 | tf_op jit(solution)/shard_map/ppermute | solution.py:20
  134.1 14.0 %copy-start.5 = (f32[1,128,16,128]{3,1,2,0:T(8,128)S(1)}, f32[1,128,16,128]{3,1,2,0:T(8,128)}, u32[]{:S(2)}) copy-start(f32[1,128,16,128]{3,1,2,0:T(8,128)} %fusion.11) | copy-start | bytes 3145732
  134.3 20.2 %collective-permute-start.7 = (f32[2,64,16,128]{3,1,2,0:T(8,128)S(1)}, f32[2,64,16,128]{3,1,2,0:T(8,128)S(1)}, u32[]{:S(2)}, u32[]{:S(2)}) collective-permute-start(f32[2,64,16,128]{3,1,2,0:T(8,128)S(1)} %broadcast_select_fusion.2), channel_id=1, source_target_pairs={{0,4},{4,0},{8,12},{12,8},{16,20},{20,16},{24,28},{28,24},{1,5},{5... | collective-permute-start | bytes 3145736 | tf_op jit(solution)/shard_map/ppermute | solution.py:20
  148.1 4.0 %copy-start.7 = (f32[1,128,16,128]{3,1,2,0:T(8,128)S(1)}, f32[1,128,16,128]{3,1,2,0:T(8,128)}, u32[]{:S(2)}) copy-start(f32[1,128,16,128]{3,1,2,0:T(8,128)} %fusion.12) | copy-start | bytes 3145732
  149.7 3.9 %copy-start.8 = (f32[2,64,16,128]{3,1,2,0:T(8,128)}, f32[2,64,16,128]{3,1,2,0:T(8,128)S(1)}, u32[]{:S(2)}) copy-start(f32[2,64,16,128]{3,1,2,0:T(8,128)S(1)} %select_add_fusion) | copy-start | bytes 3145732
  150.6 12.2 %collective-permute-start.11 = (f32[2,32,16,128]{3,1,2,0:T(8,128)}, f32[2,32,16,128]{3,1,2,0:T(8,128)}, u32[]{:S(2)}, u32[]{:S(2)}) collective-permute-start(f32[2,32,16,128]{3,1,2,0:T(8,128)} %slice_select_fusion), channel_id=1, source_target_pairs={{0,8},{8,0},{4,12},{12,4},{16,24},{24,16},{20,28},{28,20},{1,9},{9... | collective-permute-start | bytes 1572872 | tf_op jit(solution)/shard_map/ppermute | solution.py:20
  154.5 10.1 %collective-permute-start.9 = (f32[2,32,16,128]{3,1,2,0:T(8,128)}, f32[2,32,16,128]{3,1,2,0:T(8,128)}, u32[]{:S(2)}, u32[]{:S(2)}) collective-permute-start(f32[2,32,16,128]{3,1,2,0:T(8,128)} %slice_select_fusion.1), channel_id=1, source_target_pairs={{0,4},{4,0},{8,12},{12,8},{16,20},{20,16},{24,28},{28,24},{1,5},{5... | collective-permute-start | bytes 1572872 | tf_op jit(solution)/shard_map/ppermute | solution.py:20
  159.9 2.9 %copy-start.9 = (f32[2,64,16,128]{3,1,2,0:T(8,128)S(1)}, f32[2,64,16,128]{3,1,2,0:T(8,128)}, u32[]{:S(2)}) copy-start(f32[2,64,16,128]{3,1,2,0:T(8,128)} %copy-done.8) | copy-start | bytes 3145732
  164.0 5.1 %collective-permute-start.12 = (f32[2,16,16,128]{3,1,2,0:T(8,128)S(1)}, f32[2,16,16,128]{3,1,2,0:T(8,128)S(1)}, u32[]{:S(2)}, u32[]{:S(2)}) collective-permute-start(f32[2,16,16,128]{3,1,2,0:T(8,128)S(1)} %slice_select_fusion.2), channel_id=1, source_target_pairs={{0,4},{4,0},{8,12},{12,8},{16,20},{20,16},{24,28},{28,24},{1,5},{5... | collective-permute-start | bytes 786440 | tf_op jit(solution)/shard_map/ppermute | solution.py:20
  170.4 2.7 %copy-start.15 = (bf16[16,128,128]{1,2,0:T(8,128)(2,1)S(1)}, bf16[16,128,128]{1,2,0:T(8,128)(2,1)}, u32[]{:S(2)}) copy-start(bf16[16,128,128]{1,2,0:T(8,128)(2,1)} %copy-done.14) | copy-start | bytes 1572868
  170.4 2.7 %copy-start.19 = (bf16[1,128,2048]{1,2,0:T(8,128)(2,1)S(1)}, bf16[1,128,2048]{1,2,0:T(8,128)(2,1)}, u32[]{:S(2)}) copy-start(bf16[1,128,2048]{1,2,0:T(8,128)(2,1)} %copy-done.18) | copy-start | bytes 1572868
  170.4 2.7 %copy-start.28 = (f32[128,16,128]{0,2,1:T(8,128)S(1)}, f32[128,16,128]{0,2,1:T(8,128)}, u32[]{:S(2)}) copy-start(f32[128,16,128]{0,2,1:T(8,128)} %copy.268) | copy-start | bytes 3145732
  (33 other events, 49.7 us)
where the time goes:
time: 185 us; the launch traced here: 183 us
  local copies, waits for them, and re-layouts  79.1 us (43%)
  other arithmetic  38.1 us (21%)
  matrix products  26.5 us (14%)
  waiting for transfers between devices  23.2 us (13%)
  starting transfers between devices  14.6 us (8%)
    broadcast_in_dim x33, local copies, waits for them, and re-layouts, spread_rows(): jnp.where(keep_mask, row_values[:, None], jnp.zeros((), row_values.dtype))  38.7 us
    ppermute x12, waiting for transfers between devices, partner(): return lax.ppermute(block, axis, route)  23.2 us
    unnamed x143, local copies, waits for them, and re-layouts  13.6 us
    ppermute x12, starting transfers between devices, partner(): return lax.ppermute(block, axis, route)  9.53 us
    select_n x6, other arithmetic, doubling(): jnp.where(low_side, jnp.concatenate([stacked, received], concat_axis), jn...  7.42 us
    reduce_sum x3, other arithmetic, pick_rows(): jnp.sum(jnp.where(keep_mask, shaped, jnp.zeros((), tile_rows.dtype)), axi...  6.19 us
    reduce_sum x5, other arithmetic, pick_stat(): return jnp.sum(jnp.where(keep_mask, shaped, 0.0), axis=2)  6.06 us
    select_n x4, local copies, waits for them, and re-layouts, spread_stat(): jnp.where(keep_mask, row_stat[:, :, None], fill_value)  5.94 us
  transfers between devices with their start and end apart: 13, of which 4 were waited for; matrix products, arithmetic and copies ran while one was open for 28% of the time, Pallas kernels for 0%

commit v1 on v0

v1 whole, which is shorter than its diff:
```python
import functools

import jax
import jax.numpy as jnp
from jax import lax
from jax.experimental import pallas as pl
from jax.experimental.pallas import tpu as pltpu
from jax.sharding import PartitionSpec as P

F32 = jnp.float32
BF16 = jnp.bfloat16
NEG = -1e30
VMEM_LIMIT = 48 * 1024 * 1024


def exchange(value, bits):
    count = lax.axis_size("seq")
    return lax.ppermute(value, "seq", [(i, i ^ bits) for i in range(count)])


def dot(a, b):
    return jnp.dot(a, b, preferred_element_type=F32)


def dot_nt(a, b):
    return lax.dot_general(a, b, (((1,), (1,)), ((), ())), preferred_element_type=F32)


def pick_matrix(offs_ref, head, first, levels, tok):
    parts = []
    for level in range(first, levels + 1):
        rate = 2**level
        rows = tok // rate
        kept = lax.rem(offs_ref[level - 1, head], rate)
        row = lax.broadcasted_iota(jnp.int32, (rows, tok), 0)
        col = lax.broadcasted_iota(jnp.int32, (rows, tok), 1)
        parts.append((col == row * rate + kept).astype(F32))
    return jnp.concatenate(parts, axis=0).astype(BF16)


def place_matrix(offs_ref, head, first, levels, tok):
    parts = []
    for level in range(first, levels + 1):
        rate = 2**level
        rows = tok // rate
        kept = lax.rem(offs_ref[level - 1, head], rate)
        row = lax.broadcasted_iota(jnp.int32, (tok, rows), 0)
        col = lax.broadcasted_iota(jnp.int32, (tok, rows), 1)
        parts.append((row == col * rate + kept).astype(F32))
    return jnp.concatenate(parts, axis=1).astype(BF16)


def pick_kernel(levels, heads, dim, offs_ref, k_ref, v_ref, two_ref, three_ref):
    tok = k_ref.shape[0]
    n2, n3 = tok // 4, tok // 8
    for h in range(heads):
        head = pl.program_id(0) * heads + h
        pick = pick_matrix(offs_ref, head, 2, levels, tok)
        cols = slice(h * dim, (h + 1) * dim)
        kv = jnp.concatenate([k_ref[:, cols], v_ref[:, cols]], axis=1)
        got = dot(pick, kv).astype(BF16)
        out = slice(2 * h * dim, 2 * (h + 1) * dim)
        two_ref[:, out] = got[:n2]
        three_ref[:, out] = got[n2 : n2 + n3]


def pick_call(offsets, keys, values, dim):
    tok, width = keys.shape
    levels, heads = offsets.shape
    steps = 2
    per = heads // steps
    block = pl.BlockSpec((tok, per * dim), lambda i, o: (0, i))
    return pl.pallas_call(
        functools.partial(pick_kernel, levels, per, dim),
        grid_spec=pltpu.PrefetchScalarGridSpec(
            num_scalar_prefetch=1,
            grid=(steps,),
            in_specs=[block, block],
            out_specs=[
                pl.BlockSpec((tok // 4, 2 * per * dim), lambda i, o: (0, i)),
                pl.BlockSpec((tok // 8, 2 * per * dim), lambda i, o: (0, i)),
            ],
        ),
        out_shape=[
            jax.ShapeDtypeStruct((tok // 4, 2 * width), BF16),
            jax.ShapeDtypeStruct((tok // 8, 2 * width), BF16),
        ],
        compiler_params=pltpu.CompilerParams(vmem_limit_bytes=VMEM_LIMIT),
        name="pick_rows",
    )(offsets, keys, values)


def main_kernel(
    levels, per, dim, offs_ref, core_ref,
    q0, q1, k0, k1, v0, v1, g0, g1, x2, xx2, x3, xx3, y3, yy3, d3, dd3,
    dq_own, dq_oth, base_own, base_oth, xa, xb, ya, yb, da, db,
):
    tok = q0.shape[0]
    n1, n2, n3 = tok // 2, tok // 4, tok // 8
    scale = dim**-0.5
    heads = per * pl.num_programs(0)
    for h in range(per):
        head = core_ref[0] * heads + pl.program_id(0) * per + h
        pick = pick_matrix(offs_ref, head, 1, levels, tok)
        place = place_matrix(offs_ref, head, 1, levels, tok)
        cols = slice(h * dim, (h + 1) * dim)
        kc = slice(2 * h * dim, (2 * h + 1) * dim)
        vc = slice((2 * h + 1) * dim, (2 * h + 2) * dim)
        out = slice(2 * h * dim, 2 * (h + 1) * dim)
        key0, key1, val0, val1 = k0[:, cols], k1[:, cols], v0[:, cols], v1[:, cols]
        que0, que1, gra0, gra1 = q0[:, cols], q1[:, cols], g0[:, cols], g1[:, cols]
        own = dot(pick, jnp.concatenate([key0, val0], axis=1)).astype(BF16)
        oth = dot(pick, jnp.concatenate([key1, val1], axis=1)).astype(BF16)

        def rows(mine, far):
            a, b = own[:, mine], oth[:, mine]
            e = n1 + n2
            return jnp.concatenate(
                [a[:n1], b[:n1], a[n1:e], b[n1:e], x2[:, far], xx2[:, far], a[e:], b[e:]]
                + [ref[:, far] for ref in (x3, xx3, y3, yy3, d3, dd3)],
                axis=0,
            )

        keys = rows(slice(0, dim), kc)
        vals = rows(slice(dim, 2 * dim), vc)
        que = jnp.concatenate([que0, que1], axis=0)
        gra = jnp.concatenate([gra0, gra1], axis=0)
        pos = lax.broadcasted_iota(jnp.int32, (1, 2 * tok), 1)
        s0 = jnp.concatenate([dot_nt(key0, que0), dot_nt(key1, que1)], axis=1) * scale
        sc = dot_nt(keys, que) * scale
        parts = [s0]
        for level in range(1, levels + 1):
            rate = 2**level
            kept = lax.rem(offs_ref[level - 1, head], rate)
            bias = jnp.where(lax.rem(pos, rate) == kept, 0.0, NEG).astype(F32)
            parts.append(sc[(level - 1) * tok : level * tok] + bias)
        s = jnp.concatenate(parts, axis=0)
        top = jnp.max(s, axis=0, keepdims=True)
        e = jnp.exp(s - top)
        w = e * (1.0 / jnp.sum(e, axis=0, keepdims=True))
        wb = w.astype(BF16)
        p0 = jnp.concatenate([dot_nt(val0, gra0), dot_nt(val1, gra1)], axis=1)
        p = jnp.concatenate([p0, dot_nt(vals, gra)], axis=0)
        delta = jnp.sum(wb.astype(F32) * p, axis=0, keepdims=True)
        ds = (w * (p - delta)).astype(BF16)
        dsl, wl = ds[tok:], wb[tok:]
        dk = dot(dsl, que) * scale
        dv = dot(wl, gra)
        dkv = jnp.concatenate([dk, dv], axis=1).astype(BF16)
        dk00 = dot(ds[:tok, :tok], que0) * scale
        dk01 = dot(ds[:tok, tok:], que1) * scale
        dv00 = dot(wb[:tok, :tok], gra0)
        dv01 = dot(wb[:tok, tok:], gra1)
        l2, l3 = tok, 2 * tok
        mine = jnp.concatenate([dkv[:n1], dkv[l2 : l2 + n2], dkv[l3 : l3 + n3]], axis=0)
        other = jnp.concatenate(
            [dkv[n1:tok], dkv[l2 + n2 : l2 + 2 * n2], dkv[l3 + n3 : l3 + 2 * n3]], axis=0
        )
        base_own[:, out] = (jnp.concatenate([dk00, dv00], axis=1) + dot(place, mine)).astype(BF16)
        base_oth[:, out] = (jnp.concatenate([dk01, dv01], axis=1) + dot(place, other)).astype(BF16)
        xa[:n2, out] = dkv[l2 + 2 * n2 : l2 + 3 * n2]
        xb[:n2, out] = dkv[l2 + 3 * n2 : l2 + 4 * n2]
        for i, (ref, lo) in enumerate(((xa, n2), (xb, n2), (ya, 0), (yb, 0), (da, 0), (db, 0))):
            ref[lo : lo + n3, out] = dkv[l3 + (2 + i) * n3 : l3 + (3 + i) * n3]
        dqt = dot(keys.T, dsl)
        dqt0 = dot(key0.T, ds[:tok, :tok])
        dqt1 = dot(key1.T, ds[:tok, tok:])
        dq_own[:, cols] = ((dqt[:, :tok] + dqt0) * scale).T.astype(BF16)
        dq_oth[:, cols] = ((dqt[:, tok:] + dqt1) * scale).T.astype(BF16)


def main_call(offsets, core, raw, far, dim):
    tok, width = raw[0].shape
    levels, heads = offsets.shape
    half = heads // 2
    per = 2
    steps = half // per
    n2, n3 = tok // 4, tok // 8
    raw_spec = pl.BlockSpec((tok, per * dim), lambda i, o, c: (0, c[0] * steps + i))

    def far_spec(rows):
        return pl.BlockSpec((rows, 2 * per * dim), lambda i, o, c: (0, c[0] * steps + i))

    def out(rows, mult):
        return (
            pl.BlockSpec((rows, mult * per * dim), lambda i, o, c: (0, i)),
            jax.ShapeDtypeStruct((rows, mult * half * dim), BF16),
        )

    outs = [out(tok, 1), out(tok, 1), out(tok, 2), out(tok, 2)]
    outs += [out(n2 + n3, 2)] * 2 + [out(n3, 2)] * 4
    return pl.pallas_call(
        functools.partial(main_kernel, levels, per, dim),
        grid_spec=pltpu.PrefetchScalarGridSpec(
            num_scalar_prefetch=2,
            grid=(steps,),
            in_specs=[raw_spec] * 8 + [far_spec(n2)] * 2 + [far_spec(n3)] * 6,
            out_specs=[o[0] for o in outs],
        ),
        out_shape=[o[1] for o in outs],
        compiler_params=pltpu.CompilerParams(vmem_limit_bytes=VMEM_LIMIT),
        name="attention_backward",
    )(offsets, core, *raw, *far)


def final_kernel(
    levels, per, dim, offs_ref, core_ref, dqa, dqb, ba, bb, xa, xb, ya, yb, da, db, dq, dk, dv
):
    tok = dq.shape[0]
    n2 = tok // 4
    heads = per * pl.num_programs(0)
    swap = pl.program_id(0) * 2 // pl.num_programs(0) != core_ref[0]

    def work(dq_in, base, x, y, d):
        dq[...] = dq_in[...]
        for h in range(per):
            head = pl.program_id(0) * per + h
            place = place_matrix(offs_ref, head, 2, levels, tok)
            cols = slice(h * dim, (h + 1) * dim)
            src = slice(2 * h * dim, 2 * (h + 1) * dim)
            third = x[n2:, src].astype(F32) + y[:, src].astype(F32) + d[:, src].astype(F32)
            part = jnp.concatenate([x[:n2, src], third.astype(BF16)], axis=0)
            total = (base[:, src].astype(F32) + dot(place, part)).astype(BF16)
            dk[:, cols] = total[:, :dim]
            dv[:, cols] = total[:, dim:]

    @pl.when(jnp.logical_not(swap))
    def _():
        work(dqa, ba, xa, ya, da)

    @pl.when(swap)
    def _():
        work(dqb, bb, xb, yb, db)


def final_call(offsets, core, parts, dim):
    levels, heads = offsets.shape
    tok = parts[0].shape[0]
    steps = 4
    per = heads // steps

    def spec(a):
        cols = a.shape[1] * 2 // steps
        return pl.BlockSpec((a.shape[0], cols), lambda i, o, c: (0, lax.rem(i, steps // 2)))

    out = pl.BlockSpec((tok, per * dim), lambda i, o, c: (0, i))
    return pl.pallas_call(
        functools.partial(final_kernel, levels, per, dim),
        grid_spec=pltpu.PrefetchScalarGridSpec(
            num_scalar_prefetch=2,
            grid=(steps,),
            in_specs=[spec(a) for a in parts],
            out_specs=[out] * 3,
        ),
        out_shape=[jax.ShapeDtypeStruct((tok, heads * dim), BF16)] * 3,
        compiler_params=pltpu.CompilerParams(vmem_limit_bytes=VMEM_LIMIT),
        name="add_pieces",
    )(offsets, core, *parts)


def per_device(queries, keys_in, values, out_grads, offsets):
    heads = offsets.shape[1]
    dim = queries.shape[2] // heads
    sections = lax.axis_size("section")
    core = lax.rem(lax.axis_index("seq"), 2).astype(jnp.int32).reshape(1)
    grads = lax.ppermute(
        out_grads[0], "section", [(i, (i - 1) % sections) for i in range(sections)]
    )
    q, k, v = queries[0], keys_in[0], values[0]
    q_oth, k_oth, v_oth = exchange(q, 1), exchange(k, 1), exchange(v, 1)
    two, three = pick_call(offsets, k, v, dim)
    x3 = exchange(three, 2)
    y3 = exchange(three, 4)
    x2 = exchange(two, 2)
    d3 = exchange(x3, 4)
    far = []
    for piece in (x2, x3, y3, d3):
        far += [piece, exchange(piece, 1)]
    g_oth = exchange(grads, 1)
    outs = main_call(offsets, core, [q, q_oth, k, k_oth, v, v_oth, grads, g_oth], far, dim)
    dq_own, dq_oth, base_own, base_oth, xa, xb, ya, yb, da, db = outs
    parts = [dq_own, exchange(dq_oth, 1), base_own, exchange(base_oth, 1)]
    parts += [exchange(xa, 2), exchange(xb, 3), exchange(ya, 4), exchange(yb, 5)]
    parts += [exchange(da, 6), exchange(db, 7)]
    dq, dk, dv = final_call(offsets, core, parts, dim)
    return dq[None], dk[None], dv[None]


def solution(mesh):
    spec = P("section", "seq", None)
    return jax.shard_map(
        per_device,
        mesh=mesh,
        in_specs=(spec, spec, spec, spec, P()),
        out_specs=(spec, spec, spec),
        check_vma=False,
    )
```

time: 185 us -> 60.4 us (0.33)
  local copies, waits for them, and re-layouts: 79.1 us -> 0.01 us
  other arithmetic: 38.1 us -> 0 us
  matrix products: 26.5 us -> 0 us
  Pallas kernels: 0 us -> 16.5 us
  starting transfers between devices: 14.6 us -> 18 us
    broadcast_in_dim x51 -> x0, local copies, waits for them, and re-layouts: 46.3 us -> none  [the longest x33 38.7 us: spread_rows(): jnp.where(keep_mask, row_values[:, None], jnp.zeros((), row_values.dtype))]
    dot_general x24 -> x0, matrix products: 26.5 us -> none  [the longest x3 4.72 us: per_device(): jnp.einsum('hqk,qhe->khe', rounded[level_index], sel_g[level_index], pref...]
    pallas_call x0 -> x3, Pallas kernels: none -> 16.5 us  [the longest x1 11 us: main_call(): pl.pallas_call(functools.partial(main_kernel, levels, per, dim), grid_spe...]
    select_n x19 -> x0, other arithmetic: 16.3 us -> none  [the longest x6 7.42 us: doubling(): jnp.where(low_side, jnp.concatenate([stacked, received], concat_axis), jn...]
    unnamed x143 -> x6, local copies, waits for them, and re-layouts: 13.6 us -> 0.01 us
    reduce_sum x12 -> x0, other arithmetic: 13.3 us -> none  [the longest x3 6.19 us: pick_rows(): jnp.sum(jnp.where(keep_mask, shaped, jnp.zeros((), tile_rows.dtype)), axi...]
    add x9 -> x0, other arithmetic: 7.09 us -> none  [the longest x6 5.87 us: halving(): stacked = kept + passer(outgoing, bit)]
    select_n x4 -> x0, local copies, waits for them, and re-layouts: 5.94 us -> none  [spread_stat(): jnp.where(keep_mask, row_stat[:, :, None], fill_value)]
  transfers between devices with their start and end apart: 13 -> 21, of which waited for: 4 -> 10; matrix products, arithmetic and copies ran while one was open for 28% -> 0% of each run, Pallas kernels for 0% -> 3%
where the time goes in v1:
time: 60.4 us; the launch traced here: 60.2 us
  waiting for transfers between devices  25 us (41%)
  starting transfers between devices  18 us (30%)
  Pallas kernels  16.5 us (27%)
  between operations  0.71 us (1%)
    ppermute x20, waiting for transfers between devices, exchange(): return lax.ppermute(value, 'seq', [(i, i ^ bits) for i in range(count)])  25 us
    ppermute x20, starting transfers between devices, exchange(): return lax.ppermute(value, 'seq', [(i, i ^ bits) for i in range(count)])  12.9 us
    pallas_call x1, Pallas kernels, main_call(): pl.pallas_call(functools.partial(main_kernel, levels, per, dim), grid_spe...  11 us
    ppermute x1, starting transfers between devices, per_device(): lax.ppermute(out_grads[0], 'section', [(i, (i - 1) % sections) for i in r...  5.1 us
    pallas_call x1, Pallas kernels, final_call(): pl.pallas_call(functools.partial(final_kernel, levels, per, dim), grid_sp...  3.44 us
    pallas_call x1, Pallas kernels, pick_call(): pl.pallas_call(functools.partial(pick_kernel, levels, per, dim), grid_spe...  2.08 us
  transfers between devices with their start and end apart: 21, of which 10 were waited for; matrix products, arithmetic and copies ran while one was open for 0% of the time, Pallas kernels for 3%

profile of v1, /device:TPU:0, one launch (start us, length us, event | category | flops | bytes accessed | tf_op | source)
XLA Modules:
  0.0 60.2 jit_solution(13792504146871920584)
XLA Ops:
  0.6 0.0 copy-start.1
  0.6 5.1 %collective-permute-start.3 = (bf16[128,2048]{1,0:T(8,128)(2,1)}, bf16[128,2048]{1,0:T(8,128)(2,1)S(1)}, u32[]{:S(2)}, u32[]{:S(2)}) collective-permute-start(bf16[128,2048]{1,0:T(8,128)(2,1)} %bitcast.10), channel_id=1, source_target_pairs={{0,3},{1,0},{2,1},{3,2},{4,7},{5,4},{6,5},{7,6},{8,11},{9,8},{10,9... | collective-permute-start | bytes 1572872 | tf_op jit(solution)/shard_map/ppermute | solution.py:266
  5.7 0.0 copy-done.1
  5.7 2.1 %pick_rows.1 = (bf16[32,4096]{1,0:T(8,128)(2,1)S(1)}, bf16[16,4096]{1,0:T(8,128)(2,1)S(1)}) custom-call(s32[3,16]{1,0:T(4,128)S(1)} %copy-done.1, bf16[128,2048]{1,0:T(8,128)(2,1)} %bitcast.2.k_ref.k0, bf16[128,2048]{1,0:T(8,128)(2,1)} %bitcast.3.v_ref.v0), custom_call_target="tpu_custom_call" | custom-call | tf_op jit(solution)/shard_map/pick_rows/pallas_call | solution.py:73
  7.8 1.6 %collective-permute-start.9 = (bf16[16,4096]{1,0:T(8,128)(2,1)S(1)}, bf16[16,4096]{1,0:T(8,128)(2,1)S(1)}, u32[]{:S(2)}, u32[]{:S(2)}) collective-permute-start(bf16[16,4096]{1,0:T(8,128)(2,1)S(1)} %get-tuple-element.19), channel_id=1, source_target_pairs={{0,16},{4,20},{8,24},{12,28},{16,0},{20,4},{24,8},{28,12},{1,17},{... | collective-permute-start | bytes 393224 | tf_op jit(solution)/shard_map/ppermute | solution.py:18
  9.4 1.5 %collective-permute-start.7 = (bf16[16,4096]{1,0:T(8,128)(2,1)S(1)}, bf16[16,4096]{1,0:T(8,128)(2,1)S(1)}, u32[]{:S(2)}, u32[]{:S(2)}) collective-permute-start(bf16[16,4096]{1,0:T(8,128)(2,1)S(1)} %get-tuple-element.19), channel_id=1, source_target_pairs={{0,8},{4,12},{8,0},{12,4},{16,24},{20,28},{24,16},{28,20},{1,9},{5... | collective-permute-start | bytes 393224 | tf_op jit(solution)/shard_map/ppermute | solution.py:18
  10.9 2.0 %collective-permute-done.9.y3 = bf16[16,4096]{1,0:T(8,128)(2,1)S(1)} collective-permute-done((bf16[16,4096]{1,0:T(8,128)(2,1)S(1)}, bf16[16,4096]{1,0:T(8,128)(2,1)S(1)}, u32[]{:S(2)}, u32[]{:S(2)}) %collective-permute-start.9) | collective-permute-done | bytes 131104 | tf_op jit(solution)/shard_map/ppermute | solution.py:18
  12.9 0.0 collective-permute-start.10
  12.9 1.5 %collective-permute-done.7.x3 = bf16[16,4096]{1,0:T(8,128)(2,1)S(1)} collective-permute-done((bf16[16,4096]{1,0:T(8,128)(2,1)S(1)}, bf16[16,4096]{1,0:T(8,128)(2,1)S(1)}, u32[]{:S(2)}, u32[]{:S(2)}) %collective-permute-start.7) | collective-permute-done | bytes 131104 | tf_op jit(solution)/shard_map/ppermute | solution.py:18
  14.4 0.5 collective-permute-start.11
  14.9 1.5 %collective-permute-start.5 = (bf16[32,4096]{1,0:T(8,128)(2,1)S(1)}, bf16[32,4096]{1,0:T(8,128)(2,1)S(1)}, u32[]{:S(2)}, u32[]{:S(2)}) collective-permute-start(bf16[32,4096]{1,0:T(8,128)(2,1)S(1)} %get-tuple-element.18), channel_id=1, source_target_pairs={{0,8},{4,12},{8,0},{12,4},{16,24},{20,28},{24,16},{28,20},{1,9},{5... | collective-permute-start | bytes 786440 | tf_op jit(solution)/shard_map/ppermute | solution.py:18
  16.4 0.0 collective-permute-start.8
  16.4 0.0 collective-permute-done.10.yy3
  16.4 0.5 collective-permute-start.1
  16.9 2.5 %collective-permute-done.11.d3 = bf16[16,4096]{1,0:T(8,128)(2,1)S(1)} collective-permute-done((bf16[16,4096]{1,0:T(8,128)(2,1)S(1)}, bf16[16,4096]{1,0:T(8,128)(2,1)S(1)}, u32[]{:S(2)}, u32[]{:S(2)}) %collective-permute-start.11) | collective-permute-done | bytes 131104 | tf_op jit(solution)/shard_map/ppermute | solution.py:18
  19.4 0.0 copy-done
  19.4 0.0 collective-permute-start
  19.4 0.0 collective-permute-done.8.xx3
  19.4 0.5 collective-permute-start.2
  19.9 0.0 collective-permute-done.3.g0
  19.9 0.1 collective-permute-start.4
  20.0 2.9 %collective-permute-done.5.x2 = bf16[32,4096]{1,0:T(8,128)(2,1)S(1)} collective-permute-done((bf16[32,4096]{1,0:T(8,128)(2,1)S(1)}, bf16[32,4096]{1,0:T(8,128)(2,1)S(1)}, u32[]{:S(2)}, u32[]{:S(2)}) %collective-permute-start.5) | collective-permute-done | bytes 262176 | tf_op jit(solution)/shard_map/ppermute | solution.py:18
  22.8 0.0 collective-permute-start.12
  22.8 1.3 %collective-permute-done.12.dd3 = bf16[16,4096]{1,0:T(8,128)(2,1)S(1)} collective-permute-done((bf16[16,4096]{1,0:T(8,128)(2,1)S(1)}, bf16[16,4096]{1,0:T(8,128)(2,1)S(1)}, u32[]{:S(2)}, u32[]{:S(2)}) %collective-permute-start.12) | collective-permute-done | bytes 131104 | tf_op jit(solution)/shard_map/ppermute | solution.py:18
  24.2 0.1 collective-permute-start.6
  24.3 1.4 %collective-permute-done.6.xx2 = bf16[32,4096]{1,0:T(8,128)(2,1)S(1)} collective-permute-done((bf16[32,4096]{1,0:T(8,128)(2,1)S(1)}, bf16[32,4096]{1,0:T(8,128)(2,1)S(1)}, u32[]{:S(2)}, u32[]{:S(2)}) %collective-permute-start.6) | collective-permute-done | bytes 262176 | tf_op jit(solution)/shard_map/ppermute | solution.py:18
  25.7 0.0 collective-permute-done.q1
  25.7 0.0 collective-permute-done.1.k1
  25.7 0.0 collective-permute-done.2.v1
  25.7 0.0 collective-permute-done.4.g1
  25.8 11.0 %attention_backward.1 = (bf16[128,1024]{1,0:T(8,128)(2,1)S(1)}, bf16[128,1024]{1,0:T(8,128)(2,1)S(1)}, bf16[128,2048]{1,0:T(8,128)(2,1)S(1)}, bf16[128,2048]{1,0...) custom-call(s32[3,16]{1,0:T(4,128)S(1)} %copy-done.1, ...), custom_call_target="tpu_custom_call" | custom-call | tf_op jit(solution)/shard_map/attention_backward/pallas_call | solution.py:192
  36.7 0.2 collective-permute-start.14
  37.0 0.5 collective-permute-start.17
  37.5 0.1 collective-permute-start.13
  37.5 1.6 %collective-permute-start.18 = (bf16[16,2048]{1,0:T(8,128)(2,1)S(1)}, bf16[16,2048]{1,0:T(8,128)(2,1)S(1)}, u32[]{:S(2)}, u32[]{:S(2)}) collective-permute-start(bf16[16,2048]{1,0:T(8,128)(2,1)S(1)} %get-tuple-element.27), channel_id=1, source_target_pairs={{0,20},{4,16},{8,28},{12,24},{16,4},{20,0},{24,12},{28,8},{1,21},{... | collective-permute-start | bytes 196616 | tf_op jit(solution)/shard_map/ppermute | solution.py:18
  39.1 1.5 %collective-permute-start.15 = (bf16[48,2048]{1,0:T(8,128)(2,1)S(1)}, bf16[48,2048]{1,0:T(8,128)(2,1)S(1)}, u32[]{:S(2)}, u32[]{:S(2)}) collective-permute-start(bf16[48,2048]{1,0:T(8,128)(2,1)S(1)} %get-tuple-element.24), channel_id=1, source_target_pairs={{0,8},{4,12},{8,0},{12,4},{16,24},{20,28},{24,16},{28,20},{1,9},{5... | collective-permute-start | bytes 589832 | tf_op jit(solution)/shard_map/ppermute | solution.py:18
  40.6 1.3 %collective-permute-done.17.ya = bf16[16,2048]{1,0:T(8,128)(2,1)S(1)} collective-permute-done((bf16[16,2048]{1,0:T(8,128)(2,1)S(1)}, bf16[16,2048]{1,0:T(8,128)(2,1)S(1)}, u32[]{:S(2)}, u32[]{:S(2)}) %collective-permute-start.17) | collective-permute-done | bytes 65568 | tf_op jit(solution)/shard_map/ppermute | solution.py:18
  41.9 0.1 collective-permute-start.16
  42.0 0.2 collective-permute-done.18.yb
  42.2 1.7 %collective-permute-start.19 = (bf16[16,2048]{1,0:T(8,128)(2,1)S(1)}, bf16[16,2048]{1,0:T(8,128)(2,1)S(1)}, u32[]{:S(2)}, u32[]{:S(2)}) collective-permute-start(bf16[16,2048]{1,0:T(8,128)(2,1)S(1)} %get-tuple-element.28), channel_id=1, source_target_pairs={{0,24},{4,28},{8,16},{12,20},{16,8},{20,12},{24,0},{28,4},{1,25},{... | collective-permute-start | bytes 196616 | tf_op jit(solution)/shard_map/ppermute | solution.py:18
  43.8 7.7 %collective-permute-done.19.da = bf16[16,2048]{1,0:T(8,128)(2,1)S(1)} collective-permute-done((bf16[16,2048]{1,0:T(8,128)(2,1)S(1)}, bf16[16,2048]{1,0:T(8,128)(2,1)S(1)}, u32[]{:S(2)}, u32[]{:S(2)}) %collective-permute-start.19) | collective-permute-done | bytes 65568 | tf_op jit(solution)/shard_map/ppermute | solution.py:18
  51.6 1.0 %collective-permute-start.20 = (bf16[16,2048]{1,0:T(8,128)(2,1)S(1)}, bf16[16,2048]{1,0:T(8,128)(2,1)S(1)}, u32[]{:S(2)}, u32[]{:S(2)}) collective-permute-start(bf16[16,2048]{1,0:T(8,128)(2,1)S(1)} %get-tuple-element.29), channel_id=1, source_target_pairs={{0,28},{4,24},{8,20},{12,16},{16,12},{20,8},{24,4},{28,0},{1,29},{... | collective-permute-start | bytes 196616 | tf_op jit(solution)/shard_map/ppermute | solution.py:18
  52.5 4.2 %collective-permute-done.20.db = bf16[16,2048]{1,0:T(8,128)(2,1)S(1)} collective-permute-done((bf16[16,2048]{1,0:T(8,128)(2,1)S(1)}, bf16[16,2048]{1,0:T(8,128)(2,1)S(1)}, u32[]{:S(2)}, u32[]{:S(2)}) %collective-permute-start.20) | collective-permute-done | bytes 65568 | tf_op jit(solution)/shard_map/ppermute | solution.py:18
  56.7 0.0 collective-permute-done.15.xa
  56.7 0.0 collective-permute-done.16.xb
  56.8 0.0 collective-permute-done.13.dqb
  56.8 0.0 collective-permute-done.14.bb
  56.8 3.4 %add_pieces.1 = (bf16[128,2048]{1,0:T(8,128)(2,1)}, bf16[128,2048]{1,0:T(8,128)(2,1)}, bf16[128,2048]{1,0:T(8,128)(2,1)}) custom-call(s32[3,16]{1,0:T(4,128)S(1)} %copy-done.1, s32[1]{0:T(128)} %bitcast.core_ref, bf16[128,1024]{1,0:T(8,128)(2,1)S(1)} %get-tuple-element.20.dqa, bf16[128,1024]{1,0:T(8,128)(2,1)S(1)} %collective-permute-done.13.dqb, ...), custom_call_target="tpu_custom_call" | custom-call | tf_op jit(solution)/shard_map/add_pieces/pallas_call | solution.py:247
  (3 shorter events, 0.0 us)
Async XLA Ops:
  0.6 5.1 %copy-start.1 = (s32[3,16]{1,0:T(4,128)S(1)}, s32[3,16]{1,0:T(4,128)}, u32[]{:S(2)}) copy-start(s32[3,16]{1,0:T(4,128)} %offs_ref.5) | copy-start | bytes 580
  0.6 19.2 %collective-permute-start.3 = (bf16[128,2048]{1,0:T(8,128)(2,1)}, bf16[128,2048]{1,0:T(8,128)(2,1)S(1)}, u32[]{:S(2)}, u32[]{:S(2)}) collective-permute-start(bf16[128,2048]{1,0:T(8,128)(2,1)} %bitcast.10), channel_id=1, source_target_pairs={{0,3},{1,0},{2,1},{3,2},{4,7},{5,4},{6,5},{7,6},{8,11},{9,8},{10,9... | collective-permute-start | bytes 1572872 | tf_op jit(solution)/shard_map/ppermute | solution.py:266
  5.7 13.6 %copy-start = (bf16[1,128,2048]{2,1,0:T(8,128)(2,1)S(1)}, bf16[1,128,2048]{2,1,0:T(8,128)(2,1)}, u32[]{:S(2)}) copy-start(bf16[1,128,2048]{2,1,0:T(8,128)(2,1)} %param.5) | copy-start | bytes 1572868
  7.8 5.0 %collective-permute-start.9 = (bf16[16,4096]{1,0:T(8,128)(2,1)S(1)}, bf16[16,4096]{1,0:T(8,128)(2,1)S(1)}, u32[]{:S(2)}, u32[]{:S(2)}) collective-permute-start(bf16[16,4096]{1,0:T(8,128)(2,1)S(1)} %get-tuple-element.19), channel_id=1, source_target_pairs={{0,16},{4,20},{8,24},{12,28},{16,0},{20,4},{24,8},{28,12},{1,17},{... | collective-permute-start | bytes 393224 | tf_op jit(solution)/shard_map/ppermute | solution.py:18
  9.4 5.0 %collective-permute-start.7 = (bf16[16,4096]{1,0:T(8,128)(2,1)S(1)}, bf16[16,4096]{1,0:T(8,128)(2,1)S(1)}, u32[]{:S(2)}, u32[]{:S(2)}) collective-permute-start(bf16[16,4096]{1,0:T(8,128)(2,1)S(1)} %get-tuple-element.19), channel_id=1, source_target_pairs={{0,8},{4,12},{8,0},{12,4},{16,24},{20,28},{24,16},{28,20},{1,9},{5... | collective-permute-start | bytes 393224 | tf_op jit(solution)/shard_map/ppermute | solution.py:18
  12.9 3.5 %collective-permute-start.10 = (bf16[16,4096]{1,0:T(8,128)(2,1)S(1)}, bf16[16,4096]{1,0:T(8,128)(2,1)S(1)}, u32[]{:S(2)}, u32[]{:S(2)}) collective-permute-start(bf16[16,4096]{1,0:T(8,128)(2,1)S(1)} %collective-permute-done.9.y3), channel_id=1, source_target_pairs={{0,4},{4,0},{8,12},{12,8},{16,20},{20,16},{24,28},{28,24},{1,5},{5... | collective-permute-start | bytes 393224 | tf_op jit(solution)/shard_map/ppermute | solution.py:18
  14.4 5.0 %collective-permute-start.11 = (bf16[16,4096]{1,0:T(8,128)(2,1)S(1)}, bf16[16,4096]{1,0:T(8,128)(2,1)S(1)}, u32[]{:S(2)}, u32[]{:S(2)}) collective-permute-start(bf16[16,4096]{1,0:T(8,128)(2,1)S(1)} %collective-permute-done.7.x3), channel_id=1, source_target_pairs={{0,16},{4,20},{8,24},{12,28},{16,0},{20,4},{24,8},{28,12},{1,17},{... | collective-permute-start | bytes 393224 | tf_op jit(solution)/shard_map/ppermute | solution.py:18
  14.9 7.9 %collective-permute-start.5 = (bf16[32,4096]{1,0:T(8,128)(2,1)S(1)}, bf16[32,4096]{1,0:T(8,128)(2,1)S(1)}, u32[]{:S(2)}, u32[]{:S(2)}) collective-permute-start(bf16[32,4096]{1,0:T(8,128)(2,1)S(1)} %get-tuple-element.18), channel_id=1, source_target_pairs={{0,8},{4,12},{8,0},{12,4},{16,24},{20,28},{24,16},{28,20},{1,9},{5... | collective-permute-start | bytes 786440 | tf_op jit(solution)/shard_map/ppermute | solution.py:18
  16.4 3.0 %collective-permute-start.8 = (bf16[16,4096]{1,0:T(8,128)(2,1)S(1)}, bf16[16,4096]{1,0:T(8,128)(2,1)S(1)}, u32[]{:S(2)}, u32[]{:S(2)}) collective-permute-start(bf16[16,4096]{1,0:T(8,128)(2,1)S(1)} %collective-permute-done.7.x3), channel_id=1, source_target_pairs={{0,4},{4,0},{8,12},{12,8},{16,20},{20,16},{24,28},{28,24},{1,5},{5... | collective-permute-start | bytes 393224 | tf_op jit(solution)/shard_map/ppermute | solution.py:18
  16.4 9.3 %collective-permute-start.1 = (bf16[128,2048]{1,0:T(8,128)(2,1)}, bf16[128,2048]{1,0:T(8,128)(2,1)S(1)}, u32[]{:S(2)}, u32[]{:S(2)}) collective-permute-start(bf16[128,2048]{1,0:T(8,128)(2,1)} %bitcast.2.k_ref.k0), channel_id=1, source_target_pairs={{0,4},{4,0},{8,12},{12,8},{16,20},{20,16},{24,28},{28,24},{1,5},{5... | collective-permute-start | bytes 1572872 | tf_op jit(solution)/shard_map/ppermute | solution.py:18
  19.4 6.4 %collective-permute-start = (bf16[128,2048]{1,0:T(8,128)(2,1)S(1)}, bf16[128,2048]{1,0:T(8,128)(2,1)S(1)}, u32[]{:S(2)}, u32[]{:S(2)}) collective-permute-start(bf16[128,2048]{1,0:T(8,128)(2,1)S(1)} %bitcast.8), channel_id=1, source_target_pairs={{0,4},{4,0},{8,12},{12,8},{16,20},{20,16},{24,28},{28,24},{1,5},{5... | collective-permute-start | bytes 1572872 | tf_op jit(solution)/shard_map/ppermute | solution.py:18
  19.4 6.4 %collective-permute-start.2 = (bf16[128,2048]{1,0:T(8,128)(2,1)}, bf16[128,2048]{1,0:T(8,128)(2,1)}, u32[]{:S(2)}, u32[]{:S(2)}) collective-permute-start(bf16[128,2048]{1,0:T(8,128)(2,1)} %bitcast.3.v_ref.v0), channel_id=1, source_target_pairs={{0,4},{4,0},{8,12},{12,8},{16,20},{20,16},{24,28},{28,24},{1,5},{5... | collective-permute-start | bytes 1572872 | tf_op jit(solution)/shard_map/ppermute | solution.py:18
  19.9 5.9 %copy-start.2 = (bf16[128,2048]{1,0:T(8,128)(2,1)}, bf16[128,2048]{1,0:T(8,128)(2,1)S(1)}, u32[]{:S(2)}) copy-start(bf16[128,2048]{1,0:T(8,128)(2,1)S(1)} %collective-permute-done.3.g0) | copy-start | bytes 1572868
  19.9 5.9 %collective-permute-start.4 = (bf16[128,2048]{1,0:T(8,128)(2,1)S(1)}, bf16[128,2048]{1,0:T(8,128)(2,1)}, u32[]{:S(2)}, u32[]{:S(2)}) collective-permute-start(bf16[128,2048]{1,0:T(8,128)(2,1)S(1)} %collective-permute-done.3.g0), channel_id=1, source_target_pairs={{0,4},{4,0},{8,12},{12,8},{16,20},{20,16},{24,28},{28,24},{1,5},{5... | collective-permute-start | bytes 1572872 | tf_op jit(solution)/shard_map/ppermute | solution.py:18
  22.8 1.3 %collective-permute-start.12 = (bf16[16,4096]{1,0:T(8,128)(2,1)S(1)}, bf16[16,4096]{1,0:T(8,128)(2,1)S(1)}, u32[]{:S(2)}, u32[]{:S(2)}) collective-permute-start(bf16[16,4096]{1,0:T(8,128)(2,1)S(1)} %collective-permute-done.11.d3), channel_id=1, source_target_pairs={{0,4},{4,0},{8,12},{12,8},{16,20},{20,16},{24,28},{28,24},{1,5},{5... | collective-permute-start | bytes 393224 | tf_op jit(solution)/shard_map/ppermute | solution.py:18
  24.2 1.5 %collective-permute-start.6 = (bf16[32,4096]{1,0:T(8,128)(2,1)S(1)}, bf16[32,4096]{1,0:T(8,128)(2,1)S(1)}, u32[]{:S(2)}, u32[]{:S(2)}) collective-permute-start(bf16[32,4096]{1,0:T(8,128)(2,1)S(1)} %collective-permute-done.5.x2), channel_id=1, source_target_pairs={{0,4},{4,0},{8,12},{12,8},{16,20},{20,16},{24,28},{28,24},{1,5},{5... | collective-permute-start | bytes 786440 | tf_op jit(solution)/shard_map/ppermute | solution.py:18
  36.7 20.0 %collective-permute-start.14 = (bf16[128,2048]{1,0:T(8,128)(2,1)S(1)}, bf16[128,2048]{1,0:T(8,128)(2,1)S(1)}, u32[]{:S(2)}, u32[]{:S(2)}) collective-permute-start(bf16[128,2048]{1,0:T(8,128)(2,1)S(1)} %get-tuple-element.23), channel_id=1, source_target_pairs={{0,4},{4,0},{8,12},{12,8},{16,20},{20,16},{24,28},{28,24},{1,5},{5... | collective-permute-start | bytes 1572872 | tf_op jit(solution)/shard_map/ppermute | solution.py:18
  37.0 4.9 %collective-permute-start.17 = (bf16[16,2048]{1,0:T(8,128)(2,1)S(1)}, bf16[16,2048]{1,0:T(8,128)(2,1)S(1)}, u32[]{:S(2)}, u32[]{:S(2)}) collective-permute-start(bf16[16,2048]{1,0:T(8,128)(2,1)S(1)} %get-tuple-element.26), channel_id=1, source_target_pairs={{0,16},{4,20},{8,24},{12,28},{16,0},{20,4},{24,8},{28,12},{1,17},{... | collective-permute-start | bytes 196616 | tf_op jit(solution)/shard_map/ppermute | solution.py:18
  37.5 19.3 %collective-permute-start.13 = (bf16[128,1024]{1,0:T(8,128)(2,1)S(1)}, bf16[128,1024]{1,0:T(8,128)(2,1)S(1)}, u32[]{:S(2)}, u32[]{:S(2)}) collective-permute-start(bf16[128,1024]{1,0:T(8,128)(2,1)S(1)} %get-tuple-element.21), channel_id=1, source_target_pairs={{0,4},{4,0},{8,12},{12,8},{16,20},{20,16},{24,28},{28,24},{1,5},{5... | collective-permute-start | bytes 786440 | tf_op jit(solution)/shard_map/ppermute | solution.py:18
  37.5 4.6 %collective-permute-start.18 = (bf16[16,2048]{1,0:T(8,128)(2,1)S(1)}, bf16[16,2048]{1,0:T(8,128)(2,1)S(1)}, u32[]{:S(2)}, u32[]{:S(2)}) collective-permute-start(bf16[16,2048]{1,0:T(8,128)(2,1)S(1)} %get-tuple-element.27), channel_id=1, source_target_pairs={{0,20},{4,16},{8,28},{12,24},{16,4},{20,0},{24,12},{28,8},{1,21},{... | collective-permute-start | bytes 196616 | tf_op jit(solution)/shard_map/ppermute | solution.py:18
  39.1 17.6 %collective-permute-start.15 = (bf16[48,2048]{1,0:T(8,128)(2,1)S(1)}, bf16[48,2048]{1,0:T(8,128)(2,1)S(1)}, u32[]{:S(2)}, u32[]{:S(2)}) collective-permute-start(bf16[48,2048]{1,0:T(8,128)(2,1)S(1)} %get-tuple-element.24), channel_id=1, source_target_pairs={{0,8},{4,12},{8,0},{12,4},{16,24},{20,28},{24,16},{28,20},{1,9},{5... | collective-permute-start | bytes 589832 | tf_op jit(solution)/shard_map/ppermute | solution.py:18
  41.9 14.9 %collective-permute-start.16 = (bf16[48,2048]{1,0:T(8,128)(2,1)S(1)}, bf16[48,2048]{1,0:T(8,128)(2,1)S(1)}, u32[]{:S(2)}, u32[]{:S(2)}) collective-permute-start(bf16[48,2048]{1,0:T(8,128)(2,1)S(1)} %get-tuple-element.25), channel_id=1, source_target_pairs={{0,12},{4,8},{8,4},{12,0},{16,28},{20,24},{24,20},{28,16},{1,13},{... | collective-permute-start | bytes 589832 | tf_op jit(solution)/shard_map/ppermute | solution.py:18
  42.2 9.4 %collective-permute-start.19 = (bf16[16,2048]{1,0:T(8,128)(2,1)S(1)}, bf16[16,2048]{1,0:T(8,128)(2,1)S(1)}, u32[]{:S(2)}, u32[]{:S(2)}) collective-permute-start(bf16[16,2048]{1,0:T(8,128)(2,1)S(1)} %get-tuple-element.28), channel_id=1, source_target_pairs={{0,24},{4,28},{8,16},{12,20},{16,8},{20,12},{24,0},{28,4},{1,25},{... | collective-permute-start | bytes 196616 | tf_op jit(solution)/shard_map/ppermute | solution.py:18
  51.6 5.2 %collective-permute-start.20 = (bf16[16,2048]{1,0:T(8,128)(2,1)S(1)}, bf16[16,2048]{1,0:T(8,128)(2,1)S(1)}, u32[]{:S(2)}, u32[]{:S(2)}) collective-permute-start(bf16[16,2048]{1,0:T(8,128)(2,1)S(1)} %get-tuple-element.29), channel_id=1, source_target_pairs={{0,28},{4,24},{8,20},{12,16},{16,12},{20,8},{24,4},{28,0},{1,29},{... | collective-permute-start | bytes 196616 | tf_op jit(solution)/shard_map/ppermute | solution.py:18

commit v2 on v1

v2 whole, which is shorter than its diff:
```python
import functools

import jax
import jax.numpy as jnp
from jax import lax
from jax.experimental import pallas as pl
from jax.experimental.pallas import tpu as pltpu
from jax.sharding import PartitionSpec as P

F32 = jnp.float32
BF16 = jnp.bfloat16
NEG = -1e30
VMEM_LIMIT = 48 * 1024 * 1024


def params():
    return pltpu.CompilerParams(vmem_limit_bytes=VMEM_LIMIT)


def cost(micros):
    return pl.CostEstimate(flops=0, bytes_accessed=int(micros * 3.69e6), transcendentals=0)


def exchange(value, bits):
    count = lax.axis_size("seq")
    return lax.ppermute(value, "seq", [(i, i ^ bits) for i in range(count)])


def dot(a, b):
    return jnp.dot(a, b, preferred_element_type=F32)


def dot_nt(a, b):
    return lax.dot_general(a, b, (((1,), (1,)), ((), ())), preferred_element_type=F32)


def pick_matrix(offs_ref, head, first, levels, tok):
    parts = []
    for level in range(first, levels + 1):
        rate = 2**level
        rows = tok // rate
        kept = lax.rem(offs_ref[level - 1, head], rate)
        row = lax.broadcasted_iota(jnp.int32, (rows, tok), 0)
        col = lax.broadcasted_iota(jnp.int32, (rows, tok), 1)
        parts.append((col == row * rate + kept).astype(F32))
    return jnp.concatenate(parts, axis=0).astype(BF16)


def place_matrix(offs_ref, head, first, levels, tok):
    parts = []
    for level in range(first, levels + 1):
        rate = 2**level
        rows = tok // rate
        kept = lax.rem(offs_ref[level - 1, head], rate)
        row = lax.broadcasted_iota(jnp.int32, (tok, rows), 0)
        col = lax.broadcasted_iota(jnp.int32, (tok, rows), 1)
        parts.append((row == col * rate + kept).astype(F32))
    return jnp.concatenate(parts, axis=1).astype(BF16)


def pick_kernel(levels, heads, dim, offs_ref, k_ref, v_ref, two_ref, three_ref):
    tok = k_ref.shape[0]
    n2, n3 = tok // 4, tok // 8
    for h in range(heads):
        head = pl.program_id(0) * heads + h
        pick = pick_matrix(offs_ref, head, 2, levels, tok)
        cols = slice(h * dim, (h + 1) * dim)
        kv = jnp.concatenate([k_ref[:, cols], v_ref[:, cols]], axis=1)
        got = dot(pick, kv).astype(BF16)
        out = slice(2 * h * dim, 2 * (h + 1) * dim)
        two_ref[:, out] = got[:n2]
        three_ref[:, out] = got[n2 : n2 + n3]


def pick_call(offsets, keys, values, dim):
    tok, width = keys.shape
    levels, heads = offsets.shape
    steps = 2
    per = heads // steps
    block = pl.BlockSpec((tok, per * dim), lambda i, o: (0, i))
    return pl.pallas_call(
        functools.partial(pick_kernel, levels, per, dim),
        grid_spec=pltpu.PrefetchScalarGridSpec(
            num_scalar_prefetch=1,
            grid=(steps,),
            in_specs=[block, block],
            out_specs=[
                pl.BlockSpec((tok // 4, 2 * per * dim), lambda i, o: (0, i)),
                pl.BlockSpec((tok // 8, 2 * per * dim), lambda i, o: (0, i)),
            ],
        ),
        out_shape=[
            jax.ShapeDtypeStruct((tok // 4, 2 * width), BF16),
            jax.ShapeDtypeStruct((tok // 8, 2 * width), BF16),
        ],
        compiler_params=params(),
        cost_estimate=cost(2),
        name="pick_rows",
    )(offsets, keys, values)


def side(*values):
    return jnp.concatenate(values, axis=1)


def stack(*values):
    return jnp.concatenate(values, axis=0)


def split(value, terms):
    parts = []
    for _ in range(terms):
        part = value.astype(BF16)
        parts.append(part)
        value = value - part.astype(F32)
    return parts


def local_scores(pick, levels, offs_ref, head, key0, key1, ones, que0, que1):
    tok, dim = key0.shape
    pos = lax.broadcasted_iota(jnp.int32, (1, 2 * tok), 1)
    bias = jnp.where(lax.rem(pos, 2) == lax.rem(offs_ref[0, head], 2), 0.0, NEG).astype(F32)
    s0 = side(dot_nt(key0, que0), dot_nt(key1, que1)) * dim**-0.5
    s1 = dot_nt(ones, stack(que0, que1)) * dim**-0.5 + bias
    return stack(s0, s1)


def pre_kernel(
    levels, per, dim, offs_ref, core_ref, q0, q1, k0, k1, v0, v1, exps, stats, near, selq
):
    tok = q0.shape[0]
    n1 = tok // 2
    heads = per * pl.num_programs(0)
    for h in range(per):
        head = core_ref[0] * heads + pl.program_id(0) * per + h
        pick = pick_matrix(offs_ref, head, 1, levels, tok)
        cols = slice(h * dim, (h + 1) * dim)
        wide = slice(2 * h * dim, 2 * (h + 1) * dim)
        lanes = slice(2 * h * tok, 2 * (h + 1) * tok)
        own = dot(pick, side(k0[:, cols], v0[:, cols])).astype(BF16)
        oth = dot(pick, side(k1[:, cols], v1[:, cols])).astype(BF16)
        ones = stack(own[:n1], oth[:n1])
        near[:, wide] = stack(ones, own[n1:], oth[n1:])
        que0, que1 = q0[:, cols], q1[:, cols]
        far_pick = pick[n1:]
        selq[:, cols] = stack(dot(far_pick, que0), dot(far_pick, que1)).astype(BF16)
        s = local_scores(
            pick, levels, offs_ref, head, k0[:, cols], k1[:, cols], ones[:, :dim], que0, que1
        )
        top = jnp.max(s, axis=0, keepdims=True)
        e = jnp.exp(s - top)
        exps[:, lanes] = e.astype(BF16)
        stats[0:1, lanes] = top
        stats[1:2, lanes] = jnp.sum(e, axis=0, keepdims=True)


def pre_call(offsets, core, raw, dim):
    tok, width = raw[0].shape
    levels, heads = offsets.shape
    half = heads // 2
    per = 2
    steps = half // per
    raw_spec = pl.BlockSpec((tok, per * dim), lambda i, o, c: (0, c[0] * steps + i))
    sel = 2 * (tok // 4 + tok // 8)

    def out(rows, lanes, kind=BF16):
        return (
            pl.BlockSpec((rows, per * lanes), lambda i, o, c: (0, i)),
            jax.ShapeDtypeStruct((rows, half * lanes), kind),
        )

    outs = [out(2 * tok, 2 * tok), out(8, 2 * tok, F32), out(tok + sel, 2 * dim), out(sel, dim)]
    return pl.pallas_call(
        functools.partial(pre_kernel, levels, per, dim),
        grid_spec=pltpu.PrefetchScalarGridSpec(
            num_scalar_prefetch=2,
            grid=(steps,),
            in_specs=[raw_spec] * 6,
            out_specs=[o[0] for o in outs],
        ),
        out_shape=[o[1] for o in outs],
        compiler_params=params(),
        cost_estimate=cost(5),
        name="local_scores",
    )(offsets, core, *raw)


def far_kernel(
    levels, per, dim, offs_ref, core_ref, exps, stats, near, selq, v0, v1, g0, g1,
    x2, xx2, x3, xx3, y3, yy3, d3, dd3,
    xa, xb, yab, da, db, ngrad, dqt, stats2,
):
    tok = g0.shape[0]
    n1, n2, n3 = tok // 2, tok // 4, tok // 8
    sel = n2 + n3
    scale = dim**-0.5
    heads = per * pl.num_programs(0)
    lane = lax.broadcasted_iota(jnp.int32, (1, 2 * sel), 1)
    is2 = lax.rem(lane, sel) < n2
    pos = lax.broadcasted_iota(jnp.int32, (1, 2 * tok), 1)
    for h in range(per):
        head = core_ref[0] * heads + pl.program_id(0) * per + h
        pick = pick_matrix(offs_ref, head, 2, levels, tok)
        none = jnp.zeros_like(pick)
        both = stack(side(pick, none), side(none, pick))
        cols = slice(h * dim, (h + 1) * dim)
        kc = slice(2 * h * dim, (2 * h + 1) * dim)
        vc = slice((2 * h + 1) * dim, (2 * h + 2) * dim)
        wide = slice(2 * h * dim, 2 * (h + 1) * dim)
        lanes = slice(2 * h * tok, 2 * (h + 1) * tok)
        gra0, gra1 = g0[:, cols], g1[:, cols]
        gsel = stack(dot(pick, gra0), dot(pick, gra1)).astype(BF16)
        qsel = selq[:, cols]

        def rows(c):
            a, b = near[tok : tok + sel, c], near[tok + sel :, c]
            return stack(
                a[:n2], b[:n2], x2[:, c], xx2[:, c], a[n2:], b[n2:],
                *(ref[:, c] for ref in (x3, xx3, y3, yy3, d3, dd3)),
            )

        keys, vals = rows(kc), rows(vc)
        st = dot_nt(keys, qsel)
        s = jnp.where(is2, st[:tok], st[tok:]) * scale
        top = jnp.max(s, axis=0, keepdims=True)
        e = jnp.exp(s - top)
        size = jnp.sum(e, axis=0, keepdims=True)
        pt = dot_nt(vals, gsel)
        p = jnp.where(is2, pt[:tok], pt[tok:])
        dhat = jnp.sum(e * p, axis=0, keepdims=True)
        p0 = side(dot_nt(v0[:, cols], gra0), dot_nt(v1[:, cols], gra1))
        p1 = dot_nt(near[:tok, vc], stack(gra0, gra1))
        ex = exps[:, lanes]
        dloc = jnp.sum(ex[:tok].astype(F32) * p0 + ex[tok:].astype(F32) * p1, axis=0, keepdims=True)
        terms = split(top, 3) + split(size, 2) + split(dhat, 2)
        terms = stack(*terms)
        zero = jnp.zeros_like(terms)
        spread = dot(stack(jnp.where(is2, terms, zero), jnp.where(is2, zero, terms)), both)

        def level_stats(level, lo):
            rate = 2**level
            on = lax.rem(pos, rate) == lax.rem(offs_ref[level - 1, head], rate)
            t = spread[lo : lo + 1] + spread[lo + 1 : lo + 2] + spread[lo + 2 : lo + 3]
            return (
                jnp.where(on, t, NEG),
                spread[lo + 3 : lo + 4] + spread[lo + 4 : lo + 5],
                spread[lo + 5 : lo + 6] + spread[lo + 6 : lo + 7],
            )

        t1, z1 = stats[0:1, lanes], stats[1:2, lanes]
        t2, z2, d2 = level_stats(2, 0)
        t3, z3, d3v = level_stats(3, 7)
        high = jnp.maximum(t1, jnp.maximum(t2, t3))
        a1, a2, a3 = jnp.exp(t1 - high), jnp.exp(t2 - high), jnp.exp(t3 - high)
        inv = 1.0 / (a1 * z1 + a2 * z2 + a3 * z3)
        f1, f2, f3 = a1 * inv, a2 * inv, a3 * inv
        delta = f1 * dloc + f2 * d2 + f3 * d3v
        stats2[0:1, lanes] = f1
        stats2[1:2, lanes] = delta
        back = dot_nt(stack(*split(f2, 2), *split(f3, 2), *split(delta, 2)), both)
        f = jnp.where(is2, back[0:1] + back[1:2], back[2:3] + back[3:4])
        dl = back[4:5] + back[5:6]
        w = e * f
        ds = w * (p - dl)
        zero = jnp.zeros_like(w)

        def apart(value):
            return stack(jnp.where(is2, value, zero), jnp.where(is2, zero, value)).astype(BF16)

        dsm = apart(ds)
        dkv = side(dot(dsm, qsel) * scale, dot(apart(w), gsel)).astype(BF16)
        xa[:n2, wide] = dkv[2 * n2 : 3 * n2]
        xb[:n2, wide] = dkv[3 * n2 : 4 * n2]
        third = [dkv[tok + i * n3 : tok + (i + 1) * n3] for i in range(8)]
        xa[n2:, wide] = third[2]
        xb[n2:, wide] = third[3]
        yab[:, wide] = stack(third[4], third[5])
        da[:, wide] = third[6]
        db[:, wide] = third[7]
        ngrad[:, wide] = stack(dkv[:n2], third[0], dkv[n2 : 2 * n2], third[1])
        dqt[:, h * dim : h * dim + 2 * sel] = dot(keys.T, dsm).astype(BF16)


def far_call(offsets, core, pre, raw, far, dim):
    tok, width = raw[0].shape
    levels, heads = offsets.shape
    half = heads // 2
    per = 2
    steps = half // per
    n2, n3 = tok // 4, tok // 8
    raw_spec = pl.BlockSpec((tok, per * dim), lambda i, o, c: (0, c[0] * steps + i))

    def near_spec(a):
        return pl.BlockSpec((a.shape[0], a.shape[1] // steps), lambda i, o, c: (0, i))

    def far_spec(a):
        return pl.BlockSpec((a.shape[0], 2 * per * dim), lambda i, o, c: (0, c[0] * steps + i))

    def out(rows, lanes, kind=BF16):
        return (
            pl.BlockSpec((rows, per * lanes), lambda i, o, c: (0, i)),
            jax.ShapeDtypeStruct((rows, half * lanes), kind),
        )

    outs = [out(n2 + n3, 2 * dim)] * 2 + [out(2 * n3, 2 * dim)] + [out(n3, 2 * dim)] * 2
    outs += [out(2 * (n2 + n3), 2 * dim), out(dim, dim), out(8, 2 * tok, F32)]
    return pl.pallas_call(
        functools.partial(far_kernel, levels, per, dim),
        grid_spec=pltpu.PrefetchScalarGridSpec(
            num_scalar_prefetch=2,
            grid=(steps,),
            in_specs=[near_spec(a) for a in pre] + [raw_spec] * 4 + [far_spec(a) for a in far],
            out_specs=[o[0] for o in outs],
        ),
        out_shape=[o[1] for o in outs],
        compiler_params=params(),
        cost_estimate=cost(4),
        name="far_levels",
    )(offsets, core, *pre, *raw, *far)


def near_kernel(
    levels, per, dim, offs_ref, core_ref, exps, stats2, near, ngrad, dqt,
    q0, q1, k0, k1, v0, v1, g0, g1, mine, other,
):
    tok = q0.shape[0]
    n1 = tok // 2
    sel = tok // 4 + tok // 8
    scale = dim**-0.5
    heads = per * pl.num_programs(0)
    for h in range(per):
        head = core_ref[0] * heads + pl.program_id(0) * per + h
        pick = pick_matrix(offs_ref, head, 2, levels, tok)
        place = place_matrix(offs_ref, head, 1, levels, tok)
        cols = slice(h * dim, (h + 1) * dim)
        kc = slice(2 * h * dim, (2 * h + 1) * dim)
        vc = slice((2 * h + 1) * dim, (2 * h + 2) * dim)
        wide = slice(2 * h * dim, 2 * (h + 1) * dim)
        lanes = slice(2 * h * tok, 2 * (h + 1) * tok)
        que0, que1, gra0, gra1 = q0[:, cols], q1[:, cols], g0[:, cols], g1[:, cols]
        que, gra = stack(que0, que1), stack(gra0, gra1)
        p0 = side(dot_nt(v0[:, cols], gra0), dot_nt(v1[:, cols], gra1))
        p = stack(p0, dot_nt(near[:tok, vc], gra))
        w = exps[:, lanes].astype(F32) * stats2[0:1, lanes]
        wb = w.astype(BF16)
        ds = (w * (p - stats2[1:2, lanes])).astype(BF16)
        dkv1 = side(dot(ds[tok:], que) * scale, dot(wb[tok:], gra)).astype(BF16)
        ds0, ds1 = ds[:tok, :tok], ds[:tok, tok:]
        kv0 = side(dot(ds0, que0) * scale, dot(wb[:tok, :tok], gra0))
        kv1 = side(dot(ds1, que1) * scale, dot(wb[:tok, tok:], gra1))
        kv0 += dot(place, stack(dkv1[:n1], ngrad[:sel, wide]))
        kv1 += dot(place, stack(dkv1[n1:], ngrad[sel:, wide]))
        dqa = dot(near[:tok, kc].T, ds[tok:])
        dq0 = dqa[:, :tok] + dot(k0[:, cols].T, ds0)
        dq1 = dqa[:, tok:] + dot(k1[:, cols].T, ds1)
        dq0 += dot(dqt[:, h * dim : h * dim + sel], pick)
        dq1 += dot(dqt[:, h * dim + sel : h * dim + 2 * sel], pick)
        for ref, dq, kv in ((mine, dq0, kv0), (other, dq1, kv1)):
            lo = 3 * h * dim
            ref[:, lo : lo + dim] = (dq * scale).T.astype(BF16)
            ref[:, lo + dim : lo + 3 * dim] = kv.astype(BF16)


def near_call(offsets, core, mid, raw, dim):
    tok, width = raw[0].shape
    levels, heads = offsets.shape
    half = heads // 2
    per = 2
    steps = half // per
    raw_spec = pl.BlockSpec((tok, per * dim), lambda i, o, c: (0, c[0] * steps + i))

    def mid_spec(a):
        return pl.BlockSpec((a.shape[0], a.shape[1] // steps), lambda i, o, c: (0, i))

    out_spec = pl.BlockSpec((tok, 3 * per * dim), lambda i, o, c: (0, i))
    return pl.pallas_call(
        functools.partial(near_kernel, levels, per, dim),
        grid_spec=pltpu.PrefetchScalarGridSpec(
            num_scalar_prefetch=2,
            grid=(steps,),
            in_specs=[mid_spec(a) for a in mid] + [raw_spec] * 8,
            out_specs=[out_spec] * 2,
        ),
        out_shape=[jax.ShapeDtypeStruct((tok, 3 * half * dim), BF16)] * 2,
        compiler_params=params(),
        cost_estimate=cost(7),
        name="near_levels",
    )(offsets, core, *mid, *raw)


def final_kernel(
    levels, per, dim, offs_ref, core_ref, ba, bb, xa, xb, ya, yb, da, db, dq, dk, dv
):
    tok = dq.shape[0]
    n2, n3 = tok // 4, tok // 8
    heads = per * pl.num_programs(0)
    swap = pl.program_id(0) * 2 // pl.num_programs(0) != core_ref[0]

    def work(base, x, y, d):
        for h in range(per):
            head = pl.program_id(0) * per + h
            place = place_matrix(offs_ref, head, 2, levels, tok)
            cols = slice(h * dim, (h + 1) * dim)
            src = slice(2 * h * dim, 2 * (h + 1) * dim)
            lo = 3 * h * dim
            third = x[n2:, src].astype(F32) + y[:, src].astype(F32) + d[:, src].astype(F32)
            part = stack(x[:n2, src], third.astype(BF16))
            total = base[:, lo + dim : lo + 3 * dim].astype(F32) + dot(place, part)
            dq[:, cols] = base[:, lo : lo + dim]
            dk[:, cols] = total[:, :dim].astype(BF16)
            dv[:, cols] = total[:, dim:].astype(BF16)

    @pl.when(jnp.logical_not(swap))
    def _():
        work(ba, xa, ya, da)

    @pl.when(swap)
    def _():
        work(bb, xb, yb, db)


def final_call(offsets, core, parts, dim):
    levels, heads = offsets.shape
    tok = parts[0].shape[0]
    steps = 4
    per = heads // steps
    third = tok // 8

    def spec(a, far, row, rows):
        cols = a.shape[1] * 2 // steps

        def where(i, o, c):
            turn = 1 - c[0] if far else c[0]
            return row, jnp.clip(i - turn * (steps // 2), 0, steps // 2 - 1)

        return pl.BlockSpec((rows, cols), where)

    specs = []
    for i, a in enumerate(parts):
        far = i % 2 == 1
        if i in (4, 5):
            specs.append(spec(a, far, 1 if far else 0, third))
        else:
            specs.append(spec(a, far, 0, a.shape[0]))
    out = pl.BlockSpec((tok, per * dim), lambda i, o, c: (0, i))
    return pl.pallas_call(
        functools.partial(final_kernel, levels, per, dim),
        grid_spec=pltpu.PrefetchScalarGridSpec(
            num_scalar_prefetch=2,
            grid=(steps,),
            in_specs=specs,
            out_specs=[out] * 3,
        ),
        out_shape=[jax.ShapeDtypeStruct((tok, heads * dim), BF16)] * 3,
        compiler_params=params(),
        cost_estimate=cost(3),
        name="add_pieces",
    )(offsets, core, *parts)


def per_device(queries, keys_in, values, out_grads, offsets):
    heads = offsets.shape[1]
    dim = queries.shape[2] // heads
    sections = lax.axis_size("section")
    core = lax.rem(lax.axis_index("seq"), 2).astype(jnp.int32).reshape(1)
    grads = lax.ppermute(
        out_grads[0], "section", [(i, (i - 1) % sections) for i in range(sections)]
    )
    q, k, v = queries[0], keys_in[0], values[0]
    q_oth, k_oth, v_oth = exchange(q, 1), exchange(k, 1), exchange(v, 1)
    two, three = pick_call(offsets, k, v, dim)
    x3 = exchange(three, 2)
    y3 = exchange(three, 4)
    x2 = exchange(two, 2)
    d3 = exchange(x3, 4)
    exps, stats, near, selq = pre_call(offsets, core, [q, q_oth, k, k_oth, v, v_oth], dim)
    far = []
    for piece in (x2, x3, y3, d3):
        far += [piece, exchange(piece, 1)]
    g_oth = exchange(grads, 1)
    xa, xb, yab, da, db, ngrad, dqt, stats2 = far_call(
        offsets, core, [exps, stats, near, selq], [v, v_oth, grads, g_oth], far, dim
    )
    xa, xb, da, db = exchange(xa, 2), exchange(xb, 3), exchange(da, 6), exchange(db, 7)
    y = exchange(yab, 4)
    yy = exchange(y, 1)
    mine, other = near_call(
        offsets, core, [exps, stats2, near, ngrad, dqt],
        [q, q_oth, k, k_oth, v, v_oth, grads, g_oth], dim,
    )
    parts = [mine, exchange(other, 1), xa, xb, y, yy, da, db]
    dq, dk, dv = final_call(offsets, core, parts, dim)
    return dq[None], dk[None], dv[None]


def solution(mesh):
    spec = P("section", "seq", None)
    return jax.shard_map(
        per_device,
        mesh=mesh,
        in_specs=(spec, spec, spec, spec, P()),
        out_specs=(spec, spec, spec),
        check_vma=False,
    )
```

time: 60.4 us -> 71 us (1.18)
  Pallas kernels: 16.5 us -> 23.9 us
  local copies, waits for them, and re-layouts: 0.01 us -> 4.11 us
  waiting for transfers between devices: 25 us -> 23.6 us
    pallas_call x1 -> x3, Pallas kernels: 11 us -> 19.2 us  [the longest x1 8.47 us: far_call(): pl.pallas_call(functools.partial(far_kernel, levels, per, dim), grid_spec...]
    unnamed x6 -> x16, local copies, waits for them, and re-layouts: 0.01 us -> 4.11 us
    ppermute x20 -> x19, waiting for transfers between devices: 25 us -> 23.6 us  [exchange(): return lax.ppermute(value, 'seq', [(i, i ^ bits) for i in range(count)])]
    pallas_call x1, Pallas kernels: 2.08 us -> 1.15 us  [pick_call(): pl.pallas_call(functools.partial(pick_kernel, levels, per, dim), grid_spe...]
    ppermute x20 -> x19, starting transfers between devices: 12.9 us -> 13.2 us  [exchange(): return lax.ppermute(value, 'seq', [(i, i ^ bits) for i in range(count)])]
  transfers between devices with their start and end apart: 21 -> 20, of which waited for: 10 -> 7; matrix products, arithmetic and copies ran while one was open for 0% -> 0% of each run, Pallas kernels for 3% -> 6%
where the time goes in v2:
time: 71 us; the launch traced here: 70.7 us
  Pallas kernels  23.9 us (34%)
  waiting for transfers between devices  23.6 us (33%)
  starting transfers between devices  18.3 us (26%)
  local copies, waits for them, and re-layouts  4.11 us (6%)
  between operations  0.74 us (1%)
    ppermute x19, waiting for transfers between devices, exchange(): return lax.ppermute(value, 'seq', [(i, i ^ bits) for i in range(count)])  23.6 us
    ppermute x19, starting transfers between devices, exchange(): return lax.ppermute(value, 'seq', [(i, i ^ bits) for i in range(count)])  13.2 us
    pallas_call x1, Pallas kernels, far_call(): pl.pallas_call(functools.partial(far_kernel, levels, per, dim), grid_spec...  8.47 us
    pallas_call x1, Pallas kernels, near_call(): pl.pallas_call(functools.partial(near_kernel, levels, per, dim), grid_spe...  7.55 us
    ppermute x1, starting transfers between devices, per_device(): lax.ppermute(out_grads[0], 'section', [(i, (i - 1) % sections) for i in r...  5.1 us
    unnamed x16, local copies, waits for them, and re-layouts  4.11 us
    pallas_call x1, Pallas kernels, final_call(): pl.pallas_call(functools.partial(final_kernel, levels, per, dim), grid_sp...  3.47 us
    pallas_call x1, Pallas kernels, pre_call(): pl.pallas_call(functools.partial(pre_kernel, levels, per, dim), grid_spec...  3.23 us
  transfers between devices with their start and end apart: 20, of which 7 were waited for; matrix products, arithmetic and copies ran while one was open for 0% of the time, Pallas kernels for 6%

profile of v2, /device:TPU:0, one launch (start us, length us, event | category | flops | bytes accessed | tf_op | source)
XLA Modules:
  0.0 70.7 jit_solution(10270202472783634904)
XLA Ops:
  0.6 5.1 %collective-permute-start.3 = (bf16[128,2048]{1,0:T(8,128)(2,1)}, bf16[128,2048]{1,0:T(8,128)(2,1)S(1)}, u32[]{:S(2)}, u32[]{:S(2)}) collective-permute-start(bf16[128,2048]{1,0:T(8,128)(2,1)} %bitcast.20), channel_id=1, source_target_pairs={{0,3},{1,0},{2,1},{3,2},{4,7},{5,4},{6,5},{7,6},{8,11},{9,8},{10,9... | collective-permute-start | bytes 1572872 | tf_op jit(solution)/shard_map/ppermute | solution.py:466
  5.7 1.0 %copy-done = bf16[1,128,2048]{2,1,0:T(8,128)(2,1)S(1)} copy-done((bf16[1,128,2048]{2,1,0:T(8,128)(2,1)S(1)}, bf16[1,128,2048]{2,1,0:T(8,128)(2,1)}, u32[]{:S(2)}) %copy-start) | copy-done | bytes 524312
  6.8 1.0 %copy-done.2 = bf16[1,128,2048]{2,1,0:T(8,128)(2,1)S(1)} copy-done((bf16[1,128,2048]{2,1,0:T(8,128)(2,1)S(1)}, bf16[1,128,2048]{2,1,0:T(8,128)(2,1)}, u32[]{:S(2)}) %copy-start.2) | copy-done | bytes 524312
  7.8 1.1 %pick_rows.1 = (bf16[32,4096]{1,0:T(8,128)(2,1)S(1)}, bf16[16,4096]{1,0:T(8,128)(2,1)S(1)}) custom-call(s32[3,16]{1,0:T(4,128)S(1)} %copy-done.7, bf16[128,2048]{1,0:T(8,128)(2,1)S(1)} %bitcast.13, bf16[128,2048]{1,0:T(8,128)(2,1)S(1)} %bitcast.8), custom_call_target="tpu_custom_call" | custom-call | bytes 7380000 | tf_op jit(solution)/shard_map/pick_rows/pallas_call | solution.py:81
  9.0 1.6 %collective-permute-start.7 = (bf16[16,4096]{1,0:T(8,128)(2,1)S(1)}, bf16[16,4096]{1,0:T(8,128)(2,1)S(1)}, u32[]{:S(2)}, u32[]{:S(2)}) collective-permute-start(bf16[16,4096]{1,0:T(8,128)(2,1)S(1)} %get-tuple-element.27), channel_id=1, source_target_pairs={{0,8},{4,12},{8,0},{12,4},{16,24},{20,28},{24,16},{28,20},{1,9},{5... | collective-permute-start | bytes 393224 | tf_op jit(solution)/shard_map/ppermute | solution.py:26
  10.5 1.5 %collective-permute-start.9 = (bf16[16,4096]{1,0:T(8,128)(2,1)S(1)}, bf16[16,4096]{1,0:T(8,128)(2,1)}, u32[]{:S(2)}, u32[]{:S(2)}) collective-permute-start(bf16[16,4096]{1,0:T(8,128)(2,1)S(1)} %get-tuple-element.27), channel_id=1, source_target_pairs={{0,16},{4,20},{8,24},{12,28},{16,0},{20,4},{24,8},{28,12},{1,17},{... | collective-permute-start | bytes 393224 | tf_op jit(solution)/shard_map/ppermute | solution.py:26
  12.1 0.0 collective-permute-start.1
  12.1 0.5 collective-permute-start
  12.6 1.4 %collective-permute-done.7.x3 = bf16[16,4096]{1,0:T(8,128)(2,1)S(1)} collective-permute-done((bf16[16,4096]{1,0:T(8,128)(2,1)S(1)}, bf16[16,4096]{1,0:T(8,128)(2,1)S(1)}, u32[]{:S(2)}, u32[]{:S(2)}) %collective-permute-start.7) | collective-permute-done | bytes 131104 | tf_op jit(solution)/shard_map/ppermute | solution.py:26
  14.0 1.5 %collective-permute-start.11 = (bf16[16,4096]{1,0:T(8,128)(2,1)S(1)}, bf16[16,4096]{1,0:T(8,128)(2,1)}, u32[]{:S(2)}, u32[]{:S(2)}) collective-permute-start(bf16[16,4096]{1,0:T(8,128)(2,1)S(1)} %collective-permute-done.7.x3), channel_id=1, source_target_pairs={{0,16},{4,20},{8,24},{12,28},{16,0},{20,4},{24,8},{28,12},{1,17},{... | collective-permute-start | bytes 393224 | tf_op jit(solution)/shard_map/ppermute | solution.py:26
  15.5 0.2 collective-permute-done.9.y3
  15.8 0.0 collective-permute-start.2
  15.8 3.3 %collective-permute-done.11.d3 = bf16[16,4096]{1,0:T(8,128)(2,1)} collective-permute-done((bf16[16,4096]{1,0:T(8,128)(2,1)S(1)}, bf16[16,4096]{1,0:T(8,128)(2,1)}, u32[]{:S(2)}, u32[]{:S(2)}) %collective-permute-start.11) | collective-permute-done | bytes 131104 | tf_op jit(solution)/shard_map/ppermute | solution.py:26
  19.1 1.5 %collective-permute-start.5 = (bf16[32,4096]{1,0:T(8,128)(2,1)S(1)}, bf16[32,4096]{1,0:T(8,128)(2,1)S(1)}, u32[]{:S(2)}, u32[]{:S(2)}) collective-permute-start(bf16[32,4096]{1,0:T(8,128)(2,1)S(1)} %get-tuple-element.26), channel_id=1, source_target_pairs={{0,8},{4,12},{8,0},{12,4},{16,24},{20,28},{24,16},{28,20},{1,9},{5... | collective-permute-start | bytes 786440 | tf_op jit(solution)/shard_map/ppermute | solution.py:26
  20.6 0.0 collective-permute-done.3.g0
  20.6 0.0 collective-permute-start.4
  20.6 4.9 %collective-permute-done.5.x2 = bf16[32,4096]{1,0:T(8,128)(2,1)S(1)} collective-permute-done((bf16[32,4096]{1,0:T(8,128)(2,1)S(1)}, bf16[32,4096]{1,0:T(8,128)(2,1)S(1)}, u32[]{:S(2)}, u32[]{:S(2)}) %collective-permute-start.5) | collective-permute-done | bytes 262176 | tf_op jit(solution)/shard_map/ppermute | solution.py:26
  25.5 0.0 collective-permute-start.6
  25.5 0.0 collective-permute-done.q1
  25.5 0.5 collective-permute-start.8
  26.0 0.0 collective-permute-done.1.k1
  26.0 0.1 collective-permute-start.10
  26.1 0.0 collective-permute-done.2.v1
  26.1 0.4 collective-permute-start.12
  26.5 1.0 %copy-done.6 = bf16[1,128,2048]{2,1,0:T(8,128)(2,1)S(1)} copy-done((bf16[1,128,2048]{2,1,0:T(8,128)(2,1)S(1)}, bf16[1,128,2048]{2,1,0:T(8,128)(2,1)}, u32[]{:S(2)}) %copy-start.6) | copy-done | bytes 524312
  27.6 3.2 %local_scores.1 = (bf16[256,2048]{1,0:T(8,128)(2,1)S(1)}, f32[8,2048]{1,0:T(8,128)S(1)}, bf16[224,2048]{1,0:T(8,128)(2,1)S(1)}, bf16[96,1024]{1,0:T(8,128)(2,1)S(1)}) custom-call(s32[3,16]{1,0:T(4,128)S(1)} %copy-done.7, s32[1]{0:T(128)} %bitcast.core_ref, bf16[128,2048]{1,0:T(8,128)(2,1)S(1)} %bitcast.18, bf16[128,2048]{1,0:T(8,128)(2,1)S(1)} %collective-permute-done.q1, ...), custom_call_target="tpu_custom_call" | custom-call | bytes 18450000 | tf_op jit(solution)/shard_map/local_scores/pallas_call | solution.py:173
  30.8 1.0 %copy-done.4 = bf16[256,2048]{1,0:T(8,128)(2,1)} copy-done((bf16[256,2048]{1,0:T(8,128)(2,1)}, bf16[256,2048]{1,0:T(8,128)(2,1)S(1)}, u32[]{:S(2)}) %copy-start.4) | copy-done | bytes 1048600
  31.8 0.0 collective-permute-done.10.yy3
  31.8 0.0 collective-permute-done.8.xx3
  31.8 0.0 collective-permute-done.12.dd3
  31.8 0.0 collective-permute-done.6.xx2
  31.8 0.0 collective-permute-done.4.g1
  31.8 8.5 %far_levels.1 = (bf16[48,2048]{1,0:T(8,128)(2,1)S(1)}, bf16[48,2048]{1,0:T(8,128)(2,1)S(1)}, bf16[32,2048]{1,0:T(8,128)(2,1)S(1)}, bf16[16,2048]{1,0:T(8,128)(2,...) custom-call(s32[3,16]{1,0:T(4,128)S(1)} %copy-done.7, ...), custom_call_target="tpu_custom_call" | custom-call | bytes 14760000 | tf_op jit(solution)/shard_map/far_levels/pallas_call | solution.py:307
  40.3 7.5 %near_levels.1 = (bf16[128,3072]{1,0:T(8,128)(2,1)S(1)}, bf16[128,3072]{1,0:T(8,128)(2,1)}) custom-call(s32[3,16]{1,0:T(4,128)S(1)} %copy-done.7, s32[1]{0:T(128)} %bitcast.core_ref, bf16[256,2048]{1,0:T(8,128)(2,1)} %copy-done.4, f32[8,2048]{1,0:T(8,128)S(1)} %get-tuple-element.28.stats2, bf16[224,2048]{1,0:T(8,128)(2,1)} %copy-done.5, ...), custom_call_target="tpu_custom_call" | custom-call | bytes 25830000 | tf_op jit(solution)/shard_map/near_levels/pallas_call | solution.py:376
  47.8 0.1 collective-permute-start.13
  47.9 1.5 %collective-permute-start.16 = (bf16[32,2048]{1,0:T(8,128)(2,1)S(1)}, bf16[32,2048]{1,0:T(8,128)(2,1)S(1)}, u32[]{:S(2)}, u32[]{:S(2)}) collective-permute-start(bf16[32,2048]{1,0:T(8,128)(2,1)S(1)} %get-tuple-element.35), channel_id=1, source_target_pairs={{0,16},{4,20},{8,24},{12,28},{16,0},{20,4},{24,8},{28,12},{1,17},{... | collective-permute-start | bytes 393224 | tf_op jit(solution)/shard_map/ppermute | solution.py:26
  49.4 1.5 %collective-permute-start.14 = (bf16[48,2048]{1,0:T(8,128)(2,1)S(1)}, bf16[48,2048]{1,0:T(8,128)(2,1)S(1)}, u32[]{:S(2)}, u32[]{:S(2)}) collective-permute-start(bf16[48,2048]{1,0:T(8,128)(2,1)S(1)} %get-tuple-element.33), channel_id=1, source_target_pairs={{0,8},{4,12},{8,0},{12,4},{16,24},{20,28},{24,16},{28,20},{1,9},{5... | collective-permute-start | bytes 589832 | tf_op jit(solution)/shard_map/ppermute | solution.py:26
  50.9 0.0 collective-permute-start.15
  51.0 1.4 %collective-permute-start.18 = (bf16[16,2048]{1,0:T(8,128)(2,1)S(1)}, bf16[16,2048]{1,0:T(8,128)(2,1)S(1)}, u32[]{:S(2)}, u32[]{:S(2)}) collective-permute-start(bf16[16,2048]{1,0:T(8,128)(2,1)S(1)} %get-tuple-element.36), channel_id=1, source_target_pairs={{0,24},{4,28},{8,16},{12,20},{16,8},{20,12},{24,0},{28,4},{1,25},{... | collective-permute-start | bytes 196616 | tf_op jit(solution)/shard_map/ppermute | solution.py:26
  52.4 1.4 %collective-permute-done.16.ya = bf16[32,2048]{1,0:T(8,128)(2,1)S(1)} collective-permute-done((bf16[32,2048]{1,0:T(8,128)(2,1)S(1)}, bf16[32,2048]{1,0:T(8,128)(2,1)S(1)}, u32[]{:S(2)}, u32[]{:S(2)}) %collective-permute-start.16) | collective-permute-done | bytes 131104 | tf_op jit(solution)/shard_map/ppermute | solution.py:26
  53.8 0.0 collective-permute-start.17
  53.8 8.2 %collective-permute-done.18.da = bf16[16,2048]{1,0:T(8,128)(2,1)S(1)} collective-permute-done((bf16[16,2048]{1,0:T(8,128)(2,1)S(1)}, bf16[16,2048]{1,0:T(8,128)(2,1)S(1)}, u32[]{:S(2)}, u32[]{:S(2)}) %collective-permute-start.18) | collective-permute-done | bytes 65568 | tf_op jit(solution)/shard_map/ppermute | solution.py:26
  62.0 1.1 %collective-permute-start.19 = (bf16[16,2048]{1,0:T(8,128)(2,1)S(1)}, bf16[16,2048]{1,0:T(8,128)(2,1)S(1)}, u32[]{:S(2)}, u32[]{:S(2)}) collective-permute-start(bf16[16,2048]{1,0:T(8,128)(2,1)S(1)} %get-tuple-element.37), channel_id=1, source_target_pairs={{0,28},{4,24},{8,20},{12,16},{16,12},{20,8},{24,4},{28,0},{1,29},{... | collective-permute-start | bytes 196616 | tf_op jit(solution)/shard_map/ppermute | solution.py:26
  63.1 4.1 %collective-permute-done.19.db = bf16[16,2048]{1,0:T(8,128)(2,1)S(1)} collective-permute-done((bf16[16,2048]{1,0:T(8,128)(2,1)S(1)}, bf16[16,2048]{1,0:T(8,128)(2,1)S(1)}, u32[]{:S(2)}, u32[]{:S(2)}) %collective-permute-start.19) | collective-permute-done | bytes 65568 | tf_op jit(solution)/shard_map/ppermute | solution.py:26
  67.2 0.0 collective-permute-done.14.xa
  67.2 0.0 collective-permute-done.15.xb
  67.2 0.0 collective-permute-done.13.bb
  67.2 3.5 %add_pieces.1 = (bf16[128,2048]{1,0:T(8,128)(2,1)}, bf16[128,2048]{1,0:T(8,128)(2,1)}, bf16[128,2048]{1,0:T(8,128)(2,1)}) custom-call(s32[3,16]{1,0:T(4,128)S(1)} %copy-done.7, s32[1]{0:T(128)} %bitcast.core_ref, bf16[128,3072]{1,0:T(8,128)(2,1)S(1)} %get-tuple-element.31.ba, bf16[128,3072]{1,0:T(8,128)(2,1)S(1)} %collective-permute-done.13.bb, ...), custom_call_target="tpu_custom_call" | custom-call | bytes 11070000 | tf_op jit(solution)/shard_map/add_pieces/pallas_call | solution.py:446
  (13 shorter events, 0.0 us)
Async XLA Ops:
  0.6 5.1 %copy-start.7 = (s32[3,16]{1,0:T(4,128)S(1)}, s32[3,16]{1,0:T(4,128)}, u32[]{:S(2)}) copy-start(s32[3,16]{1,0:T(4,128)} %offs_ref.9) | copy-start | bytes 580
  0.6 19.9 %collective-permute-start.3 = (bf16[128,2048]{1,0:T(8,128)(2,1)}, bf16[128,2048]{1,0:T(8,128)(2,1)S(1)}, u32[]{:S(2)}, u32[]{:S(2)}) collective-permute-start(bf16[128,2048]{1,0:T(8,128)(2,1)} %bitcast.20), channel_id=1, source_target_pairs={{0,3},{1,0},{2,1},{3,2},{4,7},{5,4},{6,5},{7,6},{8,11},{9,8},{10,9... | collective-permute-start | bytes 1572872 | tf_op jit(solution)/shard_map/ppermute | solution.py:466
  5.7 1.0 %copy-start = (bf16[1,128,2048]{2,1,0:T(8,128)(2,1)S(1)}, bf16[1,128,2048]{2,1,0:T(8,128)(2,1)}, u32[]{:S(2)}) copy-start(bf16[1,128,2048]{2,1,0:T(8,128)(2,1)} %param.7) | copy-start | bytes 1572868
  6.8 1.0 %copy-start.2 = (bf16[1,128,2048]{2,1,0:T(8,128)(2,1)S(1)}, bf16[1,128,2048]{2,1,0:T(8,128)(2,1)}, u32[]{:S(2)}) copy-start(bf16[1,128,2048]{2,1,0:T(8,128)(2,1)} %param.6) | copy-start | bytes 1572868
  7.8 18.7 %copy-start.1 = (bf16[1,128,2048]{2,1,0:T(8,128)(2,1)S(1)}, bf16[1,128,2048]{2,1,0:T(8,128)(2,1)}, u32[]{:S(2)}) copy-start(bf16[1,128,2048]{2,1,0:T(8,128)(2,1)} %param.7) | copy-start | bytes 1572868
  7.8 18.7 %copy-start.3 = (bf16[1,128,2048]{2,1,0:T(8,128)(2,1)S(1)}, bf16[1,128,2048]{2,1,0:T(8,128)(2,1)}, u32[]{:S(2)}) copy-start(bf16[1,128,2048]{2,1,0:T(8,128)(2,1)} %param.6) | copy-start | bytes 1572868
  9.0 5.0 %collective-permute-start.7 = (bf16[16,4096]{1,0:T(8,128)(2,1)S(1)}, bf16[16,4096]{1,0:T(8,128)(2,1)S(1)}, u32[]{:S(2)}, u32[]{:S(2)}) collective-permute-start(bf16[16,4096]{1,0:T(8,128)(2,1)S(1)} %get-tuple-element.27), channel_id=1, source_target_pairs={{0,8},{4,12},{8,0},{12,4},{16,24},{20,28},{24,16},{28,20},{1,9},{5... | collective-permute-start | bytes 393224 | tf_op jit(solution)/shard_map/ppermute | solution.py:26
  10.5 5.2 %collective-permute-start.9 = (bf16[16,4096]{1,0:T(8,128)(2,1)S(1)}, bf16[16,4096]{1,0:T(8,128)(2,1)}, u32[]{:S(2)}, u32[]{:S(2)}) collective-permute-start(bf16[16,4096]{1,0:T(8,128)(2,1)S(1)} %get-tuple-element.27), channel_id=1, source_target_pairs={{0,16},{4,20},{8,24},{12,28},{16,0},{20,4},{24,8},{28,12},{1,17},{... | collective-permute-start | bytes 393224 | tf_op jit(solution)/shard_map/ppermute | solution.py:26
  12.1 13.9 %collective-permute-start.1 = (bf16[128,2048]{1,0:T(8,128)(2,1)S(1)}, bf16[128,2048]{1,0:T(8,128)(2,1)S(1)}, u32[]{:S(2)}, u32[]{:S(2)}) collective-permute-start(bf16[128,2048]{1,0:T(8,128)(2,1)S(1)} %bitcast.14), channel_id=1, source_target_pairs={{0,4},{4,0},{8,12},{12,8},{16,20},{20,16},{24,28},{28,24},{1,5},{5... | collective-permute-start | bytes 1572872 | tf_op jit(solution)/shard_map/ppermute | solution.py:26
  12.1 13.4 %collective-permute-start = (bf16[128,2048]{1,0:T(8,128)(2,1)}, bf16[128,2048]{1,0:T(8,128)(2,1)S(1)}, u32[]{:S(2)}, u32[]{:S(2)}) collective-permute-start(bf16[128,2048]{1,0:T(8,128)(2,1)} %bitcast.17), channel_id=1, source_target_pairs={{0,4},{4,0},{8,12},{12,8},{16,20},{20,16},{24,28},{28,24},{1,5},{5... | collective-permute-start | bytes 1572872 | tf_op jit(solution)/shard_map/ppermute | solution.py:26
  14.0 5.1 %collective-permute-start.11 = (bf16[16,4096]{1,0:T(8,128)(2,1)S(1)}, bf16[16,4096]{1,0:T(8,128)(2,1)}, u32[]{:S(2)}, u32[]{:S(2)}) collective-permute-start(bf16[16,4096]{1,0:T(8,128)(2,1)S(1)} %collective-permute-done.7.x3), channel_id=1, source_target_pairs={{0,16},{4,20},{8,24},{12,28},{16,0},{20,4},{24,8},{28,12},{1,17},{... | collective-permute-start | bytes 393224 | tf_op jit(solution)/shard_map/ppermute | solution.py:26
  15.8 10.3 %collective-permute-start.2 = (bf16[128,2048]{1,0:T(8,128)(2,1)S(1)}, bf16[128,2048]{1,0:T(8,128)(2,1)S(1)}, u32[]{:S(2)}, u32[]{:S(2)}) collective-permute-start(bf16[128,2048]{1,0:T(8,128)(2,1)S(1)} %bitcast.9), channel_id=1, source_target_pairs={{0,4},{4,0},{8,12},{12,8},{16,20},{20,16},{24,28},{28,24},{1,5},{5... | collective-permute-start | bytes 1572872 | tf_op jit(solution)/shard_map/ppermute | solution.py:26
  19.1 6.4 %collective-permute-start.5 = (bf16[32,4096]{1,0:T(8,128)(2,1)S(1)}, bf16[32,4096]{1,0:T(8,128)(2,1)S(1)}, u32[]{:S(2)}, u32[]{:S(2)}) collective-permute-start(bf16[32,4096]{1,0:T(8,128)(2,1)S(1)} %get-tuple-element.26), channel_id=1, source_target_pairs={{0,8},{4,12},{8,0},{12,4},{16,24},{20,28},{24,16},{28,20},{1,9},{5... | collective-permute-start | bytes 786440 | tf_op jit(solution)/shard_map/ppermute | solution.py:26
  20.6 11.2 %collective-permute-start.4 = (bf16[128,2048]{1,0:T(8,128)(2,1)S(1)}, bf16[128,2048]{1,0:T(8,128)(2,1)}, u32[]{:S(2)}, u32[]{:S(2)}) collective-permute-start(bf16[128,2048]{1,0:T(8,128)(2,1)S(1)} %collective-permute-done.3.g0), channel_id=1, source_target_pairs={{0,4},{4,0},{8,12},{12,8},{16,20},{20,16},{24,28},{28,24},{1,5},{5... | collective-permute-start | bytes 1572872 | tf_op jit(solution)/shard_map/ppermute | solution.py:26
  25.5 6.3 %collective-permute-start.6 = (bf16[32,4096]{1,0:T(8,128)(2,1)S(1)}, bf16[32,4096]{1,0:T(8,128)(2,1)}, u32[]{:S(2)}, u32[]{:S(2)}) collective-permute-start(bf16[32,4096]{1,0:T(8,128)(2,1)S(1)} %collective-permute-done.5.x2), channel_id=1, source_target_pairs={{0,4},{4,0},{8,12},{12,8},{16,20},{20,16},{24,28},{28,24},{1,5},{5... | collective-permute-start | bytes 786440 | tf_op jit(solution)/shard_map/ppermute | solution.py:26
  25.5 6.3 %collective-permute-start.8 = (bf16[16,4096]{1,0:T(8,128)(2,1)S(1)}, bf16[16,4096]{1,0:T(8,128)(2,1)}, u32[]{:S(2)}, u32[]{:S(2)}) collective-permute-start(bf16[16,4096]{1,0:T(8,128)(2,1)S(1)} %collective-permute-done.7.x3), channel_id=1, source_target_pairs={{0,4},{4,0},{8,12},{12,8},{16,20},{20,16},{24,28},{28,24},{1,5},{5... | collective-permute-start | bytes 393224 | tf_op jit(solution)/shard_map/ppermute | solution.py:26
  26.0 5.8 %collective-permute-start.10 = (bf16[16,4096]{1,0:T(8,128)(2,1)}, bf16[16,4096]{1,0:T(8,128)(2,1)}, u32[]{:S(2)}, u32[]{:S(2)}) collective-permute-start(bf16[16,4096]{1,0:T(8,128)(2,1)} %collective-permute-done.9.y3), channel_id=1, source_target_pairs={{0,4},{4,0},{8,12},{12,8},{16,20},{20,16},{24,28},{28,24},{1,5},{5... | collective-permute-start | bytes 393224 | tf_op jit(solution)/shard_map/ppermute | solution.py:26
  26.1 5.7 %collective-permute-start.12 = (bf16[16,4096]{1,0:T(8,128)(2,1)}, bf16[16,4096]{1,0:T(8,128)(2,1)}, u32[]{:S(2)}, u32[]{:S(2)}) collective-permute-start(bf16[16,4096]{1,0:T(8,128)(2,1)} %collective-permute-done.11.d3), channel_id=1, source_target_pairs={{0,4},{4,0},{8,12},{12,8},{16,20},{20,16},{24,28},{28,24},{1,5},{5... | collective-permute-start | bytes 393224 | tf_op jit(solution)/shard_map/ppermute | solution.py:26
  26.5 1.0 %copy-start.6 = (bf16[1,128,2048]{2,1,0:T(8,128)(2,1)S(1)}, bf16[1,128,2048]{2,1,0:T(8,128)(2,1)}, u32[]{:S(2)}) copy-start(bf16[1,128,2048]{2,1,0:T(8,128)(2,1)} %param.5) | copy-start | bytes 1572868
  30.8 1.0 %copy-start.4 = (bf16[256,2048]{1,0:T(8,128)(2,1)}, bf16[256,2048]{1,0:T(8,128)(2,1)S(1)}, u32[]{:S(2)}) copy-start(bf16[256,2048]{1,0:T(8,128)(2,1)S(1)} %get-tuple-element.22.exps) | copy-start | bytes 3145732
  31.8 8.5 %copy-start.5 = (bf16[224,2048]{1,0:T(8,128)(2,1)}, bf16[224,2048]{1,0:T(8,128)(2,1)S(1)}, u32[]{:S(2)}) copy-start(bf16[224,2048]{1,0:T(8,128)(2,1)S(1)} %get-tuple-element.24.near) | copy-start | bytes 2752516
  47.8 19.3 %collective-permute-start.13 = (bf16[128,3072]{1,0:T(8,128)(2,1)}, bf16[128,3072]{1,0:T(8,128)(2,1)S(1)}, u32[]{:S(2)}, u32[]{:S(2)}) collective-permute-start(bf16[128,3072]{1,0:T(8,128)(2,1)} %get-tuple-element.32), channel_id=1, source_target_pairs={{0,4},{4,0},{8,12},{12,8},{16,20},{20,16},{24,28},{28,24},{1,5},{5... | collective-permute-start | bytes 2359304 | tf_op jit(solution)/shard_map/ppermute | solution.py:26
  47.9 5.8 %collective-permute-start.16 = (bf16[32,2048]{1,0:T(8,128)(2,1)S(1)}, bf16[32,2048]{1,0:T(8,128)(2,1)S(1)}, u32[]{:S(2)}, u32[]{:S(2)}) collective-permute-start(bf16[32,2048]{1,0:T(8,128)(2,1)S(1)} %get-tuple-element.35), channel_id=1, source_target_pairs={{0,16},{4,20},{8,24},{12,28},{16,0},{20,4},{24,8},{28,12},{1,17},{... | collective-permute-start | bytes 393224 | tf_op jit(solution)/shard_map/ppermute | solution.py:26
  49.4 17.7 %collective-permute-start.14 = (bf16[48,2048]{1,0:T(8,128)(2,1)S(1)}, bf16[48,2048]{1,0:T(8,128)(2,1)S(1)}, u32[]{:S(2)}, u32[]{:S(2)}) collective-permute-start(bf16[48,2048]{1,0:T(8,128)(2,1)S(1)} %get-tuple-element.33), channel_id=1, source_target_pairs={{0,8},{4,12},{8,0},{12,4},{16,24},{20,28},{24,16},{28,20},{1,9},{5... | collective-permute-start | bytes 589832 | tf_op jit(solution)/shard_map/ppermute | solution.py:26
  50.9 16.2 %collective-permute-start.15 = (bf16[48,2048]{1,0:T(8,128)(2,1)S(1)}, bf16[48,2048]{1,0:T(8,128)(2,1)S(1)}, u32[]{:S(2)}, u32[]{:S(2)}) collective-permute-start(bf16[48,2048]{1,0:T(8,128)(2,1)S(1)} %get-tuple-element.34), channel_id=1, source_target_pairs={{0,12},{4,8},{8,4},{12,0},{16,28},{20,24},{24,20},{28,16},{1,13},{... | collective-permute-start | bytes 589832 | tf_op jit(solution)/shard_map/ppermute | solution.py:26
  51.0 11.0 %collective-permute-start.18 = (bf16[16,2048]{1,0:T(8,128)(2,1)S(1)}, bf16[16,2048]{1,0:T(8,128)(2,1)S(1)}, u32[]{:S(2)}, u32[]{:S(2)}) collective-permute-start(bf16[16,2048]{1,0:T(8,128)(2,1)S(1)} %get-tuple-element.36), channel_id=1, source_target_pairs={{0,24},{4,28},{8,16},{12,20},{16,8},{20,12},{24,0},{28,4},{1,25},{... | collective-permute-start | bytes 196616 | tf_op jit(solution)/shard_map/ppermute | solution.py:26
  53.8 13.4 %collective-permute-start.17 = (bf16[32,2048]{1,0:T(8,128)(2,1)S(1)}, bf16[32,2048]{1,0:T(8,128)(2,1)S(1)}, u32[]{:S(2)}, u32[]{:S(2)}) collective-permute-start(bf16[32,2048]{1,0:T(8,128)(2,1)S(1)} %collective-permute-done.16.ya), channel_id=1, source_target_pairs={{0,4},{4,0},{8,12},{12,8},{16,20},{20,16},{24,28},{28,24},{1,5},{5... | collective-permute-start | bytes 393224 | tf_op jit(solution)/shard_map/ppermute | solution.py:26
  62.0 5.2 %collective-permute-start.19 = (bf16[16,2048]{1,0:T(8,128)(2,1)S(1)}, bf16[16,2048]{1,0:T(8,128)(2,1)S(1)}, u32[]{:S(2)}, u32[]{:S(2)}) collective-permute-start(bf16[16,2048]{1,0:T(8,128)(2,1)S(1)} %get-tuple-element.37), channel_id=1, source_target_pairs={{0,28},{4,24},{8,20},{12,16},{16,12},{20,8},{24,4},{28,0},{1,29},{... | collective-permute-start | bytes 196616 | tf_op jit(solution)/shard_map/ppermute | solution.py:26

commit v3 on v2

--- a/solution.py
+++ b/solution.py
@@ -15,10 +15,6 @@
 
 def params():
     return pltpu.CompilerParams(vmem_limit_bytes=VMEM_LIMIT)
-
-
-def cost(micros):
-    return pl.CostEstimate(flops=0, bytes_accessed=int(micros * 3.69e6), transcendentals=0)
 
 
 def exchange(value, bits):
@@ -58,7 +54,8 @@
     return jnp.concatenate(parts, axis=1).astype(BF16)
 
 
-def pick_kernel(levels, heads, dim, offs_ref, k_ref, v_ref, two_ref, three_ref):
+def pick_kernel(levels, heads, dim, offs_ref, core_ref, k_ref, v_ref, q_half, k_half, v_half,
+                both_ref, three_ref, swap_ref):
     tok = k_ref.shape[0]
     n2, n3 = tok // 4, tok // 8
     for h in range(heads):
@@ -68,35 +65,51 @@
         kv = jnp.concatenate([k_ref[:, cols], v_ref[:, cols]], axis=1)
         got = dot(pick, kv).astype(BF16)
         out = slice(2 * h * dim, 2 * (h + 1) * dim)
-        two_ref[:, out] = got[:n2]
+        both_ref[:, out] = got
         three_ref[:, out] = got[n2 : n2 + n3]
 
-
-def pick_call(offsets, keys, values, dim):
+    @pl.when(pl.program_id(0) == 0)
+    def _():
+        half = q_half.shape[1]
+        for i, ref in enumerate((q_half, k_half, v_half)):
+            swap_ref[:, i * half : (i + 1) * half] = ref[...]
+
+
+def pick_call(offsets, core, queries, keys, values, dim):
     tok, width = keys.shape
     levels, heads = offsets.shape
     steps = 2
     per = heads // steps
-    block = pl.BlockSpec((tok, per * dim), lambda i, o: (0, i))
+    block = pl.BlockSpec((tok, per * dim), lambda i, o, c: (0, i))
+    half = pl.BlockSpec((tok, width // 2), lambda i, o, c: (0, 1 - c[0]))
     return pl.pallas_call(
         functools.partial(pick_kernel, levels, per, dim),
         grid_spec=pltpu.PrefetchScalarGridSpec(
-            num_scalar_prefetch=1,
+            num_scalar_prefetch=2,
             grid=(steps,),
-            in_specs=[block, block],
+            in_specs=[block, block, half, half, half],
             out_specs=[
-                pl.BlockSpec((tok // 4, 2 * per * dim), lambda i, o: (0, i)),
-                pl.BlockSpec((tok // 8, 2 * per * dim), lambda i, o: (0, i)),
+                pl.BlockSpec((tok // 4 + tok // 8, 2 * per * dim), lambda i, o, c: (0, i)),
+                pl.BlockSpec((tok // 8, 2 * per * dim), lambda i, o, c: (0, i)),
+                pl.BlockSpec((tok, 3 * width // 2), lambda i, o, c: (0, 0)),
             ],
         ),
         out_shape=[
-            jax.ShapeDtypeStruct((tok // 4, 2 * width), BF16),
+            jax.ShapeDtypeStruct((tok // 4 + tok // 8, 2 * width), BF16),
             jax.ShapeDtypeStruct((tok // 8, 2 * width), BF16),
+            jax.ShapeDtypeStruct((tok, 3 * width // 2), BF16),
         ],
         compiler_params=params(),
-        cost_estimate=cost(2),
         name="pick_rows",
-    )(offsets, keys, values)
+    )(offsets, core, keys, values, queries, keys, values)
+
+
+def own_spec(tok, cols, steps):
+    return pl.BlockSpec((tok, cols), lambda i, o, c: (0, c[0] * steps + i))
+
+
+def swap_spec(tok, cols, steps, part):
+    return pl.BlockSpec((tok, cols), lambda i, o, c: (0, part * steps + i))
 
 
 def side(*values):
@@ -160,7 +173,8 @@
     half = heads // 2
     per = 2
     steps = half // per
-    raw_spec = pl.BlockSpec((tok, per * dim), lambda i, o, c: (0, c[0] * steps + i))
+    raw_spec = own_spec(tok, per * dim, steps)
+    swapped = [swap_spec(tok, per * dim, steps, i) for i in range(3)]
     sel = 2 * (tok // 4 + tok // 8)
 
     def out(rows, lanes, kind=BF16):
@@ -175,19 +189,18 @@
         grid_spec=pltpu.PrefetchScalarGridSpec(
             num_scalar_prefetch=2,
             grid=(steps,),
-            in_specs=[raw_spec] * 6,
+            in_specs=[raw_spec, swapped[0], raw_spec, swapped[1], raw_spec, swapped[2]],
             out_specs=[o[0] for o in outs],
         ),
         out_shape=[o[1] for o in outs],
         compiler_params=params(),
-        cost_estimate=cost(5),
         name="local_scores",
     )(offsets, core, *raw)
 
 
 def far_kernel(
     levels, per, dim, offs_ref, core_ref, exps, stats, near, selq, v0, v1, g0, g1,
-    x2, xx2, x3, xx3, y3, yy3, d3, dd3,
+    x, xx, y3, yy3, d3, dd3,
     xa, xb, yab, da, db, ngrad, dqt, stats2,
 ):
     tok = g0.shape[0]
@@ -215,8 +228,8 @@
         def rows(c):
             a, b = near[tok : tok + sel, c], near[tok + sel :, c]
             return stack(
-                a[:n2], b[:n2], x2[:, c], xx2[:, c], a[n2:], b[n2:],
-                *(ref[:, c] for ref in (x3, xx3, y3, yy3, d3, dd3)),
+                a[:n2], b[:n2], x[:n2, c], xx[:n2, c], a[n2:], b[n2:], x[n2:, c], xx[n2:, c],
+                *(ref[:, c] for ref in (y3, yy3, d3, dd3)),
             )
 
         keys, vals = rows(kc), rows(vc)
@@ -288,7 +301,8 @@
     per = 2
     steps = half // per
     n2, n3 = tok // 4, tok // 8
-    raw_spec = pl.BlockSpec((tok, per * dim), lambda i, o, c: (0, c[0] * steps + i))
+    raw_spec = own_spec(tok, per * dim, steps)
+    swapped = [swap_spec(tok, per * dim, steps, i) for i in range(3)]
 
     def near_spec(a):
         return pl.BlockSpec((a.shape[0], a.shape[1] // steps), lambda i, o, c: (0, i))
@@ -309,12 +323,12 @@
         grid_spec=pltpu.PrefetchScalarGridSpec(
             num_scalar_prefetch=2,
             grid=(steps,),
-            in_specs=[near_spec(a) for a in pre] + [raw_spec] * 4 + [far_spec(a) for a in far],
+            in_specs=[near_spec(a) for a in pre] + [raw_spec, swapped[2], raw_spec, raw_spec]
+            + [far_spec(a) for a in far],
             out_specs=[o[0] for o in outs],
         ),
         out_shape=[o[1] for o in outs],
         compiler_params=params(),
-        cost_estimate=cost(4),
         name="far_levels",
     )(offsets, core, *pre, *raw, *far)
 
@@ -367,7 +381,8 @@
     half = heads // 2
     per = 2
     steps = half // per
-    raw_spec = pl.BlockSpec((tok, per * dim), lambda i, o, c: (0, c[0] * steps + i))
+    raw_spec = own_spec(tok, per * dim, steps)
+    swapped = [swap_spec(tok, per * dim, steps, i) for i in range(3)]
 
     def mid_spec(a):
         return pl.BlockSpec((a.shape[0], a.shape[1] // steps), lambda i, o, c: (0, i))
@@ -378,12 +393,12 @@
         grid_spec=pltpu.PrefetchScalarGridSpec(
             num_scalar_prefetch=2,
             grid=(steps,),
-            in_specs=[mid_spec(a) for a in mid] + [raw_spec] * 8,
+            in_specs=[mid_spec(a) for a in mid]
+            + [raw_spec, swapped[0], raw_spec, swapped[1], raw_spec, swapped[2], raw_spec, raw_spec],
             out_specs=[out_spec] * 2,
         ),
         out_shape=[jax.ShapeDtypeStruct((tok, 3 * half * dim), BF16)] * 2,
         compiler_params=params(),
-        cost_estimate=cost(7),
         name="near_levels",
     )(offsets, core, *mid, *raw)
 
@@ -453,7 +468,6 @@
         ),
         out_shape=[jax.ShapeDtypeStruct((tok, heads * dim), BF16)] * 3,
         compiler_params=params(),
-        cost_estimate=cost(3),
         name="add_pieces",
     )(offsets, core, *parts)
 
@@ -466,28 +480,27 @@
     grads = lax.ppermute(
         out_grads[0], "section", [(i, (i - 1) % sections) for i in range(sections)]
     )
-    q, k, v = queries[0], keys_in[0], values[0]
-    q_oth, k_oth, v_oth = exchange(q, 1), exchange(k, 1), exchange(v, 1)
-    two, three = pick_call(offsets, k, v, dim)
-    x3 = exchange(three, 2)
-    y3 = exchange(three, 4)
-    x2 = exchange(two, 2)
-    d3 = exchange(x3, 4)
-    exps, stats, near, selq = pre_call(offsets, core, [q, q_oth, k, k_oth, v, v_oth], dim)
+    q, k, v = (pltpu.with_memory_space_constraint(a[0], pltpu.HBM) for a in (queries, keys_in, values))
+    both, three, swap = pick_call(offsets, core, q, k, v, dim)
+    swap = exchange(swap, 1)
+    x, y, d = exchange(both, 2), exchange(three, 4), exchange(three, 6)
+    pre = pre_call(offsets, core, [q, swap, k, swap, v, swap], dim)
+    x, y, d, grads = lax.optimization_barrier((x, y, d, grads, pre[1]))[:4]
     far = []
-    for piece in (x2, x3, y3, d3):
+    for piece in (x, y, d):
         far += [piece, exchange(piece, 1)]
     g_oth = exchange(grads, 1)
     xa, xb, yab, da, db, ngrad, dqt, stats2 = far_call(
-        offsets, core, [exps, stats, near, selq], [v, v_oth, grads, g_oth], far, dim
+        offsets, core, pre, [v, swap, grads, g_oth], far, dim
     )
     xa, xb, da, db = exchange(xa, 2), exchange(xb, 3), exchange(da, 6), exchange(db, 7)
     y = exchange(yab, 4)
     yy = exchange(y, 1)
     mine, other = near_call(
-        offsets, core, [exps, stats2, near, ngrad, dqt],
-        [q, q_oth, k, k_oth, v, v_oth, grads, g_oth], dim,
+        offsets, core, [pre[0], stats2, pre[2], ngrad, dqt],
+        [q, swap, k, swap, v, swap, grads, g_oth], dim,
     )
+    other, xa, xb, da, db, y = lax.optimization_barrier((other, xa, xb, da, db, y))
     parts = [mine, exchange(other, 1), xa, xb, y, yy, da, db]
     dq, dk, dv = final_call(offsets, core, parts, dim)
     return dq[None], dk[None], dv[None]

time: 71 us -> 54.8 us (0.77)
  waiting for transfers between devices: 23.6 us -> 11.8 us
  starting transfers between devices: 18.3 us -> 15.1 us
  local copies, waits for them, and re-layouts: 4.11 us -> 1.67 us
  Pallas kernels: 23.9 us -> 25.2 us
    ppermute x19 -> x15, waiting for transfers between devices: 23.6 us -> 11.8 us  [exchange(): return lax.ppermute(value, 'seq', [(i, i ^ bits) for i in range(count)])]
    ppermute x19 -> x15, starting transfers between devices: 13.2 us -> 10.4 us  [exchange(): return lax.ppermute(value, 'seq', [(i, i ^ bits) for i in range(count)])]
    unnamed x16 -> x8, local copies, waits for them, and re-layouts: 4.11 us -> 1.67 us
    pallas_call x1, Pallas kernels: 1.15 us -> 2.43 us  [pick_call(): pl.pallas_call(functools.partial(pick_kernel, levels, per, dim), grid_spe...]
    pallas_call x1, Pallas kernels: 3.23 us -> 4.22 us  [pre_call(): pl.pallas_call(functools.partial(pre_kernel, levels, per, dim), grid_spec...]
  transfers between devices with their start and end apart: 20 -> 16, of which waited for: 7 -> 5; matrix products, arithmetic and copies ran while one was open for 0% -> 0% of each run, Pallas kernels for 6% -> 20%
where the time goes in v3:
time: 54.8 us; the launch traced here: 54.5 us
  Pallas kernels  25.2 us (46%)
  starting transfers between devices  15.1 us (28%)
  waiting for transfers between devices  11.8 us (22%)
  local copies, waits for them, and re-layouts  1.67 us (3%)
  between operations  0.73 us (1%)
    ppermute x15, waiting for transfers between devices, exchange(): return lax.ppermute(value, 'seq', [(i, i ^ bits) for i in range(count)])  11.8 us
    ppermute x15, starting transfers between devices, exchange(): return lax.ppermute(value, 'seq', [(i, i ^ bits) for i in range(count)])  10.4 us
    pallas_call x1, Pallas kernels, far_call(): pl.pallas_call(functools.partial(far_kernel, levels, per, dim), grid_spec...  8.21 us
    pallas_call x1, Pallas kernels, near_call(): pl.pallas_call(functools.partial(near_kernel, levels, per, dim), grid_spe...  6.85 us
    ppermute x1, starting transfers between devices, per_device(): lax.ppermute(out_grads[0], 'section', [(i, (i - 1) % sections) for i in r...  4.67 us
    pallas_call x1, Pallas kernels, pre_call(): pl.pallas_call(functools.partial(pre_kernel, levels, per, dim), grid_spec...  4.22 us
    pallas_call x1, Pallas kernels, final_call(): pl.pallas_call(functools.partial(final_kernel, levels, per, dim), grid_sp...  3.46 us
    pallas_call x1, Pallas kernels, pick_call(): pl.pallas_call(functools.partial(pick_kernel, levels, per, dim), grid_spe...  2.43 us
  transfers between devices with their start and end apart: 16, of which 5 were waited for; matrix products, arithmetic and copies ran while one was open for 0% of the time, Pallas kernels for 20%

profile of v3, /device:TPU:0, one launch (start us, length us, event | category | flops | bytes accessed | tf_op | source)
XLA Modules:
  0.0 54.5 jit_solution(6073006030113903393)
XLA Ops:
  0.6 0.0 copy-start.2
  0.6 0.7 %copy-done.2 = s32[3,16]{1,0:T(4,128)S(1)} copy-done((s32[3,16]{1,0:T(4,128)S(1)}, s32[3,16]{1,0:T(4,128)}, u32[]{:S(2)}) %copy-start.2) | copy-done | bytes 216
  1.3 0.0 copy-start.3
  1.3 2.4 %pick_rows.1 = (bf16[48,4096]{1,0:T(8,128)(2,1)S(1)}, bf16[16,4096]{1,0:T(8,128)(2,1)S(1)}, bf16[128,3072]{1,0:T(8,128)(2,1)S(1)}) custom-call(s32[3,16]{1,0:T(4,128)S(1)} %copy-done.2, s32[1]{0:T(128)} %bitcast.core_ref, bf16[128,2048]{1,0:T(8,128)(2,1)} %bitcast.13, bf16[128,2048]{1,0:T(8,128)(2,1)} %bitcast.8, bf16[128,2048]{1,0:T(8,128)(2,1)} %bitcast.17, ...), custom_call_target="tpu_custom_call" | custom-call | tf_op jit(solution)/shard_map/pick_rows/pallas_call | solution.py:85
  3.8 0.5 collective-permute-start
  4.3 0.0 copy-done.3
  4.3 4.7 %collective-permute-start.4 = (bf16[128,2048]{1,0:T(8,128)(2,1)S(1)}, bf16[128,2048]{1,0:T(8,128)(2,1)S(1)}, u32[]{:S(2)}, u32[]{:S(2)}) collective-permute-start(bf16[128,2048]{1,0:T(8,128)(2,1)S(1)} %bitcast.20), channel_id=1, source_target_pairs={{0,3},{1,0},{2,1},{3,2},{4,7},{5,4},{6,5},{7,6},{8,11},{9,8},{10,9... | collective-permute-start | bytes 1572872 | tf_op jit(solution)/shard_map/ppermute | solution.py:480
  8.9 1.5 %collective-permute-start.1 = (bf16[48,4096]{1,0:T(8,128)(2,1)S(1)}, bf16[48,4096]{1,0:T(8,128)(2,1)S(1)}, u32[]{:S(2)}, u32[]{:S(2)}) collective-permute-start(bf16[48,4096]{1,0:T(8,128)(2,1)S(1)} %get-tuple-element.38), channel_id=1, source_target_pairs={{0,8},{4,12},{8,0},{12,4},{16,24},{20,28},{24,16},{28,20},{1,9},{5... | collective-permute-start | bytes 1179656 | tf_op jit(solution)/shard_map/ppermute | solution.py:22
  10.4 1.5 %collective-permute-start.3 = (bf16[16,4096]{1,0:T(8,128)(2,1)S(1)}, bf16[16,4096]{1,0:T(8,128)(2,1)S(1)}, u32[]{:S(2)}, u32[]{:S(2)}) collective-permute-start(bf16[16,4096]{1,0:T(8,128)(2,1)S(1)} %get-tuple-element.39), channel_id=1, source_target_pairs={{0,24},{4,28},{8,16},{12,20},{16,8},{20,12},{24,0},{28,4},{1,25},{... | collective-permute-start | bytes 393224 | tf_op jit(solution)/shard_map/ppermute | solution.py:22
  11.9 0.5 collective-permute-start.2
  12.4 0.0 collective-permute-done.q1.k1.v1
  12.4 4.2 %local_scores.1 = (bf16[256,2048]{1,0:T(8,128)(2,1)S(1)}, f32[8,2048]{1,0:T(8,128)S(1)}, bf16[224,2048]{1,0:T(8,128)(2,1)S(1)}, bf16[96,1024]{1,0:T(8,128)(2,1)S(1)}) custom-call(s32[3,16]{1,0:T(4,128)S(1)} %copy-done.2, s32[1]{0:T(128)} %bitcast.core_ref, bf16[128,2048]{1,0:T(8,128)(2,1)} %bitcast.18, bf16[128,3072]{1,0:T(8,128)(2,1)S(1)} %collective-permute-done.q1.k1.v1, ...), custom_call_target="tpu_custom_call" | custom-call | tf_op jit(solution)/shard_map/local_scores/pallas_call | solution.py:187
  16.7 0.0 copy-start
  16.7 1.0 %copy-done = bf16[256,2048]{1,0:T(8,128)(2,1)} copy-done((bf16[256,2048]{1,0:T(8,128)(2,1)}, bf16[256,2048]{1,0:T(8,128)(2,1)S(1)}, u32[]{:S(2)}) %copy-start) | copy-done | bytes 1048600
  17.7 6.2 %collective-permute-done.3.d3 = bf16[16,4096]{1,0:T(8,128)(2,1)S(1)} collective-permute-done((bf16[16,4096]{1,0:T(8,128)(2,1)S(1)}, bf16[16,4096]{1,0:T(8,128)(2,1)S(1)}, u32[]{:S(2)}, u32[]{:S(2)}) %collective-permute-start.3) | collective-permute-done | bytes 131104 | tf_op jit(solution)/shard_map/ppermute | solution.py:22
  23.9 0.0 collective-permute-done.2.y3
  23.9 0.0 collective-permute-done.1.x
  23.9 0.0 collective-permute-done.4.g0
  23.9 0.1 collective-permute-start.5
  24.0 0.5 collective-permute-start.6
  24.5 0.1 collective-permute-start.7
  24.6 0.4 collective-permute-start.8
  25.0 1.6 %collective-permute-done.7.yy3 = bf16[16,4096]{1,0:T(8,128)(2,1)S(1)} collective-permute-done((bf16[16,4096]{1,0:T(8,128)(2,1)S(1)}, bf16[16,4096]{1,0:T(8,128)(2,1)S(1)}, u32[]{:S(2)}, u32[]{:S(2)}) %collective-permute-start.7) | collective-permute-done | bytes 131104 | tf_op jit(solution)/shard_map/ppermute | solution.py:22
  26.6 0.2 collective-permute-done.8.dd3
  26.8 0.0 collective-permute-done.6.xx
  26.8 0.0 collective-permute-done.5.g1
  26.8 0.0 copy-start.1
  26.8 8.2 %far_levels.1 = (bf16[48,2048]{1,0:T(8,128)(2,1)S(1)}, bf16[48,2048]{1,0:T(8,128)(2,1)S(1)}, bf16[32,2048]{1,0:T(8,128)(2,1)S(1)}, bf16[16,2048]{1,0:T(8,128)(2,...) custom-call(s32[3,16]{1,0:T(4,128)S(1)} %copy-done.2, ...), custom_call_target="tpu_custom_call" | custom-call | tf_op jit(solution)/shard_map/far_levels/pallas_call | solution.py:321
  35.0 1.6 %collective-permute-start.9 = (bf16[48,2048]{1,0:T(8,128)(2,1)S(1)}, bf16[48,2048]{1,0:T(8,128)(2,1)S(1)}, u32[]{:S(2)}, u32[]{:S(2)}) collective-permute-start(bf16[48,2048]{1,0:T(8,128)(2,1)S(1)} %get-tuple-element.49), channel_id=1, source_target_pairs={{0,8},{4,12},{8,0},{12,4},{16,24},{20,28},{24,16},{28,20},{1,9},{5... | collective-permute-start | bytes 589832 | tf_op jit(solution)/shard_map/ppermute | solution.py:22
  36.6 0.0 collective-permute-start.10
  36.6 0.5 collective-permute-start.13
  37.1 2.4 %collective-permute-start.11 = (bf16[16,2048]{1,0:T(8,128)(2,1)S(1)}, bf16[16,2048]{1,0:T(8,128)(2,1)S(1)}, u32[]{:S(2)}, u32[]{:S(2)}) collective-permute-start(bf16[16,2048]{1,0:T(8,128)(2,1)S(1)} %get-tuple-element.51), channel_id=1, source_target_pairs={{0,24},{4,28},{8,16},{12,20},{16,8},{20,12},{24,0},{28,4},{1,25},{... | collective-permute-start | bytes 196616 | tf_op jit(solution)/shard_map/ppermute | solution.py:22
  39.5 0.2 collective-permute-start.12
  39.7 0.0 copy-done.1
  39.7 6.9 %near_levels.1 = (bf16[128,3072]{1,0:T(8,128)(2,1)S(1)}, bf16[128,3072]{1,0:T(8,128)(2,1)S(1)}) custom-call(s32[3,16]{1,0:T(4,128)S(1)} %copy-done.2, s32[1]{0:T(128)} %bitcast.core_ref, bf16[256,2048]{1,0:T(8,128)(2,1)S(1)} %copy-done.1, f32[8,2048]{1,0:T(8,128)S(1)} %get-tuple-element.44.stats2, bf16[224,2048]{1,0:T(8,128)(2,1)S(1)} %get-tuple-element.36.near, ...), custom_call_target="tpu_custom_call" | custom-call | tf_op jit(solution)/shard_map/near_levels/pallas_call | solution.py:391
  46.6 1.7 %collective-permute-done.11.da = bf16[16,2048]{1,0:T(8,128)(2,1)S(1)} collective-permute-done((bf16[16,2048]{1,0:T(8,128)(2,1)S(1)}, bf16[16,2048]{1,0:T(8,128)(2,1)S(1)}, u32[]{:S(2)}, u32[]{:S(2)}) %collective-permute-start.11) | collective-permute-done | bytes 65568 | tf_op jit(solution)/shard_map/ppermute | solution.py:22
  48.3 0.0 collective-permute-done.12.db
  48.3 0.0 collective-permute-done.13.ya
  48.3 0.0 collective-permute-done.9.xa
  48.3 0.0 collective-permute-done.10.xb
  48.3 0.6 %collective-permute-start.14 = (bf16[128,3072]{1,0:T(8,128)(2,1)S(1)}, bf16[128,3072]{1,0:T(8,128)(2,1)S(1)}, u32[]{:S(2)}, u32[]{:S(2)}) collective-permute-start(bf16[128,3072]{1,0:T(8,128)(2,1)S(1)} %get-tuple-element.54), channel_id=1, source_target_pairs={{0,4},{4,0},{8,12},{12,8},{16,20},{20,16},{24,28},{28,24},{1,5},{5... | collective-permute-start | bytes 2359304 | tf_op jit(solution)/shard_map/ppermute | solution.py:22
  48.9 0.1 collective-permute-start.15
  49.0 2.0 %collective-permute-done.15.yb = bf16[32,2048]{1,0:T(8,128)(2,1)S(1)} collective-permute-done((bf16[32,2048]{1,0:T(8,128)(2,1)S(1)}, bf16[32,2048]{1,0:T(8,128)(2,1)S(1)}, u32[]{:S(2)}, u32[]{:S(2)}) %collective-permute-start.15) | collective-permute-done | bytes 131104 | tf_op jit(solution)/shard_map/ppermute | solution.py:22
  51.0 0.0 collective-permute-done.14.bb
  51.0 3.5 %add_pieces.1 = (bf16[128,2048]{1,0:T(8,128)(2,1)}, bf16[128,2048]{1,0:T(8,128)(2,1)}, bf16[128,2048]{1,0:T(8,128)(2,1)}) custom-call(s32[3,16]{1,0:T(4,128)S(1)} %copy-done.2, s32[1]{0:T(128)} %bitcast.core_ref, bf16[128,3072]{1,0:T(8,128)(2,1)S(1)} %get-tuple-element.47.ba, bf16[128,3072]{1,0:T(8,128)(2,1)S(1)} %collective-permute-done.14.bb, ...), custom_call_target="tpu_custom_call" | custom-call | tf_op jit(solution)/shard_map/add_pieces/pallas_call | solution.py:461
Async XLA Ops:
  0.6 0.7 %copy-start.2 = (s32[3,16]{1,0:T(4,128)S(1)}, s32[3,16]{1,0:T(4,128)}, u32[]{:S(2)}) copy-start(s32[3,16]{1,0:T(4,128)} %offs_ref.9) | copy-start | bytes 580
  1.3 3.0 %copy-start.3 = (bf16[1,128,2048]{2,1,0:T(8,128)(2,1)S(1)}, bf16[1,128,2048]{2,1,0:T(8,128)(2,1)}, u32[]{:S(2)}) copy-start(bf16[1,128,2048]{2,1,0:T(8,128)(2,1)} %param.8) | copy-start | bytes 1572868
  3.8 8.7 %collective-permute-start = (bf16[128,3072]{1,0:T(8,128)(2,1)S(1)}, bf16[128,3072]{1,0:T(8,128)(2,1)S(1)}, u32[]{:S(2)}, u32[]{:S(2)}) collective-permute-start(bf16[128,3072]{1,0:T(8,128)(2,1)S(1)} %get-tuple-element.33), channel_id=1, source_target_pairs={{0,4},{4,0},{8,12},{12,8},{16,20},{20,16},{24,28},{28,24},{1,5},{5... | collective-permute-start | bytes 2359304 | tf_op jit(solution)/shard_map/ppermute | solution.py:22
  4.3 19.6 %collective-permute-start.4 = (bf16[128,2048]{1,0:T(8,128)(2,1)S(1)}, bf16[128,2048]{1,0:T(8,128)(2,1)S(1)}, u32[]{:S(2)}, u32[]{:S(2)}) collective-permute-start(bf16[128,2048]{1,0:T(8,128)(2,1)S(1)} %bitcast.20), channel_id=1, source_target_pairs={{0,3},{1,0},{2,1},{3,2},{4,7},{5,4},{6,5},{7,6},{8,11},{9,8},{10,9... | collective-permute-start | bytes 1572872 | tf_op jit(solution)/shard_map/ppermute | solution.py:480
  8.9 14.9 %collective-permute-start.1 = (bf16[48,4096]{1,0:T(8,128)(2,1)S(1)}, bf16[48,4096]{1,0:T(8,128)(2,1)S(1)}, u32[]{:S(2)}, u32[]{:S(2)}) collective-permute-start(bf16[48,4096]{1,0:T(8,128)(2,1)S(1)} %get-tuple-element.38), channel_id=1, source_target_pairs={{0,8},{4,12},{8,0},{12,4},{16,24},{20,28},{24,16},{28,20},{1,9},{5... | collective-permute-start | bytes 1179656 | tf_op jit(solution)/shard_map/ppermute | solution.py:22
  10.4 13.4 %collective-permute-start.3 = (bf16[16,4096]{1,0:T(8,128)(2,1)S(1)}, bf16[16,4096]{1,0:T(8,128)(2,1)S(1)}, u32[]{:S(2)}, u32[]{:S(2)}) collective-permute-start(bf16[16,4096]{1,0:T(8,128)(2,1)S(1)} %get-tuple-element.39), channel_id=1, source_target_pairs={{0,24},{4,28},{8,16},{12,20},{16,8},{20,12},{24,0},{28,4},{1,25},{... | collective-permute-start | bytes 393224 | tf_op jit(solution)/shard_map/ppermute | solution.py:22
  11.9 12.0 %collective-permute-start.2 = (bf16[16,4096]{1,0:T(8,128)(2,1)S(1)}, bf16[16,4096]{1,0:T(8,128)(2,1)S(1)}, u32[]{:S(2)}, u32[]{:S(2)}) collective-permute-start(bf16[16,4096]{1,0:T(8,128)(2,1)S(1)} %get-tuple-element.39), channel_id=1, source_target_pairs={{0,16},{4,20},{8,24},{12,28},{16,0},{20,4},{24,8},{28,12},{1,17},{... | collective-permute-start | bytes 393224 | tf_op jit(solution)/shard_map/ppermute | solution.py:22
  16.7 1.0 %copy-start = (bf16[256,2048]{1,0:T(8,128)(2,1)}, bf16[256,2048]{1,0:T(8,128)(2,1)S(1)}, u32[]{:S(2)}) copy-start(bf16[256,2048]{1,0:T(8,128)(2,1)S(1)} %get-tuple-element.34.exps) | copy-start | bytes 3145732
  23.9 2.9 %collective-permute-start.5 = (bf16[128,2048]{1,0:T(8,128)(2,1)S(1)}, bf16[128,2048]{1,0:T(8,128)(2,1)S(1)}, u32[]{:S(2)}, u32[]{:S(2)}) collective-permute-start(bf16[128,2048]{1,0:T(8,128)(2,1)S(1)} %collective-permute-done.4.g0), channel_id=1, source_target_pairs={{0,4},{4,0},{8,12},{12,8},{16,20},{20,16},{24,28},{28,24},{1,5},{5... | collective-permute-start | bytes 1572872 | tf_op jit(solution)/shard_map/ppermute | solution.py:22
  24.0 2.8 %collective-permute-start.6 = (bf16[48,4096]{1,0:T(8,128)(2,1)S(1)}, bf16[48,4096]{1,0:T(8,128)(2,1)S(1)}, u32[]{:S(2)}, u32[]{:S(2)}) collective-permute-start(bf16[48,4096]{1,0:T(8,128)(2,1)S(1)} %collective-permute-done.1.x), channel_id=1, source_target_pairs={{0,4},{4,0},{8,12},{12,8},{16,20},{20,16},{24,28},{28,24},{1,5},{5... | collective-permute-start | bytes 1179656 | tf_op jit(solution)/shard_map/ppermute | solution.py:22
  24.5 2.1 %collective-permute-start.7 = (bf16[16,4096]{1,0:T(8,128)(2,1)S(1)}, bf16[16,4096]{1,0:T(8,128)(2,1)S(1)}, u32[]{:S(2)}, u32[]{:S(2)}) collective-permute-start(bf16[16,4096]{1,0:T(8,128)(2,1)S(1)} %collective-permute-done.2.y3), channel_id=1, source_target_pairs={{0,4},{4,0},{8,12},{12,8},{16,20},{20,16},{24,28},{28,24},{1,5},{5... | collective-permute-start | bytes 393224 | tf_op jit(solution)/shard_map/ppermute | solution.py:22
  24.6 2.3 %collective-permute-start.8 = (bf16[16,4096]{1,0:T(8,128)(2,1)S(1)}, bf16[16,4096]{1,0:T(8,128)(2,1)S(1)}, u32[]{:S(2)}, u32[]{:S(2)}) collective-permute-start(bf16[16,4096]{1,0:T(8,128)(2,1)S(1)} %collective-permute-done.3.d3), channel_id=1, source_target_pairs={{0,4},{4,0},{8,12},{12,8},{16,20},{20,16},{24,28},{28,24},{1,5},{5... | collective-permute-start | bytes 393224 | tf_op jit(solution)/shard_map/ppermute | solution.py:22
  26.8 12.9 %copy-start.1 = (bf16[256,2048]{1,0:T(8,128)(2,1)S(1)}, bf16[256,2048]{1,0:T(8,128)(2,1)}, u32[]{:S(2)}) copy-start(bf16[256,2048]{1,0:T(8,128)(2,1)} %copy-done) | copy-start | bytes 3145732
  35.0 13.3 %collective-permute-start.9 = (bf16[48,2048]{1,0:T(8,128)(2,1)S(1)}, bf16[48,2048]{1,0:T(8,128)(2,1)S(1)}, u32[]{:S(2)}, u32[]{:S(2)}) collective-permute-start(bf16[48,2048]{1,0:T(8,128)(2,1)S(1)} %get-tuple-element.49), channel_id=1, source_target_pairs={{0,8},{4,12},{8,0},{12,4},{16,24},{20,28},{24,16},{28,20},{1,9},{5... | collective-permute-start | bytes 589832 | tf_op jit(solution)/shard_map/ppermute | solution.py:22
  36.6 11.7 %collective-permute-start.10 = (bf16[48,2048]{1,0:T(8,128)(2,1)S(1)}, bf16[48,2048]{1,0:T(8,128)(2,1)S(1)}, u32[]{:S(2)}, u32[]{:S(2)}) collective-permute-start(bf16[48,2048]{1,0:T(8,128)(2,1)S(1)} %get-tuple-element.50), channel_id=1, source_target_pairs={{0,12},{4,8},{8,4},{12,0},{16,28},{20,24},{24,20},{28,16},{1,13},{... | collective-permute-start | bytes 589832 | tf_op jit(solution)/shard_map/ppermute | solution.py:22
  36.6 11.7 %collective-permute-start.13 = (bf16[32,2048]{1,0:T(8,128)(2,1)S(1)}, bf16[32,2048]{1,0:T(8,128)(2,1)S(1)}, u32[]{:S(2)}, u32[]{:S(2)}) collective-permute-start(bf16[32,2048]{1,0:T(8,128)(2,1)S(1)} %get-tuple-element.53), channel_id=1, source_target_pairs={{0,16},{4,20},{8,24},{12,28},{16,0},{20,4},{24,8},{28,12},{1,17},{... | collective-permute-start | bytes 393224 | tf_op jit(solution)/shard_map/ppermute | solution.py:22
  37.1 11.2 %collective-permute-start.11 = (bf16[16,2048]{1,0:T(8,128)(2,1)S(1)}, bf16[16,2048]{1,0:T(8,128)(2,1)S(1)}, u32[]{:S(2)}, u32[]{:S(2)}) collective-permute-start(bf16[16,2048]{1,0:T(8,128)(2,1)S(1)} %get-tuple-element.51), channel_id=1, source_target_pairs={{0,24},{4,28},{8,16},{12,20},{16,8},{20,12},{24,0},{28,4},{1,25},{... | collective-permute-start | bytes 196616 | tf_op jit(solution)/shard_map/ppermute | solution.py:22
  39.5 8.8 %collective-permute-start.12 = (bf16[16,2048]{1,0:T(8,128)(2,1)S(1)}, bf16[16,2048]{1,0:T(8,128)(2,1)S(1)}, u32[]{:S(2)}, u32[]{:S(2)}) collective-permute-start(bf16[16,2048]{1,0:T(8,128)(2,1)S(1)} %get-tuple-element.52), channel_id=1, source_target_pairs={{0,28},{4,24},{8,20},{12,16},{16,12},{20,8},{24,4},{28,0},{1,29},{... | collective-permute-start | bytes 196616 | tf_op jit(solution)/shard_map/ppermute | solution.py:22
  48.3 2.7 %collective-permute-start.14 = (bf16[128,3072]{1,0:T(8,128)(2,1)S(1)}, bf16[128,3072]{1,0:T(8,128)(2,1)S(1)}, u32[]{:S(2)}, u32[]{:S(2)}) collective-permute-start(bf16[128,3072]{1,0:T(8,128)(2,1)S(1)} %get-tuple-element.54), channel_id=1, source_target_pairs={{0,4},{4,0},{8,12},{12,8},{16,20},{20,16},{24,28},{28,24},{1,5},{5... | collective-permute-start | bytes 2359304 | tf_op jit(solution)/shard_map/ppermute | solution.py:22
  48.9 2.1 %collective-permute-start.15 = (bf16[32,2048]{1,0:T(8,128)(2,1)S(1)}, bf16[32,2048]{1,0:T(8,128)(2,1)S(1)}, u32[]{:S(2)}, u32[]{:S(2)}) collective-permute-start(bf16[32,2048]{1,0:T(8,128)(2,1)S(1)} %collective-permute-done.13.ya), channel_id=1, source_target_pairs={{0,4},{4,0},{8,12},{12,8},{16,20},{20,16},{24,28},{28,24},{1,5},{5... | collective-permute-start | bytes 393224 | tf_op jit(solution)/shard_map/ppermute | solution.py:22

commit v4 on v3

--- a/solution.py
+++ b/solution.py
@@ -171,7 +171,7 @@
     tok, width = raw[0].shape
     levels, heads = offsets.shape
     half = heads // 2
-    per = 2
+    per = 8
     steps = half // per
     raw_spec = own_spec(tok, per * dim, steps)
     swapped = [swap_spec(tok, per * dim, steps, i) for i in range(3)]
@@ -211,94 +211,105 @@
     lane = lax.broadcasted_iota(jnp.int32, (1, 2 * sel), 1)
     is2 = lax.rem(lane, sel) < n2
     pos = lax.broadcasted_iota(jnp.int32, (1, 2 * tok), 1)
-    for h in range(per):
-        head = core_ref[0] * heads + pl.program_id(0) * per + h
-        pick = pick_matrix(offs_ref, head, 2, levels, tok)
-        none = jnp.zeros_like(pick)
-        both = stack(side(pick, none), side(none, pick))
-        cols = slice(h * dim, (h + 1) * dim)
-        kc = slice(2 * h * dim, (2 * h + 1) * dim)
-        vc = slice((2 * h + 1) * dim, (2 * h + 2) * dim)
-        wide = slice(2 * h * dim, 2 * (h + 1) * dim)
-        lanes = slice(2 * h * tok, 2 * (h + 1) * tok)
-        gra0, gra1 = g0[:, cols], g1[:, cols]
-        gsel = stack(dot(pick, gra0), dot(pick, gra1)).astype(BF16)
-        qsel = selq[:, cols]
-
-        def rows(c):
-            a, b = near[tok : tok + sel, c], near[tok + sel :, c]
-            return stack(
-                a[:n2], b[:n2], x[:n2, c], xx[:n2, c], a[n2:], b[n2:], x[n2:, c], xx[n2:, c],
-                *(ref[:, c] for ref in (y3, yy3, d3, dd3)),
-            )
-
-        keys, vals = rows(kc), rows(vc)
-        st = dot_nt(keys, qsel)
-        s = jnp.where(is2, st[:tok], st[tok:]) * scale
-        top = jnp.max(s, axis=0, keepdims=True)
-        e = jnp.exp(s - top)
-        size = jnp.sum(e, axis=0, keepdims=True)
-        pt = dot_nt(vals, gsel)
-        p = jnp.where(is2, pt[:tok], pt[tok:])
-        dhat = jnp.sum(e * p, axis=0, keepdims=True)
-        p0 = side(dot_nt(v0[:, cols], gra0), dot_nt(v1[:, cols], gra1))
-        p1 = dot_nt(near[:tok, vc], stack(gra0, gra1))
-        ex = exps[:, lanes]
-        dloc = jnp.sum(ex[:tok].astype(F32) * p0 + ex[tok:].astype(F32) * p1, axis=0, keepdims=True)
-        terms = split(top, 3) + split(size, 2) + split(dhat, 2)
-        terms = stack(*terms)
+    first = core_ref[0] * heads + pl.program_id(0) * per
+    each = range(per)
+    cols = [slice(h * dim, (h + 1) * dim) for h in each]
+    kc = [slice(2 * h * dim, (2 * h + 1) * dim) for h in each]
+    vc = [slice((2 * h + 1) * dim, (2 * h + 2) * dim) for h in each]
+    wide = [slice(2 * h * dim, 2 * (h + 1) * dim) for h in each]
+    lanes = [slice(2 * h * tok, 2 * (h + 1) * tok) for h in each]
+
+    def rows(c):
+        a, b = near[tok : tok + sel, c], near[tok + sel :, c]
+        return stack(
+            a[:n2], b[:n2], x[:n2, c], xx[:n2, c], a[n2:], b[n2:], x[n2:, c], xx[n2:, c],
+            *(ref[:, c] for ref in (y3, yy3, d3, dd3)),
+        )
+
+    def level_pick(value):
+        return jnp.where(is2, value[:tok], value[tok:])
+
+    picks = [pick_matrix(offs_ref, first + h, 2, levels, tok) for h in each]
+    gsel = [
+        stack(dot(picks[h], g0[:, cols[h]]), dot(picks[h], g1[:, cols[h]])).astype(BF16)
+        for h in each
+    ]
+    keys = [rows(kc[h]) for h in each]
+    s = [level_pick(dot_nt(keys[h], selq[:, cols[h]])) * scale for h in each]
+    p = [level_pick(dot_nt(rows(vc[h]), gsel[h])) for h in each]
+    dloc = []
+    for h in each:
+        gra0, gra1 = g0[:, cols[h]], g1[:, cols[h]]
+        p0 = side(dot_nt(v0[:, cols[h]], gra0), dot_nt(v1[:, cols[h]], gra1))
+        p1 = dot_nt(near[:tok, vc[h]], stack(gra0, gra1))
+        ex = exps[:, lanes[h]]
+        both = ex[:tok].astype(F32) * p0 + ex[tok:].astype(F32) * p1
+        dloc.append(jnp.sum(both, axis=0, keepdims=True))
+    top = [jnp.max(a, axis=0, keepdims=True) for a in s]
+    e = [jnp.exp(a - b) for a, b in zip(s, top)]
+    size = [jnp.sum(a, axis=0, keepdims=True) for a in e]
+    dhat = [jnp.sum(a * b, axis=0, keepdims=True) for a, b in zip(e, p)]
+    none = jnp.zeros_like(picks[0])
+    spots = [stack(side(a, none), side(none, a)) for a in picks]
+    spread = []
+    for h in each:
+        terms = stack(*split(top[h], 3), *split(size[h], 2), *split(dhat[h], 2))
         zero = jnp.zeros_like(terms)
-        spread = dot(stack(jnp.where(is2, terms, zero), jnp.where(is2, zero, terms)), both)
+        apart = stack(jnp.where(is2, terms, zero), jnp.where(is2, zero, terms))
+        spread.append(dot(apart, spots[h]))
+    back = []
+    for h in each:
 
         def level_stats(level, lo):
             rate = 2**level
-            on = lax.rem(pos, rate) == lax.rem(offs_ref[level - 1, head], rate)
-            t = spread[lo : lo + 1] + spread[lo + 1 : lo + 2] + spread[lo + 2 : lo + 3]
-            return (
-                jnp.where(on, t, NEG),
-                spread[lo + 3 : lo + 4] + spread[lo + 4 : lo + 5],
-                spread[lo + 5 : lo + 6] + spread[lo + 6 : lo + 7],
-            )
-
-        t1, z1 = stats[0:1, lanes], stats[1:2, lanes]
-        t2, z2, d2 = level_stats(2, 0)
-        t3, z3, d3v = level_stats(3, 7)
+            on = lax.rem(pos, rate) == lax.rem(offs_ref[level - 1, first + h], rate)
+            t = [spread[h][lo + i : lo + i + 1] for i in range(7)]
+            return jnp.where(on, t[0] + t[1] + t[2], NEG), t[3] + t[4], t[5] + t[6]
+
+        t1, z1 = stats[0:1, lanes[h]], stats[1:2, lanes[h]]
+        t2, z2, dot2 = level_stats(2, 0)
+        t3, z3, dot3 = level_stats(3, 7)
         high = jnp.maximum(t1, jnp.maximum(t2, t3))
         a1, a2, a3 = jnp.exp(t1 - high), jnp.exp(t2 - high), jnp.exp(t3 - high)
         inv = 1.0 / (a1 * z1 + a2 * z2 + a3 * z3)
         f1, f2, f3 = a1 * inv, a2 * inv, a3 * inv
-        delta = f1 * dloc + f2 * d2 + f3 * d3v
-        stats2[0:1, lanes] = f1
-        stats2[1:2, lanes] = delta
-        back = dot_nt(stack(*split(f2, 2), *split(f3, 2), *split(delta, 2)), both)
-        f = jnp.where(is2, back[0:1] + back[1:2], back[2:3] + back[3:4])
-        dl = back[4:5] + back[5:6]
-        w = e * f
-        ds = w * (p - dl)
-        zero = jnp.zeros_like(w)
-
-        def apart(value):
-            return stack(jnp.where(is2, value, zero), jnp.where(is2, zero, value)).astype(BF16)
-
-        dsm = apart(ds)
-        dkv = side(dot(dsm, qsel) * scale, dot(apart(w), gsel)).astype(BF16)
-        xa[:n2, wide] = dkv[2 * n2 : 3 * n2]
-        xb[:n2, wide] = dkv[3 * n2 : 4 * n2]
+        delta = f1 * dloc[h] + f2 * dot2 + f3 * dot3
+        stats2[0:1, lanes[h]] = f1
+        stats2[1:2, lanes[h]] = delta
+        terms = stack(*split(f2, 2), *split(f3, 2), *split(delta, 2))
+        back.append(dot_nt(terms, spots[h]))
+
+    def apart(value):
+        zero = jnp.zeros_like(value)
+        return stack(jnp.where(is2, value, zero), jnp.where(is2, zero, value)).astype(BF16)
+
+    dsm, wm = [], []
+    for h in each:
+        b = back[h]
+        w = e[h] * jnp.where(is2, b[0:1] + b[1:2], b[2:3] + b[3:4])
+        dsm.append(apart(w * (p[h] - (b[4:5] + b[5:6]))))
+        wm.append(apart(w))
+    dk = [dot(dsm[h], selq[:, cols[h]]) * scale for h in each]
+    dv = [dot(wm[h], gsel[h]) for h in each]
+    for h in each:
+        dkv = side(dk[h], dv[h]).astype(BF16)
+        xa[:n2, wide[h]] = dkv[2 * n2 : 3 * n2]
+        xb[:n2, wide[h]] = dkv[3 * n2 : 4 * n2]
         third = [dkv[tok + i * n3 : tok + (i + 1) * n3] for i in range(8)]
-        xa[n2:, wide] = third[2]
-        xb[n2:, wide] = third[3]
-        yab[:, wide] = stack(third[4], third[5])
-        da[:, wide] = third[6]
-        db[:, wide] = third[7]
-        ngrad[:, wide] = stack(dkv[:n2], third[0], dkv[n2 : 2 * n2], third[1])
-        dqt[:, h * dim : h * dim + 2 * sel] = dot(keys.T, dsm).astype(BF16)
+        xa[n2:, wide[h]] = third[2]
+        xb[n2:, wide[h]] = third[3]
+        yab[:, wide[h]] = stack(third[4], third[5])
+        da[:, wide[h]] = third[6]
+        db[:, wide[h]] = third[7]
+        ngrad[:, wide[h]] = stack(dkv[:n2], third[0], dkv[n2 : 2 * n2], third[1])
+        dqt[:, h * dim : h * dim + 2 * sel] = dot(keys[h].T, dsm[h]).astype(BF16)
 
 
 def far_call(offsets, core, pre, raw, far, dim):
     tok, width = raw[0].shape
     levels, heads = offsets.shape
     half = heads // 2
-    per = 2
+    per = 8
     steps = half // per
     n2, n3 = tok // 4, tok // 8
     raw_spec = own_spec(tok, per * dim, steps)
@@ -379,7 +390,7 @@
     tok, width = raw[0].shape
     levels, heads = offsets.shape
     half = heads // 2
-    per = 2
+    per = 8
     steps = half // per
     raw_spec = own_spec(tok, per * dim, steps)
     swapped = [swap_spec(tok, per * dim, steps, i) for i in range(3)]
@@ -412,15 +423,17 @@
     swap = pl.program_id(0) * 2 // pl.num_programs(0) != core_ref[0]
 
     def work(base, x, y, d):
-        for h in range(per):
-            head = pl.program_id(0) * per + h
-            place = place_matrix(offs_ref, head, 2, levels, tok)
+        each = range(per)
+        place = [
+            place_matrix(offs_ref, pl.program_id(0) * per + h, 2, levels, tok) for h in each
+        ]
+        third = (x[n2:].astype(F32) + y[...].astype(F32) + d[...].astype(F32)).astype(BF16)
+        src = [slice(2 * h * dim, 2 * (h + 1) * dim) for h in each]
+        more = [dot(place[h], stack(x[:n2, src[h]], third[:, src[h]])) for h in each]
+        for h in each:
             cols = slice(h * dim, (h + 1) * dim)
-            src = slice(2 * h * dim, 2 * (h + 1) * dim)
             lo = 3 * h * dim
-            third = x[n2:, src].astype(F32) + y[:, src].astype(F32) + d[:, src].astype(F32)
-            part = stack(x[:n2, src], third.astype(BF16))
-            total = base[:, lo + dim : lo + 3 * dim].astype(F32) + dot(place, part)
+            total = base[:, lo + dim : lo + 3 * dim].astype(F32) + more[h]
             dq[:, cols] = base[:, lo : lo + dim]
             dk[:, cols] = total[:, :dim].astype(BF16)
             dv[:, cols] = total[:, dim:].astype(BF16)
@@ -437,7 +450,7 @@
 def final_call(offsets, core, parts, dim):
     levels, heads = offsets.shape
     tok = parts[0].shape[0]
-    steps = 4
+    steps = 2
     per = heads // steps
     third = tok // 8
 

time: 54.8 us -> 49.1 us (0.90)
  Pallas kernels: 25.2 us -> 17.1 us
  waiting for transfers between devices: 11.8 us -> 14.3 us
    pallas_call x1, Pallas kernels: 8.21 us -> 3.74 us  [far_call(): pl.pallas_call(functools.partial(far_kernel, levels, per, dim), grid_spec...]
    ppermute x15, waiting for transfers between devices: 11.8 us -> 14.3 us  [exchange(): return lax.ppermute(value, 'seq', [(i, i ^ bits) for i in range(count)])]
    pallas_call x1, Pallas kernels: 6.85 us -> 5.51 us  [near_call(): pl.pallas_call(functools.partial(near_kernel, levels, per, dim), grid_spe...]
    pallas_call x1, Pallas kernels: 3.46 us -> 2.31 us  [final_call(): pl.pallas_call(functools.partial(final_kernel, levels, per, dim), grid_sp...]
    pallas_call x1, Pallas kernels: 4.22 us -> 3.1 us  [pre_call(): pl.pallas_call(functools.partial(pre_kernel, levels, per, dim), grid_spec...]
  transfers between devices with their start and end apart: 16 -> 16, of which waited for: 5 -> 5; matrix products, arithmetic and copies ran while one was open for 0% -> 0% of each run, Pallas kernels for 20% -> 18%
where the time goes in v4:
time: 49.1 us; the launch traced here: 48.9 us
  Pallas kernels  17.1 us (35%)
  starting transfers between devices  15.1 us (31%)
  waiting for transfers between devices  14.3 us (29%)
  local copies, waits for them, and re-layouts  1.67 us (3%)
  between operations  0.72 us (1%)
    ppermute x15, waiting for transfers between devices, exchange(): return lax.ppermute(value, 'seq', [(i, i ^ bits) for i in range(count)])  14.3 us
    ppermute x15, starting transfers between devices, exchange(): return lax.ppermute(value, 'seq', [(i, i ^ bits) for i in range(count)])  10.4 us
    pallas_call x1, Pallas kernels, near_call(): pl.pallas_call(functools.partial(near_kernel, levels, per, dim), grid_spe...  5.51 us
    ppermute x1, starting transfers between devices, per_device(): lax.ppermute(out_grads[0], 'section', [(i, (i - 1) % sections) for i in r...  4.67 us
    pallas_call x1, Pallas kernels, far_call(): pl.pallas_call(functools.partial(far_kernel, levels, per, dim), grid_spec...  3.74 us
    pallas_call x1, Pallas kernels, pre_call(): pl.pallas_call(functools.partial(pre_kernel, levels, per, dim), grid_spec...  3.1 us
    pallas_call x1, Pallas kernels, pick_call(): pl.pallas_call(functools.partial(pick_kernel, levels, per, dim), grid_spe...  2.43 us
    pallas_call x1, Pallas kernels, final_call(): pl.pallas_call(functools.partial(final_kernel, levels, per, dim), grid_sp...  2.31 us
  transfers between devices with their start and end apart: 16, of which 5 were waited for; matrix products, arithmetic and copies ran while one was open for 0% of the time, Pallas kernels for 18%

profile of v4, /device:TPU:0, one launch (start us, length us, event | category | flops | bytes accessed | tf_op | source)
XLA Modules:
  0.0 48.9 jit_solution(12377008675935075129)
XLA Ops:
  0.6 0.0 copy-start.2
  0.6 0.7 %copy-done.2 = s32[3,16]{1,0:T(4,128)S(1)} copy-done((s32[3,16]{1,0:T(4,128)S(1)}, s32[3,16]{1,0:T(4,128)}, u32[]{:S(2)}) %copy-start.2) | copy-done | bytes 216
  1.3 0.0 copy-start.3
  1.3 2.4 %pick_rows.1 = (bf16[48,4096]{1,0:T(8,128)(2,1)S(1)}, bf16[16,4096]{1,0:T(8,128)(2,1)S(1)}, bf16[128,3072]{1,0:T(8,128)(2,1)S(1)}) custom-call(s32[3,16]{1,0:T(4,128)S(1)} %copy-done.2, s32[1]{0:T(128)} %bitcast.core_ref, bf16[128,2048]{1,0:T(8,128)(2,1)} %bitcast.13, bf16[128,2048]{1,0:T(8,128)(2,1)} %bitcast.8, bf16[128,2048]{1,0:T(8,128)(2,1)} %bitcast.17, ...), custom_call_target="tpu_custom_call" | custom-call | tf_op jit(solution)/shard_map/pick_rows/pallas_call | solution.py:85
  3.8 0.5 %collective-permute-start = (bf16[128,3072]{1,0:T(8,128)(2,1)S(1)}, bf16[128,3072]{1,0:T(8,128)(2,1)S(1)}, u32[]{:S(2)}, u32[]{:S(2)}) collective-permute-start(bf16[128,3072]{1,0:T(8,128)(2,1)S(1)} %get-tuple-element.33), channel_id=1, source_target_pairs={{0,4},{4,0},{8,12},{12,8},{16,20},{20,16},{24,28},{28,24},{1,5},{5... | collective-permute-start | bytes 2359304 | tf_op jit(solution)/shard_map/ppermute | solution.py:22
  4.3 0.0 copy-done.3
  4.3 4.7 %collective-permute-start.4 = (bf16[128,2048]{1,0:T(8,128)(2,1)S(1)}, bf16[128,2048]{1,0:T(8,128)(2,1)S(1)}, u32[]{:S(2)}, u32[]{:S(2)}) collective-permute-start(bf16[128,2048]{1,0:T(8,128)(2,1)S(1)} %bitcast.20), channel_id=1, source_target_pairs={{0,3},{1,0},{2,1},{3,2},{4,7},{5,4},{6,5},{7,6},{8,11},{9,8},{10,9... | collective-permute-start | bytes 1572872 | tf_op jit(solution)/shard_map/ppermute | solution.py:493
  8.9 1.5 %collective-permute-start.1 = (bf16[48,4096]{1,0:T(8,128)(2,1)S(1)}, bf16[48,4096]{1,0:T(8,128)(2,1)S(1)}, u32[]{:S(2)}, u32[]{:S(2)}) collective-permute-start(bf16[48,4096]{1,0:T(8,128)(2,1)S(1)} %get-tuple-element.38), channel_id=1, source_target_pairs={{0,8},{4,12},{8,0},{12,4},{16,24},{20,28},{24,16},{28,20},{1,9},{5... | collective-permute-start | bytes 1179656 | tf_op jit(solution)/shard_map/ppermute | solution.py:22
  10.4 1.5 %collective-permute-start.3 = (bf16[16,4096]{1,0:T(8,128)(2,1)S(1)}, bf16[16,4096]{1,0:T(8,128)(2,1)S(1)}, u32[]{:S(2)}, u32[]{:S(2)}) collective-permute-start(bf16[16,4096]{1,0:T(8,128)(2,1)S(1)} %get-tuple-element.39), channel_id=1, source_target_pairs={{0,24},{4,28},{8,16},{12,20},{16,8},{20,12},{24,0},{28,4},{1,25},{... | collective-permute-start | bytes 393224 | tf_op jit(solution)/shard_map/ppermute | solution.py:22
  11.9 0.5 %collective-permute-start.2 = (bf16[16,4096]{1,0:T(8,128)(2,1)S(1)}, bf16[16,4096]{1,0:T(8,128)(2,1)S(1)}, u32[]{:S(2)}, u32[]{:S(2)}) collective-permute-start(bf16[16,4096]{1,0:T(8,128)(2,1)S(1)} %get-tuple-element.39), channel_id=1, source_target_pairs={{0,16},{4,20},{8,24},{12,28},{16,0},{20,4},{24,8},{28,12},{1,17},{... | collective-permute-start | bytes 393224 | tf_op jit(solution)/shard_map/ppermute | solution.py:22
  12.4 0.0 collective-permute-done.q1.k1.v1
  12.4 3.1 %local_scores.1 = (bf16[256,2048]{1,0:T(8,128)(2,1)S(1)}, f32[8,2048]{1,0:T(8,128)S(1)}, bf16[224,2048]{1,0:T(8,128)(2,1)S(1)}, bf16[96,1024]{1,0:T(8,128)(2,1)S(1)}) custom-call(s32[3,16]{1,0:T(4,128)S(1)} %copy-done.2, s32[1]{0:T(128)} %bitcast.core_ref, bf16[128,2048]{1,0:T(8,128)(2,1)} %bitcast.18, bf16[128,3072]{1,0:T(8,128)(2,1)S(1)} %collective-permute-done.q1.k1.v1, ...), custom_call_target="tpu_custom_call" | custom-call | tf_op jit(solution)/shard_map/local_scores/pallas_call | solution.py:187
  15.5 0.0 copy-start
  15.5 1.0 %copy-done = bf16[256,2048]{1,0:T(8,128)(2,1)} copy-done((bf16[256,2048]{1,0:T(8,128)(2,1)}, bf16[256,2048]{1,0:T(8,128)(2,1)S(1)}, u32[]{:S(2)}) %copy-start) | copy-done | bytes 1048600
  16.5 7.4 %collective-permute-done.3.d3 = bf16[16,4096]{1,0:T(8,128)(2,1)S(1)} collective-permute-done((bf16[16,4096]{1,0:T(8,128)(2,1)S(1)}, bf16[16,4096]{1,0:T(8,128)(2,1)S(1)}, u32[]{:S(2)}, u32[]{:S(2)}) %collective-permute-start.3) | collective-permute-done | bytes 131104 | tf_op jit(solution)/shard_map/ppermute | solution.py:22
  23.9 0.0 collective-permute-done.2.y3
  23.9 0.0 collective-permute-done.1.x
  23.9 0.0 collective-permute-done.4.g0
  23.9 0.1 collective-permute-start.5
  24.0 0.5 %collective-permute-start.6 = (bf16[48,4096]{1,0:T(8,128)(2,1)S(1)}, bf16[48,4096]{1,0:T(8,128)(2,1)S(1)}, u32[]{:S(2)}, u32[]{:S(2)}) collective-permute-start(bf16[48,4096]{1,0:T(8,128)(2,1)S(1)} %collective-permute-done.1.x), channel_id=1, source_target_pairs={{0,4},{4,0},{8,12},{12,8},{16,20},{20,16},{24,28},{28,24},{1,5},{5... | collective-permute-start | bytes 1179656 | tf_op jit(solution)/shard_map/ppermute | solution.py:22
  24.5 0.1 collective-permute-start.7
  24.6 0.4 collective-permute-start.8
  25.0 1.6 %collective-permute-done.7.yy3 = bf16[16,4096]{1,0:T(8,128)(2,1)S(1)} collective-permute-done((bf16[16,4096]{1,0:T(8,128)(2,1)S(1)}, bf16[16,4096]{1,0:T(8,128)(2,1)S(1)}, u32[]{:S(2)}, u32[]{:S(2)}) %collective-permute-start.7) | collective-permute-done | bytes 131104 | tf_op jit(solution)/shard_map/ppermute | solution.py:22
  26.6 0.2 collective-permute-done.8.dd3
  26.8 0.0 collective-permute-done.6.xx
  26.8 0.0 collective-permute-done.5.g1
  26.8 0.0 copy-start.1
  26.8 3.7 %far_levels.1 = (bf16[48,2048]{1,0:T(8,128)(2,1)S(1)}, bf16[48,2048]{1,0:T(8,128)(2,1)S(1)}, bf16[32,2048]{1,0:T(8,128)(2,1)S(1)}, bf16[16,2048]{1,0:T(8,128)(2,...) custom-call(s32[3,16]{1,0:T(4,128)S(1)} %copy-done.2, ...), custom_call_target="tpu_custom_call" | custom-call | tf_op jit(solution)/shard_map/far_levels/pallas_call | solution.py:332
  30.6 1.6 %collective-permute-start.9 = (bf16[48,2048]{1,0:T(8,128)(2,1)S(1)}, bf16[48,2048]{1,0:T(8,128)(2,1)S(1)}, u32[]{:S(2)}, u32[]{:S(2)}) collective-permute-start(bf16[48,2048]{1,0:T(8,128)(2,1)S(1)} %get-tuple-element.49), channel_id=1, source_target_pairs={{0,8},{4,12},{8,0},{12,4},{16,24},{20,28},{24,16},{28,20},{1,9},{5... | collective-permute-start | bytes 589832 | tf_op jit(solution)/shard_map/ppermute | solution.py:22
  32.2 0.0 collective-permute-start.10
  32.2 0.5 %collective-permute-start.13 = (bf16[32,2048]{1,0:T(8,128)(2,1)S(1)}, bf16[32,2048]{1,0:T(8,128)(2,1)S(1)}, u32[]{:S(2)}, u32[]{:S(2)}) collective-permute-start(bf16[32,2048]{1,0:T(8,128)(2,1)S(1)} %get-tuple-element.53), channel_id=1, source_target_pairs={{0,16},{4,20},{8,24},{12,28},{16,0},{20,4},{24,8},{28,12},{1,17},{... | collective-permute-start | bytes 393224 | tf_op jit(solution)/shard_map/ppermute | solution.py:22
  32.7 2.4 %collective-permute-start.11 = (bf16[16,2048]{1,0:T(8,128)(2,1)S(1)}, bf16[16,2048]{1,0:T(8,128)(2,1)S(1)}, u32[]{:S(2)}, u32[]{:S(2)}) collective-permute-start(bf16[16,2048]{1,0:T(8,128)(2,1)S(1)} %get-tuple-element.51), channel_id=1, source_target_pairs={{0,24},{4,28},{8,16},{12,20},{16,8},{20,12},{24,0},{28,4},{1,25},{... | collective-permute-start | bytes 196616 | tf_op jit(solution)/shard_map/ppermute | solution.py:22
  35.1 0.2 collective-permute-start.12
  35.3 0.0 copy-done.1
  35.3 5.5 %near_levels.1 = (bf16[128,3072]{1,0:T(8,128)(2,1)S(1)}, bf16[128,3072]{1,0:T(8,128)(2,1)S(1)}) custom-call(s32[3,16]{1,0:T(4,128)S(1)} %copy-done.2, s32[1]{0:T(128)} %bitcast.core_ref, bf16[256,2048]{1,0:T(8,128)(2,1)S(1)} %copy-done.1, f32[8,2048]{1,0:T(8,128)S(1)} %get-tuple-element.44.stats2, bf16[224,2048]{1,0:T(8,128)(2,1)S(1)} %get-tuple-element.36.near, ...), custom_call_target="tpu_custom_call" | custom-call | tf_op jit(solution)/shard_map/near_levels/pallas_call | solution.py:402
  40.8 3.1 %collective-permute-done.11.da = bf16[16,2048]{1,0:T(8,128)(2,1)S(1)} collective-permute-done((bf16[16,2048]{1,0:T(8,128)(2,1)S(1)}, bf16[16,2048]{1,0:T(8,128)(2,1)S(1)}, u32[]{:S(2)}, u32[]{:S(2)}) %collective-permute-start.11) | collective-permute-done | bytes 65568 | tf_op jit(solution)/shard_map/ppermute | solution.py:22
  43.8 0.0 collective-permute-done.12.db
  43.9 0.0 collective-permute-done.13.ya
  43.9 0.0 collective-permute-done.9.xa
  43.9 0.0 collective-permute-done.10.xb
  43.9 0.6 %collective-permute-start.14 = (bf16[128,3072]{1,0:T(8,128)(2,1)S(1)}, bf16[128,3072]{1,0:T(8,128)(2,1)S(1)}, u32[]{:S(2)}, u32[]{:S(2)}) collective-permute-start(bf16[128,3072]{1,0:T(8,128)(2,1)S(1)} %get-tuple-element.54), channel_id=1, source_target_pairs={{0,4},{4,0},{8,12},{12,8},{16,20},{20,16},{24,28},{28,24},{1,5},{5... | collective-permute-start | bytes 2359304 | tf_op jit(solution)/shard_map/ppermute | solution.py:22
  44.4 0.1 collective-permute-start.15
  44.5 2.0 %collective-permute-done.15.yb = bf16[32,2048]{1,0:T(8,128)(2,1)S(1)} collective-permute-done((bf16[32,2048]{1,0:T(8,128)(2,1)S(1)}, bf16[32,2048]{1,0:T(8,128)(2,1)S(1)}, u32[]{:S(2)}, u32[]{:S(2)}) %collective-permute-start.15) | collective-permute-done | bytes 131104 | tf_op jit(solution)/shard_map/ppermute | solution.py:22
  46.5 0.0 collective-permute-done.14.bb
  46.6 2.3 %add_pieces.1 = (bf16[128,2048]{1,0:T(8,128)(2,1)}, bf16[128,2048]{1,0:T(8,128)(2,1)}, bf16[128,2048]{1,0:T(8,128)(2,1)}) custom-call(s32[3,16]{1,0:T(4,128)S(1)} %copy-done.2, s32[1]{0:T(128)} %bitcast.core_ref, bf16[128,3072]{1,0:T(8,128)(2,1)S(1)} %get-tuple-element.47.ba, bf16[128,3072]{1,0:T(8,128)(2,1)S(1)} %collective-permute-done.14.bb, ...), custom_call_target="tpu_custom_call" | custom-call | tf_op jit(solution)/shard_map/add_pieces/pallas_call | solution.py:474
Async XLA Ops:
  0.6 0.7 %copy-start.2 = (s32[3,16]{1,0:T(4,128)S(1)}, s32[3,16]{1,0:T(4,128)}, u32[]{:S(2)}) copy-start(s32[3,16]{1,0:T(4,128)} %offs_ref.9) | copy-start | bytes 580
  1.3 3.0 %copy-start.3 = (bf16[1,128,2048]{2,1,0:T(8,128)(2,1)S(1)}, bf16[1,128,2048]{2,1,0:T(8,128)(2,1)}, u32[]{:S(2)}) copy-start(bf16[1,128,2048]{2,1,0:T(8,128)(2,1)} %param.8) | copy-start | bytes 1572868
  3.8 8.7 %collective-permute-start = (bf16[128,3072]{1,0:T(8,128)(2,1)S(1)}, bf16[128,3072]{1,0:T(8,128)(2,1)S(1)}, u32[]{:S(2)}, u32[]{:S(2)}) collective-permute-start(bf16[128,3072]{1,0:T(8,128)(2,1)S(1)} %get-tuple-element.33), channel_id=1, source_target_pairs={{0,4},{4,0},{8,12},{12,8},{16,20},{20,16},{24,28},{28,24},{1,5},{5... | collective-permute-start | bytes 2359304 | tf_op jit(solution)/shard_map/ppermute | solution.py:22
  4.3 19.6 %collective-permute-start.4 = (bf16[128,2048]{1,0:T(8,128)(2,1)S(1)}, bf16[128,2048]{1,0:T(8,128)(2,1)S(1)}, u32[]{:S(2)}, u32[]{:S(2)}) collective-permute-start(bf16[128,2048]{1,0:T(8,128)(2,1)S(1)} %bitcast.20), channel_id=1, source_target_pairs={{0,3},{1,0},{2,1},{3,2},{4,7},{5,4},{6,5},{7,6},{8,11},{9,8},{10,9... | collective-permute-start | bytes 1572872 | tf_op jit(solution)/shard_map/ppermute | solution.py:493
  8.9 14.9 %collective-permute-start.1 = (bf16[48,4096]{1,0:T(8,128)(2,1)S(1)}, bf16[48,4096]{1,0:T(8,128)(2,1)S(1)}, u32[]{:S(2)}, u32[]{:S(2)}) collective-permute-start(bf16[48,4096]{1,0:T(8,128)(2,1)S(1)} %get-tuple-element.38), channel_id=1, source_target_pairs={{0,8},{4,12},{8,0},{12,4},{16,24},{20,28},{24,16},{28,20},{1,9},{5... | collective-permute-start | bytes 1179656 | tf_op jit(solution)/shard_map/ppermute | solution.py:22
  10.4 13.4 %collective-permute-start.3 = (bf16[16,4096]{1,0:T(8,128)(2,1)S(1)}, bf16[16,4096]{1,0:T(8,128)(2,1)S(1)}, u32[]{:S(2)}, u32[]{:S(2)}) collective-permute-start(bf16[16,4096]{1,0:T(8,128)(2,1)S(1)} %get-tuple-element.39), channel_id=1, source_target_pairs={{0,24},{4,28},{8,16},{12,20},{16,8},{20,12},{24,0},{28,4},{1,25},{... | collective-permute-start | bytes 393224 | tf_op jit(solution)/shard_map/ppermute | solution.py:22
  11.9 12.0 %collective-permute-start.2 = (bf16[16,4096]{1,0:T(8,128)(2,1)S(1)}, bf16[16,4096]{1,0:T(8,128)(2,1)S(1)}, u32[]{:S(2)}, u32[]{:S(2)}) collective-permute-start(bf16[16,4096]{1,0:T(8,128)(2,1)S(1)} %get-tuple-element.39), channel_id=1, source_target_pairs={{0,16},{4,20},{8,24},{12,28},{16,0},{20,4},{24,8},{28,12},{1,17},{... | collective-permute-start | bytes 393224 | tf_op jit(solution)/shard_map/ppermute | solution.py:22
  15.5 1.0 %copy-start = (bf16[256,2048]{1,0:T(8,128)(2,1)}, bf16[256,2048]{1,0:T(8,128)(2,1)S(1)}, u32[]{:S(2)}) copy-start(bf16[256,2048]{1,0:T(8,128)(2,1)S(1)} %get-tuple-element.34.exps) | copy-start | bytes 3145732
  23.9 2.9 %collective-permute-start.5 = (bf16[128,2048]{1,0:T(8,128)(2,1)S(1)}, bf16[128,2048]{1,0:T(8,128)(2,1)S(1)}, u32[]{:S(2)}, u32[]{:S(2)}) collective-permute-start(bf16[128,2048]{1,0:T(8,128)(2,1)S(1)} %collective-permute-done.4.g0), channel_id=1, source_target_pairs={{0,4},{4,0},{8,12},{12,8},{16,20},{20,16},{24,28},{28,24},{1,5},{5... | collective-permute-start | bytes 1572872 | tf_op jit(solution)/shard_map/ppermute | solution.py:22
  24.0 2.8 %collective-permute-start.6 = (bf16[48,4096]{1,0:T(8,128)(2,1)S(1)}, bf16[48,4096]{1,0:T(8,128)(2,1)S(1)}, u32[]{:S(2)}, u32[]{:S(2)}) collective-permute-start(bf16[48,4096]{1,0:T(8,128)(2,1)S(1)} %collective-permute-done.1.x), channel_id=1, source_target_pairs={{0,4},{4,0},{8,12},{12,8},{16,20},{20,16},{24,28},{28,24},{1,5},{5... | collective-permute-start | bytes 1179656 | tf_op jit(solution)/shard_map/ppermute | solution.py:22
  24.5 2.1 %collective-permute-start.7 = (bf16[16,4096]{1,0:T(8,128)(2,1)S(1)}, bf16[16,4096]{1,0:T(8,128)(2,1)S(1)}, u32[]{:S(2)}, u32[]{:S(2)}) collective-permute-start(bf16[16,4096]{1,0:T(8,128)(2,1)S(1)} %collective-permute-done.2.y3), channel_id=1, source_target_pairs={{0,4},{4,0},{8,12},{12,8},{16,20},{20,16},{24,28},{28,24},{1,5},{5... | collective-permute-start | bytes 393224 | tf_op jit(solution)/shard_map/ppermute | solution.py:22
  24.6 2.3 %collective-permute-start.8 = (bf16[16,4096]{1,0:T(8,128)(2,1)S(1)}, bf16[16,4096]{1,0:T(8,128)(2,1)S(1)}, u32[]{:S(2)}, u32[]{:S(2)}) collective-permute-start(bf16[16,4096]{1,0:T(8,128)(2,1)S(1)} %collective-permute-done.3.d3), channel_id=1, source_target_pairs={{0,4},{4,0},{8,12},{12,8},{16,20},{20,16},{24,28},{28,24},{1,5},{5... | collective-permute-start | bytes 393224 | tf_op jit(solution)/shard_map/ppermute | solution.py:22
  26.8 8.4 %copy-start.1 = (bf16[256,2048]{1,0:T(8,128)(2,1)S(1)}, bf16[256,2048]{1,0:T(8,128)(2,1)}, u32[]{:S(2)}) copy-start(bf16[256,2048]{1,0:T(8,128)(2,1)} %copy-done) | copy-start | bytes 3145732
  30.6 13.3 %collective-permute-start.9 = (bf16[48,2048]{1,0:T(8,128)(2,1)S(1)}, bf16[48,2048]{1,0:T(8,128)(2,1)S(1)}, u32[]{:S(2)}, u32[]{:S(2)}) collective-permute-start(bf16[48,2048]{1,0:T(8,128)(2,1)S(1)} %get-tuple-element.49), channel_id=1, source_target_pairs={{0,8},{4,12},{8,0},{12,4},{16,24},{20,28},{24,16},{28,20},{1,9},{5... | collective-permute-start | bytes 589832 | tf_op jit(solution)/shard_map/ppermute | solution.py:22
  32.2 11.7 %collective-permute-start.10 = (bf16[48,2048]{1,0:T(8,128)(2,1)S(1)}, bf16[48,2048]{1,0:T(8,128)(2,1)S(1)}, u32[]{:S(2)}, u32[]{:S(2)}) collective-permute-start(bf16[48,2048]{1,0:T(8,128)(2,1)S(1)} %get-tuple-element.50), channel_id=1, source_target_pairs={{0,12},{4,8},{8,4},{12,0},{16,28},{20,24},{24,20},{28,16},{1,13},{... | collective-permute-start | bytes 589832 | tf_op jit(solution)/shard_map/ppermute | solution.py:22
  32.2 11.7 %collective-permute-start.13 = (bf16[32,2048]{1,0:T(8,128)(2,1)S(1)}, bf16[32,2048]{1,0:T(8,128)(2,1)S(1)}, u32[]{:S(2)}, u32[]{:S(2)}) collective-permute-start(bf16[32,2048]{1,0:T(8,128)(2,1)S(1)} %get-tuple-element.53), channel_id=1, source_target_pairs={{0,16},{4,20},{8,24},{12,28},{16,0},{20,4},{24,8},{28,12},{1,17},{... | collective-permute-start | bytes 393224 | tf_op jit(solution)/shard_map/ppermute | solution.py:22
  32.7 11.2 %collective-permute-start.11 = (bf16[16,2048]{1,0:T(8,128)(2,1)S(1)}, bf16[16,2048]{1,0:T(8,128)(2,1)S(1)}, u32[]{:S(2)}, u32[]{:S(2)}) collective-permute-start(bf16[16,2048]{1,0:T(8,128)(2,1)S(1)} %get-tuple-element.51), channel_id=1, source_target_pairs={{0,24},{4,28},{8,16},{12,20},{16,8},{20,12},{24,0},{28,4},{1,25},{... | collective-permute-start | bytes 196616 | tf_op jit(solution)/shard_map/ppermute | solution.py:22
  35.1 8.8 %collective-permute-start.12 = (bf16[16,2048]{1,0:T(8,128)(2,1)S(1)}, bf16[16,2048]{1,0:T(8,128)(2,1)S(1)}, u32[]{:S(2)}, u32[]{:S(2)}) collective-permute-start(bf16[16,2048]{1,0:T(8,128)(2,1)S(1)} %get-tuple-element.52), channel_id=1, source_target_pairs={{0,28},{4,24},{8,20},{12,16},{16,12},{20,8},{24,4},{28,0},{1,29},{... | collective-permute-start | bytes 196616 | tf_op jit(solution)/shard_map/ppermute | solution.py:22
  43.9 2.7 %collective-permute-start.14 = (bf16[128,3072]{1,0:T(8,128)(2,1)S(1)}, bf16[128,3072]{1,0:T(8,128)(2,1)S(1)}, u32[]{:S(2)}, u32[]{:S(2)}) collective-permute-start(bf16[128,3072]{1,0:T(8,128)(2,1)S(1)} %get-tuple-element.54), channel_id=1, source_target_pairs={{0,4},{4,0},{8,12},{12,8},{16,20},{20,16},{24,28},{28,24},{1,5},{5... | collective-permute-start | bytes 2359304 | tf_op jit(solution)/shard_map/ppermute | solution.py:22
  44.4 2.1 %collective-permute-start.15 = (bf16[32,2048]{1,0:T(8,128)(2,1)S(1)}, bf16[32,2048]{1,0:T(8,128)(2,1)S(1)}, u32[]{:S(2)}, u32[]{:S(2)}) collective-permute-start(bf16[32,2048]{1,0:T(8,128)(2,1)S(1)} %collective-permute-done.13.ya), channel_id=1, source_target_pairs={{0,4},{4,0},{8,12},{12,8},{16,20},{20,16},{24,28},{28,24},{1,5},{5... | collective-permute-start | bytes 393224 | tf_op jit(solution)/shard_map/ppermute | solution.py:22

commit v5 on v4

--- a/solution.py
+++ b/solution.py
@@ -54,62 +54,70 @@
     return jnp.concatenate(parts, axis=1).astype(BF16)
 
 
-def pick_kernel(levels, heads, dim, offs_ref, core_ref, k_ref, v_ref, q_half, k_half, v_half,
-                both_ref, three_ref, swap_ref):
-    tok = k_ref.shape[0]
+def pack_kernel(core_ref, rows, out):
+    out[...] = rows[...]
+
+
+def pack_call(core, rows):
+    tok, width = rows.shape
+    half = width // 2
+    return pl.pallas_call(
+        pack_kernel,
+        grid_spec=pltpu.PrefetchScalarGridSpec(
+            num_scalar_prefetch=1,
+            grid=(1,),
+            in_specs=[pl.BlockSpec((tok, half), lambda i, c: (0, 1 - c[0]))],
+            out_specs=pl.BlockSpec((tok, half), lambda i, c: (0, 0)),
+        ),
+        out_shape=jax.ShapeDtypeStruct((tok, half), BF16),
+        compiler_params=params(),
+        name="pack_half",
+    )(core, rows)
+
+
+def pick_kernel(levels, per, dim, offs_ref, core_ref, k0, k1, v0, v1, both_ref, three_ref):
+    tok = k0.shape[0]
     n2, n3 = tok // 4, tok // 8
-    for h in range(heads):
-        head = pl.program_id(0) * heads + h
-        pick = pick_matrix(offs_ref, head, 2, levels, tok)
-        cols = slice(h * dim, (h + 1) * dim)
-        kv = jnp.concatenate([k_ref[:, cols], v_ref[:, cols]], axis=1)
-        got = dot(pick, kv).astype(BF16)
+    each = range(per)
+    picks = [pick_matrix(offs_ref, core_ref[0] * per + h, 2, levels, tok) for h in each]
+    cols = [slice(h * dim, (h + 1) * dim) for h in each]
+    own = [dot(picks[h], side(k0[:, cols[h]], v0[:, cols[h]])).astype(BF16) for h in each]
+    oth = [dot(picks[h], side(k1[:, cols[h]], v1[:, cols[h]])).astype(BF16) for h in each]
+    for h in each:
         out = slice(2 * h * dim, 2 * (h + 1) * dim)
-        both_ref[:, out] = got
-        three_ref[:, out] = got[n2 : n2 + n3]
-
-    @pl.when(pl.program_id(0) == 0)
-    def _():
-        half = q_half.shape[1]
-        for i, ref in enumerate((q_half, k_half, v_half)):
-            swap_ref[:, i * half : (i + 1) * half] = ref[...]
-
-
-def pick_call(offsets, core, queries, keys, values, dim):
-    tok, width = keys.shape
+        third = stack(own[h][n2:], oth[h][n2:])
+        both_ref[:, out] = stack(own[h][:n2], oth[h][:n2], third)
+        three_ref[:, out] = third
+
+
+def pick_call(offsets, core, raw, dim):
+    tok, width = raw[0].shape
     levels, heads = offsets.shape
-    steps = 2
-    per = heads // steps
-    block = pl.BlockSpec((tok, per * dim), lambda i, o, c: (0, i))
-    half = pl.BlockSpec((tok, width // 2), lambda i, o, c: (0, 1 - c[0]))
+    per = heads // 2
+    spec = own_spec(tok, per * dim, 1)
+
+    def out(rows):
+        return pl.BlockSpec((rows, 2 * per * dim), lambda i, o, c: (0, 0))
+
     return pl.pallas_call(
         functools.partial(pick_kernel, levels, per, dim),
         grid_spec=pltpu.PrefetchScalarGridSpec(
             num_scalar_prefetch=2,
-            grid=(steps,),
-            in_specs=[block, block, half, half, half],
-            out_specs=[
-                pl.BlockSpec((tok // 4 + tok // 8, 2 * per * dim), lambda i, o, c: (0, i)),
-                pl.BlockSpec((tok // 8, 2 * per * dim), lambda i, o, c: (0, i)),
-                pl.BlockSpec((tok, 3 * width // 2), lambda i, o, c: (0, 0)),
-            ],
+            grid=(1,),
+            in_specs=[spec] * 4,
+            out_specs=[out(tok // 2 + tok // 4), out(tok // 4)],
         ),
         out_shape=[
-            jax.ShapeDtypeStruct((tok // 4 + tok // 8, 2 * width), BF16),
-            jax.ShapeDtypeStruct((tok // 8, 2 * width), BF16),
-            jax.ShapeDtypeStruct((tok, 3 * width // 2), BF16),
+            jax.ShapeDtypeStruct((tok // 2 + tok // 4, width), BF16),
+            jax.ShapeDtypeStruct((tok // 4, width), BF16),
         ],
         compiler_params=params(),
         name="pick_rows",
-    )(offsets, core, keys, values, queries, keys, values)
+    )(offsets, core, *raw)
 
 
 def own_spec(tok, cols, steps):
     return pl.BlockSpec((tok, cols), lambda i, o, c: (0, c[0] * steps + i))
-
-
-def swap_spec(tok, cols, steps, part):
-    return pl.BlockSpec((tok, cols), lambda i, o, c: (0, part * steps + i))
 
 
 def side(*values):
@@ -150,10 +158,10 @@
         cols = slice(h * dim, (h + 1) * dim)
         wide = slice(2 * h * dim, 2 * (h + 1) * dim)
         lanes = slice(2 * h * tok, 2 * (h + 1) * tok)
-        own = dot(pick, side(k0[:, cols], v0[:, cols])).astype(BF16)
-        oth = dot(pick, side(k1[:, cols], v1[:, cols])).astype(BF16)
-        ones = stack(own[:n1], oth[:n1])
-        near[:, wide] = stack(ones, own[n1:], oth[n1:])
+        own = dot(pick[:n1], side(k0[:, cols], v0[:, cols])).astype(BF16)
+        oth = dot(pick[:n1], side(k1[:, cols], v1[:, cols])).astype(BF16)
+        ones = stack(own, oth)
+        near[:, wide] = ones
         que0, que1 = q0[:, cols], q1[:, cols]
         far_pick = pick[n1:]
         selq[:, cols] = stack(dot(far_pick, que0), dot(far_pick, que1)).astype(BF16)
@@ -174,7 +182,6 @@
     per = 8
     steps = half // per
     raw_spec = own_spec(tok, per * dim, steps)
-    swapped = [swap_spec(tok, per * dim, steps, i) for i in range(3)]
     sel = 2 * (tok // 4 + tok // 8)
 
     def out(rows, lanes, kind=BF16):
@@ -183,13 +190,13 @@
             jax.ShapeDtypeStruct((rows, half * lanes), kind),
         )
 
-    outs = [out(2 * tok, 2 * tok), out(8, 2 * tok, F32), out(tok + sel, 2 * dim), out(sel, dim)]
+    outs = [out(2 * tok, 2 * tok), out(8, 2 * tok, F32), out(tok, 2 * dim), out(sel, dim)]
     return pl.pallas_call(
         functools.partial(pre_kernel, levels, per, dim),
         grid_spec=pltpu.PrefetchScalarGridSpec(
             num_scalar_prefetch=2,
             grid=(steps,),
-            in_specs=[raw_spec, swapped[0], raw_spec, swapped[1], raw_spec, swapped[2]],
+            in_specs=[raw_spec] * 6,
             out_specs=[o[0] for o in outs],
         ),
         out_shape=[o[1] for o in outs],
@@ -200,7 +207,7 @@
 
 def far_kernel(
     levels, per, dim, offs_ref, core_ref, exps, stats, near, selq, v0, v1, g0, g1,
-    x, xx, y3, yy3, d3, dd3,
+    own, x, y, d,
     xa, xb, yab, da, db, ngrad, dqt, stats2,
 ):
     tok = g0.shape[0]
@@ -220,11 +227,9 @@
     lanes = [slice(2 * h * tok, 2 * (h + 1) * tok) for h in each]
 
     def rows(c):
-        a, b = near[tok : tok + sel, c], near[tok + sel :, c]
-        return stack(
-            a[:n2], b[:n2], x[:n2, c], xx[:n2, c], a[n2:], b[n2:], x[n2:, c], xx[n2:, c],
-            *(ref[:, c] for ref in (y3, yy3, d3, dd3)),
-        )
+        lo = 2 * n2
+        parts = own[:lo, c], x[:lo, c], own[lo:, c], x[lo:, c], y[:, c], d[:, c]
+        return stack(*parts)
 
     def level_pick(value):
         return jnp.where(is2, value[:tok], value[tok:])
@@ -305,7 +310,7 @@
         dqt[:, h * dim : h * dim + 2 * sel] = dot(keys[h].T, dsm[h]).astype(BF16)
 
 
-def far_call(offsets, core, pre, raw, far, dim):
+def far_call(offsets, core, pre, raw, grads, far, dim):
     tok, width = raw[0].shape
     levels, heads = offsets.shape
     half = heads // 2
@@ -313,13 +318,9 @@
     steps = half // per
     n2, n3 = tok // 4, tok // 8
     raw_spec = own_spec(tok, per * dim, steps)
-    swapped = [swap_spec(tok, per * dim, steps, i) for i in range(3)]
-
-    def near_spec(a):
+
+    def mid_spec(a):
         return pl.BlockSpec((a.shape[0], a.shape[1] // steps), lambda i, o, c: (0, i))
-
-    def far_spec(a):
-        return pl.BlockSpec((a.shape[0], 2 * per * dim), lambda i, o, c: (0, c[0] * steps + i))
 
     def out(rows, lanes, kind=BF16):
         return (
@@ -334,14 +335,14 @@
         grid_spec=pltpu.PrefetchScalarGridSpec(
             num_scalar_prefetch=2,
             grid=(steps,),
-            in_specs=[near_spec(a) for a in pre] + [raw_spec, swapped[2], raw_spec, raw_spec]
-            + [far_spec(a) for a in far],
+            in_specs=[mid_spec(a) for a in pre] + [raw_spec] * 2
+            + [raw_spec] + [mid_spec(a) for a in grads[1:] + far],
             out_specs=[o[0] for o in outs],
         ),
         out_shape=[o[1] for o in outs],
         compiler_params=params(),
         name="far_levels",
-    )(offsets, core, *pre, *raw, *far)
+    )(offsets, core, *pre, *raw, *grads, *far)
 
 
 def near_kernel(
@@ -386,14 +387,13 @@
             ref[:, lo + dim : lo + 3 * dim] = kv.astype(BF16)
 
 
-def near_call(offsets, core, mid, raw, dim):
+def near_call(offsets, core, mid, raw, grads, dim):
     tok, width = raw[0].shape
     levels, heads = offsets.shape
     half = heads // 2
     per = 8
     steps = half // per
     raw_spec = own_spec(tok, per * dim, steps)
-    swapped = [swap_spec(tok, per * dim, steps, i) for i in range(3)]
 
     def mid_spec(a):
         return pl.BlockSpec((a.shape[0], a.shape[1] // steps), lambda i, o, c: (0, i))
@@ -404,14 +404,13 @@
         grid_spec=pltpu.PrefetchScalarGridSpec(
             num_scalar_prefetch=2,
             grid=(steps,),
-            in_specs=[mid_spec(a) for a in mid]
-            + [raw_spec, swapped[0], raw_spec, swapped[1], raw_spec, swapped[2], raw_spec, raw_spec],
+            in_specs=[mid_spec(a) for a in mid] + [raw_spec] * 7 + [mid_spec(grads[1])],
             out_specs=[out_spec] * 2,
         ),
         out_shape=[jax.ShapeDtypeStruct((tok, 3 * half * dim), BF16)] * 2,
         compiler_params=params(),
         name="near_levels",
-    )(offsets, core, *mid, *raw)
+    )(offsets, core, *mid, *raw, *grads)
 
 
 def final_kernel(
@@ -488,30 +487,29 @@
 def per_device(queries, keys_in, values, out_grads, offsets):
     heads = offsets.shape[1]
     dim = queries.shape[2] // heads
+    core = lax.rem(lax.axis_index("seq"), 2).astype(jnp.int32).reshape(1)
+    q, k, v = (
+        pltpu.with_memory_space_constraint(a[0], pltpu.HBM) for a in (queries, keys_in, values)
+    )
     sections = lax.axis_size("section")
-    core = lax.rem(lax.axis_index("seq"), 2).astype(jnp.int32).reshape(1)
     grads = lax.ppermute(
         out_grads[0], "section", [(i, (i - 1) % sections) for i in range(sections)]
     )
-    q, k, v = (pltpu.with_memory_space_constraint(a[0], pltpu.HBM) for a in (queries, keys_in, values))
-    both, three, swap = pick_call(offsets, core, q, k, v, dim)
-    swap = exchange(swap, 1)
+    q_oth, k_oth, v_oth = exchange(q, 1), exchange(k, 1), exchange(v, 1)
+    both, three = pick_call(offsets, core, [k, k_oth, v, v_oth], dim)
     x, y, d = exchange(both, 2), exchange(three, 4), exchange(three, 6)
-    pre = pre_call(offsets, core, [q, swap, k, swap, v, swap], dim)
-    x, y, d, grads = lax.optimization_barrier((x, y, d, grads, pre[1]))[:4]
-    far = []
-    for piece in (x, y, d):
-        far += [piece, exchange(piece, 1)]
-    g_oth = exchange(grads, 1)
+    raw = [q, q_oth, k, k_oth, v, v_oth]
+    pre = pre_call(offsets, core, raw, dim)
+    y, d, grads = lax.optimization_barrier((y, d, grads, pre[1]))[:3]
+    grads = [grads, exchange(pack_call(core, grads), 1)]
     xa, xb, yab, da, db, ngrad, dqt, stats2 = far_call(
-        offsets, core, pre, [v, swap, grads, g_oth], far, dim
+        offsets, core, pre, [v, v_oth], grads, [both, x, y, d], dim
     )
     xa, xb, da, db = exchange(xa, 2), exchange(xb, 3), exchange(da, 6), exchange(db, 7)
     y = exchange(yab, 4)
     yy = exchange(y, 1)
     mine, other = near_call(
-        offsets, core, [pre[0], stats2, pre[2], ngrad, dqt],
-        [q, swap, k, swap, v, swap, grads, g_oth], dim,
+        offsets, core, [pre[0], stats2, pre[2], ngrad, dqt], raw, grads, dim
     )
     other, xa, xb, da, db, y = lax.optimization_barrier((other, xa, xb, da, db, y))
     parts = [mine, exchange(other, 1), xa, xb, y, yy, da, db]

time: 49.1 us -> 45.3 us (0.923)
  waiting for transfers between devices: 14.3 us -> 11.3 us
  starting transfers between devices: 15.1 us -> 14.6 us
    ppermute x15 -> x14, waiting for transfers between devices: 14.3 us -> 9.76 us  [exchange(): return lax.ppermute(value, 'seq', [(i, i ^ bits) for i in range(count)])]
    ppermute x1, waiting for transfers between devices: 0.01 us -> 1.54 us  [per_device(): lax.ppermute(out_grads[0], 'section', [(i, (i - 1) % sections) for i in r...]
    ppermute x15 -> x14, starting transfers between devices: 10.4 us -> 9.94 us  [exchange(): return lax.ppermute(value, 'seq', [(i, i ^ bits) for i in range(count)])]
  transfers between devices with their start and end apart: 16 -> 15, of which waited for: 5 -> 5; matrix products, arithmetic and copies ran while one was open for 0% -> 0% of each run, Pallas kernels for 18% -> 24%
where the time goes in v5:
time: 45.3 us; the launch traced here: 45.1 us
  Pallas kernels  16.8 us (37%)
  starting transfers between devices  14.6 us (32%)
  waiting for transfers between devices  11.3 us (25%)
  local copies, waits for them, and re-layouts  1.75 us (4%)
  between operations  0.69 us (2%)
    ppermute x14, starting transfers between devices, exchange(): return lax.ppermute(value, 'seq', [(i, i ^ bits) for i in range(count)])  9.94 us
    ppermute x14, waiting for transfers between devices, exchange(): return lax.ppermute(value, 'seq', [(i, i ^ bits) for i in range(count)])  9.76 us
    pallas_call x1, Pallas kernels, near_call(): pl.pallas_call(functools.partial(near_kernel, levels, per, dim), grid_spe...  5.73 us
    ppermute x1, starting transfers between devices, per_device(): lax.ppermute(out_grads[0], 'section', [(i, (i - 1) % sections) for i in r...  4.68 us
    pallas_call x1, Pallas kernels, far_call(): pl.pallas_call(functools.partial(far_kernel, levels, per, dim), grid_spec...  3.5 us
    pallas_call x1, Pallas kernels, pre_call(): pl.pallas_call(functools.partial(pre_kernel, levels, per, dim), grid_spec...  3.2 us
    pallas_call x1, Pallas kernels, final_call(): pl.pallas_call(functools.partial(final_kernel, levels, per, dim), grid_sp...  2.31 us
    pallas_call x1, Pallas kernels, pick_call(): pl.pallas_call(functools.partial(pick_kernel, levels, per, dim), grid_spe...  2.03 us
  transfers between devices with their start and end apart: 15, of which 5 were waited for; matrix products, arithmetic and copies ran while one was open for 0% of the time, Pallas kernels for 24%

profile of v5, /device:TPU:0, one launch (start us, length us, event | category | flops | bytes accessed | tf_op | source)
XLA Modules:
  0.0 45.1 jit_solution(10610213975663811657)
XLA Ops:
  0.6 0.5 %collective-permute-start.1 = (bf16[128,2048]{1,0:T(8,128)(2,1)}, bf16[128,2048]{1,0:T(8,128)(2,1)S(1)}, u32[]{:S(2)}, u32[]{:S(2)}) collective-permute-start(bf16[128,2048]{1,0:T(8,128)(2,1)} %bitcast.13), channel_id=1, source_target_pairs={{0,4},{4,0},{8,12},{12,8},{16,20},{20,16},{24,28},{28,24},{1,5},{5... | collective-permute-start | bytes 1572872 | tf_op jit(solution)/shard_map/ppermute | solution.py:22
  1.1 0.1 collective-permute-start.2
  1.2 0.4 collective-permute-start
  1.7 4.7 %collective-permute-start.5 = (bf16[128,2048]{1,0:T(8,128)(2,1)}, bf16[128,2048]{1,0:T(8,128)(2,1)S(1)}, u32[]{:S(2)}, u32[]{:S(2)}) collective-permute-start(bf16[128,2048]{1,0:T(8,128)(2,1)} %bitcast.20), channel_id=1, source_target_pairs={{0,3},{1,0},{2,1},{3,2},{4,7},{5,4},{6,5},{7,6},{8,11},{9,8},{10,9... | collective-permute-start | bytes 1572872 | tf_op jit(solution)/shard_map/ppermute | solution.py:495
  6.3 0.0 copy-start
  6.3 0.0 collective-permute-done.1.k1
  6.3 0.0 copy-start.2
  6.3 0.0 collective-permute-done.2.v1
  6.3 0.0 copy-start.1
  6.4 0.8 %copy-done.2 = bf16[128,2048]{1,0:T(8,128)(2,1)} copy-done((bf16[128,2048]{1,0:T(8,128)(2,1)}, bf16[128,2048]{1,0:T(8,128)(2,1)S(1)}, u32[]{:S(2)}) %copy-start.2) | copy-done | bytes 524312
  7.1 0.2 copy-done.1
  7.3 0.0 copy-done
  7.3 2.0 %pick_rows.1 = (bf16[96,2048]{1,0:T(8,128)(2,1)S(1)}, bf16[32,2048]{1,0:T(8,128)(2,1)S(1)}) custom-call(s32[3,16]{1,0:T(4,128)S(1)} %copy-done, s32[1]{0:T(128)} %bitcast.core_ref, bf16[128,2048]{1,0:T(8,128)(2,1)} %bitcast.14, bf16[128,2048]{1,0:T(8,128)(2,1)} %copy-done.2, bf16[128,2048]{1,0:T(8,128)(2,1)} %bitcast.9, bf16[128,2048]{1,0:T(8,128)(2,1)} %copy-done.1), custom_call_target="tpu_custom_call" | custom-call | tf_op jit(solution)/shard_map/pick_rows/pallas_call | solution.py:102
  9.3 2.5 %collective-permute-start.4 = (bf16[32,2048]{1,0:T(8,128)(2,1)S(1)}, bf16[32,2048]{1,0:T(8,128)(2,1)S(1)}, u32[]{:S(2)}, u32[]{:S(2)}) collective-permute-start(bf16[32,2048]{1,0:T(8,128)(2,1)S(1)} %get-tuple-element.35), channel_id=1, source_target_pairs={{0,24},{4,28},{8,16},{12,20},{16,8},{20,12},{24,0},{28,4},{1,25},{... | collective-permute-start | bytes 393224 | tf_op jit(solution)/shard_map/ppermute | solution.py:22
  11.9 0.5 %collective-permute-start.3 = (bf16[32,2048]{1,0:T(8,128)(2,1)S(1)}, bf16[32,2048]{1,0:T(8,128)(2,1)S(1)}, u32[]{:S(2)}, u32[]{:S(2)}) collective-permute-start(bf16[32,2048]{1,0:T(8,128)(2,1)S(1)} %get-tuple-element.35), channel_id=1, source_target_pairs={{0,16},{4,20},{8,24},{12,28},{16,0},{20,4},{24,8},{28,12},{1,17},{... | collective-permute-start | bytes 393224 | tf_op jit(solution)/shard_map/ppermute | solution.py:22
  12.4 0.5 %collective-permute-start.7 = (bf16[96,2048]{1,0:T(8,128)(2,1)S(1)}, bf16[96,2048]{1,0:T(8,128)(2,1)S(1)}, u32[]{:S(2)}, u32[]{:S(2)}) collective-permute-start(bf16[96,2048]{1,0:T(8,128)(2,1)S(1)} %get-tuple-element.37.own), channel_id=1, source_target_pairs={{0,8},{4,12},{8,0},{12,4},{16,24},{20,28},{24,16},{28,20},{1,9},{5... | collective-permute-start | bytes 1179656 | tf_op jit(solution)/shard_map/ppermute | solution.py:22
  12.9 0.0 collective-permute-done.q1
  12.9 0.0 copy-start.3
  12.9 0.8 %copy-done.3 = bf16[128,2048]{1,0:T(8,128)(2,1)} copy-done((bf16[128,2048]{1,0:T(8,128)(2,1)}, bf16[128,2048]{1,0:T(8,128)(2,1)S(1)}, u32[]{:S(2)}) %copy-start.3) | copy-done | bytes 524312
  13.7 3.2 %local_scores.1 = (bf16[256,2048]{1,0:T(8,128)(2,1)S(1)}, f32[8,2048]{1,0:T(8,128)S(1)}, bf16[128,2048]{1,0:T(8,128)(2,1)S(1)}, bf16[96,1024]{1,0:T(8,128)(2,1)S(1)}) custom-call(s32[3,16]{1,0:T(4,128)S(1)} %copy-done, s32[1]{0:T(128)} %bitcast.core_ref, bf16[128,2048]{1,0:T(8,128)(2,1)} %bitcast.18, bf16[128,2048]{1,0:T(8,128)(2,1)} %copy-done.3, ...), custom_call_target="tpu_custom_call" | custom-call | tf_op jit(solution)/shard_map/local_scores/pallas_call | solution.py:194
  16.9 1.5 %collective-permute-done.5.rows.g0 = bf16[128,2048]{1,0:T(8,128)(2,1)S(1)} collective-permute-done((bf16[128,2048]{1,0:T(8,128)(2,1)}, bf16[128,2048]{1,0:T(8,128)(2,1)S(1)}, u32[]{:S(2)}, u32[]{:S(2)}) %collective-permute-start.5) | collective-permute-done | bytes 524320 | tf_op jit(solution)/shard_map/ppermute | solution.py:495
  18.4 0.0 collective-permute-done.4.d
  18.4 0.2 collective-permute-done.3.y
  18.7 0.1 collective-permute-start.6
  18.8 5.6 %collective-permute-done.7.x = bf16[96,2048]{1,0:T(8,128)(2,1)S(1)} collective-permute-done((bf16[96,2048]{1,0:T(8,128)(2,1)S(1)}, bf16[96,2048]{1,0:T(8,128)(2,1)S(1)}, u32[]{:S(2)}, u32[]{:S(2)}) %collective-permute-start.7) | collective-permute-done | bytes 393248 | tf_op jit(solution)/shard_map/ppermute | solution.py:22
  24.4 0.0 collective-permute-done.6.g1
  24.4 3.5 %far_levels.1 = (bf16[48,2048]{1,0:T(8,128)(2,1)S(1)}, bf16[48,2048]{1,0:T(8,128)(2,1)S(1)}, bf16[32,2048]{1,0:T(8,128)(2,1)S(1)}, bf16[16,2048]{1,0:T(8,128)(2,...) custom-call(s32[3,16]{1,0:T(4,128)S(1)} %copy-done, ...), custom_call_target="tpu_custom_call" | custom-call | tf_op jit(solution)/shard_map/far_levels/pallas_call | solution.py:333
  27.9 1.6 %collective-permute-start.8 = (bf16[48,2048]{1,0:T(8,128)(2,1)S(1)}, bf16[48,2048]{1,0:T(8,128)(2,1)S(1)}, u32[]{:S(2)}, u32[]{:S(2)}) collective-permute-start(bf16[48,2048]{1,0:T(8,128)(2,1)S(1)} %get-tuple-element.45), channel_id=1, source_target_pairs={{0,8},{4,12},{8,0},{12,4},{16,24},{20,28},{24,16},{28,20},{1,9},{5... | collective-permute-start | bytes 589832 | tf_op jit(solution)/shard_map/ppermute | solution.py:22
  29.5 0.0 collective-permute-start.9
  29.5 0.5 %collective-permute-start.12 = (bf16[32,2048]{1,0:T(8,128)(2,1)S(1)}, bf16[32,2048]{1,0:T(8,128)(2,1)S(1)}, u32[]{:S(2)}, u32[]{:S(2)}) collective-permute-start(bf16[32,2048]{1,0:T(8,128)(2,1)S(1)} %get-tuple-element.49), channel_id=1, source_target_pairs={{0,16},{4,20},{8,24},{12,28},{16,0},{20,4},{24,8},{28,12},{1,17},{... | collective-permute-start | bytes 393224 | tf_op jit(solution)/shard_map/ppermute | solution.py:22
  30.0 1.7 %collective-permute-start.10 = (bf16[16,2048]{1,0:T(8,128)(2,1)S(1)}, bf16[16,2048]{1,0:T(8,128)(2,1)S(1)}, u32[]{:S(2)}, u32[]{:S(2)}) collective-permute-start(bf16[16,2048]{1,0:T(8,128)(2,1)S(1)} %get-tuple-element.47), channel_id=1, source_target_pairs={{0,24},{4,28},{8,16},{12,20},{16,8},{20,12},{24,0},{28,4},{1,25},{... | collective-permute-start | bytes 196616 | tf_op jit(solution)/shard_map/ppermute | solution.py:22
  31.6 0.9 %collective-permute-start.11 = (bf16[16,2048]{1,0:T(8,128)(2,1)S(1)}, bf16[16,2048]{1,0:T(8,128)(2,1)S(1)}, u32[]{:S(2)}, u32[]{:S(2)}) collective-permute-start(bf16[16,2048]{1,0:T(8,128)(2,1)S(1)} %get-tuple-element.48), channel_id=1, source_target_pairs={{0,28},{4,24},{8,20},{12,16},{16,12},{20,8},{24,4},{28,0},{1,29},{... | collective-permute-start | bytes 196616 | tf_op jit(solution)/shard_map/ppermute | solution.py:22
  32.6 5.7 %near_levels.1 = (bf16[128,3072]{1,0:T(8,128)(2,1)S(1)}, bf16[128,3072]{1,0:T(8,128)(2,1)S(1)}) custom-call(s32[3,16]{1,0:T(4,128)S(1)} %copy-done, s32[1]{0:T(128)} %bitcast.core_ref, bf16[256,2048]{1,0:T(8,128)(2,1)S(1)} %get-tuple-element.31.exps, f32[8,2048]{1,0:T(8,128)S(1)} %get-tuple-element.40.stats2, bf16[128,2048]{1,0:T(8,128)(2,1)S(1)} %get-tuple-element.33.near, ...), custom_call_target="tpu_custom_call" | custom-call | tf_op jit(solution)/shard_map/near_levels/pallas_call | solution.py:402
  38.3 1.8 %collective-permute-done.10.da = bf16[16,2048]{1,0:T(8,128)(2,1)S(1)} collective-permute-done((bf16[16,2048]{1,0:T(8,128)(2,1)S(1)}, bf16[16,2048]{1,0:T(8,128)(2,1)S(1)}, u32[]{:S(2)}, u32[]{:S(2)}) %collective-permute-start.10) | collective-permute-done | bytes 65568 | tf_op jit(solution)/shard_map/ppermute | solution.py:22
  40.1 0.0 collective-permute-done.11.db
  40.2 0.0 collective-permute-done.12.ya
  40.2 0.0 collective-permute-done.8.xa
  40.2 0.0 collective-permute-done.9.xb
  40.2 0.5 %collective-permute-start.13 = (bf16[128,3072]{1,0:T(8,128)(2,1)S(1)}, bf16[128,3072]{1,0:T(8,128)(2,1)S(1)}, u32[]{:S(2)}, u32[]{:S(2)}) collective-permute-start(bf16[128,3072]{1,0:T(8,128)(2,1)S(1)} %get-tuple-element.50), channel_id=1, source_target_pairs={{0,4},{4,0},{8,12},{12,8},{16,20},{20,16},{24,28},{28,24},{1,5},{5... | collective-permute-start | bytes 2359304 | tf_op jit(solution)/shard_map/ppermute | solution.py:22
  40.7 0.1 collective-permute-start.14
  40.8 2.0 %collective-permute-done.14.yb = bf16[32,2048]{1,0:T(8,128)(2,1)S(1)} collective-permute-done((bf16[32,2048]{1,0:T(8,128)(2,1)S(1)}, bf16[32,2048]{1,0:T(8,128)(2,1)S(1)}, u32[]{:S(2)}, u32[]{:S(2)}) %collective-permute-start.14) | collective-permute-done | bytes 131104 | tf_op jit(solution)/shard_map/ppermute | solution.py:22
  42.8 0.0 collective-permute-done.13.bb
  42.8 2.3 %add_pieces.1 = (bf16[128,2048]{1,0:T(8,128)(2,1)}, bf16[128,2048]{1,0:T(8,128)(2,1)}, bf16[128,2048]{1,0:T(8,128)(2,1)}) custom-call(s32[3,16]{1,0:T(4,128)S(1)} %copy-done, s32[1]{0:T(128)} %bitcast.core_ref, bf16[128,3072]{1,0:T(8,128)(2,1)S(1)} %get-tuple-element.43.ba, bf16[128,3072]{1,0:T(8,128)(2,1)S(1)} %collective-permute-done.13.bb, ...), custom_call_target="tpu_custom_call" | custom-call | tf_op jit(solution)/shard_map/add_pieces/pallas_call | solution.py:473
  (1 shorter events, 0.0 us)
Async XLA Ops:
  0.6 5.7 %collective-permute-start.1 = (bf16[128,2048]{1,0:T(8,128)(2,1)}, bf16[128,2048]{1,0:T(8,128)(2,1)S(1)}, u32[]{:S(2)}, u32[]{:S(2)}) collective-permute-start(bf16[128,2048]{1,0:T(8,128)(2,1)} %bitcast.13), channel_id=1, source_target_pairs={{0,4},{4,0},{8,12},{12,8},{16,20},{20,16},{24,28},{28,24},{1,5},{5... | collective-permute-start | bytes 1572872 | tf_op jit(solution)/shard_map/ppermute | solution.py:22
  1.1 5.2 %collective-permute-start.2 = (bf16[128,2048]{1,0:T(8,128)(2,1)}, bf16[128,2048]{1,0:T(8,128)(2,1)S(1)}, u32[]{:S(2)}, u32[]{:S(2)}) collective-permute-start(bf16[128,2048]{1,0:T(8,128)(2,1)} %bitcast.8), channel_id=1, source_target_pairs={{0,4},{4,0},{8,12},{12,8},{16,20},{20,16},{24,28},{28,24},{1,5},{5... | collective-permute-start | bytes 1572872 | tf_op jit(solution)/shard_map/ppermute | solution.py:22
  1.2 11.7 %collective-permute-start = (bf16[128,2048]{1,0:T(8,128)(2,1)}, bf16[128,2048]{1,0:T(8,128)(2,1)S(1)}, u32[]{:S(2)}, u32[]{:S(2)}) collective-permute-start(bf16[128,2048]{1,0:T(8,128)(2,1)} %bitcast.17), channel_id=1, source_target_pairs={{0,4},{4,0},{8,12},{12,8},{16,20},{20,16},{24,28},{28,24},{1,5},{5... | collective-permute-start | bytes 1572872 | tf_op jit(solution)/shard_map/ppermute | solution.py:22
  1.7 16.8 %collective-permute-start.5 = (bf16[128,2048]{1,0:T(8,128)(2,1)}, bf16[128,2048]{1,0:T(8,128)(2,1)S(1)}, u32[]{:S(2)}, u32[]{:S(2)}) collective-permute-start(bf16[128,2048]{1,0:T(8,128)(2,1)} %bitcast.20), channel_id=1, source_target_pairs={{0,3},{1,0},{2,1},{3,2},{4,7},{5,4},{6,5},{7,6},{8,11},{9,8},{10,9... | collective-permute-start | bytes 1572872 | tf_op jit(solution)/shard_map/ppermute | solution.py:495
  6.3 1.0 %copy-start = (s32[3,16]{1,0:T(4,128)S(1)}, s32[3,16]{1,0:T(4,128)}, u32[]{:S(2)}) copy-start(s32[3,16]{1,0:T(4,128)} %offs_ref.9) | copy-start | bytes 580
  6.3 0.8 %copy-start.2 = (bf16[128,2048]{1,0:T(8,128)(2,1)}, bf16[128,2048]{1,0:T(8,128)(2,1)S(1)}, u32[]{:S(2)}) copy-start(bf16[128,2048]{1,0:T(8,128)(2,1)S(1)} %collective-permute-done.1.k1) | copy-start | bytes 1572868
  6.3 1.0 %copy-start.1 = (bf16[128,2048]{1,0:T(8,128)(2,1)}, bf16[128,2048]{1,0:T(8,128)(2,1)S(1)}, u32[]{:S(2)}) copy-start(bf16[128,2048]{1,0:T(8,128)(2,1)S(1)} %collective-permute-done.2.v1) | copy-start | bytes 1572868
  9.3 9.1 %collective-permute-start.4 = (bf16[32,2048]{1,0:T(8,128)(2,1)S(1)}, bf16[32,2048]{1,0:T(8,128)(2,1)S(1)}, u32[]{:S(2)}, u32[]{:S(2)}) collective-permute-start(bf16[32,2048]{1,0:T(8,128)(2,1)S(1)} %get-tuple-element.35), channel_id=1, source_target_pairs={{0,24},{4,28},{8,16},{12,20},{16,8},{20,12},{24,0},{28,4},{1,25},{... | collective-permute-start | bytes 393224 | tf_op jit(solution)/shard_map/ppermute | solution.py:22
  11.9 6.8 %collective-permute-start.3 = (bf16[32,2048]{1,0:T(8,128)(2,1)S(1)}, bf16[32,2048]{1,0:T(8,128)(2,1)S(1)}, u32[]{:S(2)}, u32[]{:S(2)}) collective-permute-start(bf16[32,2048]{1,0:T(8,128)(2,1)S(1)} %get-tuple-element.35), channel_id=1, source_target_pairs={{0,16},{4,20},{8,24},{12,28},{16,0},{20,4},{24,8},{28,12},{1,17},{... | collective-permute-start | bytes 393224 | tf_op jit(solution)/shard_map/ppermute | solution.py:22
  12.4 12.0 %collective-permute-start.7 = (bf16[96,2048]{1,0:T(8,128)(2,1)S(1)}, bf16[96,2048]{1,0:T(8,128)(2,1)S(1)}, u32[]{:S(2)}, u32[]{:S(2)}) collective-permute-start(bf16[96,2048]{1,0:T(8,128)(2,1)S(1)} %get-tuple-element.37.own), channel_id=1, source_target_pairs={{0,8},{4,12},{8,0},{12,4},{16,24},{20,28},{24,16},{28,20},{1,9},{5... | collective-permute-start | bytes 1179656 | tf_op jit(solution)/shard_map/ppermute | solution.py:22
  12.9 0.8 %copy-start.3 = (bf16[128,2048]{1,0:T(8,128)(2,1)}, bf16[128,2048]{1,0:T(8,128)(2,1)S(1)}, u32[]{:S(2)}) copy-start(bf16[128,2048]{1,0:T(8,128)(2,1)S(1)} %collective-permute-done.q1) | copy-start | bytes 1572868
  18.7 5.7 %collective-permute-start.6 = (bf16[128,1024]{1,0:T(8,128)(2,1)S(1)}, bf16[128,1024]{1,0:T(8,128)(2,1)S(1)}, u32[]{:S(2)}, u32[]{:S(2)}) collective-permute-start(bf16[128,1024]{1,0:T(8,128)(2,1)S(1)} %pack_half.1), channel_id=1, source_target_pairs={{0,4},{4,0},{8,12},{12,8},{16,20},{20,16},{24,28},{28,24},{1,5},{5... | collective-permute-start | bytes 786440 | tf_op jit(solution)/shard_map/ppermute | solution.py:22
  27.9 12.3 %collective-permute-start.8 = (bf16[48,2048]{1,0:T(8,128)(2,1)S(1)}, bf16[48,2048]{1,0:T(8,128)(2,1)S(1)}, u32[]{:S(2)}, u32[]{:S(2)}) collective-permute-start(bf16[48,2048]{1,0:T(8,128)(2,1)S(1)} %get-tuple-element.45), channel_id=1, source_target_pairs={{0,8},{4,12},{8,0},{12,4},{16,24},{20,28},{24,16},{28,20},{1,9},{5... | collective-permute-start | bytes 589832 | tf_op jit(solution)/shard_map/ppermute | solution.py:22
  29.5 10.7 %collective-permute-start.9 = (bf16[48,2048]{1,0:T(8,128)(2,1)S(1)}, bf16[48,2048]{1,0:T(8,128)(2,1)S(1)}, u32[]{:S(2)}, u32[]{:S(2)}) collective-permute-start(bf16[48,2048]{1,0:T(8,128)(2,1)S(1)} %get-tuple-element.46), channel_id=1, source_target_pairs={{0,12},{4,8},{8,4},{12,0},{16,28},{20,24},{24,20},{28,16},{1,13},{... | collective-permute-start | bytes 589832 | tf_op jit(solution)/shard_map/ppermute | solution.py:22
  29.5 10.7 %collective-permute-start.12 = (bf16[32,2048]{1,0:T(8,128)(2,1)S(1)}, bf16[32,2048]{1,0:T(8,128)(2,1)S(1)}, u32[]{:S(2)}, u32[]{:S(2)}) collective-permute-start(bf16[32,2048]{1,0:T(8,128)(2,1)S(1)} %get-tuple-element.49), channel_id=1, source_target_pairs={{0,16},{4,20},{8,24},{12,28},{16,0},{20,4},{24,8},{28,12},{1,17},{... | collective-permute-start | bytes 393224 | tf_op jit(solution)/shard_map/ppermute | solution.py:22
  30.0 10.2 %collective-permute-start.10 = (bf16[16,2048]{1,0:T(8,128)(2,1)S(1)}, bf16[16,2048]{1,0:T(8,128)(2,1)S(1)}, u32[]{:S(2)}, u32[]{:S(2)}) collective-permute-start(bf16[16,2048]{1,0:T(8,128)(2,1)S(1)} %get-tuple-element.47), channel_id=1, source_target_pairs={{0,24},{4,28},{8,16},{12,20},{16,8},{20,12},{24,0},{28,4},{1,25},{... | collective-permute-start | bytes 196616 | tf_op jit(solution)/shard_map/ppermute | solution.py:22
  31.6 8.5 %collective-permute-start.11 = (bf16[16,2048]{1,0:T(8,128)(2,1)S(1)}, bf16[16,2048]{1,0:T(8,128)(2,1)S(1)}, u32[]{:S(2)}, u32[]{:S(2)}) collective-permute-start(bf16[16,2048]{1,0:T(8,128)(2,1)S(1)} %get-tuple-element.48), channel_id=1, source_target_pairs={{0,28},{4,24},{8,20},{12,16},{16,12},{20,8},{24,4},{28,0},{1,29},{... | collective-permute-start | bytes 196616 | tf_op jit(solution)/shard_map/ppermute | solution.py:22
  40.2 2.6 %collective-permute-start.13 = (bf16[128,3072]{1,0:T(8,128)(2,1)S(1)}, bf16[128,3072]{1,0:T(8,128)(2,1)S(1)}, u32[]{:S(2)}, u32[]{:S(2)}) collective-permute-start(bf16[128,3072]{1,0:T(8,128)(2,1)S(1)} %get-tuple-element.50), channel_id=1, source_target_pairs={{0,4},{4,0},{8,12},{12,8},{16,20},{20,16},{24,28},{28,24},{1,5},{5... | collective-permute-start | bytes 2359304 | tf_op jit(solution)/shard_map/ppermute | solution.py:22
  40.7 2.1 %collective-permute-start.14 = (bf16[32,2048]{1,0:T(8,128)(2,1)S(1)}, bf16[32,2048]{1,0:T(8,128)(2,1)S(1)}, u32[]{:S(2)}, u32[]{:S(2)}) collective-permute-start(bf16[32,2048]{1,0:T(8,128)(2,1)S(1)} %collective-permute-done.12.ya), channel_id=1, source_target_pairs={{0,4},{4,0},{8,12},{12,8},{16,20},{20,16},{24,28},{28,24},{1,5},{5... | collective-permute-start | bytes 393224 | tf_op jit(solution)/shard_map/ppermute | solution.py:22

commit v6 on v5

--- a/solution.py
+++ b/solution.py
@@ -10,7 +10,7 @@
 F32 = jnp.float32
 BF16 = jnp.bfloat16
 NEG = -1e30
-VMEM_LIMIT = 48 * 1024 * 1024
+VMEM_LIMIT = 32 * 1024 * 1024
 
 
 def params():
@@ -413,90 +413,63 @@
     )(offsets, core, *mid, *raw, *grads)
 
 
-def final_kernel(
-    levels, per, dim, offs_ref, core_ref, ba, bb, xa, xb, ya, yb, da, db, dq, dk, dv
-):
+def half_kernel(levels, per, dim, turn, offs_ref, core_ref, base, x, y, d, *refs):
+    dq, dk, dv = refs[-3:]
     tok = dq.shape[0]
     n2, n3 = tok // 4, tok // 8
-    heads = per * pl.num_programs(0)
-    swap = pl.program_id(0) * 2 // pl.num_programs(0) != core_ref[0]
-
-    def work(base, x, y, d):
-        each = range(per)
-        place = [
-            place_matrix(offs_ref, pl.program_id(0) * per + h, 2, levels, tok) for h in each
-        ]
-        third = (x[n2:].astype(F32) + y[...].astype(F32) + d[...].astype(F32)).astype(BF16)
-        src = [slice(2 * h * dim, 2 * (h + 1) * dim) for h in each]
-        more = [dot(place[h], stack(x[:n2, src[h]], third[:, src[h]])) for h in each]
-        for h in each:
-            cols = slice(h * dim, (h + 1) * dim)
-            lo = 3 * h * dim
-            total = base[:, lo + dim : lo + 3 * dim].astype(F32) + more[h]
-            dq[:, cols] = base[:, lo : lo + dim]
-            dk[:, cols] = total[:, :dim].astype(BF16)
-            dv[:, cols] = total[:, dim:].astype(BF16)
-
-    @pl.when(jnp.logical_not(swap))
-    def _():
-        work(ba, xa, ya, da)
-
-    @pl.when(swap)
-    def _():
-        work(bb, xb, yb, db)
-
-
-def final_call(offsets, core, parts, dim):
+    first = per * (1 - core_ref[0] if turn else core_ref[0])
+    each = range(per)
+    place = [place_matrix(offs_ref, first + h, 2, levels, tok) for h in each]
+    mine = y[n3:] if turn else y[:n3]
+    third = (x[n2:].astype(F32) + mine.astype(F32) + d[...].astype(F32)).astype(BF16)
+    src = [slice(2 * h * dim, 2 * (h + 1) * dim) for h in each]
+    more = [dot(place[h], stack(x[:n2, src[h]], third[:, src[h]])) for h in each]
+    for h in each:
+        cols = slice(h * dim, (h + 1) * dim)
+        lo = 3 * h * dim
+        total = base[:, lo + dim : lo + 3 * dim].astype(F32) + more[h]
+        dq[:, cols] = base[:, lo : lo + dim]
+        dk[:, cols] = total[:, :dim].astype(BF16)
+        dv[:, cols] = total[:, dim:].astype(BF16)
+
+
+def half_call(offsets, core, parts, whole, dim):
     levels, heads = offsets.shape
     tok = parts[0].shape[0]
-    steps = 2
-    per = heads // steps
-    third = tok // 8
-
-    def spec(a, far, row, rows):
-        cols = a.shape[1] * 2 // steps
-
-        def where(i, o, c):
-            turn = 1 - c[0] if far else c[0]
-            return row, jnp.clip(i - turn * (steps // 2), 0, steps // 2 - 1)
-
-        return pl.BlockSpec((rows, cols), where)
-
-    specs = []
-    for i, a in enumerate(parts):
-        far = i % 2 == 1
-        if i in (4, 5):
-            specs.append(spec(a, far, 1 if far else 0, third))
-        else:
-            specs.append(spec(a, far, 0, a.shape[0]))
-    out = pl.BlockSpec((tok, per * dim), lambda i, o, c: (0, i))
+    per = heads // 2
+    turn = len(whole) > 0
+
+    def where(i, o, c):
+        return 0, (1 - c[0] if turn else c[0])
+
     return pl.pallas_call(
-        functools.partial(final_kernel, levels, per, dim),
+        functools.partial(half_kernel, levels, per, dim, turn),
         grid_spec=pltpu.PrefetchScalarGridSpec(
             num_scalar_prefetch=2,
-            grid=(steps,),
-            in_specs=specs,
-            out_specs=[out] * 3,
+            grid=(1,),
+            in_specs=[pl.BlockSpec(memory_space=pltpu.VMEM)] * len(parts)
+            + [pl.BlockSpec(memory_space=pl.ANY)] * len(whole),
+            out_specs=[pl.BlockSpec((tok, per * dim), where)] * 3,
         ),
         out_shape=[jax.ShapeDtypeStruct((tok, heads * dim), BF16)] * 3,
+        input_output_aliases={2 + len(parts) + i: i for i in range(len(whole))},
         compiler_params=params(),
-        name="add_pieces",
-    )(offsets, core, *parts)
+        name="add_other_half" if turn else "add_own_half",
+    )(offsets, core, *parts, *whole)
 
 
 def per_device(queries, keys_in, values, out_grads, offsets):
     heads = offsets.shape[1]
     dim = queries.shape[2] // heads
     core = lax.rem(lax.axis_index("seq"), 2).astype(jnp.int32).reshape(1)
-    q, k, v = (
-        pltpu.with_memory_space_constraint(a[0], pltpu.HBM) for a in (queries, keys_in, values)
-    )
+    q, k, v = queries[0], keys_in[0], values[0]
     sections = lax.axis_size("section")
     grads = lax.ppermute(
         out_grads[0], "section", [(i, (i - 1) % sections) for i in range(sections)]
     )
     q_oth, k_oth, v_oth = exchange(q, 1), exchange(k, 1), exchange(v, 1)
-    both, three = pick_call(offsets, core, [k, k_oth, v, v_oth], dim)
+    kept = [pltpu.with_memory_space_constraint(a, pltpu.HBM) for a in (k, v)]
+    both, three = pick_call(offsets, core, [kept[0], k_oth, kept[1], v_oth], dim)
     x, y, d = exchange(both, 2), exchange(three, 4), exchange(three, 6)
     raw = [q, q_oth, k, k_oth, v, v_oth]
     pre = pre_call(offsets, core, raw, dim)
@@ -512,8 +485,8 @@
         offsets, core, [pre[0], stats2, pre[2], ngrad, dqt], raw, grads, dim
     )
     other, xa, xb, da, db, y = lax.optimization_barrier((other, xa, xb, da, db, y))
-    parts = [mine, exchange(other, 1), xa, xb, y, yy, da, db]
-    dq, dk, dv = final_call(offsets, core, parts, dim)
+    halves = half_call(offsets, core, [mine, xa, y, da], [], dim)
+    dq, dk, dv = half_call(offsets, core, [exchange(other, 1), xb, yy, db], halves, dim)
     return dq[None], dk[None], dv[None]
 
 

time: 45.3 us -> 43.3 us (0.956)
  Pallas kernels: 16.8 us -> 14.4 us
  waiting for transfers between devices: 11.3 us -> 12.8 us
  local copies, waits for them, and re-layouts: 1.75 us -> 0.68 us
    ppermute x1, waiting for transfers between devices: 1.54 us -> 4.01 us  [per_device(): lax.ppermute(out_grads[0], 'section', [(i, (i - 1) % sections) for i in r...]
    pallas_call x1 -> x2, Pallas kernels: 2.31 us -> 3.6 us  [half_call(): pl.pallas_call(functools.partial(half_kernel, levels, per, dim, turn), gr...]
    pallas_call x1, Pallas kernels: 5.73 us -> 4.46 us  [near_call(): pl.pallas_call(functools.partial(near_kernel, levels, per, dim), grid_spe...]
    pallas_call x1, Pallas kernels: 3.2 us -> 1.94 us  [pre_call(): pl.pallas_call(functools.partial(pre_kernel, levels, per, dim), grid_spec...]
    unnamed x8, local copies, waits for them, and re-layouts: 1.75 us -> 0.68 us
    pallas_call x1, Pallas kernels: 3.5 us -> 2.5 us  [far_call(): pl.pallas_call(functools.partial(far_kernel, levels, per, dim), grid_spec...]
    ppermute x14, waiting for transfers between devices: 9.76 us -> 8.78 us  [exchange(): return lax.ppermute(value, 'seq', [(i, i ^ bits) for i in range(count)])]
  transfers between devices with their start and end apart: 15 -> 15, of which waited for: 5 -> 4; matrix products, arithmetic and copies ran while one was open for 0% -> 0% of each run, Pallas kernels for 24% -> 23%
where the time goes in v6:
time: 43.3 us; the launch traced here: 43.2 us
  starting transfers between devices  14.6 us (34%)
  Pallas kernels  14.4 us (33%)
  waiting for transfers between devices  12.8 us (30%)
  between operations  0.7 us (2%)
  local copies, waits for them, and re-layouts  0.68 us (2%)
    ppermute x14, starting transfers between devices, exchange(): return lax.ppermute(value, 'seq', [(i, i ^ bits) for i in range(count)])  9.93 us
    ppermute x14, waiting for transfers between devices, exchange(): return lax.ppermute(value, 'seq', [(i, i ^ bits) for i in range(count)])  8.78 us
    ppermute x1, starting transfers between devices, per_device(): lax.ppermute(out_grads[0], 'section', [(i, (i - 1) % sections) for i in r...  4.67 us
    pallas_call x1, Pallas kernels, near_call(): pl.pallas_call(functools.partial(near_kernel, levels, per, dim), grid_spe...  4.46 us
    ppermute x1, waiting for transfers between devices, per_device(): lax.ppermute(out_grads[0], 'section', [(i, (i - 1) % sections) for i in r...  4.01 us
    pallas_call x2, Pallas kernels, half_call(): pl.pallas_call(functools.partial(half_kernel, levels, per, dim, turn), gr...  3.6 us
    pallas_call x1, Pallas kernels, far_call(): pl.pallas_call(functools.partial(far_kernel, levels, per, dim), grid_spec...  2.5 us
    pallas_call x1, Pallas kernels, pre_call(): pl.pallas_call(functools.partial(pre_kernel, levels, per, dim), grid_spec...  1.94 us
  transfers between devices with their start and end apart: 15, of which 4 were waited for; matrix products, arithmetic and copies ran while one was open for 0% of the time, Pallas kernels for 23%

profile of v6, /device:TPU:0, one launch (start us, length us, event | category | flops | bytes accessed | tf_op | source)
XLA Modules:
  0.0 43.2 jit_solution(10793911593703794618)
XLA Ops:
  0.6 0.5 %collective-permute-start.1 = (bf16[128,2048]{1,0:T(8,128)(2,1)}, bf16[128,2048]{1,0:T(8,128)(2,1)S(1)}, u32[]{:S(2)}, u32[]{:S(2)}) collective-permute-start(bf16[128,2048]{1,0:T(8,128)(2,1)} %bitcast.13), channel_id=1, source_target_pairs={{0,4},{4,0},{8,12},{12,8},{16,20},{20,16},{24,28},{28,24},{1,5},{5... | collective-permute-start | bytes 1572872 | tf_op jit(solution)/shard_map/ppermute | solution.py:22
  1.1 0.1 collective-permute-start.2
  1.2 0.4 %collective-permute-start = (bf16[128,2048]{1,0:T(8,128)(2,1)}, bf16[128,2048]{1,0:T(8,128)(2,1)S(1)}, u32[]{:S(2)}, u32[]{:S(2)}) collective-permute-start(bf16[128,2048]{1,0:T(8,128)(2,1)} %bitcast.17), channel_id=1, source_target_pairs={{0,4},{4,0},{8,12},{12,8},{16,20},{20,16},{24,28},{28,24},{1,5},{5... | collective-permute-start | bytes 1572872 | tf_op jit(solution)/shard_map/ppermute | solution.py:22
  1.7 4.7 %collective-permute-start.5 = (bf16[128,2048]{1,0:T(8,128)(2,1)}, bf16[128,2048]{1,0:T(8,128)(2,1)S(1)}, u32[]{:S(2)}, u32[]{:S(2)}) collective-permute-start(bf16[128,2048]{1,0:T(8,128)(2,1)} %bitcast.23), channel_id=1, source_target_pairs={{0,3},{1,0},{2,1},{3,2},{4,7},{5,4},{6,5},{7,6},{8,11},{9,8},{10,9... | collective-permute-start | bytes 1572872 | tf_op jit(solution)/shard_map/ppermute | solution.py:467
  6.3 0.0 copy-start.3
  6.3 0.0 collective-permute-done.1.k1
  6.3 0.0 collective-permute-done.2.v1
  6.3 0.7 %copy-done.3 = s32[3,16]{1,0:T(4,128)S(1)} copy-done((s32[3,16]{1,0:T(4,128)S(1)}, s32[3,16]{1,0:T(4,128)}, u32[]{:S(2)}) %copy-start.3) | copy-done | bytes 216
  7.0 0.0 copy-start
  7.0 0.0 copy-start.1
  7.0 0.0 copy-start.2
  7.0 1.9 %pick_rows.1 = (bf16[96,2048]{1,0:T(8,128)(2,1)S(1)}, bf16[32,2048]{1,0:T(8,128)(2,1)S(1)}) custom-call(s32[3,16]{1,0:T(4,128)S(1)} %copy-done.3, s32[1]{0:T(128)} %bitcast.core_ref, bf16[128,2048]{1,0:T(8,128)(2,1)} %bitcast.14, bf16[128,2048]{1,0:T(8,128)(2,1)S(1)} %collective-permute-done.1.k1, bf16[128,2048]{1,0:T(8,128)(2,1)} %bitcast.9, ...), custom_call_target="tpu_custom_call" | custom-call | tf_op jit(solution)/shard_map/pick_rows/pallas_call | solution.py:102
  8.9 2.5 %collective-permute-start.4 = (bf16[32,2048]{1,0:T(8,128)(2,1)S(1)}, bf16[32,2048]{1,0:T(8,128)(2,1)S(1)}, u32[]{:S(2)}, u32[]{:S(2)}) collective-permute-start(bf16[32,2048]{1,0:T(8,128)(2,1)S(1)} %get-tuple-element.38), channel_id=1, source_target_pairs={{0,24},{4,28},{8,16},{12,20},{16,8},{20,12},{24,0},{28,4},{1,25},{... | collective-permute-start | bytes 393224 | tf_op jit(solution)/shard_map/ppermute | solution.py:22
  11.4 0.5 %collective-permute-start.3 = (bf16[32,2048]{1,0:T(8,128)(2,1)S(1)}, bf16[32,2048]{1,0:T(8,128)(2,1)S(1)}, u32[]{:S(2)}, u32[]{:S(2)}) collective-permute-start(bf16[32,2048]{1,0:T(8,128)(2,1)S(1)} %get-tuple-element.38), channel_id=1, source_target_pairs={{0,16},{4,20},{8,24},{12,28},{16,0},{20,4},{24,8},{28,12},{1,17},{... | collective-permute-start | bytes 393224 | tf_op jit(solution)/shard_map/ppermute | solution.py:22
  11.9 0.5 %collective-permute-start.7 = (bf16[96,2048]{1,0:T(8,128)(2,1)S(1)}, bf16[96,2048]{1,0:T(8,128)(2,1)S(1)}, u32[]{:S(2)}, u32[]{:S(2)}) collective-permute-start(bf16[96,2048]{1,0:T(8,128)(2,1)S(1)} %get-tuple-element.40.own), channel_id=1, source_target_pairs={{0,8},{4,12},{8,0},{12,4},{16,24},{20,28},{24,16},{28,20},{1,9},{5... | collective-permute-start | bytes 1179656 | tf_op jit(solution)/shard_map/ppermute | solution.py:22
  12.5 0.0 collective-permute-done.q1
  12.5 0.0 copy-done
  12.5 0.0 copy-done.1
  12.5 0.0 copy-done.2
  12.5 1.9 %local_scores.1 = (bf16[256,2048]{1,0:T(8,128)(2,1)S(1)}, f32[8,2048]{1,0:T(8,128)S(1)}, bf16[128,2048]{1,0:T(8,128)(2,1)S(1)}, bf16[96,1024]{1,0:T(8,128)(2,1)S(1)}) custom-call(s32[3,16]{1,0:T(4,128)S(1)} %copy-done.3, s32[1]{0:T(128)} %bitcast.core_ref, bf16[128,2048]{1,0:T(8,128)(2,1)S(1)} %bitcast.18, bf16[128,2048]{1,0:T(8,128)(2,1)S(1)} %collective-permute-done.q1, ...), custom_call_target="tpu_custom_call" | custom-call | tf_op jit(solution)/shard_map/local_scores/pallas_call | solution.py:194
  14.4 4.0 %collective-permute-done.5.rows.g0 = bf16[128,2048]{1,0:T(8,128)(2,1)S(1)} collective-permute-done((bf16[128,2048]{1,0:T(8,128)(2,1)}, bf16[128,2048]{1,0:T(8,128)(2,1)S(1)}, u32[]{:S(2)}, u32[]{:S(2)}) %collective-permute-start.5) | collective-permute-done | bytes 524320 | tf_op jit(solution)/shard_map/ppermute | solution.py:467
  18.4 0.0 collective-permute-done.4.d
  18.4 0.0 collective-permute-done.3.y
  18.5 0.1 collective-permute-start.6
  18.6 5.4 %collective-permute-done.7.x = bf16[96,2048]{1,0:T(8,128)(2,1)S(1)} collective-permute-done((bf16[96,2048]{1,0:T(8,128)(2,1)S(1)}, bf16[96,2048]{1,0:T(8,128)(2,1)S(1)}, u32[]{:S(2)}, u32[]{:S(2)}) %collective-permute-start.7) | collective-permute-done | bytes 393248 | tf_op jit(solution)/shard_map/ppermute | solution.py:22
  24.0 0.0 collective-permute-done.6.g1
  24.0 2.5 %far_levels.1 = (bf16[48,2048]{1,0:T(8,128)(2,1)S(1)}, bf16[48,2048]{1,0:T(8,128)(2,1)S(1)}, bf16[32,2048]{1,0:T(8,128)(2,1)S(1)}, bf16[16,2048]{1,0:T(8,128)(2,...) custom-call(s32[3,16]{1,0:T(4,128)S(1)} %copy-done.3, ...), custom_call_target="tpu_custom_call" | custom-call | tf_op jit(solution)/shard_map/far_levels/pallas_call | solution.py:333
  26.5 1.6 %collective-permute-start.8 = (bf16[48,2048]{1,0:T(8,128)(2,1)S(1)}, bf16[48,2048]{1,0:T(8,128)(2,1)S(1)}, u32[]{:S(2)}, u32[]{:S(2)}) collective-permute-start(bf16[48,2048]{1,0:T(8,128)(2,1)S(1)} %get-tuple-element.47), channel_id=1, source_target_pairs={{0,8},{4,12},{8,0},{12,4},{16,24},{20,28},{24,16},{28,20},{1,9},{5... | collective-permute-start | bytes 589832 | tf_op jit(solution)/shard_map/ppermute | solution.py:22
  28.0 0.0 collective-permute-start.9
  28.0 0.5 %collective-permute-start.12 = (bf16[32,2048]{1,0:T(8,128)(2,1)S(1)}, bf16[32,2048]{1,0:T(8,128)(2,1)S(1)}, u32[]{:S(2)}, u32[]{:S(2)}) collective-permute-start(bf16[32,2048]{1,0:T(8,128)(2,1)S(1)} %get-tuple-element.51), channel_id=1, source_target_pairs={{0,16},{4,20},{8,24},{12,28},{16,0},{20,4},{24,8},{28,12},{1,17},{... | collective-permute-start | bytes 393224 | tf_op jit(solution)/shard_map/ppermute | solution.py:22
  28.5 1.7 %collective-permute-start.10 = (bf16[16,2048]{1,0:T(8,128)(2,1)S(1)}, bf16[16,2048]{1,0:T(8,128)(2,1)S(1)}, u32[]{:S(2)}, u32[]{:S(2)}) collective-permute-start(bf16[16,2048]{1,0:T(8,128)(2,1)S(1)} %get-tuple-element.49), channel_id=1, source_target_pairs={{0,24},{4,28},{8,16},{12,20},{16,8},{20,12},{24,0},{28,4},{1,25},{... | collective-permute-start | bytes 196616 | tf_op jit(solution)/shard_map/ppermute | solution.py:22
  30.2 0.9 %collective-permute-start.11 = (bf16[16,2048]{1,0:T(8,128)(2,1)S(1)}, bf16[16,2048]{1,0:T(8,128)(2,1)S(1)}, u32[]{:S(2)}, u32[]{:S(2)}) collective-permute-start(bf16[16,2048]{1,0:T(8,128)(2,1)S(1)} %get-tuple-element.50), channel_id=1, source_target_pairs={{0,28},{4,24},{8,20},{12,16},{16,12},{20,8},{24,4},{28,0},{1,29},{... | collective-permute-start | bytes 196616 | tf_op jit(solution)/shard_map/ppermute | solution.py:22
  31.1 4.5 %near_levels.1 = (bf16[128,3072]{1,0:T(8,128)(2,1)S(1)}, bf16[128,3072]{1,0:T(8,128)(2,1)S(1)}) custom-call(s32[3,16]{1,0:T(4,128)S(1)} %copy-done.3, s32[1]{0:T(128)} %bitcast.core_ref, bf16[256,2048]{1,0:T(8,128)(2,1)S(1)} %get-tuple-element.34.exps, f32[8,2048]{1,0:T(8,128)S(1)} %get-tuple-element.43.stats2, ...), custom_call_target="tpu_custom_call" | custom-call | tf_op jit(solution)/shard_map/near_levels/pallas_call | solution.py:402
  35.6 3.1 %collective-permute-done.10.d = bf16[16,2048]{1,0:T(8,128)(2,1)S(1)} collective-permute-done((bf16[16,2048]{1,0:T(8,128)(2,1)S(1)}, bf16[16,2048]{1,0:T(8,128)(2,1)S(1)}, u32[]{:S(2)}, u32[]{:S(2)}) %collective-permute-start.10) | collective-permute-done | bytes 65568 | tf_op jit(solution)/shard_map/ppermute | solution.py:22
  38.7 0.0 collective-permute-done.11.d
  38.7 0.0 collective-permute-done.12.y
  38.7 0.0 collective-permute-done.8.x
  38.7 0.0 collective-permute-done.9.x
  38.7 0.6 %collective-permute-start.13 = (bf16[128,3072]{1,0:T(8,128)(2,1)S(1)}, bf16[128,3072]{1,0:T(8,128)(2,1)S(1)}, u32[]{:S(2)}, u32[]{:S(2)}) collective-permute-start(bf16[128,3072]{1,0:T(8,128)(2,1)S(1)} %get-tuple-element.52), channel_id=1, source_target_pairs={{0,4},{4,0},{8,12},{12,8},{16,20},{20,16},{24,28},{28,24},{1,5},{5... | collective-permute-start | bytes 2359304 | tf_op jit(solution)/shard_map/ppermute | solution.py:22
  39.3 0.1 collective-permute-start.14
  39.4 1.8 %add_own_half.1 = (bf16[128,2048]{1,0:T(8,128)(2,1)}, bf16[128,2048]{1,0:T(8,128)(2,1)}, bf16[128,2048]{1,0:T(8,128)(2,1)}) custom-call(s32[3,16]{1,0:T(4,128)S(1)} %copy-done.3, s32[1]{0:T(128)} %bitcast.core_ref, bf16[128,3072]{1,0:T(8,128)(2,1)S(1)} %get-tuple-element.55.base, bf16[48,2048]{1,0:T(8,128)(2,1)S(1)} %collective-permute-done.8.x, ...), custom_call_target="tpu_custom_call" | custom-call | tf_op jit(solution)/shard_map/add_own_half/pallas_call | solution.py:445
  41.2 0.2 collective-permute-done.14.y
  41.4 0.0 collective-permute-done.13.base
  41.4 1.8 %add_other_half.1 = (bf16[128,2048]{1,0:T(8,128)(2,1)}, bf16[128,2048]{1,0:T(8,128)(2,1)}, bf16[128,2048]{1,0:T(8,128)(2,1)}) custom-call(s32[3,16]{1,0:T(4,128)S(1)} %copy-done.3, s32[1]{0:T(128)} %bitcast.core_ref, bf16[128,3072]{1,0:T(8,128)(2,1)S(1)} %collective-permute-done.13.base, ...), custom_call_target="tpu_custom_call", output_to_operand_aliasing={{0}: (6, {}), {1}: (7, {}), {2}: (8, {})} | custom-call | tf_op jit(solution)/shard_map/add_other_half/pallas_call | solution.py:445
  (1 shorter events, 0.0 us)
Async XLA Ops:
  0.6 5.7 %collective-permute-start.1 = (bf16[128,2048]{1,0:T(8,128)(2,1)}, bf16[128,2048]{1,0:T(8,128)(2,1)S(1)}, u32[]{:S(2)}, u32[]{:S(2)}) collective-permute-start(bf16[128,2048]{1,0:T(8,128)(2,1)} %bitcast.13), channel_id=1, source_target_pairs={{0,4},{4,0},{8,12},{12,8},{16,20},{20,16},{24,28},{28,24},{1,5},{5... | collective-permute-start | bytes 1572872 | tf_op jit(solution)/shard_map/ppermute | solution.py:22
  1.1 5.2 %collective-permute-start.2 = (bf16[128,2048]{1,0:T(8,128)(2,1)}, bf16[128,2048]{1,0:T(8,128)(2,1)S(1)}, u32[]{:S(2)}, u32[]{:S(2)}) collective-permute-start(bf16[128,2048]{1,0:T(8,128)(2,1)} %bitcast.8), channel_id=1, source_target_pairs={{0,4},{4,0},{8,12},{12,8},{16,20},{20,16},{24,28},{28,24},{1,5},{5... | collective-permute-start | bytes 1572872 | tf_op jit(solution)/shard_map/ppermute | solution.py:22
  1.2 11.2 %collective-permute-start = (bf16[128,2048]{1,0:T(8,128)(2,1)}, bf16[128,2048]{1,0:T(8,128)(2,1)S(1)}, u32[]{:S(2)}, u32[]{:S(2)}) collective-permute-start(bf16[128,2048]{1,0:T(8,128)(2,1)} %bitcast.17), channel_id=1, source_target_pairs={{0,4},{4,0},{8,12},{12,8},{16,20},{20,16},{24,28},{28,24},{1,5},{5... | collective-permute-start | bytes 1572872 | tf_op jit(solution)/shard_map/ppermute | solution.py:22
  1.7 16.8 %collective-permute-start.5 = (bf16[128,2048]{1,0:T(8,128)(2,1)}, bf16[128,2048]{1,0:T(8,128)(2,1)S(1)}, u32[]{:S(2)}, u32[]{:S(2)}) collective-permute-start(bf16[128,2048]{1,0:T(8,128)(2,1)} %bitcast.23), channel_id=1, source_target_pairs={{0,3},{1,0},{2,1},{3,2},{4,7},{5,4},{6,5},{7,6},{8,11},{9,8},{10,9... | collective-permute-start | bytes 1572872 | tf_op jit(solution)/shard_map/ppermute | solution.py:467
  6.3 0.7 %copy-start.3 = (s32[3,16]{1,0:T(4,128)S(1)}, s32[3,16]{1,0:T(4,128)}, u32[]{:S(2)}) copy-start(s32[3,16]{1,0:T(4,128)} %offs_ref.11) | copy-start | bytes 580
  7.0 5.5 %copy-start = (bf16[1,128,2048]{2,1,0:T(8,128)(2,1)S(1)}, bf16[1,128,2048]{2,1,0:T(8,128)(2,1)}, u32[]{:S(2)}) copy-start(bf16[1,128,2048]{2,1,0:T(8,128)(2,1)} %param.7) | copy-start | bytes 1572868
  7.0 5.5 %copy-start.1 = (bf16[1,128,2048]{2,1,0:T(8,128)(2,1)S(1)}, bf16[1,128,2048]{2,1,0:T(8,128)(2,1)}, u32[]{:S(2)}) copy-start(bf16[1,128,2048]{2,1,0:T(8,128)(2,1)} %param.6) | copy-start | bytes 1572868
  7.0 5.5 %copy-start.2 = (bf16[1,128,2048]{2,1,0:T(8,128)(2,1)S(1)}, bf16[1,128,2048]{2,1,0:T(8,128)(2,1)}, u32[]{:S(2)}) copy-start(bf16[1,128,2048]{2,1,0:T(8,128)(2,1)} %param.5) | copy-start | bytes 1572868
  8.9 9.5 %collective-permute-start.4 = (bf16[32,2048]{1,0:T(8,128)(2,1)S(1)}, bf16[32,2048]{1,0:T(8,128)(2,1)S(1)}, u32[]{:S(2)}, u32[]{:S(2)}) collective-permute-start(bf16[32,2048]{1,0:T(8,128)(2,1)S(1)} %get-tuple-element.38), channel_id=1, source_target_pairs={{0,24},{4,28},{8,16},{12,20},{16,8},{20,12},{24,0},{28,4},{1,25},{... | collective-permute-start | bytes 393224 | tf_op jit(solution)/shard_map/ppermute | solution.py:22
  11.4 7.0 %collective-permute-start.3 = (bf16[32,2048]{1,0:T(8,128)(2,1)S(1)}, bf16[32,2048]{1,0:T(8,128)(2,1)S(1)}, u32[]{:S(2)}, u32[]{:S(2)}) collective-permute-start(bf16[32,2048]{1,0:T(8,128)(2,1)S(1)} %get-tuple-element.38), channel_id=1, source_target_pairs={{0,16},{4,20},{8,24},{12,28},{16,0},{20,4},{24,8},{28,12},{1,17},{... | collective-permute-start | bytes 393224 | tf_op jit(solution)/shard_map/ppermute | solution.py:22
  11.9 12.0 %collective-permute-start.7 = (bf16[96,2048]{1,0:T(8,128)(2,1)S(1)}, bf16[96,2048]{1,0:T(8,128)(2,1)S(1)}, u32[]{:S(2)}, u32[]{:S(2)}) collective-permute-start(bf16[96,2048]{1,0:T(8,128)(2,1)S(1)} %get-tuple-element.40.own), channel_id=1, source_target_pairs={{0,8},{4,12},{8,0},{12,4},{16,24},{20,28},{24,16},{28,20},{1,9},{5... | collective-permute-start | bytes 1179656 | tf_op jit(solution)/shard_map/ppermute | solution.py:22
  18.5 5.5 %collective-permute-start.6 = (bf16[128,1024]{1,0:T(8,128)(2,1)S(1)}, bf16[128,1024]{1,0:T(8,128)(2,1)S(1)}, u32[]{:S(2)}, u32[]{:S(2)}) collective-permute-start(bf16[128,1024]{1,0:T(8,128)(2,1)S(1)} %pack_half.1), channel_id=1, source_target_pairs={{0,4},{4,0},{8,12},{12,8},{16,20},{20,16},{24,28},{28,24},{1,5},{5... | collective-permute-start | bytes 786440 | tf_op jit(solution)/shard_map/ppermute | solution.py:22
  26.5 12.3 %collective-permute-start.8 = (bf16[48,2048]{1,0:T(8,128)(2,1)S(1)}, bf16[48,2048]{1,0:T(8,128)(2,1)S(1)}, u32[]{:S(2)}, u32[]{:S(2)}) collective-permute-start(bf16[48,2048]{1,0:T(8,128)(2,1)S(1)} %get-tuple-element.47), channel_id=1, source_target_pairs={{0,8},{4,12},{8,0},{12,4},{16,24},{20,28},{24,16},{28,20},{1,9},{5... | collective-permute-start | bytes 589832 | tf_op jit(solution)/shard_map/ppermute | solution.py:22
  28.0 10.7 %collective-permute-start.9 = (bf16[48,2048]{1,0:T(8,128)(2,1)S(1)}, bf16[48,2048]{1,0:T(8,128)(2,1)S(1)}, u32[]{:S(2)}, u32[]{:S(2)}) collective-permute-start(bf16[48,2048]{1,0:T(8,128)(2,1)S(1)} %get-tuple-element.48), channel_id=1, source_target_pairs={{0,12},{4,8},{8,4},{12,0},{16,28},{20,24},{24,20},{28,16},{1,13},{... | collective-permute-start | bytes 589832 | tf_op jit(solution)/shard_map/ppermute | solution.py:22
  28.0 10.7 %collective-permute-start.12 = (bf16[32,2048]{1,0:T(8,128)(2,1)S(1)}, bf16[32,2048]{1,0:T(8,128)(2,1)S(1)}, u32[]{:S(2)}, u32[]{:S(2)}) collective-permute-start(bf16[32,2048]{1,0:T(8,128)(2,1)S(1)} %get-tuple-element.51), channel_id=1, source_target_pairs={{0,16},{4,20},{8,24},{12,28},{16,0},{20,4},{24,8},{28,12},{1,17},{... | collective-permute-start | bytes 393224 | tf_op jit(solution)/shard_map/ppermute | solution.py:22
  28.5 10.2 %collective-permute-start.10 = (bf16[16,2048]{1,0:T(8,128)(2,1)S(1)}, bf16[16,2048]{1,0:T(8,128)(2,1)S(1)}, u32[]{:S(2)}, u32[]{:S(2)}) collective-permute-start(bf16[16,2048]{1,0:T(8,128)(2,1)S(1)} %get-tuple-element.49), channel_id=1, source_target_pairs={{0,24},{4,28},{8,16},{12,20},{16,8},{20,12},{24,0},{28,4},{1,25},{... | collective-permute-start | bytes 196616 | tf_op jit(solution)/shard_map/ppermute | solution.py:22
  30.2 8.5 %collective-permute-start.11 = (bf16[16,2048]{1,0:T(8,128)(2,1)S(1)}, bf16[16,2048]{1,0:T(8,128)(2,1)S(1)}, u32[]{:S(2)}, u32[]{:S(2)}) collective-permute-start(bf16[16,2048]{1,0:T(8,128)(2,1)S(1)} %get-tuple-element.50), channel_id=1, source_target_pairs={{0,28},{4,24},{8,20},{12,16},{16,12},{20,8},{24,4},{28,0},{1,29},{... | collective-permute-start | bytes 196616 | tf_op jit(solution)/shard_map/ppermute | solution.py:22
  38.7 2.7 %collective-permute-start.13 = (bf16[128,3072]{1,0:T(8,128)(2,1)S(1)}, bf16[128,3072]{1,0:T(8,128)(2,1)S(1)}, u32[]{:S(2)}, u32[]{:S(2)}) collective-permute-start(bf16[128,3072]{1,0:T(8,128)(2,1)S(1)} %get-tuple-element.52), channel_id=1, source_target_pairs={{0,4},{4,0},{8,12},{12,8},{16,20},{20,16},{24,28},{28,24},{1,5},{5... | collective-permute-start | bytes 2359304 | tf_op jit(solution)/shard_map/ppermute | solution.py:22
  39.3 2.1 %collective-permute-start.14 = (bf16[32,2048]{1,0:T(8,128)(2,1)S(1)}, bf16[32,2048]{1,0:T(8,128)(2,1)S(1)}, u32[]{:S(2)}, u32[]{:S(2)}) collective-permute-start(bf16[32,2048]{1,0:T(8,128)(2,1)S(1)} %collective-permute-done.12.y), channel_id=1, source_target_pairs={{0,4},{4,0},{8,12},{12,8},{16,20},{20,16},{24,28},{28,24},{1,5},{5... | collective-permute-start | bytes 393224 | tf_op jit(solution)/shard_map/ppermute | solution.py:22

commit v7 on v6

--- a/solution.py
+++ b/solution.py
@@ -75,45 +75,64 @@
     )(core, rows)
 
 
-def pick_kernel(levels, per, dim, offs_ref, core_ref, k0, k1, v0, v1, both_ref, three_ref):
-    tok = k0.shape[0]
+def pick_kernel(
+    levels, per, dim, core_ref, offs, k0, v0, k1, v1, both_ref, three_ref, offs_ref, own_k, own_v, sems
+):
+    tok = k1.shape[0]
     n2, n3 = tok // 4, tok // 8
     each = range(per)
+    mine = pl.ds(pl.multiple_of(core_ref[0] * per * dim, per * dim), per * dim)
+    copies = [
+        pltpu.make_async_copy(src.at[:, mine], dst, sems.at[i])
+        for i, (src, dst) in enumerate(((k0, own_k), (v0, own_v)))
+    ]
+    table = pltpu.make_async_copy(offs, offs_ref, sems.at[2])
+    table.start()
+    for copy in copies:
+        copy.start()
+    table.wait()
     picks = [pick_matrix(offs_ref, core_ref[0] * per + h, 2, levels, tok) for h in each]
-    cols = [slice(h * dim, (h + 1) * dim) for h in each]
-    own = [dot(picks[h], side(k0[:, cols[h]], v0[:, cols[h]])).astype(BF16) for h in each]
-    oth = [dot(picks[h], side(k1[:, cols[h]], v1[:, cols[h]])).astype(BF16) for h in each]
-    for h in each:
-        out = slice(2 * h * dim, 2 * (h + 1) * dim)
-        third = stack(own[h][n2:], oth[h][n2:])
-        both_ref[:, out] = stack(own[h][:n2], oth[h][:n2], third)
-        three_ref[:, out] = third
-
-
-def pick_call(offsets, core, raw, dim):
-    tok, width = raw[0].shape
+
+    def work(keys, values, lo):
+        for h in each:
+            cols = slice(h * dim, (h + 1) * dim)
+            out = slice(2 * h * dim, 2 * (h + 1) * dim)
+            got = dot(picks[h], side(keys[:, cols], values[:, cols])).astype(BF16)
+            both_ref[lo * n2 : (lo + 1) * n2, out] = got[:n2]
+            both_ref[2 * n2 + lo * n3 : 2 * n2 + (lo + 1) * n3, out] = got[n2:]
+            three_ref[lo * n3 : (lo + 1) * n3, out] = got[n2:]
+
+    work(k1, v1, 1)
+    for copy in copies:
+        copy.wait()
+    work(own_k, own_v, 0)
+
+
+def pick_call(offsets, core, own, other, dim):
+    tok, width = own[0].shape
     levels, heads = offsets.shape
     per = heads // 2
-    spec = own_spec(tok, per * dim, 1)
+    spec = pl.BlockSpec((tok, per * dim), lambda i, c: (0, c[0]))
 
     def out(rows):
-        return pl.BlockSpec((rows, 2 * per * dim), lambda i, o, c: (0, 0))
-
+        return pl.BlockSpec((rows, 2 * per * dim), lambda i, c: (0, 0))
+
+    rows = [tok // 2 + tok // 4, tok // 4]
     return pl.pallas_call(
         functools.partial(pick_kernel, levels, per, dim),
         grid_spec=pltpu.PrefetchScalarGridSpec(
-            num_scalar_prefetch=2,
+            num_scalar_prefetch=1,
             grid=(1,),
-            in_specs=[spec] * 4,
-            out_specs=[out(tok // 2 + tok // 4), out(tok // 4)],
-        ),
-        out_shape=[
-            jax.ShapeDtypeStruct((tok // 2 + tok // 4, width), BF16),
-            jax.ShapeDtypeStruct((tok // 4, width), BF16),
-        ],
+            in_specs=[pl.BlockSpec(memory_space=pl.ANY)] * 3 + [spec] * 2,
+            out_specs=[out(r) for r in rows],
+            scratch_shapes=[pltpu.SMEM((levels, heads), jnp.int32)]
+            + [pltpu.VMEM((tok, per * dim), BF16)] * 2
+            + [pltpu.SemaphoreType.DMA((3,))],
+        ),
+        out_shape=[jax.ShapeDtypeStruct((r, width), BF16) for r in rows],
         compiler_params=params(),
         name="pick_rows",
-    )(offsets, core, *raw)
+    )(core, offsets, *own, *other)
 
 
 def own_spec(tok, cols, steps):
@@ -205,12 +224,59 @@
     )(offsets, core, *raw)
 
 
+def grad_kernel(levels, per, dim, offs_ref, core_ref, exps, near, v0, v1, g0, g1, selg, local):
+    tok = g0.shape[0]
+    first = core_ref[0] * per
+    each = range(per)
+    cols = [slice(h * dim, (h + 1) * dim) for h in each]
+    lanes = [slice(2 * h * tok, 2 * (h + 1) * tok) for h in each]
+    picks = [pick_matrix(offs_ref, first + h, 2, levels, tok) for h in each]
+    for h in each:
+        rows = stack(dot(picks[h], g0[:, cols[h]]), dot(picks[h], g1[:, cols[h]]))
+        selg[:, cols[h]] = rows.astype(BF16)
+    for h in each:
+        vc = slice((2 * h + 1) * dim, (2 * h + 2) * dim)
+        gra0, gra1 = g0[:, cols[h]], g1[:, cols[h]]
+        p0 = side(dot_nt(v0[:, cols[h]], gra0), dot_nt(v1[:, cols[h]], gra1))
+        p1 = dot_nt(near[:, vc], stack(gra0, gra1))
+        ex = exps[:, lanes[h]]
+        both = ex[:tok].astype(F32) * p0 + ex[tok:].astype(F32) * p1
+        local[0:1, lanes[h]] = jnp.sum(both, axis=0, keepdims=True)
+
+
+def grad_call(offsets, core, mid, raw, grads, dim):
+    tok, width = raw[0].shape
+    levels, heads = offsets.shape
+    per = heads // 2
+    raw_spec = own_spec(tok, per * dim, 1)
+    sel = 2 * (tok // 4 + tok // 8)
+
+    def whole(a):
+        return pl.BlockSpec(a.shape, lambda i, o, c: (0, 0))
+
+    outs = [
+        jax.ShapeDtypeStruct((sel, per * dim), BF16),
+        jax.ShapeDtypeStruct((8, per * 2 * tok), F32),
+    ]
+    return pl.pallas_call(
+        functools.partial(grad_kernel, levels, per, dim),
+        grid_spec=pltpu.PrefetchScalarGridSpec(
+            num_scalar_prefetch=2,
+            grid=(1,),
+            in_specs=[whole(a) for a in mid] + [raw_spec] * 3 + [whole(grads[1])],
+            out_specs=[whole(a) for a in outs],
+        ),
+        out_shape=outs,
+        compiler_params=params(),
+        name="local_delta",
+    )(offsets, core, *mid, *raw, *grads)
+
+
 def far_kernel(
-    levels, per, dim, offs_ref, core_ref, exps, stats, near, selq, v0, v1, g0, g1,
-    own, x, y, d,
+    levels, per, dim, offs_ref, core_ref, stats, selq, selg, local, own, x, y, d,
     xa, xb, yab, da, db, ngrad, dqt, stats2,
 ):
-    tok = g0.shape[0]
+    tok = dqt.shape[0]
     n1, n2, n3 = tok // 2, tok // 4, tok // 8
     sel = n2 + n3
     scale = dim**-0.5
@@ -235,21 +301,9 @@
         return jnp.where(is2, value[:tok], value[tok:])
 
     picks = [pick_matrix(offs_ref, first + h, 2, levels, tok) for h in each]
-    gsel = [
-        stack(dot(picks[h], g0[:, cols[h]]), dot(picks[h], g1[:, cols[h]])).astype(BF16)
-        for h in each
-    ]
     keys = [rows(kc[h]) for h in each]
     s = [level_pick(dot_nt(keys[h], selq[:, cols[h]])) * scale for h in each]
-    p = [level_pick(dot_nt(rows(vc[h]), gsel[h])) for h in each]
-    dloc = []
-    for h in each:
-        gra0, gra1 = g0[:, cols[h]], g1[:, cols[h]]
-        p0 = side(dot_nt(v0[:, cols[h]], gra0), dot_nt(v1[:, cols[h]], gra1))
-        p1 = dot_nt(near[:tok, vc[h]], stack(gra0, gra1))
-        ex = exps[:, lanes[h]]
-        both = ex[:tok].astype(F32) * p0 + ex[tok:].astype(F32) * p1
-        dloc.append(jnp.sum(both, axis=0, keepdims=True))
+    p = [level_pick(dot_nt(rows(vc[h]), selg[:, cols[h]])) for h in each]
     top = [jnp.max(a, axis=0, keepdims=True) for a in s]
     e = [jnp.exp(a - b) for a, b in zip(s, top)]
     size = [jnp.sum(a, axis=0, keepdims=True) for a in e]
@@ -278,7 +332,7 @@
         a1, a2, a3 = jnp.exp(t1 - high), jnp.exp(t2 - high), jnp.exp(t3 - high)
         inv = 1.0 / (a1 * z1 + a2 * z2 + a3 * z3)
         f1, f2, f3 = a1 * inv, a2 * inv, a3 * inv
-        delta = f1 * dloc[h] + f2 * dot2 + f3 * dot3
+        delta = f1 * local[0:1, lanes[h]] + f2 * dot2 + f3 * dot3
         stats2[0:1, lanes[h]] = f1
         stats2[1:2, lanes[h]] = delta
         terms = stack(*split(f2, 2), *split(f3, 2), *split(delta, 2))
@@ -295,7 +349,7 @@
         dsm.append(apart(w * (p[h] - (b[4:5] + b[5:6]))))
         wm.append(apart(w))
     dk = [dot(dsm[h], selq[:, cols[h]]) * scale for h in each]
-    dv = [dot(wm[h], gsel[h]) for h in each]
+    dv = [dot(wm[h], selg[:, cols[h]]) for h in each]
     for h in each:
         dkv = side(dk[h], dv[h]).astype(BF16)
         xa[:n2, wide[h]] = dkv[2 * n2 : 3 * n2]
@@ -310,14 +364,12 @@
         dqt[:, h * dim : h * dim + 2 * sel] = dot(keys[h].T, dsm[h]).astype(BF16)
 
 
-def far_call(offsets, core, pre, raw, grads, far, dim):
-    tok, width = raw[0].shape
+def far_call(offsets, core, mid, far, tok, dim):
     levels, heads = offsets.shape
     half = heads // 2
     per = 8
     steps = half // per
     n2, n3 = tok // 4, tok // 8
-    raw_spec = own_spec(tok, per * dim, steps)
 
     def mid_spec(a):
         return pl.BlockSpec((a.shape[0], a.shape[1] // steps), lambda i, o, c: (0, i))
@@ -335,14 +387,13 @@
         grid_spec=pltpu.PrefetchScalarGridSpec(
             num_scalar_prefetch=2,
             grid=(steps,),
-            in_specs=[mid_spec(a) for a in pre] + [raw_spec] * 2
-            + [raw_spec] + [mid_spec(a) for a in grads[1:] + far],
+            in_specs=[mid_spec(a) for a in mid + far],
             out_specs=[o[0] for o in outs],
         ),
         out_shape=[o[1] for o in outs],
         compiler_params=params(),
         name="far_levels",
-    )(offsets, core, *pre, *raw, *grads, *far)
+    )(offsets, core, *mid, *far)
 
 
 def near_kernel(
@@ -414,23 +465,40 @@
 
 
 def half_kernel(levels, per, dim, turn, offs_ref, core_ref, base, x, y, d, *refs):
-    dq, dk, dv = refs[-3:]
-    tok = dq.shape[0]
+    outs, (held, sems) = refs[-5:-2], refs[-2:]
+    tok = base.shape[0]
     n2, n3 = tok // 4, tok // 8
     first = per * (1 - core_ref[0] if turn else core_ref[0])
+    group = 2
     each = range(per)
     place = [place_matrix(offs_ref, first + h, 2, levels, tok) for h in each]
     mine = y[n3:] if turn else y[:n3]
     third = (x[n2:].astype(F32) + mine.astype(F32) + d[...].astype(F32)).astype(BF16)
     src = [slice(2 * h * dim, 2 * (h + 1) * dim) for h in each]
-    more = [dot(place[h], stack(x[:n2, src[h]], third[:, src[h]])) for h in each]
-    for h in each:
-        cols = slice(h * dim, (h + 1) * dim)
-        lo = 3 * h * dim
-        total = base[:, lo + dim : lo + 3 * dim].astype(F32) + more[h]
-        dq[:, cols] = base[:, lo : lo + dim]
-        dk[:, cols] = total[:, :dim].astype(BF16)
-        dv[:, cols] = total[:, dim:].astype(BF16)
+    copies = []
+
+    def send(part, lo, n):
+        cols = pl.ds(pl.multiple_of(first * dim + lo * dim, dim), n * dim)
+        here = held.at[part, :, pl.ds(lo * dim, n * dim)]
+        copies.append(pltpu.make_async_copy(here, outs[part].at[:, cols], sems.at[len(copies)]))
+        copies[-1].start()
+
+    for h in each:
+        held[0, :, h * dim : (h + 1) * dim] = base[:, 3 * h * dim : (3 * h + 1) * dim]
+    send(0, 0, per)
+    for lo in range(0, per, group):
+        heads = range(lo, lo + group)
+        more = [dot(place[h], stack(x[:n2, src[h]], third[:, src[h]])) for h in heads]
+        for h, add in zip(heads, more):
+            cols = slice(h * dim, (h + 1) * dim)
+            at = (3 * h + 1) * dim
+            total = (base[:, at : at + 2 * dim].astype(F32) + add).astype(BF16)
+            held[1, :, cols] = total[:, :dim]
+            held[2, :, cols] = total[:, dim:]
+        send(1, lo, group)
+        send(2, lo, group)
+    for copy in copies:
+        copy.wait()
 
 
 def half_call(offsets, core, parts, whole, dim):
@@ -438,18 +506,19 @@
     tok = parts[0].shape[0]
     per = heads // 2
     turn = len(whole) > 0
-
-    def where(i, o, c):
-        return 0, (1 - c[0] if turn else c[0])
-
+    away = pl.BlockSpec(memory_space=pl.ANY)
     return pl.pallas_call(
         functools.partial(half_kernel, levels, per, dim, turn),
         grid_spec=pltpu.PrefetchScalarGridSpec(
             num_scalar_prefetch=2,
             grid=(1,),
-            in_specs=[pl.BlockSpec(memory_space=pltpu.VMEM)] * len(parts)
-            + [pl.BlockSpec(memory_space=pl.ANY)] * len(whole),
-            out_specs=[pl.BlockSpec((tok, per * dim), where)] * 3,
+            in_specs=[pl.BlockSpec(a.shape, lambda i, o, c: (0, 0)) for a in parts]
+            + [away] * len(whole),
+            out_specs=[away] * 3,
+            scratch_shapes=[
+                pltpu.VMEM((3, tok, per * dim), BF16),
+                pltpu.SemaphoreType.DMA((1 + per,)),
+            ],
         ),
         out_shape=[jax.ShapeDtypeStruct((tok, heads * dim), BF16)] * 3,
         input_output_aliases={2 + len(parts) + i: i for i in range(len(whole))},
@@ -469,20 +538,24 @@
     )
     q_oth, k_oth, v_oth = exchange(q, 1), exchange(k, 1), exchange(v, 1)
     kept = [pltpu.with_memory_space_constraint(a, pltpu.HBM) for a in (k, v)]
-    both, three = pick_call(offsets, core, [kept[0], k_oth, kept[1], v_oth], dim)
+    both, three = pick_call(
+        pltpu.with_memory_space_constraint(offsets, pltpu.HBM), core, kept, [k_oth, v_oth], dim
+    )
     x, y, d = exchange(both, 2), exchange(three, 4), exchange(three, 6)
     raw = [q, q_oth, k, k_oth, v, v_oth]
     pre = pre_call(offsets, core, raw, dim)
     y, d, grads = lax.optimization_barrier((y, d, grads, pre[1]))[:3]
     grads = [grads, exchange(pack_call(core, grads), 1)]
+    exps, stats, near, selq = pre
+    selg, local = grad_call(offsets, core, [exps, near], [v, v_oth], grads, dim)
     xa, xb, yab, da, db, ngrad, dqt, stats2 = far_call(
-        offsets, core, pre, [v, v_oth], grads, [both, x, y, d], dim
+        offsets, core, [stats, selq, selg, local], [both, x, y, d], q.shape[0], dim
     )
     xa, xb, da, db = exchange(xa, 2), exchange(xb, 3), exchange(da, 6), exchange(db, 7)
     y = exchange(yab, 4)
     yy = exchange(y, 1)
     mine, other = near_call(
-        offsets, core, [pre[0], stats2, pre[2], ngrad, dqt], raw, grads, dim
+        offsets, core, [exps, stats2, near, ngrad, dqt], raw, grads, dim
     )
     other, xa, xb, da, db, y = lax.optimization_barrier((other, xa, xb, da, db, y))
     halves = half_call(offsets, core, [mine, xa, y, da], [], dim)

time: 43.3 us -> 42.2 us (0.975)
  local copies, waits for them, and re-layouts: 0.68 us -> 0.02 us
  waiting for transfers between devices: 12.8 us -> 12.2 us
    ppermute x14, waiting for transfers between devices: 8.78 us -> 7.03 us  [exchange(): return lax.ppermute(value, 'seq', [(i, i ^ bits) for i in range(count)])]
    pallas_call x0 -> x1, Pallas kernels: none -> 1.38 us  [grad_call(): pl.pallas_call(functools.partial(grad_kernel, levels, per, dim), grid_spe...]
    ppermute x1, waiting for transfers between devices: 4.01 us -> 5.13 us  [per_device(): lax.ppermute(out_grads[0], 'section', [(i, (i - 1) % sections) for i in r...]
    unnamed x8, local copies, waits for them, and re-layouts: 0.68 us -> 0.02 us
    pallas_call x1, Pallas kernels: 2.5 us -> 1.88 us  [far_call(): pl.pallas_call(functools.partial(far_kernel, levels, per, dim), grid_spec...]
    pallas_call x1, Pallas kernels: 1.88 us -> 1.39 us  [pick_call(): pl.pallas_call(functools.partial(pick_kernel, levels, per, dim), grid_spe...]
  transfers between devices with their start and end apart: 15 -> 15, of which waited for: 4 -> 5; matrix products, arithmetic and copies ran while one was open for 0% -> 0% of each run, Pallas kernels for 23% -> 26%
where the time goes in v7:
time: 42.2 us; the launch traced here: 42.1 us
  starting transfers between devices  14.6 us (35%)
  Pallas kernels  14.5 us (34%)
  waiting for transfers between devices  12.2 us (29%)
  between operations  0.75 us (2%)
    ppermute x14, starting transfers between devices, exchange(): return lax.ppermute(value, 'seq', [(i, i ^ bits) for i in range(count)])  9.96 us
    ppermute x14, waiting for transfers between devices, exchange(): return lax.ppermute(value, 'seq', [(i, i ^ bits) for i in range(count)])  7.03 us
    ppermute x1, waiting for transfers between devices, per_device(): lax.ppermute(out_grads[0], 'section', [(i, (i - 1) % sections) for i in r...  5.13 us
    ppermute x1, starting transfers between devices, per_device(): lax.ppermute(out_grads[0], 'section', [(i, (i - 1) % sections) for i in r...  4.67 us
    pallas_call x1, Pallas kernels, near_call(): pl.pallas_call(functools.partial(near_kernel, levels, per, dim), grid_spe...  4.47 us
    pallas_call x2, Pallas kernels, half_call(): pl.pallas_call(functools.partial(half_kernel, levels, per, dim, turn), gr...  3.41 us
    pallas_call x1, Pallas kernels, pre_call(): pl.pallas_call(functools.partial(pre_kernel, levels, per, dim), grid_spec...  1.95 us
    pallas_call x1, Pallas kernels, far_call(): pl.pallas_call(functools.partial(far_kernel, levels, per, dim), grid_spec...  1.88 us
  transfers between devices with their start and end apart: 15, of which 5 were waited for; matrix products, arithmetic and copies ran while one was open for 0% of the time, Pallas kernels for 26%

profile of v7, /device:TPU:0, one launch (start us, length us, event | category | flops | bytes accessed | tf_op | source)
XLA Modules:
  0.0 42.1 jit_solution(14464736287640610625)
XLA Ops:
  0.6 0.5 %collective-permute-start.1 = (bf16[128,2048]{1,0:T(8,128)(2,1)}, bf16[128,2048]{1,0:T(8,128)(2,1)S(1)}, u32[]{:S(2)}, u32[]{:S(2)}) collective-permute-start(bf16[128,2048]{1,0:T(8,128)(2,1)} %bitcast.13), channel_id=1, source_target_pairs={{0,4},{4,0},{8,12},{12,8},{16,20},{20,16},{24,28},{28,24},{1,5},{5... | collective-permute-start | bytes 1572872 | tf_op jit(solution)/shard_map/ppermute | solution.py:22
  1.1 0.1 collective-permute-start.2
  1.2 0.4 %collective-permute-start = (bf16[128,2048]{1,0:T(8,128)(2,1)}, bf16[128,2048]{1,0:T(8,128)(2,1)S(1)}, u32[]{:S(2)}, u32[]{:S(2)}) collective-permute-start(bf16[128,2048]{1,0:T(8,128)(2,1)} %bitcast.17), channel_id=1, source_target_pairs={{0,4},{4,0},{8,12},{12,8},{16,20},{20,16},{24,28},{28,24},{1,5},{5... | collective-permute-start | bytes 1572872 | tf_op jit(solution)/shard_map/ppermute | solution.py:22
  1.7 4.7 %collective-permute-start.5 = (bf16[128,2048]{1,0:T(8,128)(2,1)}, bf16[128,2048]{1,0:T(8,128)(2,1)S(1)}, u32[]{:S(2)}, u32[]{:S(2)}) collective-permute-start(bf16[128,2048]{1,0:T(8,128)(2,1)} %bitcast.23), channel_id=1, source_target_pairs={{0,3},{1,0},{2,1},{3,2},{4,7},{5,4},{6,5},{7,6},{8,11},{9,8},{10,9... | collective-permute-start | bytes 1572872 | tf_op jit(solution)/shard_map/ppermute | solution.py:536
  6.3 0.0 collective-permute-done.1.k1
  6.3 0.0 collective-permute-done.2.v1
  6.3 0.0 copy-start
  6.3 0.0 copy-start.1
  6.4 0.0 copy-start.2
  6.4 1.4 %pick_rows.1 = (bf16[96,2048]{1,0:T(8,128)(2,1)S(1)}, bf16[32,2048]{1,0:T(8,128)(2,1)S(1)}) custom-call(s32[1]{0:T(128)} %bitcast.core_ref, s32[3,16]{1,0:T(4,128)} %offs_ref.11, bf16[128,2048]{1,0:T(8,128)(2,1)} %bitcast.14, bf16[128,2048]{1,0:T(8,128)(2,1)} %bitcast.9, bf16[128,2048]{1,0:T(8,128)(2,1)S(1)} %collective-permute-done.1.k1, ...), custom_call_target="tpu_custom_call" | custom-call | tf_op jit(solution)/shard_map/pick_rows/pallas_call | solution.py:121
  7.8 0.0 copy-start.3
  7.8 2.5 %collective-permute-start.4 = (bf16[32,2048]{1,0:T(8,128)(2,1)S(1)}, bf16[32,2048]{1,0:T(8,128)(2,1)S(1)}, u32[]{:S(2)}, u32[]{:S(2)}) collective-permute-start(bf16[32,2048]{1,0:T(8,128)(2,1)S(1)} %get-tuple-element.40), channel_id=1, source_target_pairs={{0,24},{4,28},{8,16},{12,20},{16,8},{20,12},{24,0},{28,4},{1,25},{... | collective-permute-start | bytes 393224 | tf_op jit(solution)/shard_map/ppermute | solution.py:22
  10.3 0.5 %collective-permute-start.3 = (bf16[32,2048]{1,0:T(8,128)(2,1)S(1)}, bf16[32,2048]{1,0:T(8,128)(2,1)S(1)}, u32[]{:S(2)}, u32[]{:S(2)}) collective-permute-start(bf16[32,2048]{1,0:T(8,128)(2,1)S(1)} %get-tuple-element.40), channel_id=1, source_target_pairs={{0,16},{4,20},{8,24},{12,28},{16,0},{20,4},{24,8},{28,12},{1,17},{... | collective-permute-start | bytes 393224 | tf_op jit(solution)/shard_map/ppermute | solution.py:22
  10.8 0.5 %collective-permute-start.7 = (bf16[96,2048]{1,0:T(8,128)(2,1)S(1)}, bf16[96,2048]{1,0:T(8,128)(2,1)S(1)}, u32[]{:S(2)}, u32[]{:S(2)}) collective-permute-start(bf16[96,2048]{1,0:T(8,128)(2,1)S(1)} %get-tuple-element.44.own), channel_id=1, source_target_pairs={{0,8},{4,12},{8,0},{12,4},{16,24},{20,28},{24,16},{28,20},{1,9},{5... | collective-permute-start | bytes 1179656 | tf_op jit(solution)/shard_map/ppermute | solution.py:22
  11.3 0.0 collective-permute-done.q1
  11.3 0.0 copy-done
  11.3 0.0 copy-done.1
  11.3 0.0 copy-done.2
  11.4 0.0 copy-done.3
  11.4 1.9 %local_scores.1 = (bf16[256,2048]{1,0:T(8,128)(2,1)S(1)}, f32[8,2048]{1,0:T(8,128)S(1)}, bf16[128,2048]{1,0:T(8,128)(2,1)S(1)}, bf16[96,1024]{1,0:T(8,128)(2,1)S(1)}) custom-call(s32[3,16]{1,0:T(4,128)S(1)} %copy-done.3, s32[1]{0:T(128)} %bitcast.core_ref, bf16[128,2048]{1,0:T(8,128)(2,1)S(1)} %bitcast.18, bf16[128,2048]{1,0:T(8,128)(2,1)S(1)} %collective-permute-done.q1, ...), custom_call_target="tpu_custom_call" | custom-call | tf_op jit(solution)/shard_map/local_scores/pallas_call | solution.py:213
  13.3 5.1 %collective-permute-done.5.rows.g0 = bf16[128,2048]{1,0:T(8,128)(2,1)S(1)} collective-permute-done((bf16[128,2048]{1,0:T(8,128)(2,1)}, bf16[128,2048]{1,0:T(8,128)(2,1)S(1)}, u32[]{:S(2)}, u32[]{:S(2)}) %collective-permute-start.5) | collective-permute-done | bytes 524320 | tf_op jit(solution)/shard_map/ppermute | solution.py:536
  18.4 0.0 collective-permute-done.4.d
  18.4 0.0 collective-permute-done.3.y
  18.5 0.1 collective-permute-start.6
  18.6 1.5 %collective-permute-done.6.g1 = bf16[128,1024]{1,0:T(8,128)(2,1)S(1)} collective-permute-done((bf16[128,1024]{1,0:T(8,128)(2,1)S(1)}, bf16[128,1024]{1,0:T(8,128)(2,1)S(1)}, u32[]{:S(2)}, u32[]{:S(2)}) %collective-permute-start.6) | collective-permute-done | bytes 262176 | tf_op jit(solution)/shard_map/ppermute | solution.py:22
  20.1 1.4 %local_delta.1 = (bf16[96,1024]{1,0:T(8,128)(2,1)S(1)}, f32[8,2048]{1,0:T(8,128)S(1)}) custom-call(s32[3,16]{1,0:T(4,128)S(1)} %copy-done.3, s32[1]{0:T(128)} %bitcast.core_ref, bf16[256,2048]{1,0:T(8,128)(2,1)S(1)} %get-tuple-element.36.exps, bf16[128,2048]{1,0:T(8,128)(2,1)S(1)} %get-tuple-element.39.near, bf16[128,2048]{1,0:T(8,128)(2,1)S(1)} %bitcast.11, ...), custom_call_target="tpu_custom_call" | custom-call | tf_op jit(solution)/shard_map/local_delta/pallas_call | solution.py:261
  21.5 1.4 %collective-permute-done.7.x = bf16[96,2048]{1,0:T(8,128)(2,1)S(1)} collective-permute-done((bf16[96,2048]{1,0:T(8,128)(2,1)S(1)}, bf16[96,2048]{1,0:T(8,128)(2,1)S(1)}, u32[]{:S(2)}, u32[]{:S(2)}) %collective-permute-start.7) | collective-permute-done | bytes 393248 | tf_op jit(solution)/shard_map/ppermute | solution.py:22
  22.8 1.9 %far_levels.1 = (bf16[48,2048]{1,0:T(8,128)(2,1)S(1)}, bf16[48,2048]{1,0:T(8,128)(2,1)S(1)}, bf16[32,2048]{1,0:T(8,128)(2,1)S(1)}, bf16[16,2048]{1,0:T(8,128)(2,...) custom-call(s32[3,16]{1,0:T(4,128)S(1)} %copy-done.3, ...), custom_call_target="tpu_custom_call" | custom-call | tf_op jit(solution)/shard_map/far_levels/pallas_call | solution.py:385
  24.7 1.6 %collective-permute-start.8 = (bf16[48,2048]{1,0:T(8,128)(2,1)S(1)}, bf16[48,2048]{1,0:T(8,128)(2,1)S(1)}, u32[]{:S(2)}, u32[]{:S(2)}) collective-permute-start(bf16[48,2048]{1,0:T(8,128)(2,1)S(1)} %get-tuple-element.51), channel_id=1, source_target_pairs={{0,8},{4,12},{8,0},{12,4},{16,24},{20,28},{24,16},{28,20},{1,9},{5... | collective-permute-start | bytes 589832 | tf_op jit(solution)/shard_map/ppermute | solution.py:22
  26.3 0.0 collective-permute-start.9
  26.3 0.5 %collective-permute-start.12 = (bf16[32,2048]{1,0:T(8,128)(2,1)S(1)}, bf16[32,2048]{1,0:T(8,128)(2,1)S(1)}, u32[]{:S(2)}, u32[]{:S(2)}) collective-permute-start(bf16[32,2048]{1,0:T(8,128)(2,1)S(1)} %get-tuple-element.55), channel_id=1, source_target_pairs={{0,16},{4,20},{8,24},{12,28},{16,0},{20,4},{24,8},{28,12},{1,17},{... | collective-permute-start | bytes 393224 | tf_op jit(solution)/shard_map/ppermute | solution.py:22
  26.8 1.7 %collective-permute-start.10 = (bf16[16,2048]{1,0:T(8,128)(2,1)S(1)}, bf16[16,2048]{1,0:T(8,128)(2,1)S(1)}, u32[]{:S(2)}, u32[]{:S(2)}) collective-permute-start(bf16[16,2048]{1,0:T(8,128)(2,1)S(1)} %get-tuple-element.53), channel_id=1, source_target_pairs={{0,24},{4,28},{8,16},{12,20},{16,8},{20,12},{24,0},{28,4},{1,25},{... | collective-permute-start | bytes 196616 | tf_op jit(solution)/shard_map/ppermute | solution.py:22
  28.4 0.9 %collective-permute-start.11 = (bf16[16,2048]{1,0:T(8,128)(2,1)S(1)}, bf16[16,2048]{1,0:T(8,128)(2,1)S(1)}, u32[]{:S(2)}, u32[]{:S(2)}) collective-permute-start(bf16[16,2048]{1,0:T(8,128)(2,1)S(1)} %get-tuple-element.54), channel_id=1, source_target_pairs={{0,28},{4,24},{8,20},{12,16},{16,12},{20,8},{24,4},{28,0},{1,29},{... | collective-permute-start | bytes 196616 | tf_op jit(solution)/shard_map/ppermute | solution.py:22
  29.4 4.5 %near_levels.1 = (bf16[128,3072]{1,0:T(8,128)(2,1)S(1)}, bf16[128,3072]{1,0:T(8,128)(2,1)S(1)}) custom-call(s32[3,16]{1,0:T(4,128)S(1)} %copy-done.3, s32[1]{0:T(128)} %bitcast.core_ref, bf16[256,2048]{1,0:T(8,128)(2,1)S(1)} %get-tuple-element.36.exps, f32[8,2048]{1,0:T(8,128)S(1)} %get-tuple-element.47.stats2, ...), custom_call_target="tpu_custom_call" | custom-call | tf_op jit(solution)/shard_map/near_levels/pallas_call | solution.py:453
  33.8 3.8 %collective-permute-done.10.d = bf16[16,2048]{1,0:T(8,128)(2,1)S(1)} collective-permute-done((bf16[16,2048]{1,0:T(8,128)(2,1)S(1)}, bf16[16,2048]{1,0:T(8,128)(2,1)S(1)}, u32[]{:S(2)}, u32[]{:S(2)}) %collective-permute-start.10) | collective-permute-done | bytes 65568 | tf_op jit(solution)/shard_map/ppermute | solution.py:22
  37.7 0.0 collective-permute-done.11.d
  37.7 0.0 collective-permute-done.12.y
  37.7 0.0 collective-permute-done.8.x
  37.7 0.0 collective-permute-done.9.x
  37.7 0.6 %collective-permute-start.13 = (bf16[128,3072]{1,0:T(8,128)(2,1)S(1)}, bf16[128,3072]{1,0:T(8,128)(2,1)S(1)}, u32[]{:S(2)}, u32[]{:S(2)}) collective-permute-start(bf16[128,3072]{1,0:T(8,128)(2,1)S(1)} %get-tuple-element.56), channel_id=1, source_target_pairs={{0,4},{4,0},{8,12},{12,8},{16,20},{20,16},{24,28},{28,24},{1,5},{5... | collective-permute-start | bytes 2359304 | tf_op jit(solution)/shard_map/ppermute | solution.py:22
  38.3 0.1 collective-permute-start.14
  38.3 1.7 %add_own_half.1 = (bf16[128,2048]{1,0:T(8,128)(2,1)}, bf16[128,2048]{1,0:T(8,128)(2,1)}, bf16[128,2048]{1,0:T(8,128)(2,1)}) custom-call(s32[3,16]{1,0:T(4,128)S(1)} %copy-done.3, s32[1]{0:T(128)} %bitcast.core_ref, bf16[128,3072]{1,0:T(8,128)(2,1)S(1)} %get-tuple-element.59.base, bf16[48,2048]{1,0:T(8,128)(2,1)S(1)} %collective-permute-done.8.x, ...), custom_call_target="tpu_custom_call" | custom-call | tf_op jit(solution)/shard_map/add_own_half/pallas_call | solution.py:510
  40.0 0.3 collective-permute-done.14.y
  40.4 0.0 collective-permute-done.13.base
  40.4 1.7 %add_other_half.1 = (bf16[128,2048]{1,0:T(8,128)(2,1)}, bf16[128,2048]{1,0:T(8,128)(2,1)}, bf16[128,2048]{1,0:T(8,128)(2,1)}) custom-call(s32[3,16]{1,0:T(4,128)S(1)} %copy-done.3, s32[1]{0:T(128)} %bitcast.core_ref, bf16[128,3072]{1,0:T(8,128)(2,1)S(1)} %collective-permute-done.13.base, ...), custom_call_target="tpu_custom_call", output_to_operand_aliasing={{0}: (6, {}), {1}: (7, {}), {2}: (8, {})} | custom-call | tf_op jit(solution)/shard_map/add_other_half/pallas_call | solution.py:510
  (1 shorter events, 0.0 us)
Async XLA Ops:
  0.6 5.7 %collective-permute-start.1 = (bf16[128,2048]{1,0:T(8,128)(2,1)}, bf16[128,2048]{1,0:T(8,128)(2,1)S(1)}, u32[]{:S(2)}, u32[]{:S(2)}) collective-permute-start(bf16[128,2048]{1,0:T(8,128)(2,1)} %bitcast.13), channel_id=1, source_target_pairs={{0,4},{4,0},{8,12},{12,8},{16,20},{20,16},{24,28},{28,24},{1,5},{5... | collective-permute-start | bytes 1572872 | tf_op jit(solution)/shard_map/ppermute | solution.py:22
  1.1 5.2 %collective-permute-start.2 = (bf16[128,2048]{1,0:T(8,128)(2,1)}, bf16[128,2048]{1,0:T(8,128)(2,1)S(1)}, u32[]{:S(2)}, u32[]{:S(2)}) collective-permute-start(bf16[128,2048]{1,0:T(8,128)(2,1)} %bitcast.8), channel_id=1, source_target_pairs={{0,4},{4,0},{8,12},{12,8},{16,20},{20,16},{24,28},{28,24},{1,5},{5... | collective-permute-start | bytes 1572872 | tf_op jit(solution)/shard_map/ppermute | solution.py:22
  1.2 10.1 %collective-permute-start = (bf16[128,2048]{1,0:T(8,128)(2,1)}, bf16[128,2048]{1,0:T(8,128)(2,1)S(1)}, u32[]{:S(2)}, u32[]{:S(2)}) collective-permute-start(bf16[128,2048]{1,0:T(8,128)(2,1)} %bitcast.17), channel_id=1, source_target_pairs={{0,4},{4,0},{8,12},{12,8},{16,20},{20,16},{24,28},{28,24},{1,5},{5... | collective-permute-start | bytes 1572872 | tf_op jit(solution)/shard_map/ppermute | solution.py:22
  1.7 16.8 %collective-permute-start.5 = (bf16[128,2048]{1,0:T(8,128)(2,1)}, bf16[128,2048]{1,0:T(8,128)(2,1)S(1)}, u32[]{:S(2)}, u32[]{:S(2)}) collective-permute-start(bf16[128,2048]{1,0:T(8,128)(2,1)} %bitcast.23), channel_id=1, source_target_pairs={{0,3},{1,0},{2,1},{3,2},{4,7},{5,4},{6,5},{7,6},{8,11},{9,8},{10,9... | collective-permute-start | bytes 1572872 | tf_op jit(solution)/shard_map/ppermute | solution.py:536
  6.3 5.0 %copy-start = (bf16[1,128,2048]{2,1,0:T(8,128)(2,1)S(1)}, bf16[1,128,2048]{2,1,0:T(8,128)(2,1)}, u32[]{:S(2)}) copy-start(bf16[1,128,2048]{2,1,0:T(8,128)(2,1)} %param.7) | copy-start | bytes 1572868
  6.3 5.0 %copy-start.1 = (bf16[1,128,2048]{2,1,0:T(8,128)(2,1)S(1)}, bf16[1,128,2048]{2,1,0:T(8,128)(2,1)}, u32[]{:S(2)}) copy-start(bf16[1,128,2048]{2,1,0:T(8,128)(2,1)} %param.6) | copy-start | bytes 1572868
  6.4 5.0 %copy-start.2 = (bf16[1,128,2048]{2,1,0:T(8,128)(2,1)S(1)}, bf16[1,128,2048]{2,1,0:T(8,128)(2,1)}, u32[]{:S(2)}) copy-start(bf16[1,128,2048]{2,1,0:T(8,128)(2,1)} %param.5) | copy-start | bytes 1572868
  7.8 3.6 %copy-start.3 = (s32[3,16]{1,0:T(4,128)S(1)}, s32[3,16]{1,0:T(4,128)}, u32[]{:S(2)}) copy-start(s32[3,16]{1,0:T(4,128)} %offs_ref.11) | copy-start | bytes 580
  7.8 10.7 %collective-permute-start.4 = (bf16[32,2048]{1,0:T(8,128)(2,1)S(1)}, bf16[32,2048]{1,0:T(8,128)(2,1)S(1)}, u32[]{:S(2)}, u32[]{:S(2)}) collective-permute-start(bf16[32,2048]{1,0:T(8,128)(2,1)S(1)} %get-tuple-element.40), channel_id=1, source_target_pairs={{0,24},{4,28},{8,16},{12,20},{16,8},{20,12},{24,0},{28,4},{1,25},{... | collective-permute-start | bytes 393224 | tf_op jit(solution)/shard_map/ppermute | solution.py:22
  10.3 8.2 %collective-permute-start.3 = (bf16[32,2048]{1,0:T(8,128)(2,1)S(1)}, bf16[32,2048]{1,0:T(8,128)(2,1)S(1)}, u32[]{:S(2)}, u32[]{:S(2)}) collective-permute-start(bf16[32,2048]{1,0:T(8,128)(2,1)S(1)} %get-tuple-element.40), channel_id=1, source_target_pairs={{0,16},{4,20},{8,24},{12,28},{16,0},{20,4},{24,8},{28,12},{1,17},{... | collective-permute-start | bytes 393224 | tf_op jit(solution)/shard_map/ppermute | solution.py:22
  10.8 12.0 %collective-permute-start.7 = (bf16[96,2048]{1,0:T(8,128)(2,1)S(1)}, bf16[96,2048]{1,0:T(8,128)(2,1)S(1)}, u32[]{:S(2)}, u32[]{:S(2)}) collective-permute-start(bf16[96,2048]{1,0:T(8,128)(2,1)S(1)} %get-tuple-element.44.own), channel_id=1, source_target_pairs={{0,8},{4,12},{8,0},{12,4},{16,24},{20,28},{24,16},{28,20},{1,9},{5... | collective-permute-start | bytes 1179656 | tf_op jit(solution)/shard_map/ppermute | solution.py:22
  18.5 1.6 %collective-permute-start.6 = (bf16[128,1024]{1,0:T(8,128)(2,1)S(1)}, bf16[128,1024]{1,0:T(8,128)(2,1)S(1)}, u32[]{:S(2)}, u32[]{:S(2)}) collective-permute-start(bf16[128,1024]{1,0:T(8,128)(2,1)S(1)} %pack_half.1), channel_id=1, source_target_pairs={{0,4},{4,0},{8,12},{12,8},{16,20},{20,16},{24,28},{28,24},{1,5},{5... | collective-permute-start | bytes 786440 | tf_op jit(solution)/shard_map/ppermute | solution.py:22
  24.7 12.9 %collective-permute-start.8 = (bf16[48,2048]{1,0:T(8,128)(2,1)S(1)}, bf16[48,2048]{1,0:T(8,128)(2,1)S(1)}, u32[]{:S(2)}, u32[]{:S(2)}) collective-permute-start(bf16[48,2048]{1,0:T(8,128)(2,1)S(1)} %get-tuple-element.51), channel_id=1, source_target_pairs={{0,8},{4,12},{8,0},{12,4},{16,24},{20,28},{24,16},{28,20},{1,9},{5... | collective-permute-start | bytes 589832 | tf_op jit(solution)/shard_map/ppermute | solution.py:22
  26.3 11.4 %collective-permute-start.9 = (bf16[48,2048]{1,0:T(8,128)(2,1)S(1)}, bf16[48,2048]{1,0:T(8,128)(2,1)S(1)}, u32[]{:S(2)}, u32[]{:S(2)}) collective-permute-start(bf16[48,2048]{1,0:T(8,128)(2,1)S(1)} %get-tuple-element.52), channel_id=1, source_target_pairs={{0,12},{4,8},{8,4},{12,0},{16,28},{20,24},{24,20},{28,16},{1,13},{... | collective-permute-start | bytes 589832 | tf_op jit(solution)/shard_map/ppermute | solution.py:22
  26.3 11.4 %collective-permute-start.12 = (bf16[32,2048]{1,0:T(8,128)(2,1)S(1)}, bf16[32,2048]{1,0:T(8,128)(2,1)S(1)}, u32[]{:S(2)}, u32[]{:S(2)}) collective-permute-start(bf16[32,2048]{1,0:T(8,128)(2,1)S(1)} %get-tuple-element.55), channel_id=1, source_target_pairs={{0,16},{4,20},{8,24},{12,28},{16,0},{20,4},{24,8},{28,12},{1,17},{... | collective-permute-start | bytes 393224 | tf_op jit(solution)/shard_map/ppermute | solution.py:22
  26.8 10.9 %collective-permute-start.10 = (bf16[16,2048]{1,0:T(8,128)(2,1)S(1)}, bf16[16,2048]{1,0:T(8,128)(2,1)S(1)}, u32[]{:S(2)}, u32[]{:S(2)}) collective-permute-start(bf16[16,2048]{1,0:T(8,128)(2,1)S(1)} %get-tuple-element.53), channel_id=1, source_target_pairs={{0,24},{4,28},{8,16},{12,20},{16,8},{20,12},{24,0},{28,4},{1,25},{... | collective-permute-start | bytes 196616 | tf_op jit(solution)/shard_map/ppermute | solution.py:22
  28.4 9.2 %collective-permute-start.11 = (bf16[16,2048]{1,0:T(8,128)(2,1)S(1)}, bf16[16,2048]{1,0:T(8,128)(2,1)S(1)}, u32[]{:S(2)}, u32[]{:S(2)}) collective-permute-start(bf16[16,2048]{1,0:T(8,128)(2,1)S(1)} %get-tuple-element.54), channel_id=1, source_target_pairs={{0,28},{4,24},{8,20},{12,16},{16,12},{20,8},{24,4},{28,0},{1,29},{... | collective-permute-start | bytes 196616 | tf_op jit(solution)/shard_map/ppermute | solution.py:22
  37.7 2.7 %collective-permute-start.13 = (bf16[128,3072]{1,0:T(8,128)(2,1)S(1)}, bf16[128,3072]{1,0:T(8,128)(2,1)S(1)}, u32[]{:S(2)}, u32[]{:S(2)}) collective-permute-start(bf16[128,3072]{1,0:T(8,128)(2,1)S(1)} %get-tuple-element.56), channel_id=1, source_target_pairs={{0,4},{4,0},{8,12},{12,8},{16,20},{20,16},{24,28},{28,24},{1,5},{5... | collective-permute-start | bytes 2359304 | tf_op jit(solution)/shard_map/ppermute | solution.py:22
  38.3 2.1 %collective-permute-start.14 = (bf16[32,2048]{1,0:T(8,128)(2,1)S(1)}, bf16[32,2048]{1,0:T(8,128)(2,1)S(1)}, u32[]{:S(2)}, u32[]{:S(2)}) collective-permute-start(bf16[32,2048]{1,0:T(8,128)(2,1)S(1)} %collective-permute-done.12.y), channel_id=1, source_target_pairs={{0,4},{4,0},{8,12},{12,8},{16,20},{20,16},{24,28},{28,24},{1,5},{5... | collective-permute-start | bytes 393224 | tf_op jit(solution)/shard_map/ppermute | solution.py:22

commit v8 on v7

--- a/solution.py
+++ b/solution.py
@@ -54,11 +54,14 @@
     return jnp.concatenate(parts, axis=1).astype(BF16)
 
 
-def pack_kernel(core_ref, rows, out):
-    out[...] = rows[...]
-
-
-def pack_call(core, rows):
+def pack_kernel(core_ref, rows, *outs):
+    lo = 0
+    for out in outs:
+        out[...] = rows[:, lo : lo + out.shape[1]]
+        lo += out.shape[1]
+
+
+def pack_call(core, rows, sizes):
     tok, width = rows.shape
     half = width // 2
     return pl.pallas_call(
@@ -67,16 +70,16 @@
             num_scalar_prefetch=1,
             grid=(1,),
             in_specs=[pl.BlockSpec((tok, half), lambda i, c: (0, 1 - c[0]))],
-            out_specs=pl.BlockSpec((tok, half), lambda i, c: (0, 0)),
+            out_specs=[pl.BlockSpec((tok, n), lambda i, c: (0, 0)) for n in sizes],
         ),
-        out_shape=jax.ShapeDtypeStruct((tok, half), BF16),
+        out_shape=[jax.ShapeDtypeStruct((tok, n), BF16) for n in sizes],
         compiler_params=params(),
         name="pack_half",
     )(core, rows)
 
 
 def pick_kernel(
-    levels, per, dim, core_ref, offs, k0, v0, k1, v1, both_ref, three_ref, offs_ref, own_k, own_v, sems
+    levels, per, dim, core_ref, offs, k0, v0, k1, v1, two_ref, three_ref, offs_ref, own_k, own_v, sems
 ):
     tok = k1.shape[0]
     n2, n3 = tok // 4, tok // 8
@@ -98,8 +101,7 @@
             cols = slice(h * dim, (h + 1) * dim)
             out = slice(2 * h * dim, 2 * (h + 1) * dim)
             got = dot(picks[h], side(keys[:, cols], values[:, cols])).astype(BF16)
-            both_ref[lo * n2 : (lo + 1) * n2, out] = got[:n2]
-            both_ref[2 * n2 + lo * n3 : 2 * n2 + (lo + 1) * n3, out] = got[n2:]
+            two_ref[lo * n2 : (lo + 1) * n2, out] = got[:n2]
             three_ref[lo * n3 : (lo + 1) * n3, out] = got[n2:]
 
     work(k1, v1, 1)
@@ -117,7 +119,7 @@
     def out(rows):
         return pl.BlockSpec((rows, 2 * per * dim), lambda i, c: (0, 0))
 
-    rows = [tok // 2 + tok // 4, tok // 4]
+    rows = [tok // 2, tok // 4]
     return pl.pallas_call(
         functools.partial(pick_kernel, levels, per, dim),
         grid_spec=pltpu.PrefetchScalarGridSpec(
@@ -166,7 +168,7 @@
 
 
 def pre_kernel(
-    levels, per, dim, offs_ref, core_ref, q0, q1, k0, k1, v0, v1, exps, stats, near, selq
+    levels, per, dim, offs_ref, core_ref, q0, q1, k0, k1, v0, v1, exp0, exp1, stats, near, selq
 ):
     tok = q0.shape[0]
     n1 = tok // 2
@@ -189,7 +191,8 @@
         )
         top = jnp.max(s, axis=0, keepdims=True)
         e = jnp.exp(s - top)
-        exps[:, lanes] = e.astype(BF16)
+        for half, ref in enumerate((exp0, exp1)):
+            ref[:, h * tok : (h + 1) * tok] = e[:, half * tok : (half + 1) * tok].astype(BF16)
         stats[0:1, lanes] = top
         stats[1:2, lanes] = jnp.sum(e, axis=0, keepdims=True)
 
@@ -209,7 +212,7 @@
             jax.ShapeDtypeStruct((rows, half * lanes), kind),
         )
 
-    outs = [out(2 * tok, 2 * tok), out(8, 2 * tok, F32), out(tok, 2 * dim), out(sel, dim)]
+    outs = [out(2 * tok, tok), out(2 * tok, tok), out(8, 2 * tok, F32), out(tok, 2 * dim), out(sel, dim)]
     return pl.pallas_call(
         functools.partial(pre_kernel, levels, per, dim),
         grid_spec=pltpu.PrefetchScalarGridSpec(
@@ -224,58 +227,62 @@
     )(offsets, core, *raw)
 
 
-def grad_kernel(levels, per, dim, offs_ref, core_ref, exps, near, v0, v1, g0, g1, selg, local):
-    tok = g0.shape[0]
+def local_delta(exps, values, ones, grads):
+    tok = values.shape[0]
+    p0, p1 = dot_nt(values, grads), dot_nt(ones, grads)
+    both = exps[:tok].astype(F32) * p0 + exps[tok:].astype(F32) * p1
+    return jnp.sum(both, axis=0, keepdims=True)
+
+
+def grad_kernel(levels, per, dim, offs_ref, core_ref, exps, near, values, grads, selg, local):
+    tok = values.shape[0]
     first = core_ref[0] * per
     each = range(per)
     cols = [slice(h * dim, (h + 1) * dim) for h in each]
-    lanes = [slice(2 * h * tok, 2 * (h + 1) * tok) for h in each]
-    picks = [pick_matrix(offs_ref, first + h, 2, levels, tok) for h in each]
     for h in each:
-        rows = stack(dot(picks[h], g0[:, cols[h]]), dot(picks[h], g1[:, cols[h]]))
-        selg[:, cols[h]] = rows.astype(BF16)
+        pick = pick_matrix(offs_ref, first + h, 2, levels, tok)
+        selg[:, cols[h]] = dot(pick, grads[:, cols[h]]).astype(BF16)
     for h in each:
+        here = slice(h * tok, (h + 1) * tok)
         vc = slice((2 * h + 1) * dim, (2 * h + 2) * dim)
-        gra0, gra1 = g0[:, cols[h]], g1[:, cols[h]]
-        p0 = side(dot_nt(v0[:, cols[h]], gra0), dot_nt(v1[:, cols[h]], gra1))
-        p1 = dot_nt(near[:, vc], stack(gra0, gra1))
-        ex = exps[:, lanes[h]]
-        both = ex[:tok].astype(F32) * p0 + ex[tok:].astype(F32) * p1
-        local[0:1, lanes[h]] = jnp.sum(both, axis=0, keepdims=True)
-
-
-def grad_call(offsets, core, mid, raw, grads, dim):
-    tok, width = raw[0].shape
+        local[0:1, here] = local_delta(
+            exps[:, here], values[:, cols[h]], near[:, vc], grads[:, cols[h]]
+        )
+
+
+def grad_call(offsets, core, exps, near, values, grads, dim):
+    tok, width = values.shape
     levels, heads = offsets.shape
     per = heads // 2
     raw_spec = own_spec(tok, per * dim, 1)
-    sel = 2 * (tok // 4 + tok // 8)
 
     def whole(a):
         return pl.BlockSpec(a.shape, lambda i, o, c: (0, 0))
 
     outs = [
-        jax.ShapeDtypeStruct((sel, per * dim), BF16),
-        jax.ShapeDtypeStruct((8, per * 2 * tok), F32),
+        jax.ShapeDtypeStruct((tok // 4 + tok // 8, per * dim), BF16),
+        jax.ShapeDtypeStruct((8, per * tok), F32),
     ]
     return pl.pallas_call(
         functools.partial(grad_kernel, levels, per, dim),
         grid_spec=pltpu.PrefetchScalarGridSpec(
             num_scalar_prefetch=2,
             grid=(1,),
-            in_specs=[whole(a) for a in mid] + [raw_spec] * 3 + [whole(grads[1])],
+            in_specs=[whole(exps), whole(near), raw_spec, raw_spec],
             out_specs=[whole(a) for a in outs],
         ),
         out_shape=outs,
         compiler_params=params(),
-        name="local_delta",
-    )(offsets, core, *mid, *raw, *grads)
+        name="own_delta",
+    )(offsets, core, exps, near, values, grads)
 
 
 def far_kernel(
-    levels, per, dim, offs_ref, core_ref, stats, selq, selg, local, own, x, y, d,
-    xa, xb, yab, da, db, ngrad, dqt, stats2,
+    levels, per, dim, offs_ref, core_ref, stats, selq, selg0, local0, exp1, near, v1,
+    own2, x2, own3, x3, y3, d3, *refs
 ):
+    xa, xb, xab, yab, dab, ngrad, dqt, stats2 = refs[-8:]
+    g1 = side(*(ref[...] for ref in refs[:-8]))
     tok = dqt.shape[0]
     n1, n2, n3 = tok // 2, tok // 4, tok // 8
     sel = n2 + n3
@@ -293,17 +300,22 @@
     lanes = [slice(2 * h * tok, 2 * (h + 1) * tok) for h in each]
 
     def rows(c):
-        lo = 2 * n2
-        parts = own[:lo, c], x[:lo, c], own[lo:, c], x[lo:, c], y[:, c], d[:, c]
-        return stack(*parts)
+        return stack(*(ref[:, c] for ref in (own2, x2, own3, x3, y3, d3)))
 
     def level_pick(value):
         return jnp.where(is2, value[:tok], value[tok:])
 
     picks = [pick_matrix(offs_ref, first + h, 2, levels, tok) for h in each]
+    selg = [
+        stack(selg0[:, cols[h]], dot(picks[h], g1[:, cols[h]]).astype(BF16)) for h in each
+    ]
     keys = [rows(kc[h]) for h in each]
     s = [level_pick(dot_nt(keys[h], selq[:, cols[h]])) * scale for h in each]
-    p = [level_pick(dot_nt(rows(vc[h]), selg[:, cols[h]])) for h in each]
+    p = [level_pick(dot_nt(rows(vc[h]), selg[h])) for h in each]
+    local1 = [
+        local_delta(exp1[:, h * tok : (h + 1) * tok], v1[:, cols[h]], near[:, vc[h]], g1[:, cols[h]])
+        for h in each
+    ]
     top = [jnp.max(a, axis=0, keepdims=True) for a in s]
     e = [jnp.exp(a - b) for a, b in zip(s, top)]
     size = [jnp.sum(a, axis=0, keepdims=True) for a in e]
@@ -332,7 +344,7 @@
         a1, a2, a3 = jnp.exp(t1 - high), jnp.exp(t2 - high), jnp.exp(t3 - high)
         inv = 1.0 / (a1 * z1 + a2 * z2 + a3 * z3)
         f1, f2, f3 = a1 * inv, a2 * inv, a3 * inv
-        delta = f1 * local[0:1, lanes[h]] + f2 * dot2 + f3 * dot3
+        delta = f1 * side(local0[0:1, h * tok : (h + 1) * tok], local1[h]) + f2 * dot2 + f3 * dot3
         stats2[0:1, lanes[h]] = f1
         stats2[1:2, lanes[h]] = delta
         terms = stack(*split(f2, 2), *split(f3, 2), *split(delta, 2))
@@ -349,22 +361,20 @@
         dsm.append(apart(w * (p[h] - (b[4:5] + b[5:6]))))
         wm.append(apart(w))
     dk = [dot(dsm[h], selq[:, cols[h]]) * scale for h in each]
-    dv = [dot(wm[h], selg[:, cols[h]]) for h in each]
+    dv = [dot(wm[h], selg[h]) for h in each]
     for h in each:
         dkv = side(dk[h], dv[h]).astype(BF16)
-        xa[:n2, wide[h]] = dkv[2 * n2 : 3 * n2]
-        xb[:n2, wide[h]] = dkv[3 * n2 : 4 * n2]
+        xa[:, wide[h]] = dkv[2 * n2 : 3 * n2]
+        xb[:, wide[h]] = dkv[3 * n2 : 4 * n2]
         third = [dkv[tok + i * n3 : tok + (i + 1) * n3] for i in range(8)]
-        xa[n2:, wide[h]] = third[2]
-        xb[n2:, wide[h]] = third[3]
+        xab[:, wide[h]] = stack(third[2], third[3])
         yab[:, wide[h]] = stack(third[4], third[5])
-        da[:, wide[h]] = third[6]
-        db[:, wide[h]] = third[7]
+        dab[:, wide[h]] = stack(third[6], third[7])
         ngrad[:, wide[h]] = stack(dkv[:n2], third[0], dkv[n2 : 2 * n2], third[1])
         dqt[:, h * dim : h * dim + 2 * sel] = dot(keys[h].T, dsm[h]).astype(BF16)
 
 
-def far_call(offsets, core, mid, far, tok, dim):
+def far_call(offsets, core, mid, value, far, tok, dim):
     levels, heads = offsets.shape
     half = heads // 2
     per = 8
@@ -380,62 +390,77 @@
             jax.ShapeDtypeStruct((rows, half * lanes), kind),
         )
 
-    outs = [out(n2 + n3, 2 * dim)] * 2 + [out(2 * n3, 2 * dim)] + [out(n3, 2 * dim)] * 2
+    outs = [out(n2, 2 * dim)] * 2 + [out(2 * n3, 2 * dim)] * 3
     outs += [out(2 * (n2 + n3), 2 * dim), out(dim, dim), out(8, 2 * tok, F32)]
     return pl.pallas_call(
         functools.partial(far_kernel, levels, per, dim),
         grid_spec=pltpu.PrefetchScalarGridSpec(
             num_scalar_prefetch=2,
             grid=(steps,),
-            in_specs=[mid_spec(a) for a in mid + far],
+            in_specs=[mid_spec(a) for a in mid]
+            + [own_spec(tok, per * dim, steps)]
+            + [mid_spec(a) for a in far],
             out_specs=[o[0] for o in outs],
         ),
         out_shape=[o[1] for o in outs],
         compiler_params=params(),
         name="far_levels",
-    )(offsets, core, *mid, *far)
+    )(offsets, core, *mid, value, *far)
 
 
 def near_kernel(
-    levels, per, dim, offs_ref, core_ref, exps, stats2, near, ngrad, dqt,
-    q0, q1, k0, k1, v0, v1, g0, g1, mine, other,
+    levels, per, dim, offs_ref, core_ref, exp0, exp1, stats2, near, ngrad, dqt,
+    q0, q1, k0, k1, v0, v1, g0, *refs,
 ):
+    mine, other = refs[-2:]
+    g1 = side(*(ref[...] for ref in refs[:-2]))
     tok = q0.shape[0]
     n1 = tok // 2
     sel = tok // 4 + tok // 8
     scale = dim**-0.5
     heads = per * pl.num_programs(0)
-    for h in range(per):
-        head = core_ref[0] * heads + pl.program_id(0) * per + h
-        pick = pick_matrix(offs_ref, head, 2, levels, tok)
-        place = place_matrix(offs_ref, head, 1, levels, tok)
-        cols = slice(h * dim, (h + 1) * dim)
-        kc = slice(2 * h * dim, (2 * h + 1) * dim)
-        vc = slice((2 * h + 1) * dim, (2 * h + 2) * dim)
-        wide = slice(2 * h * dim, 2 * (h + 1) * dim)
-        lanes = slice(2 * h * tok, 2 * (h + 1) * tok)
-        que0, que1, gra0, gra1 = q0[:, cols], q1[:, cols], g0[:, cols], g1[:, cols]
-        que, gra = stack(que0, que1), stack(gra0, gra1)
-        p0 = side(dot_nt(v0[:, cols], gra0), dot_nt(v1[:, cols], gra1))
-        p = stack(p0, dot_nt(near[:tok, vc], gra))
-        w = exps[:, lanes].astype(F32) * stats2[0:1, lanes]
-        wb = w.astype(BF16)
-        ds = (w * (p - stats2[1:2, lanes])).astype(BF16)
-        dkv1 = side(dot(ds[tok:], que) * scale, dot(wb[tok:], gra)).astype(BF16)
-        ds0, ds1 = ds[:tok, :tok], ds[:tok, tok:]
-        kv0 = side(dot(ds0, que0) * scale, dot(wb[:tok, :tok], gra0))
-        kv1 = side(dot(ds1, que1) * scale, dot(wb[:tok, tok:], gra1))
-        kv0 += dot(place, stack(dkv1[:n1], ngrad[:sel, wide]))
-        kv1 += dot(place, stack(dkv1[n1:], ngrad[sel:, wide]))
-        dqa = dot(near[:tok, kc].T, ds[tok:])
-        dq0 = dqa[:, :tok] + dot(k0[:, cols].T, ds0)
-        dq1 = dqa[:, tok:] + dot(k1[:, cols].T, ds1)
-        dq0 += dot(dqt[:, h * dim : h * dim + sel], pick)
-        dq1 += dot(dqt[:, h * dim + sel : h * dim + 2 * sel], pick)
-        for ref, dq, kv in ((mine, dq0, kv0), (other, dq1, kv1)):
-            lo = 3 * h * dim
-            ref[:, lo : lo + dim] = (dq * scale).T.astype(BF16)
-            ref[:, lo + dim : lo + 3 * dim] = kv.astype(BF16)
+    first = core_ref[0] * heads + pl.program_id(0) * per
+    for lo in range(0, per, 4):
+        each = range(lo, lo + 4)
+        cols = {h: slice(h * dim, (h + 1) * dim) for h in each}
+        vc = {h: slice((2 * h + 1) * dim, (2 * h + 2) * dim) for h in each}
+        gra = {h: stack(g0[:, cols[h]], g1[:, cols[h]]) for h in each}
+        que = {h: stack(q0[:, cols[h]], q1[:, cols[h]]) for h in each}
+        wb, ds = {}, {}
+        for h in each:
+            lanes = slice(2 * h * tok, 2 * (h + 1) * tok)
+            here = slice(h * tok, (h + 1) * tok)
+            p0 = dot_nt(v0[:, cols[h]], gra[h][:tok])
+            p1 = dot_nt(v1[:, cols[h]], gra[h][tok:])
+            p = stack(side(p0, p1), dot_nt(near[:tok, vc[h]], gra[h]))
+            w = side(exp0[:, here], exp1[:, here]).astype(F32) * stats2[0:1, lanes]
+            wb[h] = w.astype(BF16)
+            ds[h] = (w * (p - stats2[1:2, lanes])).astype(BF16)
+        dkv1 = {
+            h: side(dot(ds[h][tok:], que[h]) * scale, dot(wb[h][tok:], gra[h])).astype(BF16)
+            for h in each
+        }
+        for ref, block, keys in ((mine, 0, k0), (other, 1, k1)):
+            at = slice(block * tok, (block + 1) * tok)
+            picked = slice(block * n1, (block + 1) * n1)
+            grads = slice(block * sel, (block + 1) * sel)
+            kv, dq = {}, {}
+            for h in each:
+                place = place_matrix(offs_ref, first + h, 1, levels, tok)
+                wide = slice(2 * h * dim, 2 * (h + 1) * dim)
+                d0, w0 = ds[h][:tok, at], wb[h][:tok, at]
+                kv[h] = side(dot(d0, que[h][at]) * scale, dot(w0, gra[h][at]))
+                kv[h] += dot(place, stack(dkv1[h][picked], ngrad[grads, wide]))
+            for h in each:
+                pick = pick_matrix(offs_ref, first + h, 2, levels, tok)
+                kc = slice(2 * h * dim, (2 * h + 1) * dim)
+                far = dqt[:, h * dim + block * sel : h * dim + (block + 1) * sel]
+                both = stack(keys[:, cols[h]], near[:tok, kc])
+                dq[h] = dot(both.T, ds[h][:, at]) + dot(far, pick)
+            for h in each:
+                to = 3 * h * dim
+                ref[:, to : to + dim] = (dq[h] * scale).T.astype(BF16)
+                ref[:, to + dim : to + 3 * dim] = kv[h].astype(BF16)
 
 
 def near_call(offsets, core, mid, raw, grads, dim):
@@ -455,7 +480,8 @@
         grid_spec=pltpu.PrefetchScalarGridSpec(
             num_scalar_prefetch=2,
             grid=(steps,),
-            in_specs=[mid_spec(a) for a in mid] + [raw_spec] * 7 + [mid_spec(grads[1])],
+            in_specs=[mid_spec(a) for a in mid] + [raw_spec] * 7
+            + [mid_spec(a) for a in grads[1:]],
             out_specs=[out_spec] * 2,
         ),
         out_shape=[jax.ShapeDtypeStruct((tok, 3 * half * dim), BF16)] * 2,
@@ -464,7 +490,24 @@
     )(offsets, core, *mid, *raw, *grads)
 
 
-def half_kernel(levels, per, dim, turn, offs_ref, core_ref, base, x, y, d, *refs):
+def sum_kernel(here, there, first, second):
+    total = (here[...].astype(F32) + there[...].astype(F32)).astype(BF16)
+    rows = first.shape[0]
+    first[...] = total[:rows]
+    second[...] = total[rows:]
+
+
+def sum_call(here, there):
+    rows, cols = here.shape
+    return pl.pallas_call(
+        sum_kernel,
+        out_shape=[jax.ShapeDtypeStruct((rows // 2, cols), BF16)] * 2,
+        compiler_params=params(),
+        name="add_diagonal",
+    )(here, there)
+
+
+def half_kernel(levels, per, dim, turn, offs_ref, core_ref, base, x, y, x3, *refs):
     outs, (held, sems) = refs[-5:-2], refs[-2:]
     tok = base.shape[0]
     n2, n3 = tok // 4, tok // 8
@@ -473,7 +516,7 @@
     each = range(per)
     place = [place_matrix(offs_ref, first + h, 2, levels, tok) for h in each]
     mine = y[n3:] if turn else y[:n3]
-    third = (x[n2:].astype(F32) + mine.astype(F32) + d[...].astype(F32)).astype(BF16)
+    third = (x3[...].astype(F32) + mine.astype(F32)).astype(BF16)
     src = [slice(2 * h * dim, 2 * (h + 1) * dim) for h in each]
     copies = []
 
@@ -488,7 +531,7 @@
     send(0, 0, per)
     for lo in range(0, per, group):
         heads = range(lo, lo + group)
-        more = [dot(place[h], stack(x[:n2, src[h]], third[:, src[h]])) for h in heads]
+        more = [dot(place[h], stack(x[:, src[h]], third[:, src[h]])) for h in heads]
         for h, add in zip(heads, more):
             cols = slice(h * dim, (h + 1) * dim)
             at = (3 * h + 1) * dim
@@ -538,28 +581,36 @@
     )
     q_oth, k_oth, v_oth = exchange(q, 1), exchange(k, 1), exchange(v, 1)
     kept = [pltpu.with_memory_space_constraint(a, pltpu.HBM) for a in (k, v)]
-    both, three = pick_call(
+    two, three = pick_call(
         pltpu.with_memory_space_constraint(offsets, pltpu.HBM), core, kept, [k_oth, v_oth], dim
     )
-    x, y, d = exchange(both, 2), exchange(three, 4), exchange(three, 6)
+    x3, y3, x2 = exchange(three, 2), exchange(three, 4), exchange(two, 2)
+    x3, y3 = lax.optimization_barrier((x3, y3))
+    d3 = exchange(x3, 4)
     raw = [q, q_oth, k, k_oth, v, v_oth]
     pre = pre_call(offsets, core, raw, dim)
-    y, d, grads = lax.optimization_barrier((y, d, grads, pre[1]))[:3]
-    grads = [grads, exchange(pack_call(core, grads), 1)]
-    exps, stats, near, selq = pre
-    selg, local = grad_call(offsets, core, [exps, near], [v, v_oth], grads, dim)
-    xa, xb, yab, da, db, ngrad, dqt, stats2 = far_call(
-        offsets, core, [stats, selq, selg, local], [both, x, y, d], q.shape[0], dim
+    exp0, exp1, stats, near, selq = pre
+    grads = lax.optimization_barrier((grads, stats))[0]
+    sel = grad_call(offsets, core, exp0, near, v, grads, dim)
+    half = heads // 2
+    cuts = [half * i // 3 for i in range(4)]
+    sizes = [(hi - lo) * dim for lo, hi in zip(cuts, cuts[1:])]
+    other = [exchange(piece, 1) for piece in pack_call(core, grads, sizes)]
+    other = lax.optimization_barrier((*other, sel[1]))[:-1]
+    xa, xb, xab, yab, dab, ngrad, dqt, stats2 = far_call(
+        offsets, core, [stats, selq, *sel, exp1, near], v_oth,
+        [two, x2, three, x3, y3, d3, *other], q.shape[0], dim,
     )
-    xa, xb, da, db = exchange(xa, 2), exchange(xb, 3), exchange(da, 6), exchange(db, 7)
-    y = exchange(yab, 4)
+    thirds = sum_call(xab, exchange(dab, 4))
+    xa, xb, y = exchange(xa, 2), exchange(xb, 3), exchange(yab, 4)
+    xa3, xb3 = exchange(thirds[0], 2), exchange(thirds[1], 3)
     yy = exchange(y, 1)
     mine, other = near_call(
-        offsets, core, [exps, stats2, near, ngrad, dqt], raw, grads, dim
+        offsets, core, [exp0, exp1, stats2, near, ngrad, dqt], raw, [grads, *other], dim
     )
-    other, xa, xb, da, db, y = lax.optimization_barrier((other, xa, xb, da, db, y))
-    halves = half_call(offsets, core, [mine, xa, y, da], [], dim)
-    dq, dk, dv = half_call(offsets, core, [exchange(other, 1), xb, yy, db], halves, dim)
+    other, xa, xb, xa3, xb3, y = lax.optimization_barrier((other, xa, xb, xa3, xb3, y))
+    halves = half_call(offsets, core, [mine, xa, y, xa3], [], dim)
+    dq, dk, dv = half_call(offsets, core, [exchange(other, 1), xb, yy, xb3], halves, dim)
     return dq[None], dk[None], dv[None]
 
 

time: 42.2 us -> 39.2 us (0.929)
  waiting for transfers between devices: 12.2 us -> 7.71 us
  starting transfers between devices: 14.6 us -> 17.2 us
  Pallas kernels: 14.5 us -> 13.4 us
    ppermute x1, waiting for transfers between devices: 5.13 us -> 0.2 us  [per_device(): lax.ppermute(out_grads[0], 'section', [(i, (i - 1) % sections) for i in r...]
    ppermute x14 -> x18, starting transfers between devices: 9.96 us -> 12.5 us  [exchange(): return lax.ppermute(value, 'seq', [(i, i ^ bits) for i in range(count)])]
    pallas_call x1, Pallas kernels: 4.47 us -> 2.94 us  [near_call(): pl.pallas_call(functools.partial(near_kernel, levels, per, dim), grid_spe...]
    ppermute x14 -> x18, waiting for transfers between devices: 7.03 us -> 7.51 us  [exchange(): return lax.ppermute(value, 'seq', [(i, i ^ bits) for i in range(count)])]
    pallas_call x1, Pallas kernels: 1.88 us -> 2.31 us  [far_call(): pl.pallas_call(functools.partial(far_kernel, levels, per, dim), grid_spec...]
  transfers between devices with their start and end apart: 15 -> 19, of which waited for: 5 -> 6; matrix products, arithmetic and copies ran while one was open for 0% -> 0% of each run, Pallas kernels for 26% -> 24%
where the time goes in v8:
time: 39.2 us; the launch traced here: 39.1 us
  starting transfers between devices  17.2 us (44%)
  Pallas kernels  13.4 us (34%)
  waiting for transfers between devices  7.71 us (20%)
  between operations  0.8 us (2%)
    ppermute x18, starting transfers between devices, exchange(): return lax.ppermute(value, 'seq', [(i, i ^ bits) for i in range(count)])  12.5 us
    ppermute x18, waiting for transfers between devices, exchange(): return lax.ppermute(value, 'seq', [(i, i ^ bits) for i in range(count)])  7.51 us
    ppermute x1, starting transfers between devices, per_device(): lax.ppermute(out_grads[0], 'section', [(i, (i - 1) % sections) for i in r...  4.67 us
    pallas_call x2, Pallas kernels, half_call(): pl.pallas_call(functools.partial(half_kernel, levels, per, dim, turn), gr...  3.41 us
    pallas_call x1, Pallas kernels, near_call(): pl.pallas_call(functools.partial(near_kernel, levels, per, dim), grid_spe...  2.94 us
    pallas_call x1, Pallas kernels, far_call(): pl.pallas_call(functools.partial(far_kernel, levels, per, dim), grid_spec...  2.31 us
    pallas_call x1, Pallas kernels, pre_call(): pl.pallas_call(functools.partial(pre_kernel, levels, per, dim), grid_spec...  2.07 us
    pallas_call x1, Pallas kernels, pick_call(): pl.pallas_call(functools.partial(pick_kernel, levels, per, dim), grid_spe...  1.39 us
  transfers between devices with their start and end apart: 19, of which 6 were waited for; matrix products, arithmetic and copies ran while one was open for 0% of the time, Pallas kernels for 24%

profile of v8, /device:TPU:0, one launch (start us, length us, event | category | flops | bytes accessed | tf_op | source)
XLA Modules:
  0.0 39.1 jit_solution(4713359566294456748)
XLA Ops:
  0.6 0.5 %collective-permute-start.2 = (bf16[128,2048]{1,0:T(8,128)(2,1)}, bf16[128,2048]{1,0:T(8,128)(2,1)S(1)}, u32[]{:S(2)}, u32[]{:S(2)}) collective-permute-start(bf16[128,2048]{1,0:T(8,128)(2,1)} %bitcast.8), channel_id=1, source_target_pairs={{0,4},{4,0},{8,12},{12,8},{16,20},{20,16},{24,28},{28,24},{1,5},{5... | collective-permute-start | bytes 1572872 | tf_op jit(solution)/shard_map/ppermute | solution.py:22
  1.1 0.1 collective-permute-start.1
  1.2 0.4 %collective-permute-start = (bf16[128,2048]{1,0:T(8,128)(2,1)}, bf16[128,2048]{1,0:T(8,128)(2,1)S(1)}, u32[]{:S(2)}, u32[]{:S(2)}) collective-permute-start(bf16[128,2048]{1,0:T(8,128)(2,1)} %bitcast.17), channel_id=1, source_target_pairs={{0,4},{4,0},{8,12},{12,8},{16,20},{20,16},{24,28},{28,24},{1,5},{5... | collective-permute-start | bytes 1572872 | tf_op jit(solution)/shard_map/ppermute | solution.py:22
  1.7 4.7 %collective-permute-start.3 = (bf16[128,2048]{1,0:T(8,128)(2,1)}, bf16[128,2048]{1,0:T(8,128)(2,1)S(1)}, u32[]{:S(2)}, u32[]{:S(2)}) collective-permute-start(bf16[128,2048]{1,0:T(8,128)(2,1)} %bitcast.23), channel_id=1, source_target_pairs={{0,3},{1,0},{2,1},{3,2},{4,7},{5,4},{6,5},{7,6},{8,11},{9,8},{10,9... | collective-permute-start | bytes 1572872 | tf_op jit(solution)/shard_map/ppermute | solution.py:579
  6.3 0.0 collective-permute-done.2.v1
  6.3 0.0 collective-permute-done.1.k1
  6.4 1.4 %pick_rows.1 = (bf16[64,2048]{1,0:T(8,128)(2,1)S(1)}, bf16[32,2048]{1,0:T(8,128)(2,1)S(1)}) custom-call(s32[1]{0:T(128)} %bitcast.core_ref, s32[3,16]{1,0:T(4,128)} %offs_ref.11, bf16[128,2048]{1,0:T(8,128)(2,1)} %bitcast.14, bf16[128,2048]{1,0:T(8,128)(2,1)} %bitcast.9, bf16[128,2048]{1,0:T(8,128)(2,1)S(1)} %collective-permute-done.1.k1, ...), custom_call_target="tpu_custom_call" | custom-call | tf_op jit(solution)/shard_map/pick_rows/pallas_call | solution.py:123
  7.8 0.0 copy-start.3
  7.8 1.6 %collective-permute-start.5 = (bf16[32,2048]{1,0:T(8,128)(2,1)S(1)}, bf16[32,2048]{1,0:T(8,128)(2,1)S(1)}, u32[]{:S(2)}, u32[]{:S(2)}) collective-permute-start(bf16[32,2048]{1,0:T(8,128)(2,1)S(1)} %get-tuple-element.54.own3), channel_id=1, source_target_pairs={{0,8},{4,12},{8,0},{12,4},{16,24},{20,28},{24,16},{28,20},{1,9},{5... | collective-permute-start | bytes 393224 | tf_op jit(solution)/shard_map/ppermute | solution.py:22
  9.3 1.5 %collective-permute-start.6 = (bf16[32,2048]{1,0:T(8,128)(2,1)S(1)}, bf16[32,2048]{1,0:T(8,128)(2,1)S(1)}, u32[]{:S(2)}, u32[]{:S(2)}) collective-permute-start(bf16[32,2048]{1,0:T(8,128)(2,1)S(1)} %get-tuple-element.54.own3), channel_id=1, source_target_pairs={{0,16},{4,20},{8,24},{12,28},{16,0},{20,4},{24,8},{28,12},{1,17},{... | collective-permute-start | bytes 393224 | tf_op jit(solution)/shard_map/ppermute | solution.py:22
  10.9 0.5 %collective-permute-start.4 = (bf16[64,2048]{1,0:T(8,128)(2,1)S(1)}, bf16[64,2048]{1,0:T(8,128)(2,1)S(1)}, u32[]{:S(2)}, u32[]{:S(2)}) collective-permute-start(bf16[64,2048]{1,0:T(8,128)(2,1)S(1)} %get-tuple-element.53.own2), channel_id=1, source_target_pairs={{0,8},{4,12},{8,0},{12,4},{16,24},{20,28},{24,16},{28,20},{1,9},{5... | collective-permute-start | bytes 786440 | tf_op jit(solution)/shard_map/ppermute | solution.py:22
  11.4 2.3 %collective-permute-done.5.x3 = bf16[32,2048]{1,0:T(8,128)(2,1)S(1)} collective-permute-done((bf16[32,2048]{1,0:T(8,128)(2,1)S(1)}, bf16[32,2048]{1,0:T(8,128)(2,1)S(1)}, u32[]{:S(2)}, u32[]{:S(2)}) %collective-permute-start.5) | collective-permute-done | bytes 131104 | tf_op jit(solution)/shard_map/ppermute | solution.py:22
  13.7 0.9 %collective-permute-done.6.y3 = bf16[32,2048]{1,0:T(8,128)(2,1)S(1)} collective-permute-done((bf16[32,2048]{1,0:T(8,128)(2,1)S(1)}, bf16[32,2048]{1,0:T(8,128)(2,1)S(1)}, u32[]{:S(2)}, u32[]{:S(2)}) %collective-permute-start.6) | collective-permute-done | bytes 131104 | tf_op jit(solution)/shard_map/ppermute | solution.py:22
  14.6 1.5 %collective-permute-start.7 = (bf16[32,2048]{1,0:T(8,128)(2,1)S(1)}, bf16[32,2048]{1,0:T(8,128)(2,1)S(1)}, u32[]{:S(2)}, u32[]{:S(2)}) collective-permute-start(bf16[32,2048]{1,0:T(8,128)(2,1)S(1)} %collective-permute-done.5.x3), channel_id=1, source_target_pairs={{0,16},{4,20},{8,24},{12,28},{16,0},{20,4},{24,8},{28,12},{1,17},{... | collective-permute-start | bytes 393224 | tf_op jit(solution)/shard_map/ppermute | solution.py:22
  16.1 0.0 collective-permute-done.q1
  16.2 0.0 copy-done.2
  16.2 0.0 copy-done.3
  16.2 2.1 %local_scores.1 = (bf16[256,1024]{1,0:T(8,128)(2,1)S(1)}, bf16[256,1024]{1,0:T(8,128)(2,1)S(1)}, f32[8,2048]{1,0:T(8,128)S(1)}, bf16[128,2048]{1,0:T(8,128)(2,1)S(1)}, bf16[96,1024]{1,0:T(8,128)(2,1)S(1)}) custom-call(s32[3,16]{1,0:T(4,128)S(1)} %copy-done.3, s32[1]{0:T(128)} %bitcast.core_ref, bf16[128,2048]{1,0:T(8,128)(2,1)S(1)} %bitcast.18, ...), custom_call_target="tpu_custom_call" | custom-call | tf_op jit(solution)/shard_map/local_scores/pallas_call | solution.py:216
  18.2 0.2 collective-permute-done.3.grads.rows.g0
  18.5 0.1 collective-permute-start.10
  18.6 0.5 %collective-permute-start.9 = (bf16[128,384]{1,0:T(8,128)(2,1)S(1)}, bf16[128,384]{1,0:T(8,128)(2,1)S(1)}, u32[]{:S(2)}, u32[]{:S(2)}) collective-permute-start(bf16[128,384]{1,0:T(8,128)(2,1)S(1)} %get-tuple-element.58), channel_id=1, source_target_pairs={{0,4},{4,0},{8,12},{12,8},{16,20},{20,16},{24,28},{28,24},{1,5},{5... | collective-permute-start | bytes 294920 | tf_op jit(solution)/shard_map/ppermute | solution.py:22
  19.1 0.1 collective-permute-start.8
  19.1 1.2 %own_delta.1 = (bf16[48,1024]{1,0:T(8,128)(2,1)S(1)}, f32[8,1024]{1,0:T(8,128)S(1)}) custom-call(s32[3,16]{1,0:T(4,128)S(1)} %copy-done.3, s32[1]{0:T(128)} %bitcast.core_ref, bf16[256,1024]{1,0:T(8,128)(2,1)S(1)} %get-tuple-element.45.exps.exp0, bf16[128,2048]{1,0:T(8,128)(2,1)S(1)} %get-tuple-element.49.near, bf16[128,2048]{1,0:T(8,128)(2,1)S(1)} %bitcast.11, ...), custom_call_target="tpu_custom_call" | custom-call | tf_op jit(solution)/shard_map/own_delta/pallas_call | solution.py:266
  20.3 0.0 collective-permute-done.8.refs_0_
  20.3 0.0 collective-permute-done.10.refs_2_
  20.3 0.0 collective-permute-done.9.refs_1_
  20.3 0.0 collective-permute-done.4.x2
  20.4 0.0 collective-permute-done.7.d3
  20.4 2.3 %far_levels.1 = (bf16[32,2048]{1,0:T(8,128)(2,1)S(1)}, bf16[32,2048]{1,0:T(8,128)(2,1)S(1)}, bf16[32,2048]{1,0:T(8,128)(2,1)S(1)}, bf16[32,2048]{1,0:T(8,128)(2,...) custom-call(s32[3,16]{1,0:T(4,128)S(1)} %copy-done.3, ...), custom_call_target="tpu_custom_call" | custom-call | tf_op jit(solution)/shard_map/far_levels/pallas_call | solution.py:395
  22.7 1.6 %collective-permute-start.13 = (bf16[32,2048]{1,0:T(8,128)(2,1)S(1)}, bf16[32,2048]{1,0:T(8,128)(2,1)S(1)}, u32[]{:S(2)}, u32[]{:S(2)}) collective-permute-start(bf16[32,2048]{1,0:T(8,128)(2,1)S(1)} %get-tuple-element.70), channel_id=1, source_target_pairs={{0,16},{4,20},{8,24},{12,28},{16,0},{20,4},{24,8},{28,12},{1,17},{... | collective-permute-start | bytes 393224 | tf_op jit(solution)/shard_map/ppermute | solution.py:22
  24.3 1.5 %collective-permute-start.11 = (bf16[32,2048]{1,0:T(8,128)(2,1)S(1)}, bf16[32,2048]{1,0:T(8,128)(2,1)S(1)}, u32[]{:S(2)}, u32[]{:S(2)}) collective-permute-start(bf16[32,2048]{1,0:T(8,128)(2,1)S(1)} %get-tuple-element.67), channel_id=1, source_target_pairs={{0,8},{4,12},{8,0},{12,4},{16,24},{20,28},{24,16},{28,20},{1,9},{5... | collective-permute-start | bytes 393224 | tf_op jit(solution)/shard_map/ppermute | solution.py:22
  25.8 0.0 collective-permute-start.12
  25.8 0.5 %collective-permute-start.16 = (bf16[32,2048]{1,0:T(8,128)(2,1)S(1)}, bf16[32,2048]{1,0:T(8,128)(2,1)S(1)}, u32[]{:S(2)}, u32[]{:S(2)}) collective-permute-start(bf16[32,2048]{1,0:T(8,128)(2,1)S(1)} %get-tuple-element.73), channel_id=1, source_target_pairs={{0,16},{4,20},{8,24},{12,28},{16,0},{20,4},{24,8},{28,12},{1,17},{... | collective-permute-start | bytes 393224 | tf_op jit(solution)/shard_map/ppermute | solution.py:22
  26.3 2.3 %collective-permute-done.13.there = bf16[32,2048]{1,0:T(8,128)(2,1)S(1)} collective-permute-done((bf16[32,2048]{1,0:T(8,128)(2,1)S(1)}, bf16[32,2048]{1,0:T(8,128)(2,1)S(1)}, u32[]{:S(2)}, u32[]{:S(2)}) %collective-permute-start.13) | collective-permute-done | bytes 131104 | tf_op jit(solution)/shard_map/ppermute | solution.py:22
  28.6 1.6 %collective-permute-start.14 = (bf16[16,2048]{1,0:T(8,128)(2,1)S(1)}, bf16[16,2048]{1,0:T(8,128)(2,1)S(1)}, u32[]{:S(2)}, u32[]{:S(2)}) collective-permute-start(bf16[16,2048]{1,0:T(8,128)(2,1)S(1)} %get-tuple-element.71), channel_id=1, source_target_pairs={{0,8},{4,12},{8,0},{12,4},{16,24},{20,28},{24,16},{28,20},{1,9},{5... | collective-permute-start | bytes 196616 | tf_op jit(solution)/shard_map/ppermute | solution.py:22
  30.2 0.0 collective-permute-start.15
  30.2 2.9 %near_levels.1 = (bf16[128,3072]{1,0:T(8,128)(2,1)S(1)}, bf16[128,3072]{1,0:T(8,128)(2,1)S(1)}) custom-call(s32[3,16]{1,0:T(4,128)S(1)} %copy-done.3, s32[1]{0:T(128)} %bitcast.core_ref, bf16[256,1024]{1,0:T(8,128)(2,1)S(1)} %get-tuple-element.45.exps.exp0, bf16[256,1024]{1,0:T(8,128)(2,1)S(1)} %get-tuple-element.46.exp1, ...), custom_call_target="tpu_custom_call" | custom-call | tf_op jit(solution)/shard_map/near_levels/pallas_call | solution.py:478
  33.1 0.0 collective-permute-done.11.x
  33.2 0.0 collective-permute-done.12.x
  33.2 0.0 collective-permute-done.16.y
  33.2 1.6 %collective-permute-done.14.x3 = bf16[16,2048]{1,0:T(8,128)(2,1)S(1)} collective-permute-done((bf16[16,2048]{1,0:T(8,128)(2,1)S(1)}, bf16[16,2048]{1,0:T(8,128)(2,1)S(1)}, u32[]{:S(2)}, u32[]{:S(2)}) %collective-permute-start.14) | collective-permute-done | bytes 65568 | tf_op jit(solution)/shard_map/ppermute | solution.py:22
  34.7 0.0 collective-permute-done.15.x3
  34.8 0.5 %collective-permute-start.17 = (bf16[128,3072]{1,0:T(8,128)(2,1)S(1)}, bf16[128,3072]{1,0:T(8,128)(2,1)S(1)}, u32[]{:S(2)}, u32[]{:S(2)}) collective-permute-start(bf16[128,3072]{1,0:T(8,128)(2,1)S(1)} %get-tuple-element.74), channel_id=1, source_target_pairs={{0,4},{4,0},{8,12},{12,8},{16,20},{20,16},{24,28},{28,24},{1,5},{5... | collective-permute-start | bytes 2359304 | tf_op jit(solution)/shard_map/ppermute | solution.py:22
  35.3 0.0 collective-permute-start.18
  35.3 1.7 %add_own_half.1 = (bf16[128,2048]{1,0:T(8,128)(2,1)}, bf16[128,2048]{1,0:T(8,128)(2,1)}, bf16[128,2048]{1,0:T(8,128)(2,1)}) custom-call(s32[3,16]{1,0:T(4,128)S(1)} %copy-done.3, s32[1]{0:T(128)} %bitcast.core_ref, bf16[128,3072]{1,0:T(8,128)(2,1)S(1)} %get-tuple-element.77.base, bf16[32,2048]{1,0:T(8,128)(2,1)S(1)} %collective-permute-done.11.x, ...), custom_call_target="tpu_custom_call" | custom-call | tf_op jit(solution)/shard_map/add_own_half/pallas_call | solution.py:553
  37.0 0.4 collective-permute-done.18.y
  37.4 0.0 collective-permute-done.17.base
  37.4 1.7 %add_other_half.1 = (bf16[128,2048]{1,0:T(8,128)(2,1)}, bf16[128,2048]{1,0:T(8,128)(2,1)}, bf16[128,2048]{1,0:T(8,128)(2,1)}) custom-call(s32[3,16]{1,0:T(4,128)S(1)} %copy-done.3, s32[1]{0:T(128)} %bitcast.core_ref, bf16[128,3072]{1,0:T(8,128)(2,1)S(1)} %collective-permute-done.17.base, ...), custom_call_target="tpu_custom_call", output_to_operand_aliasing={{0}: (6, {}), {1}: (7, {}), {2}: (8, {})} | custom-call | tf_op jit(solution)/shard_map/add_other_half/pallas_call | solution.py:553
  (7 shorter events, 0.1 us)
Async XLA Ops:
  0.6 5.7 %collective-permute-start.2 = (bf16[128,2048]{1,0:T(8,128)(2,1)}, bf16[128,2048]{1,0:T(8,128)(2,1)S(1)}, u32[]{:S(2)}, u32[]{:S(2)}) collective-permute-start(bf16[128,2048]{1,0:T(8,128)(2,1)} %bitcast.8), channel_id=1, source_target_pairs={{0,4},{4,0},{8,12},{12,8},{16,20},{20,16},{24,28},{28,24},{1,5},{5... | collective-permute-start | bytes 1572872 | tf_op jit(solution)/shard_map/ppermute | solution.py:22
  1.1 5.2 %collective-permute-start.1 = (bf16[128,2048]{1,0:T(8,128)(2,1)}, bf16[128,2048]{1,0:T(8,128)(2,1)S(1)}, u32[]{:S(2)}, u32[]{:S(2)}) collective-permute-start(bf16[128,2048]{1,0:T(8,128)(2,1)} %bitcast.13), channel_id=1, source_target_pairs={{0,4},{4,0},{8,12},{12,8},{16,20},{20,16},{24,28},{28,24},{1,5},{5... | collective-permute-start | bytes 1572872 | tf_op jit(solution)/shard_map/ppermute | solution.py:22
  1.2 14.9 %collective-permute-start = (bf16[128,2048]{1,0:T(8,128)(2,1)}, bf16[128,2048]{1,0:T(8,128)(2,1)S(1)}, u32[]{:S(2)}, u32[]{:S(2)}) collective-permute-start(bf16[128,2048]{1,0:T(8,128)(2,1)} %bitcast.17), channel_id=1, source_target_pairs={{0,4},{4,0},{8,12},{12,8},{16,20},{20,16},{24,28},{28,24},{1,5},{5... | collective-permute-start | bytes 1572872 | tf_op jit(solution)/shard_map/ppermute | solution.py:22
  1.7 16.8 %collective-permute-start.3 = (bf16[128,2048]{1,0:T(8,128)(2,1)}, bf16[128,2048]{1,0:T(8,128)(2,1)S(1)}, u32[]{:S(2)}, u32[]{:S(2)}) collective-permute-start(bf16[128,2048]{1,0:T(8,128)(2,1)} %bitcast.23), channel_id=1, source_target_pairs={{0,3},{1,0},{2,1},{3,2},{4,7},{5,4},{6,5},{7,6},{8,11},{9,8},{10,9... | collective-permute-start | bytes 1572872 | tf_op jit(solution)/shard_map/ppermute | solution.py:579
  6.3 9.8 %copy-start = (bf16[1,128,2048]{2,1,0:T(8,128)(2,1)S(1)}, bf16[1,128,2048]{2,1,0:T(8,128)(2,1)}, u32[]{:S(2)}) copy-start(bf16[1,128,2048]{2,1,0:T(8,128)(2,1)} %param.7) | copy-start | bytes 1572868
  6.3 9.8 %copy-start.1 = (bf16[1,128,2048]{2,1,0:T(8,128)(2,1)S(1)}, bf16[1,128,2048]{2,1,0:T(8,128)(2,1)}, u32[]{:S(2)}) copy-start(bf16[1,128,2048]{2,1,0:T(8,128)(2,1)} %param.6) | copy-start | bytes 1572868
  6.4 9.8 %copy-start.2 = (bf16[1,128,2048]{2,1,0:T(8,128)(2,1)S(1)}, bf16[1,128,2048]{2,1,0:T(8,128)(2,1)}, u32[]{:S(2)}) copy-start(bf16[1,128,2048]{2,1,0:T(8,128)(2,1)} %param.5) | copy-start | bytes 1572868
  7.8 8.4 %copy-start.3 = (s32[3,16]{1,0:T(4,128)S(1)}, s32[3,16]{1,0:T(4,128)}, u32[]{:S(2)}) copy-start(s32[3,16]{1,0:T(4,128)} %offs_ref.11) | copy-start | bytes 580
  7.8 5.9 %collective-permute-start.5 = (bf16[32,2048]{1,0:T(8,128)(2,1)S(1)}, bf16[32,2048]{1,0:T(8,128)(2,1)S(1)}, u32[]{:S(2)}, u32[]{:S(2)}) collective-permute-start(bf16[32,2048]{1,0:T(8,128)(2,1)S(1)} %get-tuple-element.54.own3), channel_id=1, source_target_pairs={{0,8},{4,12},{8,0},{12,4},{16,24},{20,28},{24,16},{28,20},{1,9},{5... | collective-permute-start | bytes 393224 | tf_op jit(solution)/shard_map/ppermute | solution.py:22
  9.3 5.3 %collective-permute-start.6 = (bf16[32,2048]{1,0:T(8,128)(2,1)S(1)}, bf16[32,2048]{1,0:T(8,128)(2,1)S(1)}, u32[]{:S(2)}, u32[]{:S(2)}) collective-permute-start(bf16[32,2048]{1,0:T(8,128)(2,1)S(1)} %get-tuple-element.54.own3), channel_id=1, source_target_pairs={{0,16},{4,20},{8,24},{12,28},{16,0},{20,4},{24,8},{28,12},{1,17},{... | collective-permute-start | bytes 393224 | tf_op jit(solution)/shard_map/ppermute | solution.py:22
  10.9 9.5 %collective-permute-start.4 = (bf16[64,2048]{1,0:T(8,128)(2,1)S(1)}, bf16[64,2048]{1,0:T(8,128)(2,1)S(1)}, u32[]{:S(2)}, u32[]{:S(2)}) collective-permute-start(bf16[64,2048]{1,0:T(8,128)(2,1)S(1)} %get-tuple-element.53.own2), channel_id=1, source_target_pairs={{0,8},{4,12},{8,0},{12,4},{16,24},{20,28},{24,16},{28,20},{1,9},{5... | collective-permute-start | bytes 786440 | tf_op jit(solution)/shard_map/ppermute | solution.py:22
  14.6 5.7 %collective-permute-start.7 = (bf16[32,2048]{1,0:T(8,128)(2,1)S(1)}, bf16[32,2048]{1,0:T(8,128)(2,1)S(1)}, u32[]{:S(2)}, u32[]{:S(2)}) collective-permute-start(bf16[32,2048]{1,0:T(8,128)(2,1)S(1)} %collective-permute-done.5.x3), channel_id=1, source_target_pairs={{0,16},{4,20},{8,24},{12,28},{16,0},{20,4},{24,8},{28,12},{1,17},{... | collective-permute-start | bytes 393224 | tf_op jit(solution)/shard_map/ppermute | solution.py:22
  18.5 1.8 %collective-permute-start.10 = (bf16[128,384]{1,0:T(8,128)(2,1)S(1)}, bf16[128,384]{1,0:T(8,128)(2,1)S(1)}, u32[]{:S(2)}, u32[]{:S(2)}) collective-permute-start(bf16[128,384]{1,0:T(8,128)(2,1)S(1)} %get-tuple-element.59), channel_id=1, source_target_pairs={{0,4},{4,0},{8,12},{12,8},{16,20},{20,16},{24,28},{28,24},{1,5},{5... | collective-permute-start | bytes 294920 | tf_op jit(solution)/shard_map/ppermute | solution.py:22
  18.6 1.8 %collective-permute-start.9 = (bf16[128,384]{1,0:T(8,128)(2,1)S(1)}, bf16[128,384]{1,0:T(8,128)(2,1)S(1)}, u32[]{:S(2)}, u32[]{:S(2)}) collective-permute-start(bf16[128,384]{1,0:T(8,128)(2,1)S(1)} %get-tuple-element.58), channel_id=1, source_target_pairs={{0,4},{4,0},{8,12},{12,8},{16,20},{20,16},{24,28},{28,24},{1,5},{5... | collective-permute-start | bytes 294920 | tf_op jit(solution)/shard_map/ppermute | solution.py:22
  19.1 1.3 %collective-permute-start.8 = (bf16[128,256]{1,0:T(8,128)(2,1)S(1)}, bf16[128,256]{1,0:T(8,128)(2,1)S(1)}, u32[]{:S(2)}, u32[]{:S(2)}) collective-permute-start(bf16[128,256]{1,0:T(8,128)(2,1)S(1)} %get-tuple-element.57), channel_id=1, source_target_pairs={{0,4},{4,0},{8,12},{12,8},{16,20},{20,16},{24,28},{28,24},{1,5},{5... | collective-permute-start | bytes 196616 | tf_op jit(solution)/shard_map/ppermute | solution.py:22
  22.7 5.9 %collective-permute-start.13 = (bf16[32,2048]{1,0:T(8,128)(2,1)S(1)}, bf16[32,2048]{1,0:T(8,128)(2,1)S(1)}, u32[]{:S(2)}, u32[]{:S(2)}) collective-permute-start(bf16[32,2048]{1,0:T(8,128)(2,1)S(1)} %get-tuple-element.70), channel_id=1, source_target_pairs={{0,16},{4,20},{8,24},{12,28},{16,0},{20,4},{24,8},{28,12},{1,17},{... | collective-permute-start | bytes 393224 | tf_op jit(solution)/shard_map/ppermute | solution.py:22
  24.3 8.9 %collective-permute-start.11 = (bf16[32,2048]{1,0:T(8,128)(2,1)S(1)}, bf16[32,2048]{1,0:T(8,128)(2,1)S(1)}, u32[]{:S(2)}, u32[]{:S(2)}) collective-permute-start(bf16[32,2048]{1,0:T(8,128)(2,1)S(1)} %get-tuple-element.67), channel_id=1, source_target_pairs={{0,8},{4,12},{8,0},{12,4},{16,24},{20,28},{24,16},{28,20},{1,9},{5... | collective-permute-start | bytes 393224 | tf_op jit(solution)/shard_map/ppermute | solution.py:22
  25.8 7.4 %collective-permute-start.12 = (bf16[32,2048]{1,0:T(8,128)(2,1)S(1)}, bf16[32,2048]{1,0:T(8,128)(2,1)S(1)}, u32[]{:S(2)}, u32[]{:S(2)}) collective-permute-start(bf16[32,2048]{1,0:T(8,128)(2,1)S(1)} %get-tuple-element.68), channel_id=1, source_target_pairs={{0,12},{4,8},{8,4},{12,0},{16,28},{20,24},{24,20},{28,16},{1,13},{... | collective-permute-start | bytes 393224 | tf_op jit(solution)/shard_map/ppermute | solution.py:22
  25.8 7.4 %collective-permute-start.16 = (bf16[32,2048]{1,0:T(8,128)(2,1)S(1)}, bf16[32,2048]{1,0:T(8,128)(2,1)S(1)}, u32[]{:S(2)}, u32[]{:S(2)}) collective-permute-start(bf16[32,2048]{1,0:T(8,128)(2,1)S(1)} %get-tuple-element.73), channel_id=1, source_target_pairs={{0,16},{4,20},{8,24},{12,28},{16,0},{20,4},{24,8},{28,12},{1,17},{... | collective-permute-start | bytes 393224 | tf_op jit(solution)/shard_map/ppermute | solution.py:22
  28.6 6.1 %collective-permute-start.14 = (bf16[16,2048]{1,0:T(8,128)(2,1)S(1)}, bf16[16,2048]{1,0:T(8,128)(2,1)S(1)}, u32[]{:S(2)}, u32[]{:S(2)}) collective-permute-start(bf16[16,2048]{1,0:T(8,128)(2,1)S(1)} %get-tuple-element.71), channel_id=1, source_target_pairs={{0,8},{4,12},{8,0},{12,4},{16,24},{20,28},{24,16},{28,20},{1,9},{5... | collective-permute-start | bytes 196616 | tf_op jit(solution)/shard_map/ppermute | solution.py:22
  30.2 4.6 %collective-permute-start.15 = (bf16[16,2048]{1,0:T(8,128)(2,1)S(1)}, bf16[16,2048]{1,0:T(8,128)(2,1)S(1)}, u32[]{:S(2)}, u32[]{:S(2)}) collective-permute-start(bf16[16,2048]{1,0:T(8,128)(2,1)S(1)} %get-tuple-element.72), channel_id=1, source_target_pairs={{0,12},{4,8},{8,4},{12,0},{16,28},{20,24},{24,20},{28,16},{1,13},{... | collective-permute-start | bytes 196616 | tf_op jit(solution)/shard_map/ppermute | solution.py:22
  34.8 2.6 %collective-permute-start.17 = (bf16[128,3072]{1,0:T(8,128)(2,1)S(1)}, bf16[128,3072]{1,0:T(8,128)(2,1)S(1)}, u32[]{:S(2)}, u32[]{:S(2)}) collective-permute-start(bf16[128,3072]{1,0:T(8,128)(2,1)S(1)} %get-tuple-element.74), channel_id=1, source_target_pairs={{0,4},{4,0},{8,12},{12,8},{16,20},{20,16},{24,28},{28,24},{1,5},{5... | collective-permute-start | bytes 2359304 | tf_op jit(solution)/shard_map/ppermute | solution.py:22
  35.3 2.1 %collective-permute-start.18 = (bf16[32,2048]{1,0:T(8,128)(2,1)S(1)}, bf16[32,2048]{1,0:T(8,128)(2,1)S(1)}, u32[]{:S(2)}, u32[]{:S(2)}) collective-permute-start(bf16[32,2048]{1,0:T(8,128)(2,1)S(1)} %collective-permute-done.16.y), channel_id=1, source_target_pairs={{0,4},{4,0},{8,12},{12,8},{16,20},{20,16},{24,28},{28,24},{1,5},{5... | collective-permute-start | bytes 393224 | tf_op jit(solution)/shard_map/ppermute | solution.py:22

commit v9 on v8

--- a/solution.py
+++ b/solution.py
@@ -324,7 +324,7 @@
     spots = [stack(side(a, none), side(none, a)) for a in picks]
     spread = []
     for h in each:
-        terms = stack(*split(top[h], 3), *split(size[h], 2), *split(dhat[h], 2))
+        terms = stack(*split(top[h], 3), *split(size[h], 2), *split(dhat[h], 3))
         zero = jnp.zeros_like(terms)
         apart = stack(jnp.where(is2, terms, zero), jnp.where(is2, zero, terms))
         spread.append(dot(apart, spots[h]))
@@ -334,12 +334,12 @@
         def level_stats(level, lo):
             rate = 2**level
             on = lax.rem(pos, rate) == lax.rem(offs_ref[level - 1, first + h], rate)
-            t = [spread[h][lo + i : lo + i + 1] for i in range(7)]
-            return jnp.where(on, t[0] + t[1] + t[2], NEG), t[3] + t[4], t[5] + t[6]
+            t = [spread[h][lo + i : lo + i + 1] for i in range(8)]
+            return jnp.where(on, t[0] + t[1] + t[2], NEG), t[3] + t[4], t[5] + t[6] + t[7]
 
         t1, z1 = stats[0:1, lanes[h]], stats[1:2, lanes[h]]
         t2, z2, dot2 = level_stats(2, 0)
-        t3, z3, dot3 = level_stats(3, 7)
+        t3, z3, dot3 = level_stats(3, 8)
         high = jnp.maximum(t1, jnp.maximum(t2, t3))
         a1, a2, a3 = jnp.exp(t1 - high), jnp.exp(t2 - high), jnp.exp(t3 - high)
         inv = 1.0 / (a1 * z1 + a2 * z2 + a3 * z3)
@@ -347,7 +347,7 @@
         delta = f1 * side(local0[0:1, h * tok : (h + 1) * tok], local1[h]) + f2 * dot2 + f3 * dot3
         stats2[0:1, lanes[h]] = f1
         stats2[1:2, lanes[h]] = delta
-        terms = stack(*split(f2, 2), *split(f3, 2), *split(delta, 2))
+        terms = stack(*split(f2, 2), *split(f3, 2), *split(delta, 3))
         back.append(dot_nt(terms, spots[h]))
 
     def apart(value):
@@ -358,7 +358,7 @@
     for h in each:
         b = back[h]
         w = e[h] * jnp.where(is2, b[0:1] + b[1:2], b[2:3] + b[3:4])
-        dsm.append(apart(w * (p[h] - (b[4:5] + b[5:6]))))
+        dsm.append(apart(w * (p[h] - (b[4:5] + b[5:6] + b[6:7]))))
         wm.append(apart(w))
     dk = [dot(dsm[h], selq[:, cols[h]]) * scale for h in each]
     dv = [dot(wm[h], selg[h]) for h in each]
@@ -412,8 +412,8 @@
     levels, per, dim, offs_ref, core_ref, exp0, exp1, stats2, near, ngrad, dqt,
     q0, q1, k0, k1, v0, v1, g0, *refs,
 ):
-    mine, other = refs[-2:]
-    g1 = side(*(ref[...] for ref in refs[:-2]))
+    mine, *others = refs[-3:]
+    g1 = side(*(ref[...] for ref in refs[:-3]))
     tok = q0.shape[0]
     n1 = tok // 2
     sel = tok // 4 + tok // 8
@@ -440,7 +440,7 @@
             h: side(dot(ds[h][tok:], que[h]) * scale, dot(wb[h][tok:], gra[h])).astype(BF16)
             for h in each
         }
-        for ref, block, keys in ((mine, 0, k0), (other, 1, k1)):
+        for block, keys in enumerate((k0, k1)):
             at = slice(block * tok, (block + 1) * tok)
             picked = slice(block * n1, (block + 1) * n1)
             grads = slice(block * sel, (block + 1) * sel)
@@ -458,7 +458,8 @@
                 both = stack(keys[:, cols[h]], near[:tok, kc])
                 dq[h] = dot(both.T, ds[h][:, at]) + dot(far, pick)
             for h in each:
-                to = 3 * h * dim
+                ref, to = (others[h // (per // 2)], h % (per // 2)) if block else (mine, h)
+                to *= 3 * dim
                 ref[:, to : to + dim] = (dq[h] * scale).T.astype(BF16)
                 ref[:, to + dim : to + 3 * dim] = kv[h].astype(BF16)
 
@@ -474,7 +475,7 @@
     def mid_spec(a):
         return pl.BlockSpec((a.shape[0], a.shape[1] // steps), lambda i, o, c: (0, i))
 
-    out_spec = pl.BlockSpec((tok, 3 * per * dim), lambda i, o, c: (0, i))
+    widths = [3 * per * dim, 3 * per * dim // 2, 3 * per * dim // 2]
     return pl.pallas_call(
         functools.partial(near_kernel, levels, per, dim),
         grid_spec=pltpu.PrefetchScalarGridSpec(
@@ -482,9 +483,9 @@
             grid=(steps,),
             in_specs=[mid_spec(a) for a in mid] + [raw_spec] * 7
             + [mid_spec(a) for a in grads[1:]],
-            out_specs=[out_spec] * 2,
-        ),
-        out_shape=[jax.ShapeDtypeStruct((tok, 3 * half * dim), BF16)] * 2,
+            out_specs=[pl.BlockSpec((tok, w), lambda i, o, c: (0, 0)) for w in widths],
+        ),
+        out_shape=[jax.ShapeDtypeStruct((tok, w), BF16) for w in widths],
         compiler_params=params(),
         name="near_levels",
     )(offsets, core, *mid, *raw, *grads)
@@ -507,67 +508,106 @@
     )(here, there)
 
 
-def half_kernel(levels, per, dim, turn, offs_ref, core_ref, base, x, y, x3, *refs):
-    outs, (held, sems) = refs[-5:-2], refs[-2:]
-    tok = base.shape[0]
-    n2, n3 = tok // 4, tok // 8
-    first = per * (1 - core_ref[0] if turn else core_ref[0])
-    group = 2
-    each = range(per)
-    place = [place_matrix(offs_ref, first + h, 2, levels, tok) for h in each]
-    mine = y[n3:] if turn else y[:n3]
-    third = (x3[...].astype(F32) + mine.astype(F32)).astype(BF16)
-    src = [slice(2 * h * dim, 2 * (h + 1) * dim) for h in each]
-    copies = []
-
-    def send(part, lo, n):
-        cols = pl.ds(pl.multiple_of(first * dim + lo * dim, dim), n * dim)
-        here = held.at[part, :, pl.ds(lo * dim, n * dim)]
-        copies.append(pltpu.make_async_copy(here, outs[part].at[:, cols], sems.at[len(copies)]))
-        copies[-1].start()
-
-    for h in each:
-        held[0, :, h * dim : (h + 1) * dim] = base[:, 3 * h * dim : (3 * h + 1) * dim]
-    send(0, 0, per)
+def add_far(levels, dim, offs_ref, first, bases, x, third, group):
+    tok = bases[0].shape[0]
+    per = sum(base.shape[1] for base in bases) // (3 * dim)
+    in_base = per // len(bases)
     for lo in range(0, per, group):
-        heads = range(lo, lo + group)
-        more = [dot(place[h], stack(x[:, src[h]], third[:, src[h]])) for h in heads]
-        for h, add in zip(heads, more):
-            cols = slice(h * dim, (h + 1) * dim)
-            at = (3 * h + 1) * dim
-            total = (base[:, at : at + 2 * dim].astype(F32) + add).astype(BF16)
-            held[1, :, cols] = total[:, :dim]
-            held[2, :, cols] = total[:, dim:]
-        send(1, lo, group)
-        send(2, lo, group)
-    for copy in copies:
-        copy.wait()
-
-
-def half_call(offsets, core, parts, whole, dim):
+        each = range(lo, lo + group)
+        src = {h: slice(2 * h * dim, 2 * (h + 1) * dim) for h in each}
+        place = {h: place_matrix(offs_ref, first + h, 2, levels, tok) for h in each}
+        more = {h: dot(place[h], stack(x[:, src[h]], third[:, src[h]])) for h in each}
+        for h in each:
+            base, at = bases[h // in_base], (3 * (h % in_base) + 1) * dim
+            yield h, (base[:, at : at + 2 * dim].astype(F32) + more[h]).astype(BF16)
+
+
+def own_kernel(levels, per, dim, offs_ref, core_ref, base, x, y, x3, dq, dk, dv):
+    n3 = x3.shape[0]
+    third = (x3[...].astype(F32) + y[:n3].astype(F32)).astype(BF16)
+    for h in range(per):
+        dq[:, h * dim : (h + 1) * dim] = base[:, 3 * h * dim : (3 * h + 1) * dim]
+    for h, total in add_far(levels, dim, offs_ref, core_ref[0] * per, [base], x, third, per):
+        cols = slice(h * dim, (h + 1) * dim)
+        dk[:, cols] = total[:, :dim]
+        dv[:, cols] = total[:, dim:]
+
+
+def own_call(offsets, core, parts, dim):
     levels, heads = offsets.shape
     tok = parts[0].shape[0]
     per = heads // 2
-    turn = len(whole) > 0
-    away = pl.BlockSpec(memory_space=pl.ANY)
-    return pl.pallas_call(
-        functools.partial(half_kernel, levels, per, dim, turn),
+    return pl.pallas_call(
+        functools.partial(own_kernel, levels, per, dim),
         grid_spec=pltpu.PrefetchScalarGridSpec(
             num_scalar_prefetch=2,
             grid=(1,),
-            in_specs=[pl.BlockSpec(a.shape, lambda i, o, c: (0, 0)) for a in parts]
-            + [away] * len(whole),
+            in_specs=[pl.BlockSpec(a.shape, lambda i, o, c: (0, 0)) for a in parts],
+            out_specs=[pl.BlockSpec((tok, per * dim), lambda i, o, c: (0, 0))] * 3,
+        ),
+        out_shape=[jax.ShapeDtypeStruct((tok, per * dim), BF16)] * 3,
+        compiler_params=params(),
+        name="add_own_half",
+    )(offsets, core, *parts)
+
+
+def final_kernel(
+    levels, per, dim, offs_ref, core_ref, own_q, own_k, own_v, base0, base1, x, y, x3,
+    dq, dk, dv, held, sems,
+):
+    outs = dq, dk, dv
+    n3 = x3.shape[0]
+    copies = []
+
+    def send(part, here, core, lo, n):
+        cols = pl.ds(pl.multiple_of((core * per + lo) * dim, dim), n * dim)
+        copies.append(pltpu.make_async_copy(here, outs[part].at[:, cols], sems.at[len(copies)]))
+        copies[-1].start()
+
+    for part, ref in enumerate((own_q, own_k, own_v)):
+        send(part, ref, core_ref[0], 0, per)
+    far_core = 1 - core_ref[0]
+    half = per // 2
+    for h in range(per):
+        base = base1 if h >= half else base0
+        at = 3 * (h % half) * dim
+        held[0, :, h * dim : (h + 1) * dim] = base[:, at : at + dim]
+    send(0, held.at[0], far_core, 0, per)
+    third = (x3[...].astype(F32) + y[n3:].astype(F32)).astype(BF16)
+    bases = [base0, base1]
+    for h, total in add_far(levels, dim, offs_ref, far_core * per, bases, x, third, 4):
+        cols = slice(h * dim, (h + 1) * dim)
+        held[1, :, cols] = total[:, :dim]
+        held[2, :, cols] = total[:, dim:]
+        if (h + 1) % 4 == 0:
+            for part in (1, 2):
+                lo = h + 1 - 4
+                send(part, held.at[part, :, pl.ds(lo * dim, 4 * dim)], far_core, lo, 4)
+    for copy in copies:
+        copy.wait()
+
+
+def final_call(offsets, core, own, parts, dim):
+    levels, heads = offsets.shape
+    tok = parts[0].shape[0]
+    per = heads // 2
+    away = pl.BlockSpec(memory_space=pl.ANY)
+    return pl.pallas_call(
+        functools.partial(final_kernel, levels, per, dim),
+        grid_spec=pltpu.PrefetchScalarGridSpec(
+            num_scalar_prefetch=2,
+            grid=(1,),
+            in_specs=[pl.BlockSpec(a.shape, lambda i, o, c: (0, 0)) for a in own + parts],
             out_specs=[away] * 3,
             scratch_shapes=[
                 pltpu.VMEM((3, tok, per * dim), BF16),
-                pltpu.SemaphoreType.DMA((1 + per,)),
+                pltpu.SemaphoreType.DMA((4 + 2 * (per // 4),)),
             ],
         ),
         out_shape=[jax.ShapeDtypeStruct((tok, heads * dim), BF16)] * 3,
-        input_output_aliases={2 + len(parts) + i: i for i in range(len(whole))},
-        compiler_params=params(),
-        name="add_other_half" if turn else "add_own_half",
-    )(offsets, core, *parts, *whole)
+        compiler_params=params(),
+        name="add_other_half",
+    )(offsets, core, *own, *parts)
 
 
 def per_device(queries, keys_in, values, out_grads, offsets):
@@ -605,12 +645,15 @@
     xa, xb, y = exchange(xa, 2), exchange(xb, 3), exchange(yab, 4)
     xa3, xb3 = exchange(thirds[0], 2), exchange(thirds[1], 3)
     yy = exchange(y, 1)
-    mine, other = near_call(
+    mine, first, second = near_call(
         offsets, core, [exp0, exp1, stats2, near, ngrad, dqt], raw, [grads, *other], dim
     )
-    other, xa, xb, xa3, xb3, y = lax.optimization_barrier((other, xa, xb, xa3, xb3, y))
-    halves = half_call(offsets, core, [mine, xa, y, xa3], [], dim)
-    dq, dk, dv = half_call(offsets, core, [exchange(other, 1), xb, yy, xb3], halves, dim)
+    first = exchange(first, 1)
+    second, xa, xb, xa3, xb3, y = lax.optimization_barrier((second, xa, xb, xa3, xb3, y))
+    own = list(own_call(offsets, core, [mine, xa, y, xa3], dim))
+    dq, dk, dv = final_call(
+        offsets, core, own, [first, exchange(second, 1), xb, yy, xb3], dim
+    )
     return dq[None], dk[None], dv[None]
 
 

time: 39.2 us -> 38.9 us (level)
  starting transfers between devices: 17.2 us -> 17.9 us
  Pallas kernels: 13.4 us -> 12.8 us
  waiting for transfers between devices: 7.71 us -> 7.23 us
    ppermute x18 -> x19, starting transfers between devices: 12.5 us -> 13.2 us  [exchange(): return lax.ppermute(value, 'seq', [(i, i ^ bits) for i in range(count)])]
    pallas_call x2, Pallas kernels: 3.41 us -> 2.83 us  [the longest x1 1.89 us: final_call(): pl.pallas_call(functools.partial(final_kernel, levels, per, dim), grid_sp...]
    ppermute x18 -> x19, waiting for transfers between devices: 7.51 us -> 7.03 us  [exchange(): return lax.ppermute(value, 'seq', [(i, i ^ bits) for i in range(count)])]
  transfers between devices with their start and end apart: 19 -> 20, of which waited for: 6 -> 6; matrix products, arithmetic and copies ran while one was open for 0% -> 0% of each run, Pallas kernels for 24% -> 22%
where the time goes in v9:
time: 38.9 us; the launch traced here: 38.7 us
  starting transfers between devices  17.9 us (46%)
  Pallas kernels  12.8 us (33%)
  waiting for transfers between devices  7.23 us (19%)
  between operations  0.79 us (2%)
    ppermute x19, starting transfers between devices, exchange(): return lax.ppermute(value, 'seq', [(i, i ^ bits) for i in range(count)])  13.2 us
    ppermute x19, waiting for transfers between devices, exchange(): return lax.ppermute(value, 'seq', [(i, i ^ bits) for i in range(count)])  7.03 us
    ppermute x1, starting transfers between devices, per_device(): lax.ppermute(out_grads[0], 'section', [(i, (i - 1) % sections) for i in r...  4.67 us
    pallas_call x1, Pallas kernels, near_call(): pl.pallas_call(functools.partial(near_kernel, levels, per, dim), grid_spe...  2.94 us
    pallas_call x1, Pallas kernels, far_call(): pl.pallas_call(functools.partial(far_kernel, levels, per, dim), grid_spec...  2.3 us
    pallas_call x1, Pallas kernels, pre_call(): pl.pallas_call(functools.partial(pre_kernel, levels, per, dim), grid_spec...  2.07 us
    pallas_call x1, Pallas kernels, final_call(): pl.pallas_call(functools.partial(final_kernel, levels, per, dim), grid_sp...  1.89 us
    pallas_call x1, Pallas kernels, pick_call(): pl.pallas_call(functools.partial(pick_kernel, levels, per, dim), grid_spe...  1.39 us
  transfers between devices with their start and end apart: 20, of which 6 were waited for; matrix products, arithmetic and copies ran while one was open for 0% of the time, Pallas kernels for 22%

profile of v9, /device:TPU:0, one launch (start us, length us, event | category | flops | bytes accessed | tf_op | source)
XLA Modules:
  0.0 38.7 jit_solution(10275018018055494862)
XLA Ops:
  0.6 0.5 %collective-permute-start.2 = (bf16[128,2048]{1,0:T(8,128)(2,1)}, bf16[128,2048]{1,0:T(8,128)(2,1)S(1)}, u32[]{:S(2)}, u32[]{:S(2)}) collective-permute-start(bf16[128,2048]{1,0:T(8,128)(2,1)} %bitcast.8), channel_id=1, source_target_pairs={{0,4},{4,0},{8,12},{12,8},{16,20},{20,16},{24,28},{28,24},{1,5},{5... | collective-permute-start | bytes 1572872 | tf_op jit(solution)/shard_map/ppermute | solution.py:22
  1.1 0.1 collective-permute-start.1
  1.2 0.4 %collective-permute-start = (bf16[128,2048]{1,0:T(8,128)(2,1)}, bf16[128,2048]{1,0:T(8,128)(2,1)S(1)}, u32[]{:S(2)}, u32[]{:S(2)}) collective-permute-start(bf16[128,2048]{1,0:T(8,128)(2,1)} %bitcast.17), channel_id=1, source_target_pairs={{0,4},{4,0},{8,12},{12,8},{16,20},{20,16},{24,28},{28,24},{1,5},{5... | collective-permute-start | bytes 1572872 | tf_op jit(solution)/shard_map/ppermute | solution.py:22
  1.7 4.7 %collective-permute-start.3 = (bf16[128,2048]{1,0:T(8,128)(2,1)}, bf16[128,2048]{1,0:T(8,128)(2,1)S(1)}, u32[]{:S(2)}, u32[]{:S(2)}) collective-permute-start(bf16[128,2048]{1,0:T(8,128)(2,1)} %bitcast.20), channel_id=1, source_target_pairs={{0,3},{1,0},{2,1},{3,2},{4,7},{5,4},{6,5},{7,6},{8,11},{9,8},{10,9... | collective-permute-start | bytes 1572872 | tf_op jit(solution)/shard_map/ppermute | solution.py:619
  6.3 0.0 collective-permute-done.2.v1
  6.3 0.0 collective-permute-done.1.k1
  6.4 1.4 %pick_rows.1 = (bf16[64,2048]{1,0:T(8,128)(2,1)S(1)}, bf16[32,2048]{1,0:T(8,128)(2,1)S(1)}) custom-call(s32[1]{0:T(128)} %bitcast.core_ref, s32[3,16]{1,0:T(4,128)} %offs_ref.11, bf16[128,2048]{1,0:T(8,128)(2,1)} %bitcast.14, bf16[128,2048]{1,0:T(8,128)(2,1)} %bitcast.9, bf16[128,2048]{1,0:T(8,128)(2,1)S(1)} %collective-permute-done.1.k1, ...), custom_call_target="tpu_custom_call" | custom-call | tf_op jit(solution)/shard_map/pick_rows/pallas_call | solution.py:123
  7.8 0.0 copy-start.3
  7.8 1.6 %collective-permute-start.5 = (bf16[32,2048]{1,0:T(8,128)(2,1)S(1)}, bf16[32,2048]{1,0:T(8,128)(2,1)S(1)}, u32[]{:S(2)}, u32[]{:S(2)}) collective-permute-start(bf16[32,2048]{1,0:T(8,128)(2,1)S(1)} %get-tuple-element.55.own3), channel_id=1, source_target_pairs={{0,8},{4,12},{8,0},{12,4},{16,24},{20,28},{24,16},{28,20},{1,9},{5... | collective-permute-start | bytes 393224 | tf_op jit(solution)/shard_map/ppermute | solution.py:22
  9.3 1.5 %collective-permute-start.6 = (bf16[32,2048]{1,0:T(8,128)(2,1)S(1)}, bf16[32,2048]{1,0:T(8,128)(2,1)S(1)}, u32[]{:S(2)}, u32[]{:S(2)}) collective-permute-start(bf16[32,2048]{1,0:T(8,128)(2,1)S(1)} %get-tuple-element.55.own3), channel_id=1, source_target_pairs={{0,16},{4,20},{8,24},{12,28},{16,0},{20,4},{24,8},{28,12},{1,17},{... | collective-permute-start | bytes 393224 | tf_op jit(solution)/shard_map/ppermute | solution.py:22
  10.9 0.5 %collective-permute-start.4 = (bf16[64,2048]{1,0:T(8,128)(2,1)S(1)}, bf16[64,2048]{1,0:T(8,128)(2,1)S(1)}, u32[]{:S(2)}, u32[]{:S(2)}) collective-permute-start(bf16[64,2048]{1,0:T(8,128)(2,1)S(1)} %get-tuple-element.54.own2), channel_id=1, source_target_pairs={{0,8},{4,12},{8,0},{12,4},{16,24},{20,28},{24,16},{28,20},{1,9},{5... | collective-permute-start | bytes 786440 | tf_op jit(solution)/shard_map/ppermute | solution.py:22
  11.4 2.3 %collective-permute-done.5.x3 = bf16[32,2048]{1,0:T(8,128)(2,1)S(1)} collective-permute-done((bf16[32,2048]{1,0:T(8,128)(2,1)S(1)}, bf16[32,2048]{1,0:T(8,128)(2,1)S(1)}, u32[]{:S(2)}, u32[]{:S(2)}) %collective-permute-start.5) | collective-permute-done | bytes 131104 | tf_op jit(solution)/shard_map/ppermute | solution.py:22
  13.7 0.9 %collective-permute-done.6.y3 = bf16[32,2048]{1,0:T(8,128)(2,1)S(1)} collective-permute-done((bf16[32,2048]{1,0:T(8,128)(2,1)S(1)}, bf16[32,2048]{1,0:T(8,128)(2,1)S(1)}, u32[]{:S(2)}, u32[]{:S(2)}) %collective-permute-start.6) | collective-permute-done | bytes 131104 | tf_op jit(solution)/shard_map/ppermute | solution.py:22
  14.6 1.5 %collective-permute-start.7 = (bf16[32,2048]{1,0:T(8,128)(2,1)S(1)}, bf16[32,2048]{1,0:T(8,128)(2,1)S(1)}, u32[]{:S(2)}, u32[]{:S(2)}) collective-permute-start(bf16[32,2048]{1,0:T(8,128)(2,1)S(1)} %collective-permute-done.5.x3), channel_id=1, source_target_pairs={{0,16},{4,20},{8,24},{12,28},{16,0},{20,4},{24,8},{28,12},{1,17},{... | collective-permute-start | bytes 393224 | tf_op jit(solution)/shard_map/ppermute | solution.py:22
  16.1 0.0 collective-permute-done.q1
  16.2 2.1 %local_scores.1 = (bf16[256,1024]{1,0:T(8,128)(2,1)S(1)}, bf16[256,1024]{1,0:T(8,128)(2,1)S(1)}, f32[8,2048]{1,0:T(8,128)S(1)}, bf16[128,2048]{1,0:T(8,128)(2,1)S(1)}, bf16[96,1024]{1,0:T(8,128)(2,1)S(1)}) custom-call(s32[3,16]{1,0:T(4,128)S(1)} %copy-done.3, s32[1]{0:T(128)} %bitcast.core_ref, bf16[128,2048]{1,0:T(8,128)(2,1)S(1)} %bitcast.18, ...), custom_call_target="tpu_custom_call" | custom-call | tf_op jit(solution)/shard_map/local_scores/pallas_call | solution.py:216
  18.2 0.2 collective-permute-done.3.grads.rows.g0
  18.5 0.1 collective-permute-start.10
  18.6 0.5 %collective-permute-start.9 = (bf16[128,384]{1,0:T(8,128)(2,1)S(1)}, bf16[128,384]{1,0:T(8,128)(2,1)S(1)}, u32[]{:S(2)}, u32[]{:S(2)}) collective-permute-start(bf16[128,384]{1,0:T(8,128)(2,1)S(1)} %get-tuple-element.59), channel_id=1, source_target_pairs={{0,4},{4,0},{8,12},{12,8},{16,20},{20,16},{24,28},{28,24},{1,5},{5... | collective-permute-start | bytes 294920 | tf_op jit(solution)/shard_map/ppermute | solution.py:22
  19.1 0.1 collective-permute-start.8
  19.1 1.2 %own_delta.1 = (bf16[48,1024]{1,0:T(8,128)(2,1)S(1)}, f32[8,1024]{1,0:T(8,128)S(1)}) custom-call(s32[3,16]{1,0:T(4,128)S(1)} %copy-done.3, s32[1]{0:T(128)} %bitcast.core_ref, bf16[256,1024]{1,0:T(8,128)(2,1)S(1)} %get-tuple-element.46.exps.exp0, bf16[128,2048]{1,0:T(8,128)(2,1)S(1)} %get-tuple-element.50.near, bf16[128,2048]{1,0:T(8,128)(2,1)S(1)} %bitcast.11, ...), custom_call_target="tpu_custom_call" | custom-call | tf_op jit(solution)/shard_map/own_delta/pallas_call | solution.py:266
  20.3 0.0 collective-permute-done.8.refs_0_
  20.3 0.0 collective-permute-done.10.refs_2_
  20.3 0.0 collective-permute-done.9.refs_1_
  20.3 0.0 collective-permute-done.4.x2
  20.4 0.0 collective-permute-done.7.d3
  20.4 2.3 %far_levels.1 = (bf16[32,2048]{1,0:T(8,128)(2,1)S(1)}, bf16[32,2048]{1,0:T(8,128)(2,1)S(1)}, bf16[32,2048]{1,0:T(8,128)(2,1)S(1)}, bf16[32,2048]{1,0:T(8,128)(2,...) custom-call(s32[3,16]{1,0:T(4,128)S(1)} %copy-done.3, ...), custom_call_target="tpu_custom_call" | custom-call | tf_op jit(solution)/shard_map/far_levels/pallas_call | solution.py:395
  22.7 1.6 %collective-permute-start.13 = (bf16[32,2048]{1,0:T(8,128)(2,1)S(1)}, bf16[32,2048]{1,0:T(8,128)(2,1)S(1)}, u32[]{:S(2)}, u32[]{:S(2)}) collective-permute-start(bf16[32,2048]{1,0:T(8,128)(2,1)S(1)} %get-tuple-element.72), channel_id=1, source_target_pairs={{0,16},{4,20},{8,24},{12,28},{16,0},{20,4},{24,8},{28,12},{1,17},{... | collective-permute-start | bytes 393224 | tf_op jit(solution)/shard_map/ppermute | solution.py:22
  24.3 1.5 %collective-permute-start.11 = (bf16[32,2048]{1,0:T(8,128)(2,1)S(1)}, bf16[32,2048]{1,0:T(8,128)(2,1)S(1)}, u32[]{:S(2)}, u32[]{:S(2)}) collective-permute-start(bf16[32,2048]{1,0:T(8,128)(2,1)S(1)} %get-tuple-element.69), channel_id=1, source_target_pairs={{0,8},{4,12},{8,0},{12,4},{16,24},{20,28},{24,16},{28,20},{1,9},{5... | collective-permute-start | bytes 393224 | tf_op jit(solution)/shard_map/ppermute | solution.py:22
  25.8 0.0 collective-permute-start.12
  25.8 0.5 %collective-permute-start.16 = (bf16[32,2048]{1,0:T(8,128)(2,1)S(1)}, bf16[32,2048]{1,0:T(8,128)(2,1)S(1)}, u32[]{:S(2)}, u32[]{:S(2)}) collective-permute-start(bf16[32,2048]{1,0:T(8,128)(2,1)S(1)} %get-tuple-element.75), channel_id=1, source_target_pairs={{0,16},{4,20},{8,24},{12,28},{16,0},{20,4},{24,8},{28,12},{1,17},{... | collective-permute-start | bytes 393224 | tf_op jit(solution)/shard_map/ppermute | solution.py:22
  26.3 2.3 %collective-permute-done.13.there = bf16[32,2048]{1,0:T(8,128)(2,1)S(1)} collective-permute-done((bf16[32,2048]{1,0:T(8,128)(2,1)S(1)}, bf16[32,2048]{1,0:T(8,128)(2,1)S(1)}, u32[]{:S(2)}, u32[]{:S(2)}) %collective-permute-start.13) | collective-permute-done | bytes 131104 | tf_op jit(solution)/shard_map/ppermute | solution.py:22
  28.6 1.6 %collective-permute-start.14 = (bf16[16,2048]{1,0:T(8,128)(2,1)S(1)}, bf16[16,2048]{1,0:T(8,128)(2,1)S(1)}, u32[]{:S(2)}, u32[]{:S(2)}) collective-permute-start(bf16[16,2048]{1,0:T(8,128)(2,1)S(1)} %get-tuple-element.73), channel_id=1, source_target_pairs={{0,8},{4,12},{8,0},{12,4},{16,24},{20,28},{24,16},{28,20},{1,9},{5... | collective-permute-start | bytes 196616 | tf_op jit(solution)/shard_map/ppermute | solution.py:22
  30.2 0.0 collective-permute-start.15
  30.2 2.9 %near_levels.1 = (bf16[128,3072]{1,0:T(8,128)(2,1)S(1)}, bf16[128,1536]{1,0:T(8,128)(2,1)S(1)}, bf16[128,1536]{1,0:T(8,128)(2,1)S(1)}) custom-call(s32[3,16]{1,0:T(4,128)S(1)} %copy-done.3, s32[1]{0:T(128)} %bitcast.core_ref, bf16[256,1024]{1,0:T(8,128)(2,1)S(1)} %get-tuple-element.46.exps.exp0, bf16[256,1024]{1,0:T(8,128)(2,1)S(1)} %get-tuple-element.47.exp1, ...), custom_call_target="tpu_custom_call" | custom-call | tf_op jit(solution)/shard_map/near_levels/pallas_call | solution.py:479
  33.1 0.0 collective-permute-done.11.x
  33.1 0.7 %collective-permute-start.17 = (bf16[128,1536]{1,0:T(8,128)(2,1)S(1)}, bf16[128,1536]{1,0:T(8,128)(2,1)S(1)}, u32[]{:S(2)}, u32[]{:S(2)}) collective-permute-start(bf16[128,1536]{1,0:T(8,128)(2,1)S(1)} %get-tuple-element.82), channel_id=1, source_target_pairs={{0,4},{4,0},{8,12},{12,8},{16,20},{20,16},{24,28},{28,24},{1,5},{5... | collective-permute-start | bytes 1179656 | tf_op jit(solution)/shard_map/ppermute | solution.py:22
  33.8 0.0 collective-permute-done.12.x
  33.9 0.0 collective-permute-done.16.y
  33.9 0.9 %collective-permute-done.14.x3 = bf16[16,2048]{1,0:T(8,128)(2,1)S(1)} collective-permute-done((bf16[16,2048]{1,0:T(8,128)(2,1)S(1)}, bf16[16,2048]{1,0:T(8,128)(2,1)S(1)}, u32[]{:S(2)}, u32[]{:S(2)}) %collective-permute-start.14) | collective-permute-done | bytes 65568 | tf_op jit(solution)/shard_map/ppermute | solution.py:22
  34.7 0.0 collective-permute-done.15.x3
  34.7 0.5 %collective-permute-start.18 = (bf16[128,1536]{1,0:T(8,128)(2,1)S(1)}, bf16[128,1536]{1,0:T(8,128)(2,1)S(1)}, u32[]{:S(2)}, u32[]{:S(2)}) collective-permute-start(bf16[128,1536]{1,0:T(8,128)(2,1)S(1)} %get-tuple-element.83), channel_id=1, source_target_pairs={{0,4},{4,0},{8,12},{12,8},{16,20},{20,16},{24,28},{28,24},{1,5},{5... | collective-permute-start | bytes 1179656 | tf_op jit(solution)/shard_map/ppermute | solution.py:22
  35.3 0.0 collective-permute-start.19
  35.3 0.9 %add_own_half.1 = (bf16[128,1024]{1,0:T(8,128)(2,1)S(1)}, bf16[128,1024]{1,0:T(8,128)(2,1)S(1)}, bf16[128,1024]{1,0:T(8,128)(2,1)S(1)}) custom-call(s32[3,16]{1,0:T(4,128)S(1)} %copy-done.3, s32[1]{0:T(128)} %bitcast.core_ref, bf16[128,3072]{1,0:T(8,128)(2,1)S(1)} %get-tuple-element.67.base, bf16[32,2048]{1,0:T(8,128)(2,1)S(1)} %collective-permute-done.11.x, ...), custom_call_target="tpu_custom_call" | custom-call | tf_op jit(solution)/shard_map/add_own_half/pallas_call | solution.py:540
  36.2 0.6 %collective-permute-done.19.y = bf16[32,2048]{1,0:T(8,128)(2,1)S(1)} collective-permute-done((bf16[32,2048]{1,0:T(8,128)(2,1)S(1)}, bf16[32,2048]{1,0:T(8,128)(2,1)S(1)}, u32[]{:S(2)}, u32[]{:S(2)}) %collective-permute-start.19) | collective-permute-done | bytes 131104 | tf_op jit(solution)/shard_map/ppermute | solution.py:22
  36.8 0.0 collective-permute-done.17.base0
  36.8 0.0 collective-permute-done.18.base1
  36.8 1.9 %add_other_half.1 = (bf16[128,2048]{1,0:T(8,128)(2,1)}, bf16[128,2048]{1,0:T(8,128)(2,1)}, bf16[128,2048]{1,0:T(8,128)(2,1)}) custom-call(s32[3,16]{1,0:T(4,128)S(1)} %copy-done.3, s32[1]{0:T(128)} %bitcast.core_ref, bf16[128,1024]{1,0:T(8,128)(2,1)S(1)} %get-tuple-element.79.own_q, bf16[128,1024]{1,0:T(8,128)(2,1)S(1)} %get-tuple-element.80.own_k, ...), custom_call_target="tpu_custom_call" | custom-call | tf_op jit(solution)/shard_map/add_other_half/pallas_call | solution.py:595
  (9 shorter events, 0.1 us)
Async XLA Ops:
  0.6 5.7 %collective-permute-start.2 = (bf16[128,2048]{1,0:T(8,128)(2,1)}, bf16[128,2048]{1,0:T(8,128)(2,1)S(1)}, u32[]{:S(2)}, u32[]{:S(2)}) collective-permute-start(bf16[128,2048]{1,0:T(8,128)(2,1)} %bitcast.8), channel_id=1, source_target_pairs={{0,4},{4,0},{8,12},{12,8},{16,20},{20,16},{24,28},{28,24},{1,5},{5... | collective-permute-start | bytes 1572872 | tf_op jit(solution)/shard_map/ppermute | solution.py:22
  1.1 5.2 %collective-permute-start.1 = (bf16[128,2048]{1,0:T(8,128)(2,1)}, bf16[128,2048]{1,0:T(8,128)(2,1)S(1)}, u32[]{:S(2)}, u32[]{:S(2)}) collective-permute-start(bf16[128,2048]{1,0:T(8,128)(2,1)} %bitcast.13), channel_id=1, source_target_pairs={{0,4},{4,0},{8,12},{12,8},{16,20},{20,16},{24,28},{28,24},{1,5},{5... | collective-permute-start | bytes 1572872 | tf_op jit(solution)/shard_map/ppermute | solution.py:22
  1.2 14.9 %collective-permute-start = (bf16[128,2048]{1,0:T(8,128)(2,1)}, bf16[128,2048]{1,0:T(8,128)(2,1)S(1)}, u32[]{:S(2)}, u32[]{:S(2)}) collective-permute-start(bf16[128,2048]{1,0:T(8,128)(2,1)} %bitcast.17), channel_id=1, source_target_pairs={{0,4},{4,0},{8,12},{12,8},{16,20},{20,16},{24,28},{28,24},{1,5},{5... | collective-permute-start | bytes 1572872 | tf_op jit(solution)/shard_map/ppermute | solution.py:22
  1.7 16.8 %collective-permute-start.3 = (bf16[128,2048]{1,0:T(8,128)(2,1)}, bf16[128,2048]{1,0:T(8,128)(2,1)S(1)}, u32[]{:S(2)}, u32[]{:S(2)}) collective-permute-start(bf16[128,2048]{1,0:T(8,128)(2,1)} %bitcast.20), channel_id=1, source_target_pairs={{0,3},{1,0},{2,1},{3,2},{4,7},{5,4},{6,5},{7,6},{8,11},{9,8},{10,9... | collective-permute-start | bytes 1572872 | tf_op jit(solution)/shard_map/ppermute | solution.py:619
  6.3 9.8 %copy-start = (bf16[1,128,2048]{2,1,0:T(8,128)(2,1)S(1)}, bf16[1,128,2048]{2,1,0:T(8,128)(2,1)}, u32[]{:S(2)}) copy-start(bf16[1,128,2048]{2,1,0:T(8,128)(2,1)} %param.7) | copy-start | bytes 1572868
  6.3 9.8 %copy-start.1 = (bf16[1,128,2048]{2,1,0:T(8,128)(2,1)S(1)}, bf16[1,128,2048]{2,1,0:T(8,128)(2,1)}, u32[]{:S(2)}) copy-start(bf16[1,128,2048]{2,1,0:T(8,128)(2,1)} %param.6) | copy-start | bytes 1572868
  6.4 9.8 %copy-start.2 = (bf16[1,128,2048]{2,1,0:T(8,128)(2,1)S(1)}, bf16[1,128,2048]{2,1,0:T(8,128)(2,1)}, u32[]{:S(2)}) copy-start(bf16[1,128,2048]{2,1,0:T(8,128)(2,1)} %param.5) | copy-start | bytes 1572868
  7.8 8.4 %copy-start.3 = (s32[3,16]{1,0:T(4,128)S(1)}, s32[3,16]{1,0:T(4,128)}, u32[]{:S(2)}) copy-start(s32[3,16]{1,0:T(4,128)} %offs_ref.11) | copy-start | bytes 580
  7.8 5.9 %collective-permute-start.5 = (bf16[32,2048]{1,0:T(8,128)(2,1)S(1)}, bf16[32,2048]{1,0:T(8,128)(2,1)S(1)}, u32[]{:S(2)}, u32[]{:S(2)}) collective-permute-start(bf16[32,2048]{1,0:T(8,128)(2,1)S(1)} %get-tuple-element.55.own3), channel_id=1, source_target_pairs={{0,8},{4,12},{8,0},{12,4},{16,24},{20,28},{24,16},{28,20},{1,9},{5... | collective-permute-start | bytes 393224 | tf_op jit(solution)/shard_map/ppermute | solution.py:22
  9.3 5.3 %collective-permute-start.6 = (bf16[32,2048]{1,0:T(8,128)(2,1)S(1)}, bf16[32,2048]{1,0:T(8,128)(2,1)S(1)}, u32[]{:S(2)}, u32[]{:S(2)}) collective-permute-start(bf16[32,2048]{1,0:T(8,128)(2,1)S(1)} %get-tuple-element.55.own3), channel_id=1, source_target_pairs={{0,16},{4,20},{8,24},{12,28},{16,0},{20,4},{24,8},{28,12},{1,17},{... | collective-permute-start | bytes 393224 | tf_op jit(solution)/shard_map/ppermute | solution.py:22
  10.9 9.5 %collective-permute-start.4 = (bf16[64,2048]{1,0:T(8,128)(2,1)S(1)}, bf16[64,2048]{1,0:T(8,128)(2,1)S(1)}, u32[]{:S(2)}, u32[]{:S(2)}) collective-permute-start(bf16[64,2048]{1,0:T(8,128)(2,1)S(1)} %get-tuple-element.54.own2), channel_id=1, source_target_pairs={{0,8},{4,12},{8,0},{12,4},{16,24},{20,28},{24,16},{28,20},{1,9},{5... | collective-permute-start | bytes 786440 | tf_op jit(solution)/shard_map/ppermute | solution.py:22
  14.6 5.7 %collective-permute-start.7 = (bf16[32,2048]{1,0:T(8,128)(2,1)S(1)}, bf16[32,2048]{1,0:T(8,128)(2,1)S(1)}, u32[]{:S(2)}, u32[]{:S(2)}) collective-permute-start(bf16[32,2048]{1,0:T(8,128)(2,1)S(1)} %collective-permute-done.5.x3), channel_id=1, source_target_pairs={{0,16},{4,20},{8,24},{12,28},{16,0},{20,4},{24,8},{28,12},{1,17},{... | collective-permute-start | bytes 393224 | tf_op jit(solution)/shard_map/ppermute | solution.py:22
  18.5 1.8 %collective-permute-start.10 = (bf16[128,384]{1,0:T(8,128)(2,1)S(1)}, bf16[128,384]{1,0:T(8,128)(2,1)S(1)}, u32[]{:S(2)}, u32[]{:S(2)}) collective-permute-start(bf16[128,384]{1,0:T(8,128)(2,1)S(1)} %get-tuple-element.60), channel_id=1, source_target_pairs={{0,4},{4,0},{8,12},{12,8},{16,20},{20,16},{24,28},{28,24},{1,5},{5... | collective-permute-start | bytes 294920 | tf_op jit(solution)/shard_map/ppermute | solution.py:22
  18.6 1.8 %collective-permute-start.9 = (bf16[128,384]{1,0:T(8,128)(2,1)S(1)}, bf16[128,384]{1,0:T(8,128)(2,1)S(1)}, u32[]{:S(2)}, u32[]{:S(2)}) collective-permute-start(bf16[128,384]{1,0:T(8,128)(2,1)S(1)} %get-tuple-element.59), channel_id=1, source_target_pairs={{0,4},{4,0},{8,12},{12,8},{16,20},{20,16},{24,28},{28,24},{1,5},{5... | collective-permute-start | bytes 294920 | tf_op jit(solution)/shard_map/ppermute | solution.py:22
  19.1 1.3 %collective-permute-start.8 = (bf16[128,256]{1,0:T(8,128)(2,1)S(1)}, bf16[128,256]{1,0:T(8,128)(2,1)S(1)}, u32[]{:S(2)}, u32[]{:S(2)}) collective-permute-start(bf16[128,256]{1,0:T(8,128)(2,1)S(1)} %get-tuple-element.58), channel_id=1, source_target_pairs={{0,4},{4,0},{8,12},{12,8},{16,20},{20,16},{24,28},{28,24},{1,5},{5... | collective-permute-start | bytes 196616 | tf_op jit(solution)/shard_map/ppermute | solution.py:22
  22.7 5.9 %collective-permute-start.13 = (bf16[32,2048]{1,0:T(8,128)(2,1)S(1)}, bf16[32,2048]{1,0:T(8,128)(2,1)S(1)}, u32[]{:S(2)}, u32[]{:S(2)}) collective-permute-start(bf16[32,2048]{1,0:T(8,128)(2,1)S(1)} %get-tuple-element.72), channel_id=1, source_target_pairs={{0,16},{4,20},{8,24},{12,28},{16,0},{20,4},{24,8},{28,12},{1,17},{... | collective-permute-start | bytes 393224 | tf_op jit(solution)/shard_map/ppermute | solution.py:22
  24.3 8.9 %collective-permute-start.11 = (bf16[32,2048]{1,0:T(8,128)(2,1)S(1)}, bf16[32,2048]{1,0:T(8,128)(2,1)S(1)}, u32[]{:S(2)}, u32[]{:S(2)}) collective-permute-start(bf16[32,2048]{1,0:T(8,128)(2,1)S(1)} %get-tuple-element.69), channel_id=1, source_target_pairs={{0,8},{4,12},{8,0},{12,4},{16,24},{20,28},{24,16},{28,20},{1,9},{5... | collective-permute-start | bytes 393224 | tf_op jit(solution)/shard_map/ppermute | solution.py:22
  25.8 8.1 %collective-permute-start.12 = (bf16[32,2048]{1,0:T(8,128)(2,1)S(1)}, bf16[32,2048]{1,0:T(8,128)(2,1)S(1)}, u32[]{:S(2)}, u32[]{:S(2)}) collective-permute-start(bf16[32,2048]{1,0:T(8,128)(2,1)S(1)} %get-tuple-element.70), channel_id=1, source_target_pairs={{0,12},{4,8},{8,4},{12,0},{16,28},{20,24},{24,20},{28,16},{1,13},{... | collective-permute-start | bytes 393224 | tf_op jit(solution)/shard_map/ppermute | solution.py:22
  25.8 8.1 %collective-permute-start.16 = (bf16[32,2048]{1,0:T(8,128)(2,1)S(1)}, bf16[32,2048]{1,0:T(8,128)(2,1)S(1)}, u32[]{:S(2)}, u32[]{:S(2)}) collective-permute-start(bf16[32,2048]{1,0:T(8,128)(2,1)S(1)} %get-tuple-element.75), channel_id=1, source_target_pairs={{0,16},{4,20},{8,24},{12,28},{16,0},{20,4},{24,8},{28,12},{1,17},{... | collective-permute-start | bytes 393224 | tf_op jit(solution)/shard_map/ppermute | solution.py:22
  28.6 6.1 %collective-permute-start.14 = (bf16[16,2048]{1,0:T(8,128)(2,1)S(1)}, bf16[16,2048]{1,0:T(8,128)(2,1)S(1)}, u32[]{:S(2)}, u32[]{:S(2)}) collective-permute-start(bf16[16,2048]{1,0:T(8,128)(2,1)S(1)} %get-tuple-element.73), channel_id=1, source_target_pairs={{0,8},{4,12},{8,0},{12,4},{16,24},{20,28},{24,16},{28,20},{1,9},{5... | collective-permute-start | bytes 196616 | tf_op jit(solution)/shard_map/ppermute | solution.py:22
  30.2 4.6 %collective-permute-start.15 = (bf16[16,2048]{1,0:T(8,128)(2,1)S(1)}, bf16[16,2048]{1,0:T(8,128)(2,1)S(1)}, u32[]{:S(2)}, u32[]{:S(2)}) collective-permute-start(bf16[16,2048]{1,0:T(8,128)(2,1)S(1)} %get-tuple-element.74), channel_id=1, source_target_pairs={{0,12},{4,8},{8,4},{12,0},{16,28},{20,24},{24,20},{28,16},{1,13},{... | collective-permute-start | bytes 196616 | tf_op jit(solution)/shard_map/ppermute | solution.py:22
  33.1 3.7 %collective-permute-start.17 = (bf16[128,1536]{1,0:T(8,128)(2,1)S(1)}, bf16[128,1536]{1,0:T(8,128)(2,1)S(1)}, u32[]{:S(2)}, u32[]{:S(2)}) collective-permute-start(bf16[128,1536]{1,0:T(8,128)(2,1)S(1)} %get-tuple-element.82), channel_id=1, source_target_pairs={{0,4},{4,0},{8,12},{12,8},{16,20},{20,16},{24,28},{28,24},{1,5},{5... | collective-permute-start | bytes 1179656 | tf_op jit(solution)/shard_map/ppermute | solution.py:22
  34.7 2.1 %collective-permute-start.18 = (bf16[128,1536]{1,0:T(8,128)(2,1)S(1)}, bf16[128,1536]{1,0:T(8,128)(2,1)S(1)}, u32[]{:S(2)}, u32[]{:S(2)}) collective-permute-start(bf16[128,1536]{1,0:T(8,128)(2,1)S(1)} %get-tuple-element.83), channel_id=1, source_target_pairs={{0,4},{4,0},{8,12},{12,8},{16,20},{20,16},{24,28},{28,24},{1,5},{5... | collective-permute-start | bytes 1179656 | tf_op jit(solution)/shard_map/ppermute | solution.py:22
  35.3 1.5 %collective-permute-start.19 = (bf16[32,2048]{1,0:T(8,128)(2,1)S(1)}, bf16[32,2048]{1,0:T(8,128)(2,1)S(1)}, u32[]{:S(2)}, u32[]{:S(2)}) collective-permute-start(bf16[32,2048]{1,0:T(8,128)(2,1)S(1)} %collective-permute-done.16.y), channel_id=1, source_target_pairs={{0,4},{4,0},{8,12},{12,8},{16,20},{20,16},{24,28},{28,24},{1,5},{5... | collective-permute-start | bytes 393224 | tf_op jit(solution)/shard_map/ppermute | solution.py:22

commit v10 on v9

--- a/solution.py
+++ b/solution.py
@@ -11,6 +11,7 @@
 BF16 = jnp.bfloat16
 NEG = -1e30
 VMEM_LIMIT = 32 * 1024 * 1024
+PIECES = 4
 
 
 def params():
@@ -412,8 +413,8 @@
     levels, per, dim, offs_ref, core_ref, exp0, exp1, stats2, near, ngrad, dqt,
     q0, q1, k0, k1, v0, v1, g0, *refs,
 ):
-    mine, *others = refs[-3:]
-    g1 = side(*(ref[...] for ref in refs[:-3]))
+    mine, *others = refs[-1 - PIECES :]
+    g1 = side(*(ref[...] for ref in refs[: -1 - PIECES]))
     tok = q0.shape[0]
     n1 = tok // 2
     sel = tok // 4 + tok // 8
@@ -458,7 +459,8 @@
                 both = stack(keys[:, cols[h]], near[:tok, kc])
                 dq[h] = dot(both.T, ds[h][:, at]) + dot(far, pick)
             for h in each:
-                ref, to = (others[h // (per // 2)], h % (per // 2)) if block else (mine, h)
+                part = per // PIECES
+                ref, to = (others[h // part], h % part) if block else (mine, h)
                 to *= 3 * dim
                 ref[:, to : to + dim] = (dq[h] * scale).T.astype(BF16)
                 ref[:, to + dim : to + 3 * dim] = kv[h].astype(BF16)
@@ -475,7 +477,7 @@
     def mid_spec(a):
         return pl.BlockSpec((a.shape[0], a.shape[1] // steps), lambda i, o, c: (0, i))
 
-    widths = [3 * per * dim, 3 * per * dim // 2, 3 * per * dim // 2]
+    widths = [3 * per * dim] + [3 * per * dim // PIECES] * PIECES
     return pl.pallas_call(
         functools.partial(near_kernel, levels, per, dim),
         grid_spec=pltpu.PrefetchScalarGridSpec(
@@ -552,10 +554,9 @@
 
 
 def final_kernel(
-    levels, per, dim, offs_ref, core_ref, own_q, own_k, own_v, base0, base1, x, y, x3,
-    dq, dk, dv, held, sems,
+    levels, per, dim, offs_ref, core_ref, own_q, own_k, own_v, x, y, x3, *refs
 ):
-    outs = dq, dk, dv
+    bases, outs, (held, sems) = refs[:PIECES], refs[PIECES : PIECES + 3], refs[-2:]
     n3 = x3.shape[0]
     copies = []
 
@@ -567,14 +568,12 @@
     for part, ref in enumerate((own_q, own_k, own_v)):
         send(part, ref, core_ref[0], 0, per)
     far_core = 1 - core_ref[0]
-    half = per // 2
+    each = per // PIECES
     for h in range(per):
-        base = base1 if h >= half else base0
-        at = 3 * (h % half) * dim
-        held[0, :, h * dim : (h + 1) * dim] = base[:, at : at + dim]
+        at = 3 * (h % each) * dim
+        held[0, :, h * dim : (h + 1) * dim] = bases[h // each][:, at : at + dim]
     send(0, held.at[0], far_core, 0, per)
     third = (x3[...].astype(F32) + y[n3:].astype(F32)).astype(BF16)
-    bases = [base0, base1]
     for h, total in add_far(levels, dim, offs_ref, far_core * per, bases, x, third, 4):
         cols = slice(h * dim, (h + 1) * dim)
         held[1, :, cols] = total[:, :dim]
@@ -589,7 +588,7 @@
 
 def final_call(offsets, core, own, parts, dim):
     levels, heads = offsets.shape
-    tok = parts[0].shape[0]
+    tok = own[0].shape[0]
     per = heads // 2
     away = pl.BlockSpec(memory_space=pl.ANY)
     return pl.pallas_call(
@@ -625,12 +624,11 @@
         pltpu.with_memory_space_constraint(offsets, pltpu.HBM), core, kept, [k_oth, v_oth], dim
     )
     x3, y3, x2 = exchange(three, 2), exchange(three, 4), exchange(two, 2)
-    x3, y3 = lax.optimization_barrier((x3, y3))
     d3 = exchange(x3, 4)
     raw = [q, q_oth, k, k_oth, v, v_oth]
     pre = pre_call(offsets, core, raw, dim)
     exp0, exp1, stats, near, selq = pre
-    grads = lax.optimization_barrier((grads, stats))[0]
+    y3, grads = lax.optimization_barrier((y3, grads, stats))[:2]
     sel = grad_call(offsets, core, exp0, near, v, grads, dim)
     half = heads // 2
     cuts = [half * i // 3 for i in range(4)]
@@ -645,15 +643,13 @@
     xa, xb, y = exchange(xa, 2), exchange(xb, 3), exchange(yab, 4)
     xa3, xb3 = exchange(thirds[0], 2), exchange(thirds[1], 3)
     yy = exchange(y, 1)
-    mine, first, second = near_call(
+    mine, *others = near_call(
         offsets, core, [exp0, exp1, stats2, near, ngrad, dqt], raw, [grads, *other], dim
     )
-    first = exchange(first, 1)
-    second, xa, xb, xa3, xb3, y = lax.optimization_barrier((second, xa, xb, xa3, xb3, y))
+    last, xa, xb, xa3, xb3, y = lax.optimization_barrier((others[-1], xa, xb, xa3, xb3, y))
+    bases = [exchange(piece, 1) for piece in (*others[:-1], last)]
     own = list(own_call(offsets, core, [mine, xa, y, xa3], dim))
-    dq, dk, dv = final_call(
-        offsets, core, own, [first, exchange(second, 1), xb, yy, xb3], dim
-    )
+    dq, dk, dv = final_call(offsets, core, own, [xb, yy, xb3, *bases], dim)
     return dq[None], dk[None], dv[None]
 
 

time: 38.9 us -> 38.7 us (level)
  waiting for transfers between devices: 7.23 us -> 6.5 us
  starting transfers between devices: 17.9 us -> 18.4 us
    ppermute x19 -> x21, waiting for transfers between devices: 7.03 us -> 5.86 us  [exchange(): return lax.ppermute(value, 'seq', [(i, i ^ bits) for i in range(count)])]
    ppermute x19 -> x21, starting transfers between devices: 13.2 us -> 13.7 us  [exchange(): return lax.ppermute(value, 'seq', [(i, i ^ bits) for i in range(count)])]
    ppermute x1, waiting for transfers between devices: 0.2 us -> 0.64 us  [per_device(): lax.ppermute(out_grads[0], 'section', [(i, (i - 1) % sections) for i in r...]
  transfers between devices with their start and end apart: 20 -> 22, of which waited for: 6 -> 5; matrix products, arithmetic and copies ran while one was open for 0% -> 0% of each run, Pallas kernels for 22% -> 22%
where the time goes in v10:
time: 38.7 us; the launch traced here: 38.5 us
  starting transfers between devices  18.4 us (48%)
  Pallas kernels  12.8 us (33%)
  waiting for transfers between devices  6.5 us (17%)
  between operations  0.8 us (2%)
    ppermute x21, starting transfers between devices, exchange(): return lax.ppermute(value, 'seq', [(i, i ^ bits) for i in range(count)])  13.7 us
    ppermute x21, waiting for transfers between devices, exchange(): return lax.ppermute(value, 'seq', [(i, i ^ bits) for i in range(count)])  5.86 us
    ppermute x1, starting transfers between devices, per_device(): lax.ppermute(out_grads[0], 'section', [(i, (i - 1) % sections) for i in r...  4.67 us
    pallas_call x1, Pallas kernels, near_call(): pl.pallas_call(functools.partial(near_kernel, levels, per, dim), grid_spe...  2.94 us
    pallas_call x1, Pallas kernels, far_call(): pl.pallas_call(functools.partial(far_kernel, levels, per, dim), grid_spec...  2.31 us
    pallas_call x1, Pallas kernels, pre_call(): pl.pallas_call(functools.partial(pre_kernel, levels, per, dim), grid_spec...  2.07 us
    pallas_call x1, Pallas kernels, final_call(): pl.pallas_call(functools.partial(final_kernel, levels, per, dim), grid_sp...  1.89 us
    pallas_call x1, Pallas kernels, pick_call(): pl.pallas_call(functools.partial(pick_kernel, levels, per, dim), grid_spe...  1.39 us
  transfers between devices with their start and end apart: 22, of which 5 were waited for; matrix products, arithmetic and copies ran while one was open for 0% of the time, Pallas kernels for 22%

profile of v10, /device:TPU:0, one launch (start us, length us, event | category | flops | bytes accessed | tf_op | source)
XLA Modules:
  0.0 38.5 jit_solution(7153756116860357447)
XLA Ops:
  0.6 0.5 %collective-permute-start.2 = (bf16[128,2048]{1,0:T(8,128)(2,1)}, bf16[128,2048]{1,0:T(8,128)(2,1)S(1)}, u32[]{:S(2)}, u32[]{:S(2)}) collective-permute-start(bf16[128,2048]{1,0:T(8,128)(2,1)} %bitcast.8), channel_id=1, source_target_pairs={{0,4},{4,0},{8,12},{12,8},{16,20},{20,16},{24,28},{28,24},{1,5},{5... | collective-permute-start | bytes 1572872 | tf_op jit(solution)/shard_map/ppermute | solution.py:23
  1.1 0.1 collective-permute-start.1
  1.2 0.4 %collective-permute-start = (bf16[128,2048]{1,0:T(8,128)(2,1)}, bf16[128,2048]{1,0:T(8,128)(2,1)S(1)}, u32[]{:S(2)}, u32[]{:S(2)}) collective-permute-start(bf16[128,2048]{1,0:T(8,128)(2,1)} %bitcast.17), channel_id=1, source_target_pairs={{0,4},{4,0},{8,12},{12,8},{16,20},{20,16},{24,28},{28,24},{1,5},{5... | collective-permute-start | bytes 1572872 | tf_op jit(solution)/shard_map/ppermute | solution.py:23
  1.7 4.7 %collective-permute-start.4 = (bf16[128,2048]{1,0:T(8,128)(2,1)}, bf16[128,2048]{1,0:T(8,128)(2,1)S(1)}, u32[]{:S(2)}, u32[]{:S(2)}) collective-permute-start(bf16[128,2048]{1,0:T(8,128)(2,1)} %bitcast.20), channel_id=1, source_target_pairs={{0,3},{1,0},{2,1},{3,2},{4,7},{5,4},{6,5},{7,6},{8,11},{9,8},{10,9... | collective-permute-start | bytes 1572872 | tf_op jit(solution)/shard_map/ppermute | solution.py:618
  6.3 0.0 collective-permute-done.2.v1
  6.3 0.0 collective-permute-done.1.k1
  6.4 1.4 %pick_rows.1 = (bf16[64,2048]{1,0:T(8,128)(2,1)S(1)}, bf16[32,2048]{1,0:T(8,128)(2,1)S(1)}) custom-call(s32[1]{0:T(128)} %bitcast.core_ref, s32[3,16]{1,0:T(4,128)} %offs_ref.11, bf16[128,2048]{1,0:T(8,128)(2,1)} %bitcast.14, bf16[128,2048]{1,0:T(8,128)(2,1)} %bitcast.9, bf16[128,2048]{1,0:T(8,128)(2,1)S(1)} %collective-permute-done.1.k1, ...), custom_call_target="tpu_custom_call" | custom-call | tf_op jit(solution)/shard_map/pick_rows/pallas_call | solution.py:124
  7.8 0.0 copy-start.3
  7.8 1.6 %collective-permute-start.6 = (bf16[32,2048]{1,0:T(8,128)(2,1)S(1)}, bf16[32,2048]{1,0:T(8,128)(2,1)S(1)}, u32[]{:S(2)}, u32[]{:S(2)}) collective-permute-start(bf16[32,2048]{1,0:T(8,128)(2,1)S(1)} %get-tuple-element.52.own3), channel_id=1, source_target_pairs={{0,8},{4,12},{8,0},{12,4},{16,24},{20,28},{24,16},{28,20},{1,9},{5... | collective-permute-start | bytes 393224 | tf_op jit(solution)/shard_map/ppermute | solution.py:23
  9.3 0.5 %collective-permute-start.5 = (bf16[64,2048]{1,0:T(8,128)(2,1)S(1)}, bf16[64,2048]{1,0:T(8,128)(2,1)S(1)}, u32[]{:S(2)}, u32[]{:S(2)}) collective-permute-start(bf16[64,2048]{1,0:T(8,128)(2,1)S(1)} %get-tuple-element.56.own2), channel_id=1, source_target_pairs={{0,8},{4,12},{8,0},{12,4},{16,24},{20,28},{24,16},{28,20},{1,9},{5... | collective-permute-start | bytes 786440 | tf_op jit(solution)/shard_map/ppermute | solution.py:23
  9.9 1.5 %collective-permute-start.3 = (bf16[32,2048]{1,0:T(8,128)(2,1)S(1)}, bf16[32,2048]{1,0:T(8,128)(2,1)S(1)}, u32[]{:S(2)}, u32[]{:S(2)}) collective-permute-start(bf16[32,2048]{1,0:T(8,128)(2,1)S(1)} %get-tuple-element.52.own3), channel_id=1, source_target_pairs={{0,16},{4,20},{8,24},{12,28},{16,0},{20,4},{24,8},{28,12},{1,17},{... | collective-permute-start | bytes 393224 | tf_op jit(solution)/shard_map/ppermute | solution.py:23
  11.4 2.8 %collective-permute-done.6.x3 = bf16[32,2048]{1,0:T(8,128)(2,1)S(1)} collective-permute-done((bf16[32,2048]{1,0:T(8,128)(2,1)S(1)}, bf16[32,2048]{1,0:T(8,128)(2,1)S(1)}, u32[]{:S(2)}, u32[]{:S(2)}) %collective-permute-start.6) | collective-permute-done | bytes 131104 | tf_op jit(solution)/shard_map/ppermute | solution.py:23
  14.2 1.5 %collective-permute-start.7 = (bf16[32,2048]{1,0:T(8,128)(2,1)S(1)}, bf16[32,2048]{1,0:T(8,128)(2,1)S(1)}, u32[]{:S(2)}, u32[]{:S(2)}) collective-permute-start(bf16[32,2048]{1,0:T(8,128)(2,1)S(1)} %collective-permute-done.6.x3), channel_id=1, source_target_pairs={{0,16},{4,20},{8,24},{12,28},{16,0},{20,4},{24,8},{28,12},{1,17},{... | collective-permute-start | bytes 393224 | tf_op jit(solution)/shard_map/ppermute | solution.py:23
  15.7 0.0 collective-permute-done.q1
  15.7 2.1 %local_scores.1 = (bf16[256,1024]{1,0:T(8,128)(2,1)S(1)}, bf16[256,1024]{1,0:T(8,128)(2,1)S(1)}, f32[8,2048]{1,0:T(8,128)S(1)}, bf16[128,2048]{1,0:T(8,128)(2,1)S(1)}, bf16[96,1024]{1,0:T(8,128)(2,1)S(1)}) custom-call(s32[3,16]{1,0:T(4,128)S(1)} %copy-done.3, s32[1]{0:T(128)} %bitcast.core_ref, bf16[128,2048]{1,0:T(8,128)(2,1)S(1)} %bitcast.18, ...), custom_call_target="tpu_custom_call" | custom-call | tf_op jit(solution)/shard_map/local_scores/pallas_call | solution.py:217
  17.8 0.6 %collective-permute-done.4.grads.rows.g0 = bf16[128,2048]{1,0:T(8,128)(2,1)S(1)} collective-permute-done((bf16[128,2048]{1,0:T(8,128)(2,1)}, bf16[128,2048]{1,0:T(8,128)(2,1)S(1)}, u32[]{:S(2)}, u32[]{:S(2)}) %collective-permute-start.4) | collective-permute-done | bytes 524320 | tf_op jit(solution)/shard_map/ppermute | solution.py:618
  18.4 0.0 collective-permute-done.3.y3
  18.5 0.1 collective-permute-start.10
  18.6 0.5 %collective-permute-start.9 = (bf16[128,384]{1,0:T(8,128)(2,1)S(1)}, bf16[128,384]{1,0:T(8,128)(2,1)S(1)}, u32[]{:S(2)}, u32[]{:S(2)}) collective-permute-start(bf16[128,384]{1,0:T(8,128)(2,1)S(1)} %get-tuple-element.59), channel_id=1, source_target_pairs={{0,4},{4,0},{8,12},{12,8},{16,20},{20,16},{24,28},{28,24},{1,5},{5... | collective-permute-start | bytes 294920 | tf_op jit(solution)/shard_map/ppermute | solution.py:23
  19.1 0.1 collective-permute-start.8
  19.1 1.2 %own_delta.1 = (bf16[48,1024]{1,0:T(8,128)(2,1)S(1)}, f32[8,1024]{1,0:T(8,128)S(1)}) custom-call(s32[3,16]{1,0:T(4,128)S(1)} %copy-done.3, s32[1]{0:T(128)} %bitcast.core_ref, bf16[256,1024]{1,0:T(8,128)(2,1)S(1)} %get-tuple-element.47.exps.exp0, bf16[128,2048]{1,0:T(8,128)(2,1)S(1)} %get-tuple-element.51.near, bf16[128,2048]{1,0:T(8,128)(2,1)S(1)} %bitcast.11, ...), custom_call_target="tpu_custom_call" | custom-call | tf_op jit(solution)/shard_map/own_delta/pallas_call | solution.py:267
  20.3 0.0 collective-permute-done.8.refs_0_
  20.3 0.0 collective-permute-done.10.refs_2_
  20.3 0.0 collective-permute-done.9.refs_1_
  20.4 0.0 collective-permute-done.5.x2
  20.4 0.0 collective-permute-done.7.d3
  20.4 2.3 %far_levels.1 = (bf16[32,2048]{1,0:T(8,128)(2,1)S(1)}, bf16[32,2048]{1,0:T(8,128)(2,1)S(1)}, bf16[32,2048]{1,0:T(8,128)(2,1)S(1)}, bf16[32,2048]{1,0:T(8,128)(2,...) custom-call(s32[3,16]{1,0:T(4,128)S(1)} %copy-done.3, ...), custom_call_target="tpu_custom_call" | custom-call | tf_op jit(solution)/shard_map/far_levels/pallas_call | solution.py:396
  22.7 1.6 %collective-permute-start.13 = (bf16[32,2048]{1,0:T(8,128)(2,1)S(1)}, bf16[32,2048]{1,0:T(8,128)(2,1)S(1)}, u32[]{:S(2)}, u32[]{:S(2)}) collective-permute-start(bf16[32,2048]{1,0:T(8,128)(2,1)S(1)} %get-tuple-element.72), channel_id=1, source_target_pairs={{0,16},{4,20},{8,24},{12,28},{16,0},{20,4},{24,8},{28,12},{1,17},{... | collective-permute-start | bytes 393224 | tf_op jit(solution)/shard_map/ppermute | solution.py:23
  24.3 1.5 %collective-permute-start.11 = (bf16[32,2048]{1,0:T(8,128)(2,1)S(1)}, bf16[32,2048]{1,0:T(8,128)(2,1)S(1)}, u32[]{:S(2)}, u32[]{:S(2)}) collective-permute-start(bf16[32,2048]{1,0:T(8,128)(2,1)S(1)} %get-tuple-element.69), channel_id=1, source_target_pairs={{0,8},{4,12},{8,0},{12,4},{16,24},{20,28},{24,16},{28,20},{1,9},{5... | collective-permute-start | bytes 393224 | tf_op jit(solution)/shard_map/ppermute | solution.py:23
  25.8 0.0 collective-permute-start.12
  25.8 0.5 %collective-permute-start.16 = (bf16[32,2048]{1,0:T(8,128)(2,1)S(1)}, bf16[32,2048]{1,0:T(8,128)(2,1)S(1)}, u32[]{:S(2)}, u32[]{:S(2)}) collective-permute-start(bf16[32,2048]{1,0:T(8,128)(2,1)S(1)} %get-tuple-element.75), channel_id=1, source_target_pairs={{0,16},{4,20},{8,24},{12,28},{16,0},{20,4},{24,8},{28,12},{1,17},{... | collective-permute-start | bytes 393224 | tf_op jit(solution)/shard_map/ppermute | solution.py:23
  26.3 2.3 %collective-permute-done.13.there = bf16[32,2048]{1,0:T(8,128)(2,1)S(1)} collective-permute-done((bf16[32,2048]{1,0:T(8,128)(2,1)S(1)}, bf16[32,2048]{1,0:T(8,128)(2,1)S(1)}, u32[]{:S(2)}, u32[]{:S(2)}) %collective-permute-start.13) | collective-permute-done | bytes 131104 | tf_op jit(solution)/shard_map/ppermute | solution.py:23
  28.6 1.6 %collective-permute-start.14 = (bf16[16,2048]{1,0:T(8,128)(2,1)S(1)}, bf16[16,2048]{1,0:T(8,128)(2,1)S(1)}, u32[]{:S(2)}, u32[]{:S(2)}) collective-permute-start(bf16[16,2048]{1,0:T(8,128)(2,1)S(1)} %get-tuple-element.73), channel_id=1, source_target_pairs={{0,8},{4,12},{8,0},{12,4},{16,24},{20,28},{24,16},{28,20},{1,9},{5... | collective-permute-start | bytes 196616 | tf_op jit(solution)/shard_map/ppermute | solution.py:23
  30.2 0.0 collective-permute-start.15
  30.2 2.9 %near_levels.1 = (bf16[128,3072]{1,0:T(8,128)(2,1)S(1)}, bf16[128,768]{1,0:T(8,128)(2,1)S(1)}, bf16[128,768]{1,0:T(8,128)(2,1)S(1)}, bf16[128,768]{1,0:T(8,128)(2,1)S(1)}, bf16[128,768]{1,0:T(8,128)(2,1)S(1)}) custom-call(s32[3,16]{1,0:T(4,128)S(1)} %copy-done.3, s32[1]{0:T(128)} %bitcast.core_ref, bf16[256,1024]{1,0:T(8,128)(2,1)S(1)} %get-tuple-element.47.exps.exp0, ...), custom_call_target="tpu_custom_call" | custom-call | tf_op jit(solution)/shard_map/near_levels/pallas_call | solution.py:481
  33.2 0.7 %collective-permute-start.18 = (bf16[128,768]{1,0:T(8,128)(2,1)S(1)}, bf16[128,768]{1,0:T(8,128)(2,1)S(1)}, u32[]{:S(2)}, u32[]{:S(2)}) collective-permute-start(bf16[128,768]{1,0:T(8,128)(2,1)S(1)} %get-tuple-element.84), channel_id=1, source_target_pairs={{0,4},{4,0},{8,12},{12,8},{16,20},{20,16},{24,28},{28,24},{1,5},{5... | collective-permute-start | bytes 589832 | tf_op jit(solution)/shard_map/ppermute | solution.py:23
  33.9 0.1 collective-permute-start.19
  34.0 0.0 collective-permute-done.16.y
  34.0 0.4 %collective-permute-start.20 = (bf16[128,768]{1,0:T(8,128)(2,1)S(1)}, bf16[128,768]{1,0:T(8,128)(2,1)S(1)}, u32[]{:S(2)}, u32[]{:S(2)}) collective-permute-start(bf16[128,768]{1,0:T(8,128)(2,1)S(1)} %get-tuple-element.86), channel_id=1, source_target_pairs={{0,4},{4,0},{8,12},{12,8},{16,20},{20,16},{24,28},{28,24},{1,5},{5... | collective-permute-start | bytes 589832 | tf_op jit(solution)/shard_map/ppermute | solution.py:23
  34.4 0.4 collective-permute-done.14.x3
  34.8 0.0 collective-permute-done.15.x3
  34.8 0.5 %collective-permute-start.21 = (bf16[128,768]{1,0:T(8,128)(2,1)S(1)}, bf16[128,768]{1,0:T(8,128)(2,1)S(1)}, u32[]{:S(2)}, u32[]{:S(2)}) collective-permute-start(bf16[128,768]{1,0:T(8,128)(2,1)S(1)} %get-tuple-element.87), channel_id=1, source_target_pairs={{0,4},{4,0},{8,12},{12,8},{16,20},{20,16},{24,28},{28,24},{1,5},{5... | collective-permute-start | bytes 589832 | tf_op jit(solution)/shard_map/ppermute | solution.py:23
  35.3 0.0 collective-permute-start.17
  35.3 0.9 %add_own_half.1 = (bf16[128,1024]{1,0:T(8,128)(2,1)S(1)}, bf16[128,1024]{1,0:T(8,128)(2,1)S(1)}, bf16[128,1024]{1,0:T(8,128)(2,1)S(1)}) custom-call(s32[3,16]{1,0:T(4,128)S(1)} %copy-done.3, s32[1]{0:T(128)} %bitcast.core_ref, bf16[128,3072]{1,0:T(8,128)(2,1)S(1)} %get-tuple-element.67.base, bf16[32,2048]{1,0:T(8,128)(2,1)S(1)} %collective-permute-done.11.x, ...), custom_call_target="tpu_custom_call" | custom-call | tf_op jit(solution)/shard_map/add_own_half/pallas_call | solution.py:542
  36.2 0.0 collective-permute-done.18.refs_0_
  36.2 0.0 collective-permute-done.19.refs_1_
  36.3 0.4 collective-permute-done.17.y
  36.6 1.9 %add_other_half.1 = (bf16[128,2048]{1,0:T(8,128)(2,1)}, bf16[128,2048]{1,0:T(8,128)(2,1)}, bf16[128,2048]{1,0:T(8,128)(2,1)}) custom-call(s32[3,16]{1,0:T(4,128)S(1)} %copy-done.3, s32[1]{0:T(128)} %bitcast.core_ref, bf16[128,1024]{1,0:T(8,128)(2,1)S(1)} %get-tuple-element.79.own_q, bf16[128,1024]{1,0:T(8,128)(2,1)S(1)} %get-tuple-element.80.own_k, ...), custom_call_target="tpu_custom_call" | custom-call | tf_op jit(solution)/shard_map/add_other_half/pallas_call | solution.py:594
  (13 shorter events, 0.1 us)
Async XLA Ops:
  0.6 5.7 %collective-permute-start.2 = (bf16[128,2048]{1,0:T(8,128)(2,1)}, bf16[128,2048]{1,0:T(8,128)(2,1)S(1)}, u32[]{:S(2)}, u32[]{:S(2)}) collective-permute-start(bf16[128,2048]{1,0:T(8,128)(2,1)} %bitcast.8), channel_id=1, source_target_pairs={{0,4},{4,0},{8,12},{12,8},{16,20},{20,16},{24,28},{28,24},{1,5},{5... | collective-permute-start | bytes 1572872 | tf_op jit(solution)/shard_map/ppermute | solution.py:23
  1.1 5.2 %collective-permute-start.1 = (bf16[128,2048]{1,0:T(8,128)(2,1)}, bf16[128,2048]{1,0:T(8,128)(2,1)S(1)}, u32[]{:S(2)}, u32[]{:S(2)}) collective-permute-start(bf16[128,2048]{1,0:T(8,128)(2,1)} %bitcast.13), channel_id=1, source_target_pairs={{0,4},{4,0},{8,12},{12,8},{16,20},{20,16},{24,28},{28,24},{1,5},{5... | collective-permute-start | bytes 1572872 | tf_op jit(solution)/shard_map/ppermute | solution.py:23
  1.2 14.5 %collective-permute-start = (bf16[128,2048]{1,0:T(8,128)(2,1)}, bf16[128,2048]{1,0:T(8,128)(2,1)S(1)}, u32[]{:S(2)}, u32[]{:S(2)}) collective-permute-start(bf16[128,2048]{1,0:T(8,128)(2,1)} %bitcast.17), channel_id=1, source_target_pairs={{0,4},{4,0},{8,12},{12,8},{16,20},{20,16},{24,28},{28,24},{1,5},{5... | collective-permute-start | bytes 1572872 | tf_op jit(solution)/shard_map/ppermute | solution.py:23
  1.7 16.8 %collective-permute-start.4 = (bf16[128,2048]{1,0:T(8,128)(2,1)}, bf16[128,2048]{1,0:T(8,128)(2,1)S(1)}, u32[]{:S(2)}, u32[]{:S(2)}) collective-permute-start(bf16[128,2048]{1,0:T(8,128)(2,1)} %bitcast.20), channel_id=1, source_target_pairs={{0,3},{1,0},{2,1},{3,2},{4,7},{5,4},{6,5},{7,6},{8,11},{9,8},{10,9... | collective-permute-start | bytes 1572872 | tf_op jit(solution)/shard_map/ppermute | solution.py:618
  6.3 9.4 %copy-start = (bf16[1,128,2048]{2,1,0:T(8,128)(2,1)S(1)}, bf16[1,128,2048]{2,1,0:T(8,128)(2,1)}, u32[]{:S(2)}) copy-start(bf16[1,128,2048]{2,1,0:T(8,128)(2,1)} %param.7) | copy-start | bytes 1572868
  6.3 9.4 %copy-start.1 = (bf16[1,128,2048]{2,1,0:T(8,128)(2,1)S(1)}, bf16[1,128,2048]{2,1,0:T(8,128)(2,1)}, u32[]{:S(2)}) copy-start(bf16[1,128,2048]{2,1,0:T(8,128)(2,1)} %param.6) | copy-start | bytes 1572868
  6.4 9.4 %copy-start.2 = (bf16[1,128,2048]{2,1,0:T(8,128)(2,1)S(1)}, bf16[1,128,2048]{2,1,0:T(8,128)(2,1)}, u32[]{:S(2)}) copy-start(bf16[1,128,2048]{2,1,0:T(8,128)(2,1)} %param.5) | copy-start | bytes 1572868
  7.8 8.0 %copy-start.3 = (s32[3,16]{1,0:T(4,128)S(1)}, s32[3,16]{1,0:T(4,128)}, u32[]{:S(2)}) copy-start(s32[3,16]{1,0:T(4,128)} %offs_ref.11) | copy-start | bytes 580
  7.8 6.4 %collective-permute-start.6 = (bf16[32,2048]{1,0:T(8,128)(2,1)S(1)}, bf16[32,2048]{1,0:T(8,128)(2,1)S(1)}, u32[]{:S(2)}, u32[]{:S(2)}) collective-permute-start(bf16[32,2048]{1,0:T(8,128)(2,1)S(1)} %get-tuple-element.52.own3), channel_id=1, source_target_pairs={{0,8},{4,12},{8,0},{12,4},{16,24},{20,28},{24,16},{28,20},{1,9},{5... | collective-permute-start | bytes 393224 | tf_op jit(solution)/shard_map/ppermute | solution.py:23
  9.3 11.0 %collective-permute-start.5 = (bf16[64,2048]{1,0:T(8,128)(2,1)S(1)}, bf16[64,2048]{1,0:T(8,128)(2,1)S(1)}, u32[]{:S(2)}, u32[]{:S(2)}) collective-permute-start(bf16[64,2048]{1,0:T(8,128)(2,1)S(1)} %get-tuple-element.56.own2), channel_id=1, source_target_pairs={{0,8},{4,12},{8,0},{12,4},{16,24},{20,28},{24,16},{28,20},{1,9},{5... | collective-permute-start | bytes 786440 | tf_op jit(solution)/shard_map/ppermute | solution.py:23
  9.9 8.6 %collective-permute-start.3 = (bf16[32,2048]{1,0:T(8,128)(2,1)S(1)}, bf16[32,2048]{1,0:T(8,128)(2,1)S(1)}, u32[]{:S(2)}, u32[]{:S(2)}) collective-permute-start(bf16[32,2048]{1,0:T(8,128)(2,1)S(1)} %get-tuple-element.52.own3), channel_id=1, source_target_pairs={{0,16},{4,20},{8,24},{12,28},{16,0},{20,4},{24,8},{28,12},{1,17},{... | collective-permute-start | bytes 393224 | tf_op jit(solution)/shard_map/ppermute | solution.py:23
  14.2 6.2 %collective-permute-start.7 = (bf16[32,2048]{1,0:T(8,128)(2,1)S(1)}, bf16[32,2048]{1,0:T(8,128)(2,1)S(1)}, u32[]{:S(2)}, u32[]{:S(2)}) collective-permute-start(bf16[32,2048]{1,0:T(8,128)(2,1)S(1)} %collective-permute-done.6.x3), channel_id=1, source_target_pairs={{0,16},{4,20},{8,24},{12,28},{16,0},{20,4},{24,8},{28,12},{1,17},{... | collective-permute-start | bytes 393224 | tf_op jit(solution)/shard_map/ppermute | solution.py:23
  18.5 1.9 %collective-permute-start.10 = (bf16[128,384]{1,0:T(8,128)(2,1)S(1)}, bf16[128,384]{1,0:T(8,128)(2,1)S(1)}, u32[]{:S(2)}, u32[]{:S(2)}) collective-permute-start(bf16[128,384]{1,0:T(8,128)(2,1)S(1)} %get-tuple-element.60), channel_id=1, source_target_pairs={{0,4},{4,0},{8,12},{12,8},{16,20},{20,16},{24,28},{28,24},{1,5},{5... | collective-permute-start | bytes 294920 | tf_op jit(solution)/shard_map/ppermute | solution.py:23
  18.6 1.8 %collective-permute-start.9 = (bf16[128,384]{1,0:T(8,128)(2,1)S(1)}, bf16[128,384]{1,0:T(8,128)(2,1)S(1)}, u32[]{:S(2)}, u32[]{:S(2)}) collective-permute-start(bf16[128,384]{1,0:T(8,128)(2,1)S(1)} %get-tuple-element.59), channel_id=1, source_target_pairs={{0,4},{4,0},{8,12},{12,8},{16,20},{20,16},{24,28},{28,24},{1,5},{5... | collective-permute-start | bytes 294920 | tf_op jit(solution)/shard_map/ppermute | solution.py:23
  19.1 1.3 %collective-permute-start.8 = (bf16[128,256]{1,0:T(8,128)(2,1)S(1)}, bf16[128,256]{1,0:T(8,128)(2,1)S(1)}, u32[]{:S(2)}, u32[]{:S(2)}) collective-permute-start(bf16[128,256]{1,0:T(8,128)(2,1)S(1)} %get-tuple-element.58), channel_id=1, source_target_pairs={{0,4},{4,0},{8,12},{12,8},{16,20},{20,16},{24,28},{28,24},{1,5},{5... | collective-permute-start | bytes 196616 | tf_op jit(solution)/shard_map/ppermute | solution.py:23
  22.7 5.9 %collective-permute-start.13 = (bf16[32,2048]{1,0:T(8,128)(2,1)S(1)}, bf16[32,2048]{1,0:T(8,128)(2,1)S(1)}, u32[]{:S(2)}, u32[]{:S(2)}) collective-permute-start(bf16[32,2048]{1,0:T(8,128)(2,1)S(1)} %get-tuple-element.72), channel_id=1, source_target_pairs={{0,16},{4,20},{8,24},{12,28},{16,0},{20,4},{24,8},{28,12},{1,17},{... | collective-permute-start | bytes 393224 | tf_op jit(solution)/shard_map/ppermute | solution.py:23
  24.3 8.9 %collective-permute-start.11 = (bf16[32,2048]{1,0:T(8,128)(2,1)S(1)}, bf16[32,2048]{1,0:T(8,128)(2,1)S(1)}, u32[]{:S(2)}, u32[]{:S(2)}) collective-permute-start(bf16[32,2048]{1,0:T(8,128)(2,1)S(1)} %get-tuple-element.69), channel_id=1, source_target_pairs={{0,8},{4,12},{8,0},{12,4},{16,24},{20,28},{24,16},{28,20},{1,9},{5... | collective-permute-start | bytes 393224 | tf_op jit(solution)/shard_map/ppermute | solution.py:23
  25.8 8.1 %collective-permute-start.12 = (bf16[32,2048]{1,0:T(8,128)(2,1)S(1)}, bf16[32,2048]{1,0:T(8,128)(2,1)S(1)}, u32[]{:S(2)}, u32[]{:S(2)}) collective-permute-start(bf16[32,2048]{1,0:T(8,128)(2,1)S(1)} %get-tuple-element.70), channel_id=1, source_target_pairs={{0,12},{4,8},{8,4},{12,0},{16,28},{20,24},{24,20},{28,16},{1,13},{... | collective-permute-start | bytes 393224 | tf_op jit(solution)/shard_map/ppermute | solution.py:23
  25.8 8.2 %collective-permute-start.16 = (bf16[32,2048]{1,0:T(8,128)(2,1)S(1)}, bf16[32,2048]{1,0:T(8,128)(2,1)S(1)}, u32[]{:S(2)}, u32[]{:S(2)}) collective-permute-start(bf16[32,2048]{1,0:T(8,128)(2,1)S(1)} %get-tuple-element.75), channel_id=1, source_target_pairs={{0,16},{4,20},{8,24},{12,28},{16,0},{20,4},{24,8},{28,12},{1,17},{... | collective-permute-start | bytes 393224 | tf_op jit(solution)/shard_map/ppermute | solution.py:23
  28.6 6.1 %collective-permute-start.14 = (bf16[16,2048]{1,0:T(8,128)(2,1)S(1)}, bf16[16,2048]{1,0:T(8,128)(2,1)S(1)}, u32[]{:S(2)}, u32[]{:S(2)}) collective-permute-start(bf16[16,2048]{1,0:T(8,128)(2,1)S(1)} %get-tuple-element.73), channel_id=1, source_target_pairs={{0,8},{4,12},{8,0},{12,4},{16,24},{20,28},{24,16},{28,20},{1,9},{5... | collective-permute-start | bytes 196616 | tf_op jit(solution)/shard_map/ppermute | solution.py:23
  30.2 4.6 %collective-permute-start.15 = (bf16[16,2048]{1,0:T(8,128)(2,1)S(1)}, bf16[16,2048]{1,0:T(8,128)(2,1)S(1)}, u32[]{:S(2)}, u32[]{:S(2)}) collective-permute-start(bf16[16,2048]{1,0:T(8,128)(2,1)S(1)} %get-tuple-element.74), channel_id=1, source_target_pairs={{0,12},{4,8},{8,4},{12,0},{16,28},{20,24},{24,20},{28,16},{1,13},{... | collective-permute-start | bytes 196616 | tf_op jit(solution)/shard_map/ppermute | solution.py:23
  33.2 3.1 %collective-permute-start.18 = (bf16[128,768]{1,0:T(8,128)(2,1)S(1)}, bf16[128,768]{1,0:T(8,128)(2,1)S(1)}, u32[]{:S(2)}, u32[]{:S(2)}) collective-permute-start(bf16[128,768]{1,0:T(8,128)(2,1)S(1)} %get-tuple-element.84), channel_id=1, source_target_pairs={{0,4},{4,0},{8,12},{12,8},{16,20},{20,16},{24,28},{28,24},{1,5},{5... | collective-permute-start | bytes 589832 | tf_op jit(solution)/shard_map/ppermute | solution.py:23
  33.9 2.4 %collective-permute-start.19 = (bf16[128,768]{1,0:T(8,128)(2,1)S(1)}, bf16[128,768]{1,0:T(8,128)(2,1)S(1)}, u32[]{:S(2)}, u32[]{:S(2)}) collective-permute-start(bf16[128,768]{1,0:T(8,128)(2,1)S(1)} %get-tuple-element.85), channel_id=1, source_target_pairs={{0,4},{4,0},{8,12},{12,8},{16,20},{20,16},{24,28},{28,24},{1,5},{5... | collective-permute-start | bytes 589832 | tf_op jit(solution)/shard_map/ppermute | solution.py:23
  34.0 2.3 %collective-permute-start.20 = (bf16[128,768]{1,0:T(8,128)(2,1)S(1)}, bf16[128,768]{1,0:T(8,128)(2,1)S(1)}, u32[]{:S(2)}, u32[]{:S(2)}) collective-permute-start(bf16[128,768]{1,0:T(8,128)(2,1)S(1)} %get-tuple-element.86), channel_id=1, source_target_pairs={{0,4},{4,0},{8,12},{12,8},{16,20},{20,16},{24,28},{28,24},{1,5},{5... | collective-permute-start | bytes 589832 | tf_op jit(solution)/shard_map/ppermute | solution.py:23
  34.8 1.9 %collective-permute-start.21 = (bf16[128,768]{1,0:T(8,128)(2,1)S(1)}, bf16[128,768]{1,0:T(8,128)(2,1)S(1)}, u32[]{:S(2)}, u32[]{:S(2)}) collective-permute-start(bf16[128,768]{1,0:T(8,128)(2,1)S(1)} %get-tuple-element.87), channel_id=1, source_target_pairs={{0,4},{4,0},{8,12},{12,8},{16,20},{20,16},{24,28},{28,24},{1,5},{5... | collective-permute-start | bytes 589832 | tf_op jit(solution)/shard_map/ppermute | solution.py:23
  35.3 1.3 %collective-permute-start.17 = (bf16[32,2048]{1,0:T(8,128)(2,1)S(1)}, bf16[32,2048]{1,0:T(8,128)(2,1)S(1)}, u32[]{:S(2)}, u32[]{:S(2)}) collective-permute-start(bf16[32,2048]{1,0:T(8,128)(2,1)S(1)} %collective-permute-done.16.y), channel_id=1, source_target_pairs={{0,4},{4,0},{8,12},{12,8},{16,20},{20,16},{24,28},{28,24},{1,5},{5... | collective-permute-start | bytes 393224 | tf_op jit(solution)/shard_map/ppermute | solution.py:23

commit v11 on v10

--- a/solution.py
+++ b/solution.py
@@ -44,15 +44,16 @@
 
 
 def place_matrix(offs_ref, head, first, levels, tok):
-    parts = []
+    total = sum(tok // 2**level for level in range(first, levels + 1))
+    col = lax.broadcasted_iota(jnp.int32, (1, total), 1)
+    target, lo = jnp.zeros_like(col), 0
     for level in range(first, levels + 1):
         rate = 2**level
-        rows = tok // rate
         kept = lax.rem(offs_ref[level - 1, head], rate)
-        row = lax.broadcasted_iota(jnp.int32, (tok, rows), 0)
-        col = lax.broadcasted_iota(jnp.int32, (tok, rows), 1)
-        parts.append((row == col * rate + kept).astype(F32))
-    return jnp.concatenate(parts, axis=1).astype(BF16)
+        target = jnp.where(col >= lo, (col - lo) * rate + kept, target)
+        lo += tok // rate
+    row = lax.broadcasted_iota(jnp.int32, (tok, total), 0)
+    return (row == target).astype(F32).astype(BF16)
 
 
 def pack_kernel(core_ref, rows, *outs):

time: 38.7 us -> 38.6 us (level)
  no operation moved by 1% of the time
where the time goes in v11:
time: 38.6 us; the launch traced here: 38.5 us
  starting transfers between devices  18.4 us (48%)
  Pallas kernels  12.5 us (32%)
  waiting for transfers between devices  6.72 us (17%)
  between operations  0.8 us (2%)
    ppermute x21, starting transfers between devices, exchange(): return lax.ppermute(value, 'seq', [(i, i ^ bits) for i in range(count)])  13.7 us
    ppermute x21, waiting for transfers between devices, exchange(): return lax.ppermute(value, 'seq', [(i, i ^ bits) for i in range(count)])  6.09 us
    ppermute x1, starting transfers between devices, per_device(): lax.ppermute(out_grads[0], 'section', [(i, (i - 1) % sections) for i in r...  4.67 us
    pallas_call x1, Pallas kernels, near_call(): pl.pallas_call(functools.partial(near_kernel, levels, per, dim), grid_spe...  2.76 us
    pallas_call x1, Pallas kernels, far_call(): pl.pallas_call(functools.partial(far_kernel, levels, per, dim), grid_spec...  2.31 us
    pallas_call x1, Pallas kernels, pre_call(): pl.pallas_call(functools.partial(pre_kernel, levels, per, dim), grid_spec...  2.07 us
    pallas_call x1, Pallas kernels, final_call(): pl.pallas_call(functools.partial(final_kernel, levels, per, dim), grid_sp...  1.83 us
    pallas_call x1, Pallas kernels, pick_call(): pl.pallas_call(functools.partial(pick_kernel, levels, per, dim), grid_spe...  1.39 us
  transfers between devices with their start and end apart: 22, of which 5 were waited for; matrix products, arithmetic and copies ran while one was open for 0% of the time, Pallas kernels for 22%

profile of v11, /device:TPU:0, one launch (start us, length us, event | category | flops | bytes accessed | tf_op | source)
XLA Modules:
  0.0 38.5 jit_solution(8054837021613619547)
XLA Ops:
  0.6 0.5 %collective-permute-start.2 = (bf16[128,2048]{1,0:T(8,128)(2,1)}, bf16[128,2048]{1,0:T(8,128)(2,1)S(1)}, u32[]{:S(2)}, u32[]{:S(2)}) collective-permute-start(bf16[128,2048]{1,0:T(8,128)(2,1)} %bitcast.8), channel_id=1, source_target_pairs={{0,4},{4,0},{8,12},{12,8},{16,20},{20,16},{24,28},{28,24},{1,5},{5... | collective-permute-start | bytes 1572872 | tf_op jit(solution)/shard_map/ppermute | solution.py:23
  1.1 0.1 collective-permute-start.1
  1.2 0.4 %collective-permute-start = (bf16[128,2048]{1,0:T(8,128)(2,1)}, bf16[128,2048]{1,0:T(8,128)(2,1)S(1)}, u32[]{:S(2)}, u32[]{:S(2)}) collective-permute-start(bf16[128,2048]{1,0:T(8,128)(2,1)} %bitcast.17), channel_id=1, source_target_pairs={{0,4},{4,0},{8,12},{12,8},{16,20},{20,16},{24,28},{28,24},{1,5},{5... | collective-permute-start | bytes 1572872 | tf_op jit(solution)/shard_map/ppermute | solution.py:23
  1.7 4.7 %collective-permute-start.4 = (bf16[128,2048]{1,0:T(8,128)(2,1)}, bf16[128,2048]{1,0:T(8,128)(2,1)S(1)}, u32[]{:S(2)}, u32[]{:S(2)}) collective-permute-start(bf16[128,2048]{1,0:T(8,128)(2,1)} %bitcast.20), channel_id=1, source_target_pairs={{0,3},{1,0},{2,1},{3,2},{4,7},{5,4},{6,5},{7,6},{8,11},{9,8},{10,9... | collective-permute-start | bytes 1572872 | tf_op jit(solution)/shard_map/ppermute | solution.py:619
  6.3 0.0 collective-permute-done.2.v1
  6.3 0.0 collective-permute-done.1.k1
  6.4 1.4 %pick_rows.1 = (bf16[64,2048]{1,0:T(8,128)(2,1)S(1)}, bf16[32,2048]{1,0:T(8,128)(2,1)S(1)}) custom-call(s32[1]{0:T(128)} %bitcast.core_ref, s32[3,16]{1,0:T(4,128)} %offs_ref.11, bf16[128,2048]{1,0:T(8,128)(2,1)} %bitcast.14, bf16[128,2048]{1,0:T(8,128)(2,1)} %bitcast.9, bf16[128,2048]{1,0:T(8,128)(2,1)S(1)} %collective-permute-done.1.k1, ...), custom_call_target="tpu_custom_call" | custom-call | tf_op jit(solution)/shard_map/pick_rows/pallas_call | solution.py:125
  7.8 0.0 copy-start.3
  7.8 1.6 %collective-permute-start.6 = (bf16[32,2048]{1,0:T(8,128)(2,1)S(1)}, bf16[32,2048]{1,0:T(8,128)(2,1)S(1)}, u32[]{:S(2)}, u32[]{:S(2)}) collective-permute-start(bf16[32,2048]{1,0:T(8,128)(2,1)S(1)} %get-tuple-element.52.own3), channel_id=1, source_target_pairs={{0,8},{4,12},{8,0},{12,4},{16,24},{20,28},{24,16},{28,20},{1,9},{5... | collective-permute-start | bytes 393224 | tf_op jit(solution)/shard_map/ppermute | solution.py:23
  9.3 0.5 %collective-permute-start.5 = (bf16[64,2048]{1,0:T(8,128)(2,1)S(1)}, bf16[64,2048]{1,0:T(8,128)(2,1)S(1)}, u32[]{:S(2)}, u32[]{:S(2)}) collective-permute-start(bf16[64,2048]{1,0:T(8,128)(2,1)S(1)} %get-tuple-element.56.own2), channel_id=1, source_target_pairs={{0,8},{4,12},{8,0},{12,4},{16,24},{20,28},{24,16},{28,20},{1,9},{5... | collective-permute-start | bytes 786440 | tf_op jit(solution)/shard_map/ppermute | solution.py:23
  9.9 1.5 %collective-permute-start.3 = (bf16[32,2048]{1,0:T(8,128)(2,1)S(1)}, bf16[32,2048]{1,0:T(8,128)(2,1)S(1)}, u32[]{:S(2)}, u32[]{:S(2)}) collective-permute-start(bf16[32,2048]{1,0:T(8,128)(2,1)S(1)} %get-tuple-element.52.own3), channel_id=1, source_target_pairs={{0,16},{4,20},{8,24},{12,28},{16,0},{20,4},{24,8},{28,12},{1,17},{... | collective-permute-start | bytes 393224 | tf_op jit(solution)/shard_map/ppermute | solution.py:23
  11.4 2.8 %collective-permute-done.6.x3 = bf16[32,2048]{1,0:T(8,128)(2,1)S(1)} collective-permute-done((bf16[32,2048]{1,0:T(8,128)(2,1)S(1)}, bf16[32,2048]{1,0:T(8,128)(2,1)S(1)}, u32[]{:S(2)}, u32[]{:S(2)}) %collective-permute-start.6) | collective-permute-done | bytes 131104 | tf_op jit(solution)/shard_map/ppermute | solution.py:23
  14.2 1.5 %collective-permute-start.7 = (bf16[32,2048]{1,0:T(8,128)(2,1)S(1)}, bf16[32,2048]{1,0:T(8,128)(2,1)S(1)}, u32[]{:S(2)}, u32[]{:S(2)}) collective-permute-start(bf16[32,2048]{1,0:T(8,128)(2,1)S(1)} %collective-permute-done.6.x3), channel_id=1, source_target_pairs={{0,16},{4,20},{8,24},{12,28},{16,0},{20,4},{24,8},{28,12},{1,17},{... | collective-permute-start | bytes 393224 | tf_op jit(solution)/shard_map/ppermute | solution.py:23
  15.7 0.0 collective-permute-done.q1
  15.7 2.1 %local_scores.1 = (bf16[256,1024]{1,0:T(8,128)(2,1)S(1)}, bf16[256,1024]{1,0:T(8,128)(2,1)S(1)}, f32[8,2048]{1,0:T(8,128)S(1)}, bf16[128,2048]{1,0:T(8,128)(2,1)S(1)}, bf16[96,1024]{1,0:T(8,128)(2,1)S(1)}) custom-call(s32[3,16]{1,0:T(4,128)S(1)} %copy-done.3, s32[1]{0:T(128)} %bitcast.core_ref, bf16[128,2048]{1,0:T(8,128)(2,1)S(1)} %bitcast.18, ...), custom_call_target="tpu_custom_call" | custom-call | tf_op jit(solution)/shard_map/local_scores/pallas_call | solution.py:218
  17.8 0.6 %collective-permute-done.4.grads.rows.g0 = bf16[128,2048]{1,0:T(8,128)(2,1)S(1)} collective-permute-done((bf16[128,2048]{1,0:T(8,128)(2,1)}, bf16[128,2048]{1,0:T(8,128)(2,1)S(1)}, u32[]{:S(2)}, u32[]{:S(2)}) %collective-permute-start.4) | collective-permute-done | bytes 524320 | tf_op jit(solution)/shard_map/ppermute | solution.py:619
  18.4 0.0 collective-permute-done.3.y3
  18.5 0.1 collective-permute-start.10
  18.6 0.5 %collective-permute-start.9 = (bf16[128,384]{1,0:T(8,128)(2,1)S(1)}, bf16[128,384]{1,0:T(8,128)(2,1)S(1)}, u32[]{:S(2)}, u32[]{:S(2)}) collective-permute-start(bf16[128,384]{1,0:T(8,128)(2,1)S(1)} %get-tuple-element.59), channel_id=1, source_target_pairs={{0,4},{4,0},{8,12},{12,8},{16,20},{20,16},{24,28},{28,24},{1,5},{5... | collective-permute-start | bytes 294920 | tf_op jit(solution)/shard_map/ppermute | solution.py:23
  19.1 0.1 collective-permute-start.8
  19.1 1.2 %own_delta.1 = (bf16[48,1024]{1,0:T(8,128)(2,1)S(1)}, f32[8,1024]{1,0:T(8,128)S(1)}) custom-call(s32[3,16]{1,0:T(4,128)S(1)} %copy-done.3, s32[1]{0:T(128)} %bitcast.core_ref, bf16[256,1024]{1,0:T(8,128)(2,1)S(1)} %get-tuple-element.47.exps.exp0, bf16[128,2048]{1,0:T(8,128)(2,1)S(1)} %get-tuple-element.51.near, bf16[128,2048]{1,0:T(8,128)(2,1)S(1)} %bitcast.11, ...), custom_call_target="tpu_custom_call" | custom-call | tf_op jit(solution)/shard_map/own_delta/pallas_call | solution.py:268
  20.3 0.0 collective-permute-done.10.refs_2_
  20.3 0.0 collective-permute-done.9.refs_1_
  20.4 0.0 collective-permute-done.7.d3
  20.4 2.3 %far_levels.1 = (bf16[32,2048]{1,0:T(8,128)(2,1)S(1)}, bf16[32,2048]{1,0:T(8,128)(2,1)S(1)}, bf16[32,2048]{1,0:T(8,128)(2,1)S(1)}, bf16[32,2048]{1,0:T(8,128)(2,...) custom-call(s32[3,16]{1,0:T(4,128)S(1)} %copy-done.3, ...), custom_call_target="tpu_custom_call" | custom-call | tf_op jit(solution)/shard_map/far_levels/pallas_call | solution.py:397
  22.7 1.6 %collective-permute-start.13 = (bf16[32,2048]{1,0:T(8,128)(2,1)S(1)}, bf16[32,2048]{1,0:T(8,128)(2,1)S(1)}, u32[]{:S(2)}, u32[]{:S(2)}) collective-permute-start(bf16[32,2048]{1,0:T(8,128)(2,1)S(1)} %get-tuple-element.72), channel_id=1, source_target_pairs={{0,16},{4,20},{8,24},{12,28},{16,0},{20,4},{24,8},{28,12},{1,17},{... | collective-permute-start | bytes 393224 | tf_op jit(solution)/shard_map/ppermute | solution.py:23
  24.3 1.5 %collective-permute-start.11 = (bf16[32,2048]{1,0:T(8,128)(2,1)S(1)}, bf16[32,2048]{1,0:T(8,128)(2,1)S(1)}, u32[]{:S(2)}, u32[]{:S(2)}) collective-permute-start(bf16[32,2048]{1,0:T(8,128)(2,1)S(1)} %get-tuple-element.69), channel_id=1, source_target_pairs={{0,8},{4,12},{8,0},{12,4},{16,24},{20,28},{24,16},{28,20},{1,9},{5... | collective-permute-start | bytes 393224 | tf_op jit(solution)/shard_map/ppermute | solution.py:23
  25.8 0.0 collective-permute-start.12
  25.8 0.5 %collective-permute-start.16 = (bf16[32,2048]{1,0:T(8,128)(2,1)S(1)}, bf16[32,2048]{1,0:T(8,128)(2,1)S(1)}, u32[]{:S(2)}, u32[]{:S(2)}) collective-permute-start(bf16[32,2048]{1,0:T(8,128)(2,1)S(1)} %get-tuple-element.75), channel_id=1, source_target_pairs={{0,16},{4,20},{8,24},{12,28},{16,0},{20,4},{24,8},{28,12},{1,17},{... | collective-permute-start | bytes 393224 | tf_op jit(solution)/shard_map/ppermute | solution.py:23
  26.3 2.3 %collective-permute-done.13.there = bf16[32,2048]{1,0:T(8,128)(2,1)S(1)} collective-permute-done((bf16[32,2048]{1,0:T(8,128)(2,1)S(1)}, bf16[32,2048]{1,0:T(8,128)(2,1)S(1)}, u32[]{:S(2)}, u32[]{:S(2)}) %collective-permute-start.13) | collective-permute-done | bytes 131104 | tf_op jit(solution)/shard_map/ppermute | solution.py:23
  28.6 1.6 %collective-permute-start.14 = (bf16[16,2048]{1,0:T(8,128)(2,1)S(1)}, bf16[16,2048]{1,0:T(8,128)(2,1)S(1)}, u32[]{:S(2)}, u32[]{:S(2)}) collective-permute-start(bf16[16,2048]{1,0:T(8,128)(2,1)S(1)} %get-tuple-element.73), channel_id=1, source_target_pairs={{0,8},{4,12},{8,0},{12,4},{16,24},{20,28},{24,16},{28,20},{1,9},{5... | collective-permute-start | bytes 196616 | tf_op jit(solution)/shard_map/ppermute | solution.py:23
  30.2 2.8 %near_levels.1 = (bf16[128,3072]{1,0:T(8,128)(2,1)S(1)}, bf16[128,768]{1,0:T(8,128)(2,1)S(1)}, bf16[128,768]{1,0:T(8,128)(2,1)S(1)}, bf16[128,768]{1,0:T(8,128)(2,1)S(1)}, bf16[128,768]{1,0:T(8,128)(2,1)S(1)}) custom-call(s32[3,16]{1,0:T(4,128)S(1)} %copy-done.3, s32[1]{0:T(128)} %bitcast.core_ref, bf16[256,1024]{1,0:T(8,128)(2,1)S(1)} %get-tuple-element.47.exps.exp0, ...), custom_call_target="tpu_custom_call" | custom-call | tf_op jit(solution)/shard_map/near_levels/pallas_call | solution.py:482
  33.0 0.0 collective-permute-done.11.x
  33.0 0.7 %collective-permute-start.18 = (bf16[128,768]{1,0:T(8,128)(2,1)S(1)}, bf16[128,768]{1,0:T(8,128)(2,1)S(1)}, u32[]{:S(2)}, u32[]{:S(2)}) collective-permute-start(bf16[128,768]{1,0:T(8,128)(2,1)S(1)} %get-tuple-element.84), channel_id=1, source_target_pairs={{0,4},{4,0},{8,12},{12,8},{16,20},{20,16},{24,28},{28,24},{1,5},{5... | collective-permute-start | bytes 589832 | tf_op jit(solution)/shard_map/ppermute | solution.py:23
  33.7 0.0 collective-permute-done.12.x
  33.7 0.1 collective-permute-start.19
  33.8 0.0 collective-permute-done.16.y
  33.8 0.4 %collective-permute-start.20 = (bf16[128,768]{1,0:T(8,128)(2,1)S(1)}, bf16[128,768]{1,0:T(8,128)(2,1)S(1)}, u32[]{:S(2)}, u32[]{:S(2)}) collective-permute-start(bf16[128,768]{1,0:T(8,128)(2,1)S(1)} %get-tuple-element.86), channel_id=1, source_target_pairs={{0,4},{4,0},{8,12},{12,8},{16,20},{20,16},{24,28},{28,24},{1,5},{5... | collective-permute-start | bytes 589832 | tf_op jit(solution)/shard_map/ppermute | solution.py:23
  34.2 0.6 %collective-permute-done.14.x3 = bf16[16,2048]{1,0:T(8,128)(2,1)S(1)} collective-permute-done((bf16[16,2048]{1,0:T(8,128)(2,1)S(1)}, bf16[16,2048]{1,0:T(8,128)(2,1)S(1)}, u32[]{:S(2)}, u32[]{:S(2)}) %collective-permute-start.14) | collective-permute-done | bytes 65568 | tf_op jit(solution)/shard_map/ppermute | solution.py:23
  34.8 0.0 collective-permute-done.15.x3
  34.8 0.5 %collective-permute-start.21 = (bf16[128,768]{1,0:T(8,128)(2,1)S(1)}, bf16[128,768]{1,0:T(8,128)(2,1)S(1)}, u32[]{:S(2)}, u32[]{:S(2)}) collective-permute-start(bf16[128,768]{1,0:T(8,128)(2,1)S(1)} %get-tuple-element.87), channel_id=1, source_target_pairs={{0,4},{4,0},{8,12},{12,8},{16,20},{20,16},{24,28},{28,24},{1,5},{5... | collective-permute-start | bytes 589832 | tf_op jit(solution)/shard_map/ppermute | solution.py:23
  35.3 0.0 collective-permute-start.17
  35.3 0.9 %add_own_half.1 = (bf16[128,1024]{1,0:T(8,128)(2,1)S(1)}, bf16[128,1024]{1,0:T(8,128)(2,1)S(1)}, bf16[128,1024]{1,0:T(8,128)(2,1)S(1)}) custom-call(s32[3,16]{1,0:T(4,128)S(1)} %copy-done.3, s32[1]{0:T(128)} %bitcast.core_ref, bf16[128,3072]{1,0:T(8,128)(2,1)S(1)} %get-tuple-element.67.base, bf16[32,2048]{1,0:T(8,128)(2,1)S(1)} %collective-permute-done.11.x, ...), custom_call_target="tpu_custom_call" | custom-call | tf_op jit(solution)/shard_map/add_own_half/pallas_call | solution.py:543
  36.2 0.0 collective-permute-done.18.refs_0_
  36.2 0.0 collective-permute-done.19.refs_1_
  36.2 0.4 %collective-permute-done.17.y = bf16[32,2048]{1,0:T(8,128)(2,1)S(1)} collective-permute-done((bf16[32,2048]{1,0:T(8,128)(2,1)S(1)}, bf16[32,2048]{1,0:T(8,128)(2,1)S(1)}, u32[]{:S(2)}, u32[]{:S(2)}) %collective-permute-start.17) | collective-permute-done | bytes 131104 | tf_op jit(solution)/shard_map/ppermute | solution.py:23
  36.6 0.0 collective-permute-done.21.refs_3_
  36.6 1.8 %add_other_half.1 = (bf16[128,2048]{1,0:T(8,128)(2,1)}, bf16[128,2048]{1,0:T(8,128)(2,1)}, bf16[128,2048]{1,0:T(8,128)(2,1)}) custom-call(s32[3,16]{1,0:T(4,128)S(1)} %copy-done.3, s32[1]{0:T(128)} %bitcast.core_ref, bf16[128,1024]{1,0:T(8,128)(2,1)S(1)} %get-tuple-element.79.own_q, bf16[128,1024]{1,0:T(8,128)(2,1)S(1)} %get-tuple-element.80.own_k, ...), custom_call_target="tpu_custom_call" | custom-call | tf_op jit(solution)/shard_map/add_other_half/pallas_call | solution.py:595
  (13 shorter events, 0.1 us)
Async XLA Ops:
  0.6 5.7 %collective-permute-start.2 = (bf16[128,2048]{1,0:T(8,128)(2,1)}, bf16[128,2048]{1,0:T(8,128)(2,1)S(1)}, u32[]{:S(2)}, u32[]{:S(2)}) collective-permute-start(bf16[128,2048]{1,0:T(8,128)(2,1)} %bitcast.8), channel_id=1, source_target_pairs={{0,4},{4,0},{8,12},{12,8},{16,20},{20,16},{24,28},{28,24},{1,5},{5... | collective-permute-start | bytes 1572872 | tf_op jit(solution)/shard_map/ppermute | solution.py:23
  1.1 5.2 %collective-permute-start.1 = (bf16[128,2048]{1,0:T(8,128)(2,1)}, bf16[128,2048]{1,0:T(8,128)(2,1)S(1)}, u32[]{:S(2)}, u32[]{:S(2)}) collective-permute-start(bf16[128,2048]{1,0:T(8,128)(2,1)} %bitcast.13), channel_id=1, source_target_pairs={{0,4},{4,0},{8,12},{12,8},{16,20},{20,16},{24,28},{28,24},{1,5},{5... | collective-permute-start | bytes 1572872 | tf_op jit(solution)/shard_map/ppermute | solution.py:23
  1.2 14.5 %collective-permute-start = (bf16[128,2048]{1,0:T(8,128)(2,1)}, bf16[128,2048]{1,0:T(8,128)(2,1)S(1)}, u32[]{:S(2)}, u32[]{:S(2)}) collective-permute-start(bf16[128,2048]{1,0:T(8,128)(2,1)} %bitcast.17), channel_id=1, source_target_pairs={{0,4},{4,0},{8,12},{12,8},{16,20},{20,16},{24,28},{28,24},{1,5},{5... | collective-permute-start | bytes 1572872 | tf_op jit(solution)/shard_map/ppermute | solution.py:23
  1.7 16.8 %collective-permute-start.4 = (bf16[128,2048]{1,0:T(8,128)(2,1)}, bf16[128,2048]{1,0:T(8,128)(2,1)S(1)}, u32[]{:S(2)}, u32[]{:S(2)}) collective-permute-start(bf16[128,2048]{1,0:T(8,128)(2,1)} %bitcast.20), channel_id=1, source_target_pairs={{0,3},{1,0},{2,1},{3,2},{4,7},{5,4},{6,5},{7,6},{8,11},{9,8},{10,9... | collective-permute-start | bytes 1572872 | tf_op jit(solution)/shard_map/ppermute | solution.py:619
  6.3 9.4 %copy-start = (bf16[1,128,2048]{2,1,0:T(8,128)(2,1)S(1)}, bf16[1,128,2048]{2,1,0:T(8,128)(2,1)}, u32[]{:S(2)}) copy-start(bf16[1,128,2048]{2,1,0:T(8,128)(2,1)} %param.7) | copy-start | bytes 1572868
  6.3 9.4 %copy-start.1 = (bf16[1,128,2048]{2,1,0:T(8,128)(2,1)S(1)}, bf16[1,128,2048]{2,1,0:T(8,128)(2,1)}, u32[]{:S(2)}) copy-start(bf16[1,128,2048]{2,1,0:T(8,128)(2,1)} %param.6) | copy-start | bytes 1572868
  6.4 9.4 %copy-start.2 = (bf16[1,128,2048]{2,1,0:T(8,128)(2,1)S(1)}, bf16[1,128,2048]{2,1,0:T(8,128)(2,1)}, u32[]{:S(2)}) copy-start(bf16[1,128,2048]{2,1,0:T(8,128)(2,1)} %param.5) | copy-start | bytes 1572868
  7.8 8.0 %copy-start.3 = (s32[3,16]{1,0:T(4,128)S(1)}, s32[3,16]{1,0:T(4,128)}, u32[]{:S(2)}) copy-start(s32[3,16]{1,0:T(4,128)} %offs_ref.11) | copy-start | bytes 580
  7.8 6.4 %collective-permute-start.6 = (bf16[32,2048]{1,0:T(8,128)(2,1)S(1)}, bf16[32,2048]{1,0:T(8,128)(2,1)S(1)}, u32[]{:S(2)}, u32[]{:S(2)}) collective-permute-start(bf16[32,2048]{1,0:T(8,128)(2,1)S(1)} %get-tuple-element.52.own3), channel_id=1, source_target_pairs={{0,8},{4,12},{8,0},{12,4},{16,24},{20,28},{24,16},{28,20},{1,9},{5... | collective-permute-start | bytes 393224 | tf_op jit(solution)/shard_map/ppermute | solution.py:23
  9.3 11.0 %collective-permute-start.5 = (bf16[64,2048]{1,0:T(8,128)(2,1)S(1)}, bf16[64,2048]{1,0:T(8,128)(2,1)S(1)}, u32[]{:S(2)}, u32[]{:S(2)}) collective-permute-start(bf16[64,2048]{1,0:T(8,128)(2,1)S(1)} %get-tuple-element.56.own2), channel_id=1, source_target_pairs={{0,8},{4,12},{8,0},{12,4},{16,24},{20,28},{24,16},{28,20},{1,9},{5... | collective-permute-start | bytes 786440 | tf_op jit(solution)/shard_map/ppermute | solution.py:23
  9.9 8.6 %collective-permute-start.3 = (bf16[32,2048]{1,0:T(8,128)(2,1)S(1)}, bf16[32,2048]{1,0:T(8,128)(2,1)S(1)}, u32[]{:S(2)}, u32[]{:S(2)}) collective-permute-start(bf16[32,2048]{1,0:T(8,128)(2,1)S(1)} %get-tuple-element.52.own3), channel_id=1, source_target_pairs={{0,16},{4,20},{8,24},{12,28},{16,0},{20,4},{24,8},{28,12},{1,17},{... | collective-permute-start | bytes 393224 | tf_op jit(solution)/shard_map/ppermute | solution.py:23
  14.2 6.2 %collective-permute-start.7 = (bf16[32,2048]{1,0:T(8,128)(2,1)S(1)}, bf16[32,2048]{1,0:T(8,128)(2,1)S(1)}, u32[]{:S(2)}, u32[]{:S(2)}) collective-permute-start(bf16[32,2048]{1,0:T(8,128)(2,1)S(1)} %collective-permute-done.6.x3), channel_id=1, source_target_pairs={{0,16},{4,20},{8,24},{12,28},{16,0},{20,4},{24,8},{28,12},{1,17},{... | collective-permute-start | bytes 393224 | tf_op jit(solution)/shard_map/ppermute | solution.py:23
  18.5 1.9 %collective-permute-start.10 = (bf16[128,384]{1,0:T(8,128)(2,1)S(1)}, bf16[128,384]{1,0:T(8,128)(2,1)S(1)}, u32[]{:S(2)}, u32[]{:S(2)}) collective-permute-start(bf16[128,384]{1,0:T(8,128)(2,1)S(1)} %get-tuple-element.60), channel_id=1, source_target_pairs={{0,4},{4,0},{8,12},{12,8},{16,20},{20,16},{24,28},{28,24},{1,5},{5... | collective-permute-start | bytes 294920 | tf_op jit(solution)/shard_map/ppermute | solution.py:23
  18.6 1.8 %collective-permute-start.9 = (bf16[128,384]{1,0:T(8,128)(2,1)S(1)}, bf16[128,384]{1,0:T(8,128)(2,1)S(1)}, u32[]{:S(2)}, u32[]{:S(2)}) collective-permute-start(bf16[128,384]{1,0:T(8,128)(2,1)S(1)} %get-tuple-element.59), channel_id=1, source_target_pairs={{0,4},{4,0},{8,12},{12,8},{16,20},{20,16},{24,28},{28,24},{1,5},{5... | collective-permute-start | bytes 294920 | tf_op jit(solution)/shard_map/ppermute | solution.py:23
  19.1 1.3 %collective-permute-start.8 = (bf16[128,256]{1,0:T(8,128)(2,1)S(1)}, bf16[128,256]{1,0:T(8,128)(2,1)S(1)}, u32[]{:S(2)}, u32[]{:S(2)}) collective-permute-start(bf16[128,256]{1,0:T(8,128)(2,1)S(1)} %get-tuple-element.58), channel_id=1, source_target_pairs={{0,4},{4,0},{8,12},{12,8},{16,20},{20,16},{24,28},{28,24},{1,5},{5... | collective-permute-start | bytes 196616 | tf_op jit(solution)/shard_map/ppermute | solution.py:23
  22.7 5.9 %collective-permute-start.13 = (bf16[32,2048]{1,0:T(8,128)(2,1)S(1)}, bf16[32,2048]{1,0:T(8,128)(2,1)S(1)}, u32[]{:S(2)}, u32[]{:S(2)}) collective-permute-start(bf16[32,2048]{1,0:T(8,128)(2,1)S(1)} %get-tuple-element.72), channel_id=1, source_target_pairs={{0,16},{4,20},{8,24},{12,28},{16,0},{20,4},{24,8},{28,12},{1,17},{... | collective-permute-start | bytes 393224 | tf_op jit(solution)/shard_map/ppermute | solution.py:23
  24.3 8.7 %collective-permute-start.11 = (bf16[32,2048]{1,0:T(8,128)(2,1)S(1)}, bf16[32,2048]{1,0:T(8,128)(2,1)S(1)}, u32[]{:S(2)}, u32[]{:S(2)}) collective-permute-start(bf16[32,2048]{1,0:T(8,128)(2,1)S(1)} %get-tuple-element.69), channel_id=1, source_target_pairs={{0,8},{4,12},{8,0},{12,4},{16,24},{20,28},{24,16},{28,20},{1,9},{5... | collective-permute-start | bytes 393224 | tf_op jit(solution)/shard_map/ppermute | solution.py:23
  25.8 7.9 %collective-permute-start.12 = (bf16[32,2048]{1,0:T(8,128)(2,1)S(1)}, bf16[32,2048]{1,0:T(8,128)(2,1)S(1)}, u32[]{:S(2)}, u32[]{:S(2)}) collective-permute-start(bf16[32,2048]{1,0:T(8,128)(2,1)S(1)} %get-tuple-element.70), channel_id=1, source_target_pairs={{0,12},{4,8},{8,4},{12,0},{16,28},{20,24},{24,20},{28,16},{1,13},{... | collective-permute-start | bytes 393224 | tf_op jit(solution)/shard_map/ppermute | solution.py:23
  25.8 8.0 %collective-permute-start.16 = (bf16[32,2048]{1,0:T(8,128)(2,1)S(1)}, bf16[32,2048]{1,0:T(8,128)(2,1)S(1)}, u32[]{:S(2)}, u32[]{:S(2)}) collective-permute-start(bf16[32,2048]{1,0:T(8,128)(2,1)S(1)} %get-tuple-element.75), channel_id=1, source_target_pairs={{0,16},{4,20},{8,24},{12,28},{16,0},{20,4},{24,8},{28,12},{1,17},{... | collective-permute-start | bytes 393224 | tf_op jit(solution)/shard_map/ppermute | solution.py:23
  28.6 6.1 %collective-permute-start.14 = (bf16[16,2048]{1,0:T(8,128)(2,1)S(1)}, bf16[16,2048]{1,0:T(8,128)(2,1)S(1)}, u32[]{:S(2)}, u32[]{:S(2)}) collective-permute-start(bf16[16,2048]{1,0:T(8,128)(2,1)S(1)} %get-tuple-element.73), channel_id=1, source_target_pairs={{0,8},{4,12},{8,0},{12,4},{16,24},{20,28},{24,16},{28,20},{1,9},{5... | collective-permute-start | bytes 196616 | tf_op jit(solution)/shard_map/ppermute | solution.py:23
  30.2 4.6 %collective-permute-start.15 = (bf16[16,2048]{1,0:T(8,128)(2,1)S(1)}, bf16[16,2048]{1,0:T(8,128)(2,1)S(1)}, u32[]{:S(2)}, u32[]{:S(2)}) collective-permute-start(bf16[16,2048]{1,0:T(8,128)(2,1)S(1)} %get-tuple-element.74), channel_id=1, source_target_pairs={{0,12},{4,8},{8,4},{12,0},{16,28},{20,24},{24,20},{28,16},{1,13},{... | collective-permute-start | bytes 196616 | tf_op jit(solution)/shard_map/ppermute | solution.py:23
  33.0 3.2 %collective-permute-start.18 = (bf16[128,768]{1,0:T(8,128)(2,1)S(1)}, bf16[128,768]{1,0:T(8,128)(2,1)S(1)}, u32[]{:S(2)}, u32[]{:S(2)}) collective-permute-start(bf16[128,768]{1,0:T(8,128)(2,1)S(1)} %get-tuple-element.84), channel_id=1, source_target_pairs={{0,4},{4,0},{8,12},{12,8},{16,20},{20,16},{24,28},{28,24},{1,5},{5... | collective-permute-start | bytes 589832 | tf_op jit(solution)/shard_map/ppermute | solution.py:23
  33.7 2.5 %collective-permute-start.19 = (bf16[128,768]{1,0:T(8,128)(2,1)S(1)}, bf16[128,768]{1,0:T(8,128)(2,1)S(1)}, u32[]{:S(2)}, u32[]{:S(2)}) collective-permute-start(bf16[128,768]{1,0:T(8,128)(2,1)S(1)} %get-tuple-element.85), channel_id=1, source_target_pairs={{0,4},{4,0},{8,12},{12,8},{16,20},{20,16},{24,28},{28,24},{1,5},{5... | collective-permute-start | bytes 589832 | tf_op jit(solution)/shard_map/ppermute | solution.py:23
  33.8 2.4 %collective-permute-start.20 = (bf16[128,768]{1,0:T(8,128)(2,1)S(1)}, bf16[128,768]{1,0:T(8,128)(2,1)S(1)}, u32[]{:S(2)}, u32[]{:S(2)}) collective-permute-start(bf16[128,768]{1,0:T(8,128)(2,1)S(1)} %get-tuple-element.86), channel_id=1, source_target_pairs={{0,4},{4,0},{8,12},{12,8},{16,20},{20,16},{24,28},{28,24},{1,5},{5... | collective-permute-start | bytes 589832 | tf_op jit(solution)/shard_map/ppermute | solution.py:23
  34.8 1.9 %collective-permute-start.21 = (bf16[128,768]{1,0:T(8,128)(2,1)S(1)}, bf16[128,768]{1,0:T(8,128)(2,1)S(1)}, u32[]{:S(2)}, u32[]{:S(2)}) collective-permute-start(bf16[128,768]{1,0:T(8,128)(2,1)S(1)} %get-tuple-element.87), channel_id=1, source_target_pairs={{0,4},{4,0},{8,12},{12,8},{16,20},{20,16},{24,28},{28,24},{1,5},{5... | collective-permute-start | bytes 589832 | tf_op jit(solution)/shard_map/ppermute | solution.py:23
  35.3 1.3 %collective-permute-start.17 = (bf16[32,2048]{1,0:T(8,128)(2,1)S(1)}, bf16[32,2048]{1,0:T(8,128)(2,1)S(1)}, u32[]{:S(2)}, u32[]{:S(2)}) collective-permute-start(bf16[32,2048]{1,0:T(8,128)(2,1)S(1)} %collective-permute-done.16.y), channel_id=1, source_target_pairs={{0,4},{4,0},{8,12},{12,8},{16,20},{20,16},{24,28},{28,24},{1,5},{5... | collective-permute-start | bytes 393224 | tf_op jit(solution)/shard_map/ppermute | solution.py:23

commit v12 on v11

--- a/solution.py
+++ b/solution.py
@@ -241,15 +241,16 @@
     first = core_ref[0] * per
     each = range(per)
     cols = [slice(h * dim, (h + 1) * dim) for h in each]
-    for h in each:
-        pick = pick_matrix(offs_ref, first + h, 2, levels, tok)
-        selg[:, cols[h]] = dot(pick, grads[:, cols[h]]).astype(BF16)
+    picks = [pick_matrix(offs_ref, first + h, 2, levels, tok) for h in each]
+    rows = [dot(picks[h], grads[:, cols[h]]).astype(BF16) for h in each]
+    vc = [slice((2 * h + 1) * dim, (2 * h + 2) * dim) for h in each]
+    p0 = [dot_nt(values[:, cols[h]], grads[:, cols[h]]) for h in each]
+    p1 = [dot_nt(near[:, vc[h]], grads[:, cols[h]]) for h in each]
     for h in each:
         here = slice(h * tok, (h + 1) * tok)
-        vc = slice((2 * h + 1) * dim, (2 * h + 2) * dim)
-        local[0:1, here] = local_delta(
-            exps[:, here], values[:, cols[h]], near[:, vc], grads[:, cols[h]]
-        )
+        selg[:, cols[h]] = rows[h]
+        both = exps[:tok, here].astype(F32) * p0[h] + exps[tok:, here].astype(F32) * p1[h]
+        local[0:1, here] = jnp.sum(both, axis=0, keepdims=True)
 
 
 def grad_call(offsets, core, exps, near, values, grads, dim):
@@ -283,9 +284,9 @@
     levels, per, dim, offs_ref, core_ref, stats, selq, selg0, local0, exp1, near, v1,
     own2, x2, own3, x3, y3, d3, *refs
 ):
-    xa, xb, xab, yab, dab, ngrad, dqt, stats2 = refs[-8:]
-    g1 = side(*(ref[...] for ref in refs[:-8]))
-    tok = dqt.shape[0]
+    xa, xb, xab, yab, dab, dsms, wms, selg1, stats2 = refs[-9:]
+    g1 = side(*(ref[...] for ref in refs[:-9]))
+    tok = g1.shape[0]
     n1, n2, n3 = tok // 2, tok // 4, tok // 8
     sel = n2 + n3
     scale = dim**-0.5
@@ -362,18 +363,21 @@
         w = e[h] * jnp.where(is2, b[0:1] + b[1:2], b[2:3] + b[3:4])
         dsm.append(apart(w * (p[h] - (b[4:5] + b[5:6] + b[6:7]))))
         wm.append(apart(w))
-    dk = [dot(dsm[h], selq[:, cols[h]]) * scale for h in each]
-    dv = [dot(wm[h], selg[h]) for h in each]
+    def away(value):
+        return stack(value[2 * n2 : tok], value[tok + 2 * n3 :])
+
+    dk = [dot(away(dsm[h]), selq[:, cols[h]]) * scale for h in each]
+    dv = [dot(away(wm[h]), selg[h]) for h in each]
     for h in each:
         dkv = side(dk[h], dv[h]).astype(BF16)
-        xa[:, wide[h]] = dkv[2 * n2 : 3 * n2]
-        xb[:, wide[h]] = dkv[3 * n2 : 4 * n2]
-        third = [dkv[tok + i * n3 : tok + (i + 1) * n3] for i in range(8)]
-        xab[:, wide[h]] = stack(third[2], third[3])
-        yab[:, wide[h]] = stack(third[4], third[5])
-        dab[:, wide[h]] = stack(third[6], third[7])
-        ngrad[:, wide[h]] = stack(dkv[:n2], third[0], dkv[n2 : 2 * n2], third[1])
-        dqt[:, h * dim : h * dim + 2 * sel] = dot(keys[h].T, dsm[h]).astype(BF16)
+        xa[:, wide[h]] = dkv[:n2]
+        xb[:, wide[h]] = dkv[n2 : 2 * n2]
+        for i, ref in enumerate((xab, yab, dab)):
+            lo = 2 * n2 + 2 * i * n3
+            ref[:, wide[h]] = dkv[lo : lo + 2 * n3]
+        dsms[:, h * dim : h * dim + 2 * sel] = dsm[h]
+        wms[:, h * dim : h * dim + 2 * sel] = wm[h]
+        selg1[:, cols[h]] = selg[h][sel:]
 
 
 def far_call(offsets, core, mid, value, far, tok, dim):
@@ -393,7 +397,7 @@
         )
 
     outs = [out(n2, 2 * dim)] * 2 + [out(2 * n3, 2 * dim)] * 3
-    outs += [out(2 * (n2 + n3), 2 * dim), out(dim, dim), out(8, 2 * tok, F32)]
+    outs += [out(2 * tok, dim)] * 2 + [out(n2 + n3, dim), out(8, 2 * tok, F32)]
     return pl.pallas_call(
         functools.partial(far_kernel, levels, per, dim),
         grid_spec=pltpu.PrefetchScalarGridSpec(
@@ -411,14 +415,16 @@
 
 
 def near_kernel(
-    levels, per, dim, offs_ref, core_ref, exp0, exp1, stats2, near, ngrad, dqt,
+    levels, per, dim, offs_ref, core_ref, exp0, exp1, stats2, near, dsms, wms, selq, selg0, selg1,
+    own2, x2, own3, x3, y3, d3,
     q0, q1, k0, k1, v0, v1, g0, *refs,
 ):
     mine, *others = refs[-1 - PIECES :]
     g1 = side(*(ref[...] for ref in refs[: -1 - PIECES]))
     tok = q0.shape[0]
     n1 = tok // 2
-    sel = tok // 4 + tok // 8
+    n2, n3 = tok // 4, tok // 8
+    sel = n2 + n3
     scale = dim**-0.5
     heads = per * pl.num_programs(0)
     first = core_ref[0] * heads + pl.program_id(0) * per
@@ -442,6 +448,22 @@
             h: side(dot(ds[h][tok:], que[h]) * scale, dot(wb[h][tok:], gra[h])).astype(BF16)
             for h in each
         }
+        ngrad, dqt = {}, {}
+
+        def here_rows(value):
+            return stack(
+                value[:n2], value[tok : tok + n3], value[n2 : 2 * n2], value[tok + n3 : tok + 2 * n3]
+            )
+
+        for h in each:
+            used = slice(h * dim, h * dim + 2 * sel)
+            dsm, wm = dsms[:, used], wms[:, used]
+            gsel = stack(selg0[:, cols[h]], selg1[:, cols[h]])
+            dk = dot(here_rows(dsm), selq[:, cols[h]]) * scale
+            ngrad[h] = side(dk, dot(here_rows(wm), gsel)).astype(BF16)
+            kc = slice(2 * h * dim, (2 * h + 1) * dim)
+            keys = stack(*(ref[:, kc] for ref in (own2, x2, own3, x3, y3, d3)))
+            dqt[h] = dot(keys.T, dsm).astype(BF16)
         for block, keys in enumerate((k0, k1)):
             at = slice(block * tok, (block + 1) * tok)
             picked = slice(block * n1, (block + 1) * n1)
@@ -449,14 +471,13 @@
             kv, dq = {}, {}
             for h in each:
                 place = place_matrix(offs_ref, first + h, 1, levels, tok)
-                wide = slice(2 * h * dim, 2 * (h + 1) * dim)
                 d0, w0 = ds[h][:tok, at], wb[h][:tok, at]
                 kv[h] = side(dot(d0, que[h][at]) * scale, dot(w0, gra[h][at]))
-                kv[h] += dot(place, stack(dkv1[h][picked], ngrad[grads, wide]))
+                kv[h] += dot(place, stack(dkv1[h][picked], ngrad[h][grads]))
             for h in each:
                 pick = pick_matrix(offs_ref, first + h, 2, levels, tok)
                 kc = slice(2 * h * dim, (2 * h + 1) * dim)
-                far = dqt[:, h * dim + block * sel : h * dim + (block + 1) * sel]
+                far = dqt[h][:, block * sel : (block + 1) * sel]
                 both = stack(keys[:, cols[h]], near[:tok, kc])
                 dq[h] = dot(both.T, ds[h][:, at]) + dot(far, pick)
             for h in each:
@@ -511,26 +532,33 @@
     )(here, there)
 
 
-def add_far(levels, dim, offs_ref, first, bases, x, third, group):
-    tok = bases[0].shape[0]
+def add_far(dim, place, bases, x, third, group):
     per = sum(base.shape[1] for base in bases) // (3 * dim)
     in_base = per // len(bases)
     for lo in range(0, per, group):
         each = range(lo, lo + group)
         src = {h: slice(2 * h * dim, 2 * (h + 1) * dim) for h in each}
-        place = {h: place_matrix(offs_ref, first + h, 2, levels, tok) for h in each}
-        more = {h: dot(place[h], stack(x[:, src[h]], third[:, src[h]])) for h in each}
+        more = {h: dot(place(h), stack(x[:, src[h]], third[:, src[h]])) for h in each}
         for h in each:
             base, at = bases[h // in_base], (3 * (h % in_base) + 1) * dim
             yield h, (base[:, at : at + 2 * dim].astype(F32) + more[h]).astype(BF16)
 
 
-def own_kernel(levels, per, dim, offs_ref, core_ref, base, x, y, x3, dq, dk, dv):
+def own_kernel(levels, per, dim, offs_ref, core_ref, base, x, y, x3, dq, dk, dv, places):
     n3 = x3.shape[0]
     third = (x3[...].astype(F32) + y[:n3].astype(F32)).astype(BF16)
     for h in range(per):
         dq[:, h * dim : (h + 1) * dim] = base[:, 3 * h * dim : (3 * h + 1) * dim]
-    for h, total in add_far(levels, dim, offs_ref, core_ref[0] * per, [base], x, third, per):
+    tok, sel = base.shape[0], 3 * n3
+    far_core = 1 - core_ref[0]
+    for h in range(per):
+        place = place_matrix(offs_ref, far_core * per + h, 2, levels, tok)
+        places[:, h * dim : h * dim + sel] = place
+
+    def here(h):
+        return place_matrix(offs_ref, core_ref[0] * per + h, 2, levels, tok)
+
+    for h, total in add_far(dim, here, [base], x, third, per):
         cols = slice(h * dim, (h + 1) * dim)
         dk[:, cols] = total[:, :dim]
         dv[:, cols] = total[:, dim:]
@@ -546,16 +574,16 @@
             num_scalar_prefetch=2,
             grid=(1,),
             in_specs=[pl.BlockSpec(a.shape, lambda i, o, c: (0, 0)) for a in parts],
-            out_specs=[pl.BlockSpec((tok, per * dim), lambda i, o, c: (0, 0))] * 3,
-        ),
-        out_shape=[jax.ShapeDtypeStruct((tok, per * dim), BF16)] * 3,
+            out_specs=[pl.BlockSpec((tok, per * dim), lambda i, o, c: (0, 0))] * 4,
+        ),
+        out_shape=[jax.ShapeDtypeStruct((tok, per * dim), BF16)] * 4,
         compiler_params=params(),
         name="add_own_half",
     )(offsets, core, *parts)
 
 
 def final_kernel(
-    levels, per, dim, offs_ref, core_ref, own_q, own_k, own_v, x, y, x3, *refs
+    levels, per, dim, offs_ref, core_ref, own_q, own_k, own_v, places, x, y, x3, *refs
 ):
     bases, outs, (held, sems) = refs[:PIECES], refs[PIECES : PIECES + 3], refs[-2:]
     n3 = x3.shape[0]
@@ -575,7 +603,11 @@
         held[0, :, h * dim : (h + 1) * dim] = bases[h // each][:, at : at + dim]
     send(0, held.at[0], far_core, 0, per)
     third = (x3[...].astype(F32) + y[n3:].astype(F32)).astype(BF16)
-    for h, total in add_far(levels, dim, offs_ref, far_core * per, bases, x, third, 4):
+
+    def place(h):
+        return places[:, h * dim : h * dim + 3 * n3]
+
+    for h, total in add_far(dim, place, bases, x, third, 4):
         cols = slice(h * dim, (h + 1) * dim)
         held[1, :, cols] = total[:, :dim]
         held[2, :, cols] = total[:, dim:]
@@ -636,7 +668,7 @@
     sizes = [(hi - lo) * dim for lo, hi in zip(cuts, cuts[1:])]
     other = [exchange(piece, 1) for piece in pack_call(core, grads, sizes)]
     other = lax.optimization_barrier((*other, sel[1]))[:-1]
-    xa, xb, xab, yab, dab, ngrad, dqt, stats2 = far_call(
+    xa, xb, xab, yab, dab, dsms, wms, selg1, stats2 = far_call(
         offsets, core, [stats, selq, *sel, exp1, near], v_oth,
         [two, x2, three, x3, y3, d3, *other], q.shape[0], dim,
     )
@@ -645,7 +677,7 @@
     xa3, xb3 = exchange(thirds[0], 2), exchange(thirds[1], 3)
     yy = exchange(y, 1)
     mine, *others = near_call(
-        offsets, core, [exp0, exp1, stats2, near, ngrad, dqt], raw, [grads, *other], dim
+        offsets, core, [exp0, exp1, stats2, near, dsms, wms, selq, sel[0], selg1, two, x2, three, x3, y3, d3], raw, [grads, *other], dim
     )
     last, xa, xb, xa3, xb3, y = lax.optimization_barrier((others[-1], xa, xb, xa3, xb3, y))
     bases = [exchange(piece, 1) for piece in (*others[:-1], last)]

time: 38.6 us -> 38.5 us (level)
  transfers between devices with their start and end apart: 22 -> 22, of which waited for: 5 -> 5; matrix products, arithmetic and copies ran while one was open for 0% -> 0% of each run, Pallas kernels for 22% -> 23%
where the time goes in v12:
time: 38.5 us; the launch traced here: 38.3 us
  starting transfers between devices  18.4 us (48%)
  Pallas kernels  12.7 us (33%)
  waiting for transfers between devices  6.4 us (17%)
  between operations  0.81 us (2%)
    ppermute x21, starting transfers between devices, exchange(): return lax.ppermute(value, 'seq', [(i, i ^ bits) for i in range(count)])  13.7 us
    ppermute x21, waiting for transfers between devices, exchange(): return lax.ppermute(value, 'seq', [(i, i ^ bits) for i in range(count)])  5.76 us
    ppermute x1, starting transfers between devices, per_device(): lax.ppermute(out_grads[0], 'section', [(i, (i - 1) % sections) for i in r...  4.67 us
    pallas_call x1, Pallas kernels, near_call(): pl.pallas_call(functools.partial(near_kernel, levels, per, dim), grid_spe...  3.03 us
    pallas_call x1, Pallas kernels, far_call(): pl.pallas_call(functools.partial(far_kernel, levels, per, dim), grid_spec...  2.26 us
    pallas_call x1, Pallas kernels, pre_call(): pl.pallas_call(functools.partial(pre_kernel, levels, per, dim), grid_spec...  2.07 us
    pallas_call x1, Pallas kernels, final_call(): pl.pallas_call(functools.partial(final_kernel, levels, per, dim), grid_sp...  1.78 us
    pallas_call x1, Pallas kernels, pick_call(): pl.pallas_call(functools.partial(pick_kernel, levels, per, dim), grid_spe...  1.39 us
  transfers between devices with their start and end apart: 22, of which 5 were waited for; matrix products, arithmetic and copies ran while one was open for 0% of the time, Pallas kernels for 23%

profile of v12, /device:TPU:0, one launch (start us, length us, event | category | flops | bytes accessed | tf_op | source)
XLA Modules:
  0.0 38.3 jit_solution(7688397399332465737)
XLA Ops:
  0.6 0.5 %collective-permute-start.2 = (bf16[128,2048]{1,0:T(8,128)(2,1)}, bf16[128,2048]{1,0:T(8,128)(2,1)S(1)}, u32[]{:S(2)}, u32[]{:S(2)}) collective-permute-start(bf16[128,2048]{1,0:T(8,128)(2,1)} %bitcast.8), channel_id=1, source_target_pairs={{0,4},{4,0},{8,12},{12,8},{16,20},{20,16},{24,28},{28,24},{1,5},{5... | collective-permute-start | bytes 1572872 | tf_op jit(solution)/shard_map/ppermute | solution.py:23
  1.1 0.1 collective-permute-start.1
  1.2 0.4 %collective-permute-start = (bf16[128,2048]{1,0:T(8,128)(2,1)}, bf16[128,2048]{1,0:T(8,128)(2,1)S(1)}, u32[]{:S(2)}, u32[]{:S(2)}) collective-permute-start(bf16[128,2048]{1,0:T(8,128)(2,1)} %bitcast.17), channel_id=1, source_target_pairs={{0,4},{4,0},{8,12},{12,8},{16,20},{20,16},{24,28},{28,24},{1,5},{5... | collective-permute-start | bytes 1572872 | tf_op jit(solution)/shard_map/ppermute | solution.py:23
  1.7 4.7 %collective-permute-start.4 = (bf16[128,2048]{1,0:T(8,128)(2,1)}, bf16[128,2048]{1,0:T(8,128)(2,1)S(1)}, u32[]{:S(2)}, u32[]{:S(2)}) collective-permute-start(bf16[128,2048]{1,0:T(8,128)(2,1)} %bitcast.20), channel_id=1, source_target_pairs={{0,3},{1,0},{2,1},{3,2},{4,7},{5,4},{6,5},{7,6},{8,11},{9,8},{10,9... | collective-permute-start | bytes 1572872 | tf_op jit(solution)/shard_map/ppermute | solution.py:651
  6.3 0.0 collective-permute-done.2.v1
  6.3 0.0 collective-permute-done.1.k1
  6.4 1.4 %pick_rows.1 = (bf16[64,2048]{1,0:T(8,128)(2,1)S(1)}, bf16[32,2048]{1,0:T(8,128)(2,1)S(1)}) custom-call(s32[1]{0:T(128)} %bitcast.core_ref, s32[3,16]{1,0:T(4,128)} %offs_ref.11, bf16[128,2048]{1,0:T(8,128)(2,1)} %bitcast.14, bf16[128,2048]{1,0:T(8,128)(2,1)} %bitcast.9, bf16[128,2048]{1,0:T(8,128)(2,1)S(1)} %collective-permute-done.1.k1, ...), custom_call_target="tpu_custom_call" | custom-call | tf_op jit(solution)/shard_map/pick_rows/pallas_call | solution.py:125
  7.8 0.0 copy-start.3
  7.8 1.6 %collective-permute-start.6 = (bf16[32,2048]{1,0:T(8,128)(2,1)S(1)}, bf16[32,2048]{1,0:T(8,128)(2,1)S(1)}, u32[]{:S(2)}, u32[]{:S(2)}) collective-permute-start(bf16[32,2048]{1,0:T(8,128)(2,1)S(1)} %get-tuple-element.54.own3), channel_id=1, source_target_pairs={{0,8},{4,12},{8,0},{12,4},{16,24},{20,28},{24,16},{28,20},{1,9},{5... | collective-permute-start | bytes 393224 | tf_op jit(solution)/shard_map/ppermute | solution.py:23
  9.3 0.5 %collective-permute-start.5 = (bf16[64,2048]{1,0:T(8,128)(2,1)S(1)}, bf16[64,2048]{1,0:T(8,128)(2,1)S(1)}, u32[]{:S(2)}, u32[]{:S(2)}) collective-permute-start(bf16[64,2048]{1,0:T(8,128)(2,1)S(1)} %get-tuple-element.58.own2), channel_id=1, source_target_pairs={{0,8},{4,12},{8,0},{12,4},{16,24},{20,28},{24,16},{28,20},{1,9},{5... | collective-permute-start | bytes 786440 | tf_op jit(solution)/shard_map/ppermute | solution.py:23
  9.9 1.5 %collective-permute-start.3 = (bf16[32,2048]{1,0:T(8,128)(2,1)S(1)}, bf16[32,2048]{1,0:T(8,128)(2,1)S(1)}, u32[]{:S(2)}, u32[]{:S(2)}) collective-permute-start(bf16[32,2048]{1,0:T(8,128)(2,1)S(1)} %get-tuple-element.54.own3), channel_id=1, source_target_pairs={{0,16},{4,20},{8,24},{12,28},{16,0},{20,4},{24,8},{28,12},{1,17},{... | collective-permute-start | bytes 393224 | tf_op jit(solution)/shard_map/ppermute | solution.py:23
  11.4 2.8 %collective-permute-done.6.x3 = bf16[32,2048]{1,0:T(8,128)(2,1)S(1)} collective-permute-done((bf16[32,2048]{1,0:T(8,128)(2,1)S(1)}, bf16[32,2048]{1,0:T(8,128)(2,1)S(1)}, u32[]{:S(2)}, u32[]{:S(2)}) %collective-permute-start.6) | collective-permute-done | bytes 131104 | tf_op jit(solution)/shard_map/ppermute | solution.py:23
  14.2 1.5 %collective-permute-start.7 = (bf16[32,2048]{1,0:T(8,128)(2,1)S(1)}, bf16[32,2048]{1,0:T(8,128)(2,1)S(1)}, u32[]{:S(2)}, u32[]{:S(2)}) collective-permute-start(bf16[32,2048]{1,0:T(8,128)(2,1)S(1)} %collective-permute-done.6.x3), channel_id=1, source_target_pairs={{0,16},{4,20},{8,24},{12,28},{16,0},{20,4},{24,8},{28,12},{1,17},{... | collective-permute-start | bytes 393224 | tf_op jit(solution)/shard_map/ppermute | solution.py:23
  15.7 0.0 collective-permute-done.q1
  15.7 2.1 %local_scores.1 = (bf16[256,1024]{1,0:T(8,128)(2,1)S(1)}, bf16[256,1024]{1,0:T(8,128)(2,1)S(1)}, f32[8,2048]{1,0:T(8,128)S(1)}, bf16[128,2048]{1,0:T(8,128)(2,1)S(1)}, bf16[96,1024]{1,0:T(8,128)(2,1)S(1)}) custom-call(s32[3,16]{1,0:T(4,128)S(1)} %copy-done.3, s32[1]{0:T(128)} %bitcast.core_ref, bf16[128,2048]{1,0:T(8,128)(2,1)S(1)} %bitcast.18, ...), custom_call_target="tpu_custom_call" | custom-call | tf_op jit(solution)/shard_map/local_scores/pallas_call | solution.py:218
  17.8 0.6 %collective-permute-done.4.grads.rows.g0 = bf16[128,2048]{1,0:T(8,128)(2,1)S(1)} collective-permute-done((bf16[128,2048]{1,0:T(8,128)(2,1)}, bf16[128,2048]{1,0:T(8,128)(2,1)S(1)}, u32[]{:S(2)}, u32[]{:S(2)}) %collective-permute-start.4) | collective-permute-done | bytes 524320 | tf_op jit(solution)/shard_map/ppermute | solution.py:651
  18.4 0.0 collective-permute-done.3.y3
  18.5 0.1 collective-permute-start.10
  18.6 0.5 %collective-permute-start.9 = (bf16[128,384]{1,0:T(8,128)(2,1)S(1)}, bf16[128,384]{1,0:T(8,128)(2,1)S(1)}, u32[]{:S(2)}, u32[]{:S(2)}) collective-permute-start(bf16[128,384]{1,0:T(8,128)(2,1)S(1)} %get-tuple-element.61), channel_id=1, source_target_pairs={{0,4},{4,0},{8,12},{12,8},{16,20},{20,16},{24,28},{28,24},{1,5},{5... | collective-permute-start | bytes 294920 | tf_op jit(solution)/shard_map/ppermute | solution.py:23
  19.1 0.1 collective-permute-start.8
  19.1 1.2 %own_delta.1 = (bf16[48,1024]{1,0:T(8,128)(2,1)S(1)}, f32[8,1024]{1,0:T(8,128)S(1)}) custom-call(s32[3,16]{1,0:T(4,128)S(1)} %copy-done.3, s32[1]{0:T(128)} %bitcast.core_ref, bf16[256,1024]{1,0:T(8,128)(2,1)S(1)} %get-tuple-element.49.exps.exp0, bf16[128,2048]{1,0:T(8,128)(2,1)S(1)} %get-tuple-element.53.near, bf16[128,2048]{1,0:T(8,128)(2,1)S(1)} %bitcast.11, ...), custom_call_target="tpu_custom_call" | custom-call | tf_op jit(solution)/shard_map/own_delta/pallas_call | solution.py:269
  20.3 0.0 collective-permute-done.8.refs_0_
  20.3 0.0 collective-permute-done.10.refs_2_
  20.3 0.0 collective-permute-done.9.refs_1_
  20.3 0.0 collective-permute-done.5.x2
  20.4 0.0 collective-permute-done.7.d3
  20.4 2.3 %far_levels.1 = (bf16[32,2048]{1,0:T(8,128)(2,1)S(1)}, bf16[32,2048]{1,0:T(8,128)(2,1)S(1)}, bf16[32,2048]{1,0:T(8,128)(2,1)S(1)}, bf16[32,2048]{1,0:T(8,128)(2,...) custom-call(s32[3,16]{1,0:T(4,128)S(1)} %copy-done.3, ...), custom_call_target="tpu_custom_call" | custom-call | tf_op jit(solution)/shard_map/far_levels/pallas_call | solution.py:401
  22.6 1.6 %collective-permute-start.13 = (bf16[32,2048]{1,0:T(8,128)(2,1)S(1)}, bf16[32,2048]{1,0:T(8,128)(2,1)S(1)}, u32[]{:S(2)}, u32[]{:S(2)}) collective-permute-start(bf16[32,2048]{1,0:T(8,128)(2,1)S(1)} %get-tuple-element.75), channel_id=1, source_target_pairs={{0,16},{4,20},{8,24},{12,28},{16,0},{20,4},{24,8},{28,12},{1,17},{... | collective-permute-start | bytes 393224 | tf_op jit(solution)/shard_map/ppermute | solution.py:23
  24.2 1.5 %collective-permute-start.11 = (bf16[32,2048]{1,0:T(8,128)(2,1)S(1)}, bf16[32,2048]{1,0:T(8,128)(2,1)S(1)}, u32[]{:S(2)}, u32[]{:S(2)}) collective-permute-start(bf16[32,2048]{1,0:T(8,128)(2,1)S(1)} %get-tuple-element.72), channel_id=1, source_target_pairs={{0,8},{4,12},{8,0},{12,4},{16,24},{20,28},{24,16},{28,20},{1,9},{5... | collective-permute-start | bytes 393224 | tf_op jit(solution)/shard_map/ppermute | solution.py:23
  25.7 0.0 collective-permute-start.12
  25.7 0.5 %collective-permute-start.16 = (bf16[32,2048]{1,0:T(8,128)(2,1)S(1)}, bf16[32,2048]{1,0:T(8,128)(2,1)S(1)}, u32[]{:S(2)}, u32[]{:S(2)}) collective-permute-start(bf16[32,2048]{1,0:T(8,128)(2,1)S(1)} %get-tuple-element.78), channel_id=1, source_target_pairs={{0,16},{4,20},{8,24},{12,28},{16,0},{20,4},{24,8},{28,12},{1,17},{... | collective-permute-start | bytes 393224 | tf_op jit(solution)/shard_map/ppermute | solution.py:23
  26.2 2.3 %collective-permute-done.13.there = bf16[32,2048]{1,0:T(8,128)(2,1)S(1)} collective-permute-done((bf16[32,2048]{1,0:T(8,128)(2,1)S(1)}, bf16[32,2048]{1,0:T(8,128)(2,1)S(1)}, u32[]{:S(2)}, u32[]{:S(2)}) %collective-permute-start.13) | collective-permute-done | bytes 131104 | tf_op jit(solution)/shard_map/ppermute | solution.py:23
  28.6 1.5 %collective-permute-start.14 = (bf16[16,2048]{1,0:T(8,128)(2,1)S(1)}, bf16[16,2048]{1,0:T(8,128)(2,1)S(1)}, u32[]{:S(2)}, u32[]{:S(2)}) collective-permute-start(bf16[16,2048]{1,0:T(8,128)(2,1)S(1)} %get-tuple-element.76), channel_id=1, source_target_pairs={{0,8},{4,12},{8,0},{12,4},{16,24},{20,28},{24,16},{28,20},{1,9},{5... | collective-permute-start | bytes 196616 | tf_op jit(solution)/shard_map/ppermute | solution.py:23
  30.1 0.0 collective-permute-start.15
  30.1 3.0 %near_levels.1 = (bf16[128,3072]{1,0:T(8,128)(2,1)S(1)}, bf16[128,768]{1,0:T(8,128)(2,1)S(1)}, bf16[128,768]{1,0:T(8,128)(2,1)S(1)}, bf16[128,768]{1,0:T(8,128)(2,1)S(1)}, bf16[128,768]{1,0:T(8,128)(2,1)S(1)}) custom-call(s32[3,16]{1,0:T(4,128)S(1)} %copy-done.3, s32[1]{0:T(128)} %bitcast.core_ref, bf16[256,1024]{1,0:T(8,128)(2,1)S(1)} %get-tuple-element.49.exps.exp0, ...), custom_call_target="tpu_custom_call" | custom-call | tf_op jit(solution)/shard_map/near_levels/pallas_call | solution.py:503
  33.2 0.7 %collective-permute-start.18 = (bf16[128,768]{1,0:T(8,128)(2,1)S(1)}, bf16[128,768]{1,0:T(8,128)(2,1)S(1)}, u32[]{:S(2)}, u32[]{:S(2)}) collective-permute-start(bf16[128,768]{1,0:T(8,128)(2,1)S(1)} %get-tuple-element.88), channel_id=1, source_target_pairs={{0,4},{4,0},{8,12},{12,8},{16,20},{20,16},{24,28},{28,24},{1,5},{5... | collective-permute-start | bytes 589832 | tf_op jit(solution)/shard_map/ppermute | solution.py:23
  33.9 0.0 collective-permute-done.12.x
  33.9 0.1 collective-permute-start.19
  34.0 0.0 collective-permute-done.16.y
  34.0 0.4 %collective-permute-start.20 = (bf16[128,768]{1,0:T(8,128)(2,1)S(1)}, bf16[128,768]{1,0:T(8,128)(2,1)S(1)}, u32[]{:S(2)}, u32[]{:S(2)}) collective-permute-start(bf16[128,768]{1,0:T(8,128)(2,1)S(1)} %get-tuple-element.90), channel_id=1, source_target_pairs={{0,4},{4,0},{8,12},{12,8},{16,20},{20,16},{24,28},{28,24},{1,5},{5... | collective-permute-start | bytes 589832 | tf_op jit(solution)/shard_map/ppermute | solution.py:23
  34.4 0.3 collective-permute-done.14.x3
  34.7 0.0 collective-permute-done.15.x3
  34.7 0.5 %collective-permute-start.21 = (bf16[128,768]{1,0:T(8,128)(2,1)S(1)}, bf16[128,768]{1,0:T(8,128)(2,1)S(1)}, u32[]{:S(2)}, u32[]{:S(2)}) collective-permute-start(bf16[128,768]{1,0:T(8,128)(2,1)S(1)} %get-tuple-element.91), channel_id=1, source_target_pairs={{0,4},{4,0},{8,12},{12,8},{16,20},{20,16},{24,28},{28,24},{1,5},{5... | collective-permute-start | bytes 589832 | tf_op jit(solution)/shard_map/ppermute | solution.py:23
  35.2 0.0 collective-permute-start.17
  35.2 1.0 %add_own_half.1 = (bf16[128,1024]{1,0:T(8,128)(2,1)S(1)}, bf16[128,1024]{1,0:T(8,128)(2,1)S(1)}, bf16[128,1024]{1,0:T(8,128)(2,1)S(1)}, bf16[128,1024]{1,0:T(8,128)(2,1)S(1)}) custom-call(s32[3,16]{1,0:T(4,128)S(1)} %copy-done.3, s32[1]{0:T(128)} %bitcast.core_ref, bf16[128,3072]{1,0:T(8,128)(2,1)S(1)} %get-tuple-element.70.base, ...), custom_call_target="tpu_custom_call" | custom-call | tf_op jit(solution)/shard_map/add_own_half/pallas_call | solution.py:571
  36.2 0.0 collective-permute-done.18.refs_0_
  36.2 0.3 collective-permute-done.17.y
  36.6 1.8 %add_other_half.1 = (bf16[128,2048]{1,0:T(8,128)(2,1)}, bf16[128,2048]{1,0:T(8,128)(2,1)}, bf16[128,2048]{1,0:T(8,128)(2,1)}) custom-call(s32[3,16]{1,0:T(4,128)S(1)} %copy-done.3, s32[1]{0:T(128)} %bitcast.core_ref, bf16[128,1024]{1,0:T(8,128)(2,1)S(1)} %get-tuple-element.82.own_q, bf16[128,1024]{1,0:T(8,128)(2,1)S(1)} %get-tuple-element.83.own_k, ...), custom_call_target="tpu_custom_call" | custom-call | tf_op jit(solution)/shard_map/add_other_half/pallas_call | solution.py:627
  (13 shorter events, 0.1 us)
Async XLA Ops:
  0.6 5.7 %collective-permute-start.2 = (bf16[128,2048]{1,0:T(8,128)(2,1)}, bf16[128,2048]{1,0:T(8,128)(2,1)S(1)}, u32[]{:S(2)}, u32[]{:S(2)}) collective-permute-start(bf16[128,2048]{1,0:T(8,128)(2,1)} %bitcast.8), channel_id=1, source_target_pairs={{0,4},{4,0},{8,12},{12,8},{16,20},{20,16},{24,28},{28,24},{1,5},{5... | collective-permute-start | bytes 1572872 | tf_op jit(solution)/shard_map/ppermute | solution.py:23
  1.1 5.2 %collective-permute-start.1 = (bf16[128,2048]{1,0:T(8,128)(2,1)}, bf16[128,2048]{1,0:T(8,128)(2,1)S(1)}, u32[]{:S(2)}, u32[]{:S(2)}) collective-permute-start(bf16[128,2048]{1,0:T(8,128)(2,1)} %bitcast.13), channel_id=1, source_target_pairs={{0,4},{4,0},{8,12},{12,8},{16,20},{20,16},{24,28},{28,24},{1,5},{5... | collective-permute-start | bytes 1572872 | tf_op jit(solution)/shard_map/ppermute | solution.py:23
  1.2 14.5 %collective-permute-start = (bf16[128,2048]{1,0:T(8,128)(2,1)}, bf16[128,2048]{1,0:T(8,128)(2,1)S(1)}, u32[]{:S(2)}, u32[]{:S(2)}) collective-permute-start(bf16[128,2048]{1,0:T(8,128)(2,1)} %bitcast.17), channel_id=1, source_target_pairs={{0,4},{4,0},{8,12},{12,8},{16,20},{20,16},{24,28},{28,24},{1,5},{5... | collective-permute-start | bytes 1572872 | tf_op jit(solution)/shard_map/ppermute | solution.py:23
  1.7 16.8 %collective-permute-start.4 = (bf16[128,2048]{1,0:T(8,128)(2,1)}, bf16[128,2048]{1,0:T(8,128)(2,1)S(1)}, u32[]{:S(2)}, u32[]{:S(2)}) collective-permute-start(bf16[128,2048]{1,0:T(8,128)(2,1)} %bitcast.20), channel_id=1, source_target_pairs={{0,3},{1,0},{2,1},{3,2},{4,7},{5,4},{6,5},{7,6},{8,11},{9,8},{10,9... | collective-permute-start | bytes 1572872 | tf_op jit(solution)/shard_map/ppermute | solution.py:651
  6.3 9.4 %copy-start = (bf16[1,128,2048]{2,1,0:T(8,128)(2,1)S(1)}, bf16[1,128,2048]{2,1,0:T(8,128)(2,1)}, u32[]{:S(2)}) copy-start(bf16[1,128,2048]{2,1,0:T(8,128)(2,1)} %param.7) | copy-start | bytes 1572868
  6.3 9.4 %copy-start.1 = (bf16[1,128,2048]{2,1,0:T(8,128)(2,1)S(1)}, bf16[1,128,2048]{2,1,0:T(8,128)(2,1)}, u32[]{:S(2)}) copy-start(bf16[1,128,2048]{2,1,0:T(8,128)(2,1)} %param.6) | copy-start | bytes 1572868
  6.4 9.4 %copy-start.2 = (bf16[1,128,2048]{2,1,0:T(8,128)(2,1)S(1)}, bf16[1,128,2048]{2,1,0:T(8,128)(2,1)}, u32[]{:S(2)}) copy-start(bf16[1,128,2048]{2,1,0:T(8,128)(2,1)} %param.5) | copy-start | bytes 1572868
  7.8 8.0 %copy-start.3 = (s32[3,16]{1,0:T(4,128)S(1)}, s32[3,16]{1,0:T(4,128)}, u32[]{:S(2)}) copy-start(s32[3,16]{1,0:T(4,128)} %offs_ref.11) | copy-start | bytes 580
  7.8 6.4 %collective-permute-start.6 = (bf16[32,2048]{1,0:T(8,128)(2,1)S(1)}, bf16[32,2048]{1,0:T(8,128)(2,1)S(1)}, u32[]{:S(2)}, u32[]{:S(2)}) collective-permute-start(bf16[32,2048]{1,0:T(8,128)(2,1)S(1)} %get-tuple-element.54.own3), channel_id=1, source_target_pairs={{0,8},{4,12},{8,0},{12,4},{16,24},{20,28},{24,16},{28,20},{1,9},{5... | collective-permute-start | bytes 393224 | tf_op jit(solution)/shard_map/ppermute | solution.py:23
  9.3 11.0 %collective-permute-start.5 = (bf16[64,2048]{1,0:T(8,128)(2,1)S(1)}, bf16[64,2048]{1,0:T(8,128)(2,1)S(1)}, u32[]{:S(2)}, u32[]{:S(2)}) collective-permute-start(bf16[64,2048]{1,0:T(8,128)(2,1)S(1)} %get-tuple-element.58.own2), channel_id=1, source_target_pairs={{0,8},{4,12},{8,0},{12,4},{16,24},{20,28},{24,16},{28,20},{1,9},{5... | collective-permute-start | bytes 786440 | tf_op jit(solution)/shard_map/ppermute | solution.py:23
  9.9 8.6 %collective-permute-start.3 = (bf16[32,2048]{1,0:T(8,128)(2,1)S(1)}, bf16[32,2048]{1,0:T(8,128)(2,1)S(1)}, u32[]{:S(2)}, u32[]{:S(2)}) collective-permute-start(bf16[32,2048]{1,0:T(8,128)(2,1)S(1)} %get-tuple-element.54.own3), channel_id=1, source_target_pairs={{0,16},{4,20},{8,24},{12,28},{16,0},{20,4},{24,8},{28,12},{1,17},{... | collective-permute-start | bytes 393224 | tf_op jit(solution)/shard_map/ppermute | solution.py:23
  14.2 6.2 %collective-permute-start.7 = (bf16[32,2048]{1,0:T(8,128)(2,1)S(1)}, bf16[32,2048]{1,0:T(8,128)(2,1)S(1)}, u32[]{:S(2)}, u32[]{:S(2)}) collective-permute-start(bf16[32,2048]{1,0:T(8,128)(2,1)S(1)} %collective-permute-done.6.x3), channel_id=1, source_target_pairs={{0,16},{4,20},{8,24},{12,28},{16,0},{20,4},{24,8},{28,12},{1,17},{... | collective-permute-start | bytes 393224 | tf_op jit(solution)/shard_map/ppermute | solution.py:23
  18.5 1.8 %collective-permute-start.10 = (bf16[128,384]{1,0:T(8,128)(2,1)S(1)}, bf16[128,384]{1,0:T(8,128)(2,1)S(1)}, u32[]{:S(2)}, u32[]{:S(2)}) collective-permute-start(bf16[128,384]{1,0:T(8,128)(2,1)S(1)} %get-tuple-element.62), channel_id=1, source_target_pairs={{0,4},{4,0},{8,12},{12,8},{16,20},{20,16},{24,28},{28,24},{1,5},{5... | collective-permute-start | bytes 294920 | tf_op jit(solution)/shard_map/ppermute | solution.py:23
  18.6 1.8 %collective-permute-start.9 = (bf16[128,384]{1,0:T(8,128)(2,1)S(1)}, bf16[128,384]{1,0:T(8,128)(2,1)S(1)}, u32[]{:S(2)}, u32[]{:S(2)}) collective-permute-start(bf16[128,384]{1,0:T(8,128)(2,1)S(1)} %get-tuple-element.61), channel_id=1, source_target_pairs={{0,4},{4,0},{8,12},{12,8},{16,20},{20,16},{24,28},{28,24},{1,5},{5... | collective-permute-start | bytes 294920 | tf_op jit(solution)/shard_map/ppermute | solution.py:23
  19.1 1.3 %collective-permute-start.8 = (bf16[128,256]{1,0:T(8,128)(2,1)S(1)}, bf16[128,256]{1,0:T(8,128)(2,1)S(1)}, u32[]{:S(2)}, u32[]{:S(2)}) collective-permute-start(bf16[128,256]{1,0:T(8,128)(2,1)S(1)} %get-tuple-element.60), channel_id=1, source_target_pairs={{0,4},{4,0},{8,12},{12,8},{16,20},{20,16},{24,28},{28,24},{1,5},{5... | collective-permute-start | bytes 196616 | tf_op jit(solution)/shard_map/ppermute | solution.py:23
  22.6 5.9 %collective-permute-start.13 = (bf16[32,2048]{1,0:T(8,128)(2,1)S(1)}, bf16[32,2048]{1,0:T(8,128)(2,1)S(1)}, u32[]{:S(2)}, u32[]{:S(2)}) collective-permute-start(bf16[32,2048]{1,0:T(8,128)(2,1)S(1)} %get-tuple-element.75), channel_id=1, source_target_pairs={{0,16},{4,20},{8,24},{12,28},{16,0},{20,4},{24,8},{28,12},{1,17},{... | collective-permute-start | bytes 393224 | tf_op jit(solution)/shard_map/ppermute | solution.py:23
  24.2 8.9 %collective-permute-start.11 = (bf16[32,2048]{1,0:T(8,128)(2,1)S(1)}, bf16[32,2048]{1,0:T(8,128)(2,1)S(1)}, u32[]{:S(2)}, u32[]{:S(2)}) collective-permute-start(bf16[32,2048]{1,0:T(8,128)(2,1)S(1)} %get-tuple-element.72), channel_id=1, source_target_pairs={{0,8},{4,12},{8,0},{12,4},{16,24},{20,28},{24,16},{28,20},{1,9},{5... | collective-permute-start | bytes 393224 | tf_op jit(solution)/shard_map/ppermute | solution.py:23
  25.7 8.2 %collective-permute-start.12 = (bf16[32,2048]{1,0:T(8,128)(2,1)S(1)}, bf16[32,2048]{1,0:T(8,128)(2,1)S(1)}, u32[]{:S(2)}, u32[]{:S(2)}) collective-permute-start(bf16[32,2048]{1,0:T(8,128)(2,1)S(1)} %get-tuple-element.73), channel_id=1, source_target_pairs={{0,12},{4,8},{8,4},{12,0},{16,28},{20,24},{24,20},{28,16},{1,13},{... | collective-permute-start | bytes 393224 | tf_op jit(solution)/shard_map/ppermute | solution.py:23
  25.7 8.2 %collective-permute-start.16 = (bf16[32,2048]{1,0:T(8,128)(2,1)S(1)}, bf16[32,2048]{1,0:T(8,128)(2,1)S(1)}, u32[]{:S(2)}, u32[]{:S(2)}) collective-permute-start(bf16[32,2048]{1,0:T(8,128)(2,1)S(1)} %get-tuple-element.78), channel_id=1, source_target_pairs={{0,16},{4,20},{8,24},{12,28},{16,0},{20,4},{24,8},{28,12},{1,17},{... | collective-permute-start | bytes 393224 | tf_op jit(solution)/shard_map/ppermute | solution.py:23
  28.6 6.1 %collective-permute-start.14 = (bf16[16,2048]{1,0:T(8,128)(2,1)S(1)}, bf16[16,2048]{1,0:T(8,128)(2,1)S(1)}, u32[]{:S(2)}, u32[]{:S(2)}) collective-permute-start(bf16[16,2048]{1,0:T(8,128)(2,1)S(1)} %get-tuple-element.76), channel_id=1, source_target_pairs={{0,8},{4,12},{8,0},{12,4},{16,24},{20,28},{24,16},{28,20},{1,9},{5... | collective-permute-start | bytes 196616 | tf_op jit(solution)/shard_map/ppermute | solution.py:23
  30.1 4.6 %collective-permute-start.15 = (bf16[16,2048]{1,0:T(8,128)(2,1)S(1)}, bf16[16,2048]{1,0:T(8,128)(2,1)S(1)}, u32[]{:S(2)}, u32[]{:S(2)}) collective-permute-start(bf16[16,2048]{1,0:T(8,128)(2,1)S(1)} %get-tuple-element.77), channel_id=1, source_target_pairs={{0,12},{4,8},{8,4},{12,0},{16,28},{20,24},{24,20},{28,16},{1,13},{... | collective-permute-start | bytes 196616 | tf_op jit(solution)/shard_map/ppermute | solution.py:23
  33.2 3.0 %collective-permute-start.18 = (bf16[128,768]{1,0:T(8,128)(2,1)S(1)}, bf16[128,768]{1,0:T(8,128)(2,1)S(1)}, u32[]{:S(2)}, u32[]{:S(2)}) collective-permute-start(bf16[128,768]{1,0:T(8,128)(2,1)S(1)} %get-tuple-element.88), channel_id=1, source_target_pairs={{0,4},{4,0},{8,12},{12,8},{16,20},{20,16},{24,28},{28,24},{1,5},{5... | collective-permute-start | bytes 589832 | tf_op jit(solution)/shard_map/ppermute | solution.py:23
  33.9 2.3 %collective-permute-start.19 = (bf16[128,768]{1,0:T(8,128)(2,1)S(1)}, bf16[128,768]{1,0:T(8,128)(2,1)S(1)}, u32[]{:S(2)}, u32[]{:S(2)}) collective-permute-start(bf16[128,768]{1,0:T(8,128)(2,1)S(1)} %get-tuple-element.89), channel_id=1, source_target_pairs={{0,4},{4,0},{8,12},{12,8},{16,20},{20,16},{24,28},{28,24},{1,5},{5... | collective-permute-start | bytes 589832 | tf_op jit(solution)/shard_map/ppermute | solution.py:23
  34.0 2.2 %collective-permute-start.20 = (bf16[128,768]{1,0:T(8,128)(2,1)S(1)}, bf16[128,768]{1,0:T(8,128)(2,1)S(1)}, u32[]{:S(2)}, u32[]{:S(2)}) collective-permute-start(bf16[128,768]{1,0:T(8,128)(2,1)S(1)} %get-tuple-element.90), channel_id=1, source_target_pairs={{0,4},{4,0},{8,12},{12,8},{16,20},{20,16},{24,28},{28,24},{1,5},{5... | collective-permute-start | bytes 589832 | tf_op jit(solution)/shard_map/ppermute | solution.py:23
  34.7 1.9 %collective-permute-start.21 = (bf16[128,768]{1,0:T(8,128)(2,1)S(1)}, bf16[128,768]{1,0:T(8,128)(2,1)S(1)}, u32[]{:S(2)}, u32[]{:S(2)}) collective-permute-start(bf16[128,768]{1,0:T(8,128)(2,1)S(1)} %get-tuple-element.91), channel_id=1, source_target_pairs={{0,4},{4,0},{8,12},{12,8},{16,20},{20,16},{24,28},{28,24},{1,5},{5... | collective-permute-start | bytes 589832 | tf_op jit(solution)/shard_map/ppermute | solution.py:23
  35.2 1.3 %collective-permute-start.17 = (bf16[32,2048]{1,0:T(8,128)(2,1)S(1)}, bf16[32,2048]{1,0:T(8,128)(2,1)S(1)}, u32[]{:S(2)}, u32[]{:S(2)}) collective-permute-start(bf16[32,2048]{1,0:T(8,128)(2,1)S(1)} %collective-permute-done.16.y), channel_id=1, source_target_pairs={{0,4},{4,0},{8,12},{12,8},{16,20},{20,16},{24,28},{28,24},{1,5},{5... | collective-permute-start | bytes 393224 | tf_op jit(solution)/shard_map/ppermute | solution.py:23

commit v13 on v12

--- a/solution.py
+++ b/solution.py
@@ -354,8 +354,9 @@
         back.append(dot_nt(terms, spots[h]))
 
     def apart(value):
+        value = value.astype(BF16)
         zero = jnp.zeros_like(value)
-        return stack(jnp.where(is2, value, zero), jnp.where(is2, zero, value)).astype(BF16)
+        return stack(jnp.where(is2, value, zero), jnp.where(is2, zero, value))
 
     dsm, wm = [], []
     for h in each:

time: 38.5 us -> 38.4 us (level)
  no operation moved by 1% of the time
where the time goes in v13:
time: 38.4 us; the launch traced here: 38.3 us
  starting transfers between devices  18.4 us (48%)
  Pallas kernels  12.7 us (33%)
  waiting for transfers between devices  6.4 us (17%)
  between operations  0.81 us (2%)
    ppermute x21, starting transfers between devices, exchange(): return lax.ppermute(value, 'seq', [(i, i ^ bits) for i in range(count)])  13.7 us
    ppermute x21, waiting for transfers between devices, exchange(): return lax.ppermute(value, 'seq', [(i, i ^ bits) for i in range(count)])  5.76 us
    ppermute x1, starting transfers between devices, per_device(): lax.ppermute(out_grads[0], 'section', [(i, (i - 1) % sections) for i in r...  4.67 us
    pallas_call x1, Pallas kernels, near_call(): pl.pallas_call(functools.partial(near_kernel, levels, per, dim), grid_spe...  3.03 us
    pallas_call x1, Pallas kernels, far_call(): pl.pallas_call(functools.partial(far_kernel, levels, per, dim), grid_spec...  2.22 us
    pallas_call x1, Pallas kernels, pre_call(): pl.pallas_call(functools.partial(pre_kernel, levels, per, dim), grid_spec...  2.07 us
    pallas_call x1, Pallas kernels, final_call(): pl.pallas_call(functools.partial(final_kernel, levels, per, dim), grid_sp...  1.78 us
    pallas_call x1, Pallas kernels, pick_call(): pl.pallas_call(functools.partial(pick_kernel, levels, per, dim), grid_spe...  1.39 us
  transfers between devices with their start and end apart: 22, of which 5 were waited for; matrix products, arithmetic and copies ran while one was open for 0% of the time, Pallas kernels for 23%

profile of v13, /device:TPU:0, one launch (start us, length us, event | category | flops | bytes accessed | tf_op | source)
XLA Modules:
  0.0 38.3 jit_solution(9995006484693860174)
XLA Ops:
  0.6 0.5 %collective-permute-start.2 = (bf16[128,2048]{1,0:T(8,128)(2,1)}, bf16[128,2048]{1,0:T(8,128)(2,1)S(1)}, u32[]{:S(2)}, u32[]{:S(2)}) collective-permute-start(bf16[128,2048]{1,0:T(8,128)(2,1)} %bitcast.8), channel_id=1, source_target_pairs={{0,4},{4,0},{8,12},{12,8},{16,20},{20,16},{24,28},{28,24},{1,5},{5... | collective-permute-start | bytes 1572872 | tf_op jit(solution)/shard_map/ppermute | solution.py:23
  1.1 0.1 collective-permute-start.1
  1.2 0.4 %collective-permute-start = (bf16[128,2048]{1,0:T(8,128)(2,1)}, bf16[128,2048]{1,0:T(8,128)(2,1)S(1)}, u32[]{:S(2)}, u32[]{:S(2)}) collective-permute-start(bf16[128,2048]{1,0:T(8,128)(2,1)} %bitcast.17), channel_id=1, source_target_pairs={{0,4},{4,0},{8,12},{12,8},{16,20},{20,16},{24,28},{28,24},{1,5},{5... | collective-permute-start | bytes 1572872 | tf_op jit(solution)/shard_map/ppermute | solution.py:23
  1.7 4.7 %collective-permute-start.4 = (bf16[128,2048]{1,0:T(8,128)(2,1)}, bf16[128,2048]{1,0:T(8,128)(2,1)S(1)}, u32[]{:S(2)}, u32[]{:S(2)}) collective-permute-start(bf16[128,2048]{1,0:T(8,128)(2,1)} %bitcast.20), channel_id=1, source_target_pairs={{0,3},{1,0},{2,1},{3,2},{4,7},{5,4},{6,5},{7,6},{8,11},{9,8},{10,9... | collective-permute-start | bytes 1572872 | tf_op jit(solution)/shard_map/ppermute | solution.py:652
  6.3 0.0 collective-permute-done.2.v1
  6.3 0.0 collective-permute-done.1.k1
  6.4 1.4 %pick_rows.1 = (bf16[64,2048]{1,0:T(8,128)(2,1)S(1)}, bf16[32,2048]{1,0:T(8,128)(2,1)S(1)}) custom-call(s32[1]{0:T(128)} %bitcast.core_ref, s32[3,16]{1,0:T(4,128)} %offs_ref.11, bf16[128,2048]{1,0:T(8,128)(2,1)} %bitcast.14, bf16[128,2048]{1,0:T(8,128)(2,1)} %bitcast.9, bf16[128,2048]{1,0:T(8,128)(2,1)S(1)} %collective-permute-done.1.k1, ...), custom_call_target="tpu_custom_call" | custom-call | tf_op jit(solution)/shard_map/pick_rows/pallas_call | solution.py:125
  7.8 0.0 copy-start.3
  7.8 1.6 %collective-permute-start.6 = (bf16[32,2048]{1,0:T(8,128)(2,1)S(1)}, bf16[32,2048]{1,0:T(8,128)(2,1)S(1)}, u32[]{:S(2)}, u32[]{:S(2)}) collective-permute-start(bf16[32,2048]{1,0:T(8,128)(2,1)S(1)} %get-tuple-element.54.own3), channel_id=1, source_target_pairs={{0,8},{4,12},{8,0},{12,4},{16,24},{20,28},{24,16},{28,20},{1,9},{5... | collective-permute-start | bytes 393224 | tf_op jit(solution)/shard_map/ppermute | solution.py:23
  9.3 0.5 %collective-permute-start.5 = (bf16[64,2048]{1,0:T(8,128)(2,1)S(1)}, bf16[64,2048]{1,0:T(8,128)(2,1)S(1)}, u32[]{:S(2)}, u32[]{:S(2)}) collective-permute-start(bf16[64,2048]{1,0:T(8,128)(2,1)S(1)} %get-tuple-element.58.own2), channel_id=1, source_target_pairs={{0,8},{4,12},{8,0},{12,4},{16,24},{20,28},{24,16},{28,20},{1,9},{5... | collective-permute-start | bytes 786440 | tf_op jit(solution)/shard_map/ppermute | solution.py:23
  9.9 1.5 %collective-permute-start.3 = (bf16[32,2048]{1,0:T(8,128)(2,1)S(1)}, bf16[32,2048]{1,0:T(8,128)(2,1)S(1)}, u32[]{:S(2)}, u32[]{:S(2)}) collective-permute-start(bf16[32,2048]{1,0:T(8,128)(2,1)S(1)} %get-tuple-element.54.own3), channel_id=1, source_target_pairs={{0,16},{4,20},{8,24},{12,28},{16,0},{20,4},{24,8},{28,12},{1,17},{... | collective-permute-start | bytes 393224 | tf_op jit(solution)/shard_map/ppermute | solution.py:23
  11.4 2.8 %collective-permute-done.6.x3 = bf16[32,2048]{1,0:T(8,128)(2,1)S(1)} collective-permute-done((bf16[32,2048]{1,0:T(8,128)(2,1)S(1)}, bf16[32,2048]{1,0:T(8,128)(2,1)S(1)}, u32[]{:S(2)}, u32[]{:S(2)}) %collective-permute-start.6) | collective-permute-done | bytes 131104 | tf_op jit(solution)/shard_map/ppermute | solution.py:23
  14.2 1.5 %collective-permute-start.7 = (bf16[32,2048]{1,0:T(8,128)(2,1)S(1)}, bf16[32,2048]{1,0:T(8,128)(2,1)S(1)}, u32[]{:S(2)}, u32[]{:S(2)}) collective-permute-start(bf16[32,2048]{1,0:T(8,128)(2,1)S(1)} %collective-permute-done.6.x3), channel_id=1, source_target_pairs={{0,16},{4,20},{8,24},{12,28},{16,0},{20,4},{24,8},{28,12},{1,17},{... | collective-permute-start | bytes 393224 | tf_op jit(solution)/shard_map/ppermute | solution.py:23
  15.7 0.0 collective-permute-done.q1
  15.7 2.1 %local_scores.1 = (bf16[256,1024]{1,0:T(8,128)(2,1)S(1)}, bf16[256,1024]{1,0:T(8,128)(2,1)S(1)}, f32[8,2048]{1,0:T(8,128)S(1)}, bf16[128,2048]{1,0:T(8,128)(2,1)S(1)}, bf16[96,1024]{1,0:T(8,128)(2,1)S(1)}) custom-call(s32[3,16]{1,0:T(4,128)S(1)} %copy-done.3, s32[1]{0:T(128)} %bitcast.core_ref, bf16[128,2048]{1,0:T(8,128)(2,1)S(1)} %bitcast.18, ...), custom_call_target="tpu_custom_call" | custom-call | tf_op jit(solution)/shard_map/local_scores/pallas_call | solution.py:218
  17.8 0.6 %collective-permute-done.4.grads.rows.g0 = bf16[128,2048]{1,0:T(8,128)(2,1)S(1)} collective-permute-done((bf16[128,2048]{1,0:T(8,128)(2,1)}, bf16[128,2048]{1,0:T(8,128)(2,1)S(1)}, u32[]{:S(2)}, u32[]{:S(2)}) %collective-permute-start.4) | collective-permute-done | bytes 524320 | tf_op jit(solution)/shard_map/ppermute | solution.py:652
  18.4 0.0 collective-permute-done.3.y3
  18.5 0.1 collective-permute-start.10
  18.6 0.5 %collective-permute-start.9 = (bf16[128,384]{1,0:T(8,128)(2,1)S(1)}, bf16[128,384]{1,0:T(8,128)(2,1)S(1)}, u32[]{:S(2)}, u32[]{:S(2)}) collective-permute-start(bf16[128,384]{1,0:T(8,128)(2,1)S(1)} %get-tuple-element.61), channel_id=1, source_target_pairs={{0,4},{4,0},{8,12},{12,8},{16,20},{20,16},{24,28},{28,24},{1,5},{5... | collective-permute-start | bytes 294920 | tf_op jit(solution)/shard_map/ppermute | solution.py:23
  19.1 0.1 collective-permute-start.8
  19.1 1.2 %own_delta.1 = (bf16[48,1024]{1,0:T(8,128)(2,1)S(1)}, f32[8,1024]{1,0:T(8,128)S(1)}) custom-call(s32[3,16]{1,0:T(4,128)S(1)} %copy-done.3, s32[1]{0:T(128)} %bitcast.core_ref, bf16[256,1024]{1,0:T(8,128)(2,1)S(1)} %get-tuple-element.49.exps.exp0, bf16[128,2048]{1,0:T(8,128)(2,1)S(1)} %get-tuple-element.53.near, bf16[128,2048]{1,0:T(8,128)(2,1)S(1)} %bitcast.11, ...), custom_call_target="tpu_custom_call" | custom-call | tf_op jit(solution)/shard_map/own_delta/pallas_call | solution.py:269
  20.3 0.0 collective-permute-done.8.refs_0_
  20.3 0.0 collective-permute-done.10.refs_2_
  20.4 0.0 collective-permute-done.7.d3
  20.4 2.2 %far_levels.1 = (bf16[32,2048]{1,0:T(8,128)(2,1)S(1)}, bf16[32,2048]{1,0:T(8,128)(2,1)S(1)}, bf16[32,2048]{1,0:T(8,128)(2,1)S(1)}, bf16[32,2048]{1,0:T(8,128)(2,...) custom-call(s32[3,16]{1,0:T(4,128)S(1)} %copy-done.3, ...), custom_call_target="tpu_custom_call" | custom-call | tf_op jit(solution)/shard_map/far_levels/pallas_call | solution.py:402
  22.6 1.6 %collective-permute-start.13 = (bf16[32,2048]{1,0:T(8,128)(2,1)S(1)}, bf16[32,2048]{1,0:T(8,128)(2,1)S(1)}, u32[]{:S(2)}, u32[]{:S(2)}) collective-permute-start(bf16[32,2048]{1,0:T(8,128)(2,1)S(1)} %get-tuple-element.75), channel_id=1, source_target_pairs={{0,16},{4,20},{8,24},{12,28},{16,0},{20,4},{24,8},{28,12},{1,17},{... | collective-permute-start | bytes 393224 | tf_op jit(solution)/shard_map/ppermute | solution.py:23
  24.2 1.5 %collective-permute-start.11 = (bf16[32,2048]{1,0:T(8,128)(2,1)S(1)}, bf16[32,2048]{1,0:T(8,128)(2,1)S(1)}, u32[]{:S(2)}, u32[]{:S(2)}) collective-permute-start(bf16[32,2048]{1,0:T(8,128)(2,1)S(1)} %get-tuple-element.72), channel_id=1, source_target_pairs={{0,8},{4,12},{8,0},{12,4},{16,24},{20,28},{24,16},{28,20},{1,9},{5... | collective-permute-start | bytes 393224 | tf_op jit(solution)/shard_map/ppermute | solution.py:23
  25.7 0.0 collective-permute-start.12
  25.7 0.5 %collective-permute-start.16 = (bf16[32,2048]{1,0:T(8,128)(2,1)S(1)}, bf16[32,2048]{1,0:T(8,128)(2,1)S(1)}, u32[]{:S(2)}, u32[]{:S(2)}) collective-permute-start(bf16[32,2048]{1,0:T(8,128)(2,1)S(1)} %get-tuple-element.78), channel_id=1, source_target_pairs={{0,16},{4,20},{8,24},{12,28},{16,0},{20,4},{24,8},{28,12},{1,17},{... | collective-permute-start | bytes 393224 | tf_op jit(solution)/shard_map/ppermute | solution.py:23
  26.2 2.3 %collective-permute-done.13.there = bf16[32,2048]{1,0:T(8,128)(2,1)S(1)} collective-permute-done((bf16[32,2048]{1,0:T(8,128)(2,1)S(1)}, bf16[32,2048]{1,0:T(8,128)(2,1)S(1)}, u32[]{:S(2)}, u32[]{:S(2)}) %collective-permute-start.13) | collective-permute-done | bytes 131104 | tf_op jit(solution)/shard_map/ppermute | solution.py:23
  28.5 1.5 %collective-permute-start.14 = (bf16[16,2048]{1,0:T(8,128)(2,1)S(1)}, bf16[16,2048]{1,0:T(8,128)(2,1)S(1)}, u32[]{:S(2)}, u32[]{:S(2)}) collective-permute-start(bf16[16,2048]{1,0:T(8,128)(2,1)S(1)} %get-tuple-element.76), channel_id=1, source_target_pairs={{0,8},{4,12},{8,0},{12,4},{16,24},{20,28},{24,16},{28,20},{1,9},{5... | collective-permute-start | bytes 196616 | tf_op jit(solution)/shard_map/ppermute | solution.py:23
  30.1 0.0 collective-permute-start.15
  30.1 3.0 %near_levels.1 = (bf16[128,3072]{1,0:T(8,128)(2,1)S(1)}, bf16[128,768]{1,0:T(8,128)(2,1)S(1)}, bf16[128,768]{1,0:T(8,128)(2,1)S(1)}, bf16[128,768]{1,0:T(8,128)(2,1)S(1)}, bf16[128,768]{1,0:T(8,128)(2,1)S(1)}) custom-call(s32[3,16]{1,0:T(4,128)S(1)} %copy-done.3, s32[1]{0:T(128)} %bitcast.core_ref, bf16[256,1024]{1,0:T(8,128)(2,1)S(1)} %get-tuple-element.49.exps.exp0, ...), custom_call_target="tpu_custom_call" | custom-call | tf_op jit(solution)/shard_map/near_levels/pallas_call | solution.py:504
  33.1 0.0 collective-permute-done.11.x
  33.1 0.7 %collective-permute-start.18 = (bf16[128,768]{1,0:T(8,128)(2,1)S(1)}, bf16[128,768]{1,0:T(8,128)(2,1)S(1)}, u32[]{:S(2)}, u32[]{:S(2)}) collective-permute-start(bf16[128,768]{1,0:T(8,128)(2,1)S(1)} %get-tuple-element.88), channel_id=1, source_target_pairs={{0,4},{4,0},{8,12},{12,8},{16,20},{20,16},{24,28},{28,24},{1,5},{5... | collective-permute-start | bytes 589832 | tf_op jit(solution)/shard_map/ppermute | solution.py:23
  33.8 0.0 collective-permute-done.12.x
  33.9 0.1 collective-permute-start.19
  33.9 0.0 collective-permute-done.16.y
  33.9 0.4 %collective-permute-start.20 = (bf16[128,768]{1,0:T(8,128)(2,1)S(1)}, bf16[128,768]{1,0:T(8,128)(2,1)S(1)}, u32[]{:S(2)}, u32[]{:S(2)}) collective-permute-start(bf16[128,768]{1,0:T(8,128)(2,1)S(1)} %get-tuple-element.90), channel_id=1, source_target_pairs={{0,4},{4,0},{8,12},{12,8},{16,20},{20,16},{24,28},{28,24},{1,5},{5... | collective-permute-start | bytes 589832 | tf_op jit(solution)/shard_map/ppermute | solution.py:23
  34.4 0.3 collective-permute-done.14.x3
  34.6 0.5 %collective-permute-start.21 = (bf16[128,768]{1,0:T(8,128)(2,1)S(1)}, bf16[128,768]{1,0:T(8,128)(2,1)S(1)}, u32[]{:S(2)}, u32[]{:S(2)}) collective-permute-start(bf16[128,768]{1,0:T(8,128)(2,1)S(1)} %get-tuple-element.91), channel_id=1, source_target_pairs={{0,4},{4,0},{8,12},{12,8},{16,20},{20,16},{24,28},{28,24},{1,5},{5... | collective-permute-start | bytes 589832 | tf_op jit(solution)/shard_map/ppermute | solution.py:23
  35.2 0.0 collective-permute-start.17
  35.2 1.0 %add_own_half.1 = (bf16[128,1024]{1,0:T(8,128)(2,1)S(1)}, bf16[128,1024]{1,0:T(8,128)(2,1)S(1)}, bf16[128,1024]{1,0:T(8,128)(2,1)S(1)}, bf16[128,1024]{1,0:T(8,128)(2,1)S(1)}) custom-call(s32[3,16]{1,0:T(4,128)S(1)} %copy-done.3, s32[1]{0:T(128)} %bitcast.core_ref, bf16[128,3072]{1,0:T(8,128)(2,1)S(1)} %get-tuple-element.70.base, ...), custom_call_target="tpu_custom_call" | custom-call | tf_op jit(solution)/shard_map/add_own_half/pallas_call | solution.py:572
  36.1 0.0 collective-permute-done.19.refs_1_
  36.2 0.0 collective-permute-done.20.refs_2_
  36.2 0.3 collective-permute-done.17.y
  36.5 0.0 collective-permute-done.21.refs_3_
  36.5 1.8 %add_other_half.1 = (bf16[128,2048]{1,0:T(8,128)(2,1)}, bf16[128,2048]{1,0:T(8,128)(2,1)}, bf16[128,2048]{1,0:T(8,128)(2,1)}) custom-call(s32[3,16]{1,0:T(4,128)S(1)} %copy-done.3, s32[1]{0:T(128)} %bitcast.core_ref, bf16[128,1024]{1,0:T(8,128)(2,1)S(1)} %get-tuple-element.82.own_q, bf16[128,1024]{1,0:T(8,128)(2,1)S(1)} %get-tuple-element.83.own_k, ...), custom_call_target="tpu_custom_call" | custom-call | tf_op jit(solution)/shard_map/add_other_half/pallas_call | solution.py:628
  (13 shorter events, 0.1 us)
Async XLA Ops:
  0.6 5.7 %collective-permute-start.2 = (bf16[128,2048]{1,0:T(8,128)(2,1)}, bf16[128,2048]{1,0:T(8,128)(2,1)S(1)}, u32[]{:S(2)}, u32[]{:S(2)}) collective-permute-start(bf16[128,2048]{1,0:T(8,128)(2,1)} %bitcast.8), channel_id=1, source_target_pairs={{0,4},{4,0},{8,12},{12,8},{16,20},{20,16},{24,28},{28,24},{1,5},{5... | collective-permute-start | bytes 1572872 | tf_op jit(solution)/shard_map/ppermute | solution.py:23
  1.1 5.2 %collective-permute-start.1 = (bf16[128,2048]{1,0:T(8,128)(2,1)}, bf16[128,2048]{1,0:T(8,128)(2,1)S(1)}, u32[]{:S(2)}, u32[]{:S(2)}) collective-permute-start(bf16[128,2048]{1,0:T(8,128)(2,1)} %bitcast.13), channel_id=1, source_target_pairs={{0,4},{4,0},{8,12},{12,8},{16,20},{20,16},{24,28},{28,24},{1,5},{5... | collective-permute-start | bytes 1572872 | tf_op jit(solution)/shard_map/ppermute | solution.py:23
  1.2 14.5 %collective-permute-start = (bf16[128,2048]{1,0:T(8,128)(2,1)}, bf16[128,2048]{1,0:T(8,128)(2,1)S(1)}, u32[]{:S(2)}, u32[]{:S(2)}) collective-permute-start(bf16[128,2048]{1,0:T(8,128)(2,1)} %bitcast.17), channel_id=1, source_target_pairs={{0,4},{4,0},{8,12},{12,8},{16,20},{20,16},{24,28},{28,24},{1,5},{5... | collective-permute-start | bytes 1572872 | tf_op jit(solution)/shard_map/ppermute | solution.py:23
  1.7 16.8 %collective-permute-start.4 = (bf16[128,2048]{1,0:T(8,128)(2,1)}, bf16[128,2048]{1,0:T(8,128)(2,1)S(1)}, u32[]{:S(2)}, u32[]{:S(2)}) collective-permute-start(bf16[128,2048]{1,0:T(8,128)(2,1)} %bitcast.20), channel_id=1, source_target_pairs={{0,3},{1,0},{2,1},{3,2},{4,7},{5,4},{6,5},{7,6},{8,11},{9,8},{10,9... | collective-permute-start | bytes 1572872 | tf_op jit(solution)/shard_map/ppermute | solution.py:652
  6.3 9.4 %copy-start = (bf16[1,128,2048]{2,1,0:T(8,128)(2,1)S(1)}, bf16[1,128,2048]{2,1,0:T(8,128)(2,1)}, u32[]{:S(2)}) copy-start(bf16[1,128,2048]{2,1,0:T(8,128)(2,1)} %param.7) | copy-start | bytes 1572868
  6.3 9.4 %copy-start.1 = (bf16[1,128,2048]{2,1,0:T(8,128)(2,1)S(1)}, bf16[1,128,2048]{2,1,0:T(8,128)(2,1)}, u32[]{:S(2)}) copy-start(bf16[1,128,2048]{2,1,0:T(8,128)(2,1)} %param.6) | copy-start | bytes 1572868
  6.4 9.4 %copy-start.2 = (bf16[1,128,2048]{2,1,0:T(8,128)(2,1)S(1)}, bf16[1,128,2048]{2,1,0:T(8,128)(2,1)}, u32[]{:S(2)}) copy-start(bf16[1,128,2048]{2,1,0:T(8,128)(2,1)} %param.5) | copy-start | bytes 1572868
  7.8 8.0 %copy-start.3 = (s32[3,16]{1,0:T(4,128)S(1)}, s32[3,16]{1,0:T(4,128)}, u32[]{:S(2)}) copy-start(s32[3,16]{1,0:T(4,128)} %offs_ref.11) | copy-start | bytes 580
  7.8 6.4 %collective-permute-start.6 = (bf16[32,2048]{1,0:T(8,128)(2,1)S(1)}, bf16[32,2048]{1,0:T(8,128)(2,1)S(1)}, u32[]{:S(2)}, u32[]{:S(2)}) collective-permute-start(bf16[32,2048]{1,0:T(8,128)(2,1)S(1)} %get-tuple-element.54.own3), channel_id=1, source_target_pairs={{0,8},{4,12},{8,0},{12,4},{16,24},{20,28},{24,16},{28,20},{1,9},{5... | collective-permute-start | bytes 393224 | tf_op jit(solution)/shard_map/ppermute | solution.py:23
  9.3 11.0 %collective-permute-start.5 = (bf16[64,2048]{1,0:T(8,128)(2,1)S(1)}, bf16[64,2048]{1,0:T(8,128)(2,1)S(1)}, u32[]{:S(2)}, u32[]{:S(2)}) collective-permute-start(bf16[64,2048]{1,0:T(8,128)(2,1)S(1)} %get-tuple-element.58.own2), channel_id=1, source_target_pairs={{0,8},{4,12},{8,0},{12,4},{16,24},{20,28},{24,16},{28,20},{1,9},{5... | collective-permute-start | bytes 786440 | tf_op jit(solution)/shard_map/ppermute | solution.py:23
  9.9 8.6 %collective-permute-start.3 = (bf16[32,2048]{1,0:T(8,128)(2,1)S(1)}, bf16[32,2048]{1,0:T(8,128)(2,1)S(1)}, u32[]{:S(2)}, u32[]{:S(2)}) collective-permute-start(bf16[32,2048]{1,0:T(8,128)(2,1)S(1)} %get-tuple-element.54.own3), channel_id=1, source_target_pairs={{0,16},{4,20},{8,24},{12,28},{16,0},{20,4},{24,8},{28,12},{1,17},{... | collective-permute-start | bytes 393224 | tf_op jit(solution)/shard_map/ppermute | solution.py:23
  14.2 6.2 %collective-permute-start.7 = (bf16[32,2048]{1,0:T(8,128)(2,1)S(1)}, bf16[32,2048]{1,0:T(8,128)(2,1)S(1)}, u32[]{:S(2)}, u32[]{:S(2)}) collective-permute-start(bf16[32,2048]{1,0:T(8,128)(2,1)S(1)} %collective-permute-done.6.x3), channel_id=1, source_target_pairs={{0,16},{4,20},{8,24},{12,28},{16,0},{20,4},{24,8},{28,12},{1,17},{... | collective-permute-start | bytes 393224 | tf_op jit(solution)/shard_map/ppermute | solution.py:23
  18.5 1.8 %collective-permute-start.10 = (bf16[128,384]{1,0:T(8,128)(2,1)S(1)}, bf16[128,384]{1,0:T(8,128)(2,1)S(1)}, u32[]{:S(2)}, u32[]{:S(2)}) collective-permute-start(bf16[128,384]{1,0:T(8,128)(2,1)S(1)} %get-tuple-element.62), channel_id=1, source_target_pairs={{0,4},{4,0},{8,12},{12,8},{16,20},{20,16},{24,28},{28,24},{1,5},{5... | collective-permute-start | bytes 294920 | tf_op jit(solution)/shard_map/ppermute | solution.py:23
  18.6 1.8 %collective-permute-start.9 = (bf16[128,384]{1,0:T(8,128)(2,1)S(1)}, bf16[128,384]{1,0:T(8,128)(2,1)S(1)}, u32[]{:S(2)}, u32[]{:S(2)}) collective-permute-start(bf16[128,384]{1,0:T(8,128)(2,1)S(1)} %get-tuple-element.61), channel_id=1, source_target_pairs={{0,4},{4,0},{8,12},{12,8},{16,20},{20,16},{24,28},{28,24},{1,5},{5... | collective-permute-start | bytes 294920 | tf_op jit(solution)/shard_map/ppermute | solution.py:23
  19.1 1.3 %collective-permute-start.8 = (bf16[128,256]{1,0:T(8,128)(2,1)S(1)}, bf16[128,256]{1,0:T(8,128)(2,1)S(1)}, u32[]{:S(2)}, u32[]{:S(2)}) collective-permute-start(bf16[128,256]{1,0:T(8,128)(2,1)S(1)} %get-tuple-element.60), channel_id=1, source_target_pairs={{0,4},{4,0},{8,12},{12,8},{16,20},{20,16},{24,28},{28,24},{1,5},{5... | collective-permute-start | bytes 196616 | tf_op jit(solution)/shard_map/ppermute | solution.py:23
  22.6 5.9 %collective-permute-start.13 = (bf16[32,2048]{1,0:T(8,128)(2,1)S(1)}, bf16[32,2048]{1,0:T(8,128)(2,1)S(1)}, u32[]{:S(2)}, u32[]{:S(2)}) collective-permute-start(bf16[32,2048]{1,0:T(8,128)(2,1)S(1)} %get-tuple-element.75), channel_id=1, source_target_pairs={{0,16},{4,20},{8,24},{12,28},{16,0},{20,4},{24,8},{28,12},{1,17},{... | collective-permute-start | bytes 393224 | tf_op jit(solution)/shard_map/ppermute | solution.py:23
  24.2 9.0 %collective-permute-start.11 = (bf16[32,2048]{1,0:T(8,128)(2,1)S(1)}, bf16[32,2048]{1,0:T(8,128)(2,1)S(1)}, u32[]{:S(2)}, u32[]{:S(2)}) collective-permute-start(bf16[32,2048]{1,0:T(8,128)(2,1)S(1)} %get-tuple-element.72), channel_id=1, source_target_pairs={{0,8},{4,12},{8,0},{12,4},{16,24},{20,28},{24,16},{28,20},{1,9},{5... | collective-permute-start | bytes 393224 | tf_op jit(solution)/shard_map/ppermute | solution.py:23
  25.7 8.2 %collective-permute-start.12 = (bf16[32,2048]{1,0:T(8,128)(2,1)S(1)}, bf16[32,2048]{1,0:T(8,128)(2,1)S(1)}, u32[]{:S(2)}, u32[]{:S(2)}) collective-permute-start(bf16[32,2048]{1,0:T(8,128)(2,1)S(1)} %get-tuple-element.73), channel_id=1, source_target_pairs={{0,12},{4,8},{8,4},{12,0},{16,28},{20,24},{24,20},{28,16},{1,13},{... | collective-permute-start | bytes 393224 | tf_op jit(solution)/shard_map/ppermute | solution.py:23
  25.7 8.3 %collective-permute-start.16 = (bf16[32,2048]{1,0:T(8,128)(2,1)S(1)}, bf16[32,2048]{1,0:T(8,128)(2,1)S(1)}, u32[]{:S(2)}, u32[]{:S(2)}) collective-permute-start(bf16[32,2048]{1,0:T(8,128)(2,1)S(1)} %get-tuple-element.78), channel_id=1, source_target_pairs={{0,16},{4,20},{8,24},{12,28},{16,0},{20,4},{24,8},{28,12},{1,17},{... | collective-permute-start | bytes 393224 | tf_op jit(solution)/shard_map/ppermute | solution.py:23
  28.5 6.1 %collective-permute-start.14 = (bf16[16,2048]{1,0:T(8,128)(2,1)S(1)}, bf16[16,2048]{1,0:T(8,128)(2,1)S(1)}, u32[]{:S(2)}, u32[]{:S(2)}) collective-permute-start(bf16[16,2048]{1,0:T(8,128)(2,1)S(1)} %get-tuple-element.76), channel_id=1, source_target_pairs={{0,8},{4,12},{8,0},{12,4},{16,24},{20,28},{24,16},{28,20},{1,9},{5... | collective-permute-start | bytes 196616 | tf_op jit(solution)/shard_map/ppermute | solution.py:23
  30.1 4.6 %collective-permute-start.15 = (bf16[16,2048]{1,0:T(8,128)(2,1)S(1)}, bf16[16,2048]{1,0:T(8,128)(2,1)S(1)}, u32[]{:S(2)}, u32[]{:S(2)}) collective-permute-start(bf16[16,2048]{1,0:T(8,128)(2,1)S(1)} %get-tuple-element.77), channel_id=1, source_target_pairs={{0,12},{4,8},{8,4},{12,0},{16,28},{20,24},{24,20},{28,16},{1,13},{... | collective-permute-start | bytes 196616 | tf_op jit(solution)/shard_map/ppermute | solution.py:23
  33.1 3.0 %collective-permute-start.18 = (bf16[128,768]{1,0:T(8,128)(2,1)S(1)}, bf16[128,768]{1,0:T(8,128)(2,1)S(1)}, u32[]{:S(2)}, u32[]{:S(2)}) collective-permute-start(bf16[128,768]{1,0:T(8,128)(2,1)S(1)} %get-tuple-element.88), channel_id=1, source_target_pairs={{0,4},{4,0},{8,12},{12,8},{16,20},{20,16},{24,28},{28,24},{1,5},{5... | collective-permute-start | bytes 589832 | tf_op jit(solution)/shard_map/ppermute | solution.py:23
  33.9 2.3 %collective-permute-start.19 = (bf16[128,768]{1,0:T(8,128)(2,1)S(1)}, bf16[128,768]{1,0:T(8,128)(2,1)S(1)}, u32[]{:S(2)}, u32[]{:S(2)}) collective-permute-start(bf16[128,768]{1,0:T(8,128)(2,1)S(1)} %get-tuple-element.89), channel_id=1, source_target_pairs={{0,4},{4,0},{8,12},{12,8},{16,20},{20,16},{24,28},{28,24},{1,5},{5... | collective-permute-start | bytes 589832 | tf_op jit(solution)/shard_map/ppermute | solution.py:23
  33.9 2.2 %collective-permute-start.20 = (bf16[128,768]{1,0:T(8,128)(2,1)S(1)}, bf16[128,768]{1,0:T(8,128)(2,1)S(1)}, u32[]{:S(2)}, u32[]{:S(2)}) collective-permute-start(bf16[128,768]{1,0:T(8,128)(2,1)S(1)} %get-tuple-element.90), channel_id=1, source_target_pairs={{0,4},{4,0},{8,12},{12,8},{16,20},{20,16},{24,28},{28,24},{1,5},{5... | collective-permute-start | bytes 589832 | tf_op jit(solution)/shard_map/ppermute | solution.py:23
  34.6 1.9 %collective-permute-start.21 = (bf16[128,768]{1,0:T(8,128)(2,1)S(1)}, bf16[128,768]{1,0:T(8,128)(2,1)S(1)}, u32[]{:S(2)}, u32[]{:S(2)}) collective-permute-start(bf16[128,768]{1,0:T(8,128)(2,1)S(1)} %get-tuple-element.91), channel_id=1, source_target_pairs={{0,4},{4,0},{8,12},{12,8},{16,20},{20,16},{24,28},{28,24},{1,5},{5... | collective-permute-start | bytes 589832 | tf_op jit(solution)/shard_map/ppermute | solution.py:23
  35.2 1.3 %collective-permute-start.17 = (bf16[32,2048]{1,0:T(8,128)(2,1)S(1)}, bf16[32,2048]{1,0:T(8,128)(2,1)S(1)}, u32[]{:S(2)}, u32[]{:S(2)}) collective-permute-start(bf16[32,2048]{1,0:T(8,128)(2,1)S(1)} %collective-permute-done.16.y), channel_id=1, source_target_pairs={{0,4},{4,0},{8,12},{12,8},{16,20},{20,16},{24,28},{28,24},{1,5},{5... | collective-permute-start | bytes 393224 | tf_op jit(solution)/shard_map/ppermute | solution.py:23
